TPU v7x, 32 devices: a whole 2x2x4 slice. The times are simulated.
32 devices in a mesh: gx: 4 (over z), gy: 2 (over x), gz: 4 (over y, core).
Axes of the slice: x: 2, y: 2, z: 4, core: 2. Of those that a mesh axis runs over, the one named last changes fastest.
Arguments:
- magnetization: float32 [3, 64, 256, 256], P(None, 'gz', 'gx', 'gy'), may hold values from -6 to 6
- stiffness: float32 [64, 256, 256], P('gz', 'gx', 'gy'), may hold values from 0.02 to 0.2
- residual_top: float32 [256, 256], P('gx', ('gy', 'gz')), may hold values from -6 to 6
- residual_side: float32 [256, 64], P('gy', 'gz'), may hold values from -6 to 6
- top_kernel: float32 [2, 2, 2048, 2048], P(None, None, ('gx', 'gy', 'gz')), may hold values from -6 to 6
- side_kernel: float32 [2, 2, 128, 2048], P(None, None, ('gy', 'gz')), may hold values from -6 to 6
Outputs:
- gradient: float32 [3, 64, 256, 256], P(None, 'gz', 'gx', 'gy')
All inputs are finite; a program needn't handle non-finite values.
Results may differ from a plain program's by a relative error of at most 0.0001.
Values sent between devices are 32-bit elements; how exact they have to be, the bound alone decides.
No kernel may reach another device: no remote copies, remote signals or barrier semaphores. Data moves between devices by JAX's collectives and lax.ppermute only.
A program may use at most 64 MiB of HBM per device.

v0:
```python
import functools
import math

import jax
import jax.numpy as jnp
import ml_dtypes
import numpy as np
from jax import lax
from jax.experimental import pallas as pl
from jax.experimental.pallas import tpu as pltpu
from jax.sharding import PartitionSpec as P

LANES = 128
TILE = 8
INNER = 256
ALL = ("gx", "gy", "gz")
f32 = jnp.float32
bf16 = jnp.bfloat16


def split(values):
    high = values.astype(bf16)
    return high, (values - high.astype(f32)).astype(bf16)


def dot3(left, right):
    high, low = split(left)
    def one(a, b):
        return lax.dot_general(a, b, (((1,), (0,)), ((), ())), preferred_element_type=f32)
    return one(high, right[0]) + one(low, right[0]) + one(high, right[1])


def transform_tables(extent, size):
    x = np.arange(extent)
    angle = (np.outer(x, np.arange(INNER)) % size) * (2.0 * math.pi / size)
    forward = np.concatenate([np.cos(angle), np.sin(angle)], 0).astype(np.float32)
    backward = np.concatenate([np.cos(angle).T, np.sin(angle).T], 0).astype(np.float32)

    def parts(table):
        high = table.astype(ml_dtypes.bfloat16)
        return high, (table - high.astype(np.float32)).astype(ml_dtypes.bfloat16)

    outer = size // INNER
    turn = (np.outer(np.arange(outer), x) % outer) * (2.0 * math.pi / outer)
    turns = np.stack([np.cos(turn), np.sin(turn)]).astype(np.float32)
    return parts(forward), parts(backward), turns


def phases(first, second, size):
    angle = (first * second % size).astype(f32) * (2.0 * math.pi / size)
    return jnp.cos(angle), jnp.sin(angle)


def image_kernel(
    counts, gathered, y_table, z_table, fh, fl, bh, bl, turns, top, side, y_back, z_back, out
):
    count_x, count_y, count_z, top_rows = counts
    group = count_y * count_z
    half = LANES // 2
    kys = top.shape[2]
    kzs = side.shape[2]
    forward = (fh[...], fl[...])
    backward = (bh[...], bl[...])

    blocks = [
        gathered[g * group : (g + 1) * group, 0:top_rows, :].reshape(group * top_rows, LANES)
        for g in range(count_x)
    ]
    mixed = dot3(y_table[...], split(jnp.concatenate(blocks, axis=1)))
    low_half, high_half = mixed[: 2 * kys], mixed[2 * kys :]
    lane = lax.broadcasted_iota(jnp.int32, (2 * kys, LANES), 1)
    pieces = []
    for g in range(0, count_x, 2):
        a = slice(g * LANES, (g + 1) * LANES)
        b = slice((g + 1) * LANES, (g + 2) * LANES)
        pieces.append(
            jnp.where(
                lane < half,
                low_half[:, a] + pltpu.roll(high_half[:, a], half, 1),
                pltpu.roll(low_half[:, b], half, 1) + high_half[:, b],
            )
        )
    top_lines = jnp.concatenate(pieces, axis=1)

    side_blocks = []
    for y in range(count_y):
        rows = [
            gathered[(x * count_y + y) * count_z + z, top_rows : top_rows + TILE, :]
            for x in range(count_x)
            for z in range(count_z)
        ]
        side_blocks.append(jnp.concatenate(rows, axis=0))
    side_lines = dot3(z_table[...], split(jnp.concatenate(side_blocks, axis=1)))

    real = jnp.concatenate([top_lines[:kys], side_lines[:kzs]], axis=0)
    imag = jnp.concatenate([top_lines[kys:], side_lines[kzs:]], axis=0)
    rows = kys + kzs
    total_real = total_imag = None
    for b in range(turns.shape[1]):
        cosine, sine = turns[0, b : b + 1, :], turns[1, b : b + 1, :]
        turned_real = real * cosine + imag * sine
        turned_imag = imag * cosine - real * sine
        waves = dot3(
            jnp.concatenate(
                [
                    jnp.concatenate([turned_real, turned_imag], axis=1),
                    jnp.concatenate([turned_imag, -turned_real], axis=1),
                ],
                axis=0,
            ),
            forward,
        )
        wave_real, wave_imag = waves[:rows], waves[rows:]
        columns = slice(b * INNER, (b + 1) * INNER)
        weighted_real, weighted_imag = [], []
        for c in range(2):
            for kernel, part in ((top, slice(0, kys)), (side, slice(kys, rows))):
                kernel_real, kernel_imag = kernel[c, 0, :, columns], kernel[c, 1, :, columns]
                weighted_real.append(
                    kernel_real * wave_real[part] + kernel_imag * wave_imag[part]
                )
                weighted_imag.append(
                    kernel_real * wave_imag[part] - kernel_imag * wave_real[part]
                )
        weighted_real = jnp.concatenate(weighted_real, axis=0)
        weighted_imag = jnp.concatenate(weighted_imag, axis=0)
        back = dot3(
            jnp.concatenate(
                [
                    jnp.concatenate([weighted_real, -weighted_imag], axis=1),
                    jnp.concatenate([weighted_imag, weighted_real], axis=1),
                ],
                axis=0,
            ),
            backward,
        )
        back_real, back_imag = back[: 2 * rows], back[2 * rows :]
        if b == 0:
            total_real, total_imag = back_real, back_imag
        else:
            total_real = total_real + (back_real * cosine - back_imag * sine)
            total_imag = total_imag + (back_real * sine + back_imag * cosine)

    y_parts = split(y_back[...])
    depth_rows = []
    quarter = (out.shape[1] - TILE) // 2
    block_x = quarter * count_z
    for c in range(2):
        start = c * rows
        lines = jnp.concatenate(
            [total_real[start : start + kys], total_imag[start : start + kys]], axis=0
        )
        image = dot3(lines.T, y_parts)
        for x in range(count_x):
            for y in range(count_y):
                for z in range(count_z):
                    first = x * block_x + z * quarter
                    out[
                        (x * count_y + y) * count_z + z, c * quarter : (c + 1) * quarter, :
                    ] = image[first : first + quarter, y * LANES : (y + 1) * LANES]
        depth_rows.append(total_real[start + kys : start + rows])
        depth_rows.append(total_imag[start + kys : start + rows])
    side_image = dot3(z_back[...], split(jnp.concatenate(depth_rows, axis=0)))
    for y in range(count_y):
        for z in range(count_z):
            block = side_image[z * TILE : (z + 1) * TILE, y * LANES : (y + 1) * LANES]
            for x in range(count_x):
                out[(x * count_y + y) * count_z + z, 2 * quarter :, :] = block


def image_parts(gathered, top_kernel, side_kernel, counts, block_x, top_rows, depth_block):
    count_x, count_y, count_z = counts
    group = count_y * count_z
    here = [lax.axis_index(axis) for axis in ALL]
    kys, size = top_kernel.shape[2:]
    kzs = side_kernel.shape[2]
    depth_size = kzs * group
    extent = count_y * LANES
    share = depth_block // count_x
    block_y = top_rows * 2

    ky = ((here[0] * count_y + here[1]) * count_z + here[2]) * kys + lax.iota(jnp.int32, kys)
    kz = (here[1] * count_z + here[2]) * kzs + lax.iota(jnp.int32, kzs)

    row = lax.iota(jnp.int32, group * top_rows)
    y_tables = []
    for h in range(2):
        y = row // top_rows * block_y + h * top_rows + row % top_rows
        cosine, sine = phases(ky[:, None], y[None, :], size)
        y_tables += [cosine, -sine]
    y_table = jnp.concatenate(y_tables, axis=0)

    row = lax.iota(jnp.int32, count_x * count_z * TILE)
    inside = row % TILE
    z = row // TILE % count_z * depth_block + row // (TILE * count_z) * share + inside
    cosine, sine = phases(kz[:, None], z[None, :], depth_size)
    z_table = jnp.where((inside < share)[None, :], jnp.concatenate([cosine, -sine], axis=0), 0.0)

    cosine, sine = phases(ky[:, None], lax.iota(jnp.int32, extent)[None, :], size)
    y_back = jnp.concatenate([cosine, -sine], axis=0) * (1.0 / (size * size))

    row = lax.iota(jnp.int32, count_z * TILE)
    z = row // TILE * depth_block + here[0] * share + row % TILE % share
    cosine, sine = phases(z[:, None], kz[None, :], depth_size)
    both = jnp.concatenate([cosine, -sine], axis=1) * (1.0 / (size * depth_size))
    component = (row % TILE // share)[:, None]
    z_back = jnp.concatenate(
        [jnp.where(component == 0, both, 0.0), jnp.where(component == 1, both, 0.0)], axis=1
    )

    forward, backward, turns = transform_tables(extent, size)
    out_rows = 2 * (block_x // count_z) + TILE
    return pl.pallas_call(
        functools.partial(image_kernel, counts + (top_rows,)),
        out_shape=jax.ShapeDtypeStruct((count_x * group, out_rows, LANES), f32),
        compiler_params=pltpu.CompilerParams(vmem_limit_bytes=56 * 1024 * 1024),
        name="images",
    )(
        gathered,
        y_table,
        z_table,
        *(jnp.asarray(t) for t in forward + backward),
        jnp.asarray(turns),
        top_kernel,
        side_kernel,
        y_back,
        z_back,
    )


def faces_kernel(magnetization, stiffness, z_first, z_last, x_first, x_last, y_faces):
    depth, across = stiffness.shape[:2]
    lane = lax.broadcasted_iota(jnp.int32, (across, LANES), 1)
    sides = jnp.zeros((across, LANES), f32)
    for field in range(4):
        ref = stiffness if field == 3 else magnetization.at[field]
        z_first[field] = ref[0]
        z_last[field] = ref[depth - 1]
        x_first[field] = ref[:, 0, :]
        x_last[field] = ref[:, across - 1, :]
        for z in range(depth):
            column = field * depth + z
            values = ref[z]
            sides = jnp.where(lane == column, values[:, 0:1], sides)
            sides = jnp.where(lane == column + 4 * depth, values[:, LANES - 1 : LANES], sides)
    y_faces[...] = sides


def exchange_kernel(
    magnetization,
    stiffness,
    z_next,
    z_before,
    x_next,
    x_before,
    y_next,
    y_before,
    out,
):
    depth, across = stiffness.shape[:2]
    lane = lax.broadcasted_iota(jnp.int32, (across, LANES), 1)
    sublane = lax.broadcasted_iota(jnp.int32, (across, LANES), 0)
    last_lane, first_lane = lane == LANES - 1, lane == 0
    last_row, first_row = sublane == across - 1, sublane == 0

    def weight(a, b):
        return 2.0 * a * b / (a + b)

    def one(z, field):
        ref = stiffness if field == 3 else magnetization.at[field]
        centre = ref[z]
        column = field * depth + z
        along = jnp.where(
            last_lane, y_next[:, column : column + 1], pltpu.roll(centre, LANES - 1, 1)
        )
        across_next = jnp.where(
            last_row, x_next[field, z : z + 1, :], pltpu.roll(centre, across - 1, 0)
        )
        along_before = y_before[:, 4 * depth + column : 4 * depth + column + 1]
        across_before = x_before[field, z : z + 1, :]
        return centre, along, across_next, along_before, across_before

    below_weight = weight(z_before[3], stiffness[0])
    below = [below_weight * (z_before[c] - magnetization[c, 0]) for c in range(3)]
    for z in range(depth):
        s, s_along, s_across, s_along_before, s_across_before = one(z, 3)
        s_above = stiffness[z + 1] if z + 1 < depth else z_next[3]
        w_along, w_across, w_above = weight(s, s_along), weight(s, s_across), weight(s, s_above)
        w_along_before = weight(s_along_before, s[:, 0:1])
        w_across_before = weight(s_across_before, s[0:1, :])
        for c in range(3):
            m, m_along, m_across, m_along_before, m_across_before = one(z, c)
            m_above = magnetization[c, z + 1] if z + 1 < depth else z_next[c]
            up = w_above * (m - m_above)
            flux_along = w_along * (m - m_along)
            flux_across = w_across * (m - m_across)
            edge_along = w_along_before * (m_along_before - m[:, 0:1])
            edge_across = w_across_before * (m_across_before - m[0:1, :])
            lower_along = jnp.where(first_lane, edge_along, pltpu.roll(flux_along, 1, 1))
            lower_across = jnp.where(first_row, edge_across, pltpu.roll(flux_across, 1, 0))
            total = (up - below[c]) + (flux_across - lower_across) + (flux_along - lower_along)
            out[c, z] = 2.0 * total
            below[c] = up


def shifted(block, axis, distance):
    count = lax.axis_size(axis)
    route = [(i, i + distance) for i in range(count) if 0 <= i + distance < count]
    return lax.ppermute(block, axis, route)


def exchange(magnetization, stiffness):
    depth, across, along = stiffness.shape
    shape = jax.ShapeDtypeStruct
    z_first, z_last, x_first, x_last, y_faces = pl.pallas_call(
        faces_kernel,
        out_shape=[
            shape((4, across, along), f32),
            shape((4, across, along), f32),
            shape((4, depth, along), f32),
            shape((4, depth, along), f32),
            shape((across, LANES), f32),
        ],
        name="faces",
    )(magnetization, stiffness)
    z_next, z_before = shifted(z_first, "gz", -1), shifted(z_last, "gz", 1)
    x_next, x_before = shifted(x_first, "gx", -1), shifted(x_last, "gx", 1)
    if lax.axis_size("gy") == 2:
        other = lax.ppermute(y_faces, "gy", [(0, 1), (1, 0)])
        at = lax.axis_index("gy")
        y_next, y_before = jnp.where(at == 0, other, 0.0), jnp.where(at == 1, other, 0.0)
    else:
        y_next, y_before = shifted(y_faces, "gy", -1), shifted(y_faces, "gy", 1)
    return pl.pallas_call(
        exchange_kernel,
        out_shape=shape(magnetization.shape, f32),
        compiler_params=pltpu.CompilerParams(vmem_limit_bytes=32 * 1024 * 1024),
        name="exchange",
    )(magnetization, stiffness, z_next, z_before, x_next, x_before, y_next, y_before)


def on_device(magnetization, stiffness, residual_top, residual_side, top_kernel, side_kernel):
    counts = tuple(lax.axis_size(axis) for axis in ALL)
    count_x, count_y, count_z = counts
    devices = count_x * count_y * count_z
    depth_block = stiffness.shape[0]
    block_x, block_y = residual_top.shape
    top_rows = block_y // 2
    share = depth_block // count_x

    top_piece = residual_top.T.reshape(2, top_rows, block_x)
    top_piece = jnp.concatenate([top_piece[0], top_piece[1]], axis=1)
    side_piece = lax.dynamic_slice_in_dim(
        residual_side.T, lax.axis_index("gx") * share, share, axis=0
    )
    piece = jnp.concatenate(
        [top_piece, side_piece, jnp.zeros((TILE - share, LANES), f32)], axis=0
    )
    rows = piece.shape[0]
    sent = jnp.broadcast_to(piece[None], (devices, rows, LANES)).reshape(devices * rows, LANES)
    gathered = lax.all_to_all(sent, ALL, 0, 0, tiled=True).reshape(devices, rows, LANES)

    exchange_grad = exchange(magnetization, stiffness)

    parts = image_parts(
        gathered, top_kernel, side_kernel, counts, block_x, top_rows, depth_block
    )
    rows = parts.shape[1]
    arrived = lax.all_to_all(parts.reshape(devices * rows, LANES), ALL, 0, 0, tiled=True)
    arrived = arrived.reshape(devices, rows, LANES)
    top_sum = jnp.sum(arrived[:, : rows - TILE], axis=0)
    side_sum = jnp.sum(
        arrived[:, rows - TILE :].reshape(count_x, count_y * count_z, TILE, LANES), axis=1
    )
    side = side_sum[:, : 2 * share].reshape(count_x, 2, share, LANES)
    side = jnp.swapaxes(side, 0, 1).reshape(2, depth_block, 1, LANES)
    top = lax.all_gather(top_sum, "gz", axis=0)
    top = jnp.swapaxes(top.reshape(count_z, 2, block_x // count_z, LANES), 0, 1)
    top = top.reshape(2, 1, block_x, LANES)
    return jnp.stack(
        [
            exchange_grad[0] + top[0],
            exchange_grad[1] + top[1] + side[0],
            exchange_grad[2] + side[1],
        ]
    )


def solution(mesh):
    placed = (
        P(None, "gz", "gx", "gy"),
        P("gz", "gx", "gy"),
        P("gx", ("gy", "gz")),
        P("gy", "gz"),
        P(None, None, ("gx", "gy", "gz"), None),
        P(None, None, ("gy", "gz"), None),
    )
    return jax.shard_map(
        on_device, mesh=mesh, in_specs=placed, out_specs=P(None, "gz", "gx", "gy"), check_vma=False
    )
```

profile of v0, /device:TPU:0, one launch (start us, length us, event | category | flops | bytes accessed | tf_op | source)
XLA Modules:
  0.0 71.8 jit_solution(5457984768536621718)
XLA Ops:
  0.0 0.7 %fusion.37 = (f32[16,64]{1,0:T(8,128)S(1)}, f32[16,64]{1,0:T(8,128)S(1)}) fusion(f32[32,64]{1,0:T(8,128)} %bitcast.21), kind=kLoop, calls=%fused_computation.113 | loop fusion | bytes 16384 | tf_op jit(solution)/shard_map/slice | solution.py:352
  0.7 0.1 pad.18.clone
  0.8 0.1 maximum_maximum_fusion
  0.9 0.8 %broadcast_in_dim.58 = f32[32,24,128]{2,1,0:T(8,128)} broadcast(f32[24,128]{1,0:T(8,128)S(1)} %maximum_maximum_fusion), dimensions={1,2} | broadcast | bytes 405504 | tf_op jit(solution)/shard_map/broadcast_in_dim | solution.py:360
  1.7 7.3 %all-to-all-start = ((f32[32,24,128]{2,1,0:T(8,128)}), f32[32,24,128]{2,1,0:T(8,128)S(1)}, u32[]{:S(2)}, u32[]{:S(2)}) async-start(f32[32,24,128]{2,1,0:T(8,128)} %broadcast_in_dim.58), calls=%async_computation | async-start | bytes 786432 | tf_op jit(solution)/shard_map/all_to_all | solution.py:361
  9.1 0.3 fusion.13
  9.4 0.2 fusion.22
  9.6 0.1 broadcast_select_fusion.3
  9.7 0.7 pad_maximum_fusion.2.z_back
  10.4 0.7 maximum_multiply_fusion.y_back
  11.0 0.3 fusion.18
  11.4 0.7 pad_maximum_fusion.1.y_table
  12.0 0.1 fusion.23
  12.2 0.6 maximum_select_fusion.z_table
  12.8 9.4 %all-to-all-done.gathered = f32[32,24,128]{2,1,0:T(8,128)S(1)} async-done(((f32[32,24,128]{2,1,0:T(8,128)}), f32[32,24,128]{2,1,0:T(8,128)S(1)}, u32[]{:S(2)}, u32[]{:S(2)}) %all-to-all-start) | async-done | bytes 393248 | tf_op jit(solution)/shard_map/all_to_all | solution.py:361
  22.2 0.8 %copy-done.3 = f32[32,24,128]{2,1,0:T(8,128)} copy-done((f32[32,24,128]{2,1,0:T(8,128)}, f32[32,24,128]{2,1,0:T(8,128)S(1)}, u32[]{:S(2)}) %copy-start.3) | copy-done | bytes 393240
  22.9 8.2 %images.1 = f32[32,40,128]{2,1,0:T(8,128)} custom-call(f32[32,24,128]{2,1,0:T(8,128)} %copy-done.3, f32[256,128]{1,0:T(8,128)} %pad_maximum_fusion.1.y_table, f32[32,128]{1,0:T(8,128)} %maximum_select_fusion.z_table, bf16[512,256]{1,0:T(8,128)(2,1)} %constant.212.clone.fh.bh, bf16[512,256]{1,0:T(8,128)(2,1)} %constant.213.clone.fl.bl, ...), custom_call_target="tpu_custom_call" | custom-call | tf_op jit(solution)/shard_map/images/pallas_call | solution.py:213
  31.2 3.5 %all-to-all-start.1 = ((f32[32,40,128]{2,1,0:T(8,128)}), f32[32,40,128]{2,1,0:T(8,128)}, u32[]{:S(2)}, u32[]{:S(2)}) async-start(f32[32,40,128]{2,1,0:T(8,128)} %images.1), calls=%async_computation.1 | async-start | bytes 1310720 | tf_op jit(solution)/shard_map/all_to_all | solution.py:369
  34.6 3.6 %faces.1 = (f32[4,64,128]{2,1,0:T(8,128)}, f32[4,64,128]{2,1,0:T(8,128)}, f32[4,16,128]{2,1,0:T(8,128)}, f32[4,16,128]{2,1,0:T(8,128)}, f32[64,128]{1,0:T(8,128)}) custom-call(f32[3,16,64,128]{3,2,1,0:T(8,128)} %magnetization.3, f32[16,64,128]{2,1,0:T(8,128)} %stiffness.3), custom_call_target="tpu_custom_call" | custom-call | tf_op jit(solution)/shard_map/faces/pallas_call | solution.py:315
  38.2 1.6 %collective-permute-start.4 = (f32[64,128]{1,0:T(8,128)}, f32[64,128]{1,0:T(8,128)S(1)}, u32[]{:S(2)}, u32[]{:S(2)}) collective-permute-start(f32[64,128]{1,0:T(8,128)} %get-tuple-element.14), channel_id=1, source_target_pairs={{0,4},{4,0},{1,5},{5,1},{2,6},{6,2},{3,7},{7,3},{8,12},{12,8},{9,1... | collective-permute-start | bytes 98312 | tf_op jit(solution)/shard_map/ppermute | solution.py:329
  39.8 1.3 %collective-permute-start.2 = (f32[4,16,128]{2,1,0:T(8,128)}, f32[4,16,128]{2,1,0:T(8,128)S(1)}, u32[]{:S(2)}, u32[]{:S(2)}) collective-permute-start(f32[4,16,128]{2,1,0:T(8,128)} %get-tuple-element.12), channel_id=1, source_target_pairs={{8,0},{16,8},{24,16},{9,1},{17,9},{25,17},{10,2},{18,10},{26,18},{... | collective-permute-start | bytes 98312 | tf_op jit(solution)/shard_map/ppermute | solution.py:309
  41.1 4.5 %collective-permute-start.3 = (f32[4,16,128]{2,1,0:T(8,128)}, f32[4,16,128]{2,1,0:T(8,128)S(1)}, u32[]{:S(2)}, u32[]{:S(2)}) collective-permute-start(f32[4,16,128]{2,1,0:T(8,128)} %get-tuple-element.13), channel_id=1, source_target_pairs={{0,8},{8,16},{16,24},{1,9},{9,17},{17,25},{2,10},{10,18},{18,26},{... | collective-permute-start | bytes 98312 | tf_op jit(solution)/shard_map/ppermute | solution.py:309
  45.6 1.3 %collective-permute-start = (f32[4,64,128]{2,1,0:T(8,128)}, f32[4,64,128]{2,1,0:T(8,128)S(1)}, u32[]{:S(2)}, u32[]{:S(2)}) collective-permute-start(f32[4,64,128]{2,1,0:T(8,128)} %get-tuple-element.10), channel_id=1, source_target_pairs={{1,0},{2,1},{3,2},{5,4},{6,5},{7,6},{9,8},{10,9},{11,10},{13,12},{... | collective-permute-start | bytes 393224 | tf_op jit(solution)/shard_map/ppermute | solution.py:309
  46.9 3.0 %collective-permute-start.1 = (f32[4,64,128]{2,1,0:T(8,128)}, f32[4,64,128]{2,1,0:T(8,128)S(1)}, u32[]{:S(2)}, u32[]{:S(2)}) collective-permute-start(f32[4,64,128]{2,1,0:T(8,128)} %get-tuple-element.11), channel_id=1, source_target_pairs={{0,1},{1,2},{2,3},{4,5},{5,6},{6,7},{8,9},{9,10},{10,11},{12,13},{... | collective-permute-start | bytes 393224 | tf_op jit(solution)/shard_map/ppermute | solution.py:309
  50.1 1.1 %collective-permute-done.1.z_before = f32[4,64,128]{2,1,0:T(8,128)S(1)} collective-permute-done((f32[4,64,128]{2,1,0:T(8,128)}, f32[4,64,128]{2,1,0:T(8,128)S(1)}, u32[]{:S(2)}, u32[]{:S(2)}) %collective-permute-start.1) | collective-permute-done | bytes 131104 | tf_op jit(solution)/shard_map/ppermute | solution.py:309
  51.2 1.0 %copy-done.2 = f32[16,64,128]{2,1,0:T(8,128)S(1)} copy-done((f32[16,64,128]{2,1,0:T(8,128)S(1)}, f32[16,64,128]{2,1,0:T(8,128)}, u32[]{:S(2)}) %copy-start.2) | copy-done | bytes 524312
  52.2 8.4 %exchange.1 = f32[3,16,64,128]{3,2,1,0:T(8,128)S(1)} custom-call(f32[3,16,64,128]{3,2,1,0:T(8,128)S(1)} %copy-done.1, f32[16,64,128]{2,1,0:T(8,128)S(1)} %copy-done.2, f32[4,64,128]{2,1,0:T(8,128)S(1)} %collective-permute-done.z_next, f32[4,64,128]{2,1,0:T(8,128)S(1)} %collective-permute-done.1.z_before, f32[4,16,128]{2,1,0:T(8,128)S(1)} %collective-permute-done.2.x_next, ...), custom_call_target="tpu_custom_call" | custom-call | tf_op jit(solution)/shard_map/exchange/pallas_call | solution.py:334
  60.6 0.9 %bitcast_reduce_fusion = f32[4,8,128]{2,1,0:T(8,128)S(1)} fusion(f32[32,40,128]{2,1,0:T(8,128)} %all-to-all-done.1), kind=kLoop, calls=%fused_computation.8 | loop fusion | flops 28672 | bytes 147456 | tf_op jit(solution)/shard_map/reduce_sum | solution.py:372
  61.5 1.1 %slice_reduce_fusion = f32[32,128]{1,0:T(8,128)S(1)} fusion(f32[32,40,128]{2,1,0:T(8,128)} %all-to-all-done.1), kind=kLoop, calls=%fused_computation.4 | loop fusion | flops 126976 | bytes 540672 | tf_op jit(solution)/shard_map/reduce_sum | solution.py:371
  62.6 7.6 %all-gather = f32[128,128]{1,0:T(8,128)S(1)} all-gather(f32[32,128]{1,0:T(8,128)S(1)} %slice_reduce_fusion), channel_id=2, replica_groups=mesh['gx'=4,'gy'=2,'gz'=4] {'gz'}, dimensions={0}, use_global_device_ids=true | all-gather | bytes 81920 | tf_op jit(solution)/shard_map/all_gather | solution.py:377
  70.3 0.2 slice_add_fusion.2
  70.5 1.3 %pad_maximum_fusion = f32[3,16,64,128]{3,2,1,0:T(8,128)} fusion(f32[1,16,64,128]{3,2,1,0:T(8,128)S(1)} %get-tuple-element.16, f32[1,16,64,128]{3,2,1,0:T(8,128)S(1)} %get-tuple-element.17, f32[1,16,64,128]{3,2,1,0:T(8,128)S(1)} %get-tuple-element.15), kind=kLoop, calls=%fused_computation | loop fusion | flops 786432 | bytes 3145728 | tf_op jit(solution)/shard_map/stack | solution.py:380
  (23 shorter events, 0.1 us)
Async XLA Ops:
  0.0 0.8 %copy-start = (f32[128,16]{0,1:T(8,128)S(1)}, f32[128,16]{0,1:T(8,128)}, u32[]{:S(2)}) copy-start(f32[128,16]{0,1:T(8,128)} %param.14) | copy-start | bytes 24580
  1.7 20.5 %all-to-all-start = ((f32[32,24,128]{2,1,0:T(8,128)}), f32[32,24,128]{2,1,0:T(8,128)S(1)}, u32[]{:S(2)}, u32[]{:S(2)}) async-start(f32[32,24,128]{2,1,0:T(8,128)} %broadcast_in_dim.58), calls=%async_computation | async-start | bytes 786432 | tf_op jit(solution)/shard_map/all_to_all | solution.py:361
  22.2 0.8 %copy-start.3 = (f32[32,24,128]{2,1,0:T(8,128)}, f32[32,24,128]{2,1,0:T(8,128)S(1)}, u32[]{:S(2)}) copy-start(f32[32,24,128]{2,1,0:T(8,128)S(1)} %all-to-all-done.gathered) | copy-start | bytes 1179652
  31.2 20.0 %copy-start.1 = (f32[3,16,64,128]{3,2,1,0:T(8,128)S(1)}, f32[3,16,64,128]{3,2,1,0:T(8,128)}, u32[]{:S(2)}) copy-start(f32[3,16,64,128]{3,2,1,0:T(8,128)} %magnetization.3) | copy-start | bytes 4718596
  31.2 29.4 %all-to-all-start.1 = ((f32[32,40,128]{2,1,0:T(8,128)}), f32[32,40,128]{2,1,0:T(8,128)}, u32[]{:S(2)}, u32[]{:S(2)}) async-start(f32[32,40,128]{2,1,0:T(8,128)} %images.1), calls=%async_computation.1 | async-start | bytes 1310720 | tf_op jit(solution)/shard_map/all_to_all | solution.py:369
  38.2 11.8 %collective-permute-start.4 = (f32[64,128]{1,0:T(8,128)}, f32[64,128]{1,0:T(8,128)S(1)}, u32[]{:S(2)}, u32[]{:S(2)}) collective-permute-start(f32[64,128]{1,0:T(8,128)} %get-tuple-element.14), channel_id=1, source_target_pairs={{0,4},{4,0},{1,5},{5,1},{2,6},{6,2},{3,7},{7,3},{8,12},{12,8},{9,1... | collective-permute-start | bytes 98312 | tf_op jit(solution)/shard_map/ppermute | solution.py:329
  39.8 10.2 %collective-permute-start.2 = (f32[4,16,128]{2,1,0:T(8,128)}, f32[4,16,128]{2,1,0:T(8,128)S(1)}, u32[]{:S(2)}, u32[]{:S(2)}) collective-permute-start(f32[4,16,128]{2,1,0:T(8,128)} %get-tuple-element.12), channel_id=1, source_target_pairs={{8,0},{16,8},{24,16},{9,1},{17,9},{25,17},{10,2},{18,10},{26,18},{... | collective-permute-start | bytes 98312 | tf_op jit(solution)/shard_map/ppermute | solution.py:309
  41.1 8.9 %collective-permute-start.3 = (f32[4,16,128]{2,1,0:T(8,128)}, f32[4,16,128]{2,1,0:T(8,128)S(1)}, u32[]{:S(2)}, u32[]{:S(2)}) collective-permute-start(f32[4,16,128]{2,1,0:T(8,128)} %get-tuple-element.13), channel_id=1, source_target_pairs={{0,8},{8,16},{16,24},{1,9},{9,17},{17,25},{2,10},{10,18},{18,26},{... | collective-permute-start | bytes 98312 | tf_op jit(solution)/shard_map/ppermute | solution.py:309
  45.6 4.4 %collective-permute-start = (f32[4,64,128]{2,1,0:T(8,128)}, f32[4,64,128]{2,1,0:T(8,128)S(1)}, u32[]{:S(2)}, u32[]{:S(2)}) collective-permute-start(f32[4,64,128]{2,1,0:T(8,128)} %get-tuple-element.10), channel_id=1, source_target_pairs={{1,0},{2,1},{3,2},{5,4},{6,5},{7,6},{9,8},{10,9},{11,10},{13,12},{... | collective-permute-start | bytes 393224 | tf_op jit(solution)/shard_map/ppermute | solution.py:309
  46.9 4.2 %collective-permute-start.1 = (f32[4,64,128]{2,1,0:T(8,128)}, f32[4,64,128]{2,1,0:T(8,128)S(1)}, u32[]{:S(2)}, u32[]{:S(2)}) collective-permute-start(f32[4,64,128]{2,1,0:T(8,128)} %get-tuple-element.11), channel_id=1, source_target_pairs={{0,1},{1,2},{2,3},{4,5},{5,6},{6,7},{8,9},{9,10},{10,11},{12,13},{... | collective-permute-start | bytes 393224 | tf_op jit(solution)/shard_map/ppermute | solution.py:309
  51.2 1.0 %copy-start.2 = (f32[16,64,128]{2,1,0:T(8,128)S(1)}, f32[16,64,128]{2,1,0:T(8,128)}, u32[]{:S(2)}) copy-start(f32[16,64,128]{2,1,0:T(8,128)} %stiffness.3) | copy-start | bytes 1572868
where the time goes:
time: 72.3 us; the launch traced here: 71.8 us
  starting transfers between devices  22.5 us (31%)
  Pallas kernels  20.2 us (28%)
  waiting for transfers between devices  10.5 us (15%)
  blocking collectives  7.62 us (11%)
  other arithmetic  7.33 us (10%)
  local copies, waits for them, and re-layouts  3.41 us (5%)
    ppermute x4, starting transfers between devices, shifted(): return lax.ppermute(block, axis, route)  10.2 us
    all_to_all x1, waiting for transfers between devices, on_device(): lax.all_to_all(sent, ALL, 0, 0, tiled=True).reshape(devices, rows, LANES)  9.38 us
    pallas_call x1, Pallas kernels, exchange(): pl.pallas_call(exchange_kernel, out_shape=shape(magnetization.shape, f32)...  8.38 us
    pallas_call x1, Pallas kernels, image_parts(): pl.pallas_call(functools.partial(image_kernel, counts + (top_rows,)), out...  8.25 us
    all_gather x1, blocking collectives, on_device(): top = lax.all_gather(top_sum, 'gz', axis=0)  7.62 us
    all_to_all x1, starting transfers between devices, on_device(): lax.all_to_all(sent, ALL, 0, 0, tiled=True).reshape(devices, rows, LANES)  7.3 us
    pallas_call x1, Pallas kernels, exchange(): pl.pallas_call(faces_kernel, out_shape=[shape((4, across, along), f32), s...  3.59 us
    all_to_all x1, starting transfers between devices, on_device(): lax.all_to_all(parts.reshape(devices * rows, LANES), ALL, 0, 0, tiled=True)  3.47 us
  transfers between devices with their start and end apart: 7, of which 2 were waited for; matrix products, arithmetic and copies ran while one was open for 5% of the time, Pallas kernels for 17%

commit v1 on v0

--- a/solution.py
+++ b/solution.py
@@ -309,7 +309,7 @@
     return lax.ppermute(block, axis, route)
 
 
-def exchange(magnetization, stiffness):
+def exchange_halos(magnetization, stiffness):
     depth, across, along = stiffness.shape
     shape = jax.ShapeDtypeStruct
     z_first, z_last, x_first, x_last, y_faces = pl.pallas_call(
@@ -331,17 +331,317 @@
         y_next, y_before = jnp.where(at == 0, other, 0.0), jnp.where(at == 1, other, 0.0)
     else:
         y_next, y_before = shifted(y_faces, "gy", -1), shifted(y_faces, "gy", 1)
+    return z_next, z_before, x_next, x_before, y_next, y_before
+
+
+def exchange_of(magnetization, stiffness, halos):
     return pl.pallas_call(
         exchange_kernel,
-        out_shape=shape(magnetization.shape, f32),
+        out_shape=jax.ShapeDtypeStruct(magnetization.shape, f32),
         compiler_params=pltpu.CompilerParams(vmem_limit_bytes=32 * 1024 * 1024),
         name="exchange",
-    )(magnetization, stiffness, z_next, z_before, x_next, x_before, y_next, y_before)
+    )(magnetization, stiffness, *halos)
+
+
+def line_tables(counts, top_rows, kys, size):
+    group = counts[1] * counts[2]
+    row = np.arange(group * top_rows)
+    j = np.arange(kys)
+    start = np.arange(counts[0] * group) * kys
+    steps, offsets = [], []
+    for h in range(2):
+        y = row // top_rows * top_rows * 2 + h * top_rows + row % top_rows
+        for values, into in ((j, steps), (start, offsets)):
+            angle = (np.outer(values, y) % size) * (2.0 * math.pi / size)
+            into += [np.cos(angle), np.sin(angle)]
+    steps = np.stack(steps).astype(np.float32)
+    offsets = np.stack(offsets, axis=1).astype(np.float32)
+    return steps, np.pad(offsets, ((0, 0), (0, TILE - 4), (0, 0)))
+
+
+def depth_tables(group, kzs, depth):
+    size = group * kzs
+    kz = np.arange(size).reshape(group, kzs, 1)
+    angle = (kz * np.arange(depth) % size) * (2.0 * math.pi / size)
+    there = np.concatenate([np.cos(angle), -np.sin(angle)], axis=1).astype(np.float32)
+    back = np.swapaxes(there, 1, 2)
+    return there, back
+
+
+def stacked_product(real, imag, tables, sign):
+    if sign < 0:
+        upper = jnp.concatenate([real, imag], axis=1)
+        lower = jnp.concatenate([imag, -real], axis=1)
+    else:
+        upper = jnp.concatenate([real, -imag], axis=1)
+        lower = jnp.concatenate([imag, real], axis=1)
+    return dot3(jnp.concatenate([upper, lower], axis=0), tables)
+
+
+def back_and_forth(real, imag, kernel, high, low, turns):
+    tables = (high[...], low[...])
+    rows = real.shape[0]
+    total_real = total_imag = None
+    for b in range(turns.shape[1]):
+        cosine, sine = turns[0, b : b + 1, :], turns[1, b : b + 1, :]
+        waves = stacked_product(
+            real * cosine + imag * sine, imag * cosine - real * sine, tables, -1
+        )
+        wave_real, wave_imag = waves[:rows], waves[rows:]
+        columns = slice(b * INNER, (b + 1) * INNER)
+        weighted_real, weighted_imag = [], []
+        for c in range(2):
+            kernel_real, kernel_imag = kernel[c, 0, :, columns], kernel[c, 1, :, columns]
+            weighted_real.append(kernel_real * wave_real + kernel_imag * wave_imag)
+            weighted_imag.append(kernel_real * wave_imag - kernel_imag * wave_real)
+        back = stacked_product(
+            jnp.concatenate(weighted_real, axis=0),
+            jnp.concatenate(weighted_imag, axis=0),
+            tables,
+            1,
+        )
+        back_real, back_imag = back[: 2 * rows], back[2 * rows :]
+        if b == 0:
+            total_real, total_imag = back_real, back_imag
+        else:
+            total_real = total_real + (back_real * cosine - back_imag * sine)
+            total_imag = total_imag + (back_real * sine + back_imag * cosine)
+    return [
+        (total_real[c * rows : (c + 1) * rows], total_imag[c * rows : (c + 1) * rows])
+        for c in range(2)
+    ]
+
+
+def lines_kernel(counts, here, gathered, steps, offsets, high, low, turns, kernel, out):
+    count_x, count_y, count_z = counts
+    group = count_y * count_z
+    top_rows = gathered.shape[1]
+    half = LANES // 2
+    kys = kernel.shape[2]
+    offset = offsets[here[0]]
+    table = []
+    for h in range(2):
+        step_cos, step_sin = steps[2 * h], steps[2 * h + 1]
+        offset_cos, offset_sin = offset[2 * h : 2 * h + 1], offset[2 * h + 1 : 2 * h + 2]
+        table.append(step_cos * offset_cos - step_sin * offset_sin)
+        table.append(-(step_sin * offset_cos + step_cos * offset_sin))
+    blocks = [
+        gathered[g * group : (g + 1) * group].reshape(group * top_rows, LANES)
+        for g in range(count_x)
+    ]
+    mixed = dot3(jnp.concatenate(table, axis=0), split(jnp.concatenate(blocks, axis=1)))
+    low_half, high_half = mixed[: 2 * kys], mixed[2 * kys :]
+    lane = lax.broadcasted_iota(jnp.int32, (2 * kys, LANES), 1)
+    pieces = []
+    for g in range(0, count_x, 2):
+        a = slice(g * LANES, (g + 1) * LANES)
+        b = slice((g + 1) * LANES, (g + 2) * LANES)
+        pieces.append(
+            jnp.where(
+                lane < half,
+                low_half[:, a] + pltpu.roll(high_half[:, a], half, 1),
+                pltpu.roll(low_half[:, b], half, 1) + high_half[:, b],
+            )
+        )
+    lines = jnp.concatenate(pieces, axis=1)
+    images = back_and_forth(lines[:kys], lines[kys:], kernel, high, low, turns)
+    for c in range(2):
+        block = jnp.concatenate(images[c], axis=0).T
+        out[:, c * TILE : (c + 1) * TILE, :] = block.reshape(count_x * group, TILE, LANES)
+
+
+def side_kernel_body(counts, here, gathered, there, back, high, low, turns, kernel, out):
+    count_y, count_z = counts[1:]
+    depth_block = gathered.shape[1]
+    kzs = kernel.shape[2]
+    blocks = [
+        gathered[y * count_z : (y + 1) * count_z].reshape(count_z * depth_block, LANES)
+        for y in range(count_y)
+    ]
+    lines = dot3(there[here[0]], split(jnp.concatenate(blocks, axis=1)))
+    images = back_and_forth(lines[:kzs], lines[kzs:], kernel, high, low, turns)
+    scale = 1.0 / (count_y * count_z * kzs * kernel.shape[3])
+    for c in range(2):
+        image = dot3(back[here[0]] * scale, split(jnp.concatenate(images[c], axis=0)))
+        for y in range(count_y):
+            for z in range(count_z):
+                out[y * count_z + z, c * depth_block : (c + 1) * depth_block, :] = image[
+                    z * depth_block : (z + 1) * depth_block, y * LANES : (y + 1) * LANES
+                ]
+
+
+def rows_kernel(counts, arrived, side, high, low, turns, out):
+    count_y, count_z = counts[1:]
+    per_turn = arrived.shape[0] // turns.shape[1]
+    half = LANES // 2
+    lane = lax.broadcasted_iota(jnp.int32, (2 * TILE, LANES), 1)
+    real, imag = [], []
+    for b in range(turns.shape[1]):
+        real_pieces, imag_pieces = [], []
+        for g in range(b * per_turn, (b + 1) * per_turn, 2):
+            first, second = arrived[g], arrived[g + 1]
+            real_pieces.append(jnp.where(lane < half, first, pltpu.roll(second, half, 1)))
+            imag_pieces.append(jnp.where(lane < half, pltpu.roll(first, half, 1), second))
+        real.append(jnp.concatenate(real_pieces, axis=1))
+        imag.append(jnp.concatenate(imag_pieces, axis=1))
+    back = stacked_product(
+        jnp.concatenate(real, axis=0), jnp.concatenate(imag, axis=0), (high[...], low[...]), 1
+    )
+    middle = back.shape[0] // 2
+    size = turns.shape[1] * INNER
+    total = None
+    for b in range(turns.shape[1]):
+        part = slice(b * 2 * TILE, (b + 1) * 2 * TILE)
+        term = back[:middle][part] * turns[0, b : b + 1, :]
+        term = term - back[middle:][part] * turns[1, b : b + 1, :]
+        total = term if b == 0 else total + term
+    total = total * (1.0 / (size * size))
+    for y in range(count_y):
+        for z in range(count_z):
+            out[y * count_z + z, 0 : 2 * TILE, :] = total[:, y * LANES : (y + 1) * LANES]
+    out[:, 2 * TILE :, :] = side[...]
+
+
+def sum_kernel(exchange_grad, arrived, out):
+    depth = exchange_grad.shape[1]
+    group = arrived.shape[0]
+    side = [None, None]
+    top = [None, None]
+    for c in range(2):
+        rows = slice(2 * TILE + c * depth, 2 * TILE + (c + 1) * depth)
+        total = arrived[0, rows, :]
+        for p in range(1, group):
+            total = total + arrived[p, rows, :]
+        side[c] = total
+        top[c] = arrived[:, c * TILE : (c + 1) * TILE, :].reshape(group * TILE, LANES)
+    for z in range(depth):
+        out[0, z] = exchange_grad[0, z] + top[0]
+        out[1, z] = exchange_grad[1, z] + top[1] + side[0][z : z + 1]
+        out[2, z] = exchange_grad[2, z] + side[1][z : z + 1]
+
+
+MIB = 1024 * 1024
+SMEM = pl.BlockSpec(memory_space=pltpu.SMEM)
+VMEM = pl.BlockSpec(memory_space=pltpu.VMEM)
+
+
+def call(body, name, shape, limit, *operands, scalars=0):
+    return pl.pallas_call(
+        body,
+        out_shape=jax.ShapeDtypeStruct(shape, f32),
+        in_specs=[SMEM] * scalars + [VMEM] * (len(operands) - scalars),
+        out_specs=VMEM,
+        compiler_params=pltpu.CompilerParams(vmem_limit_bytes=limit * MIB),
+        name=name,
+    )(*operands)
+
+
+def fast_on_device(magnetization, stiffness, residual_top, residual_side, top_kernel, side_kernel):
+    counts = tuple(lax.axis_size(axis) for axis in ALL)
+    count_x, count_y, count_z = counts
+    group = count_y * count_z
+    devices = count_x * group
+    block_x, block_y = residual_top.shape
+    depth_block = stiffness.shape[0]
+    top_rows = block_y // 2
+    kys, size = top_kernel.shape[2:]
+    kzs = side_kernel.shape[2]
+    extent = count_x * block_x
+    here = [lax.axis_index(axis) for axis in ALL]
+    plane_index = here[1] * count_z + here[2]
+    index = (here[0] * group + plane_index).reshape(1)
+    plane_index = plane_index.reshape(1)
+    (high, low), _, turns = transform_tables(extent, size)
+    high, low, turns = jnp.asarray(high), jnp.asarray(low), jnp.asarray(turns)
+    steps, offsets = line_tables(counts, top_rows, kys, size)
+    there, back = depth_tables(group, kzs, depth_block * count_z)
+
+    piece = residual_top.T.reshape(2, top_rows, block_x)
+    piece = jnp.concatenate([piece[0], piece[1]], axis=1)
+    sent = jnp.broadcast_to(piece[None], (devices, top_rows, LANES))
+    gathered = lax.all_to_all(sent, ALL, 0, 0, tiled=True)
+
+    sent = jnp.broadcast_to(residual_side.T[None], (group, depth_block, LANES))
+    side_gathered = lax.all_to_all(sent, ("gy", "gz"), 0, 0, tiled=True)
+
+    halos = exchange_halos(magnetization, stiffness)
+    gathered, side_gathered, halos = lax.optimization_barrier((gathered, side_gathered, halos))
+
+    lines = call(
+        functools.partial(lines_kernel, counts),
+        "lines",
+        (devices, 2 * TILE, LANES),
+        24,
+        index,
+        gathered,
+        jnp.asarray(steps),
+        jnp.asarray(offsets),
+        high,
+        low,
+        turns,
+        top_kernel,
+        scalars=1,
+    )
+    arrived = lax.all_to_all(lines, ALL, 0, 0, tiled=True)
+    side = call(
+        functools.partial(side_kernel_body, counts),
+        "side",
+        (group, 2 * depth_block, LANES),
+        16,
+        plane_index,
+        side_gathered,
+        jnp.asarray(there),
+        jnp.asarray(back),
+        high,
+        low,
+        turns,
+        side_kernel,
+        scalars=1,
+    )
+    exchange_grad = exchange_of(magnetization, stiffness, halos)
+    arrived, side, exchange_grad = lax.optimization_barrier((arrived, side, exchange_grad))
+    rows = call(
+        functools.partial(rows_kernel, counts),
+        "rows",
+        (group, 2 * TILE + 2 * depth_block, LANES),
+        16,
+        arrived,
+        side,
+        high,
+        low,
+        turns,
+    )
+    arrived = lax.all_to_all(rows, ("gy", "gz"), 0, 0, tiled=True)
+    return call(sum_kernel, "gradient", magnetization.shape, 16, exchange_grad, arrived)
+
+
+def fits(counts, stiffness, residual_top, residual_side, top_kernel, side_kernel):
+    count_x, count_y, count_z = counts
+    block_x, block_y = residual_top.shape
+    group = count_y * count_z
+    return (
+        2 * block_x == LANES
+        and 2 * top_kernel.shape[2] == LANES
+        and stiffness.shape[2] == LANES
+        and block_x == group * TILE
+        and block_y * group == count_x * block_x == INNER
+        and count_y * LANES == INNER
+        and block_y % 16 == 0
+        and count_x % 2 == 0
+        and (count_x * group) % (2 * top_kernel.shape[3] // INNER) == 0
+        and INNER == top_kernel.shape[2] * count_z
+        and stiffness.shape[0] % 16 == 0
+        and side_kernel.shape[2] % 16 == 0
+    )
 
 
 def on_device(magnetization, stiffness, residual_top, residual_side, top_kernel, side_kernel):
     counts = tuple(lax.axis_size(axis) for axis in ALL)
     count_x, count_y, count_z = counts
+    if fits(counts, stiffness, residual_top, residual_side, top_kernel, side_kernel):
+        return fast_on_device(
+            magnetization, stiffness, residual_top, residual_side, top_kernel, side_kernel
+        )
     devices = count_x * count_y * count_z
     depth_block = stiffness.shape[0]
     block_x, block_y = residual_top.shape
@@ -360,7 +660,9 @@
     sent = jnp.broadcast_to(piece[None], (devices, rows, LANES)).reshape(devices * rows, LANES)
     gathered = lax.all_to_all(sent, ALL, 0, 0, tiled=True).reshape(devices, rows, LANES)
 
-    exchange_grad = exchange(magnetization, stiffness)
+    exchange_grad = exchange_of(
+        magnetization, stiffness, exchange_halos(magnetization, stiffness)
+    )
 
     parts = image_parts(
         gathered, top_kernel, side_kernel, counts, block_x, top_rows, depth_block

time: 72.3 us -> 77.1 us (1.066)
  local copies, waits for them, and re-layouts: 3.41 us -> 14.2 us
  waiting for transfers between devices: 10.5 us -> 3.85 us
  other arithmetic: 7.33 us -> 0.7 us
  starting transfers between devices: 22.5 us -> 26.8 us
  blocking collectives: 7.62 us -> 9.15 us
  Pallas kernels: 20.2 us -> 21.4 us
    unnamed x8 -> x50, local copies, waits for them, and re-layouts: 1.8 us -> 11.3 us
    all_to_all x0 -> x1, blocking collectives: none -> 9.15 us  [fast_on_device(): arrived = lax.all_to_all(rows, ('gy', 'gz'), 0, 0, tiled=True)]
    all_gather x1 -> x0, blocking collectives: 7.62 us -> none  [on_device(): top = lax.all_gather(top_sum, 'gz', axis=0)]
    all_to_all x2 -> x3, waiting for transfers between devices: 9.38 us -> 3.84 us  [the longest x1 3.83 us: fast_on_device(): side_gathered = lax.all_to_all(sent, ('gy', 'gz'), 0, 0, tiled=True)]
    all_to_all x2 -> x3, starting transfers between devices: 10.8 us -> 14.9 us  [the longest x1 5.55 us: fast_on_device(): arrived = lax.all_to_all(lines, ALL, 0, 0, tiled=True)]
    reduce_sum x2 -> x0, other arithmetic: 2.02 us -> none  [the longest x1 1.1 us: on_device(): top_sum = jnp.sum(arrived[:, :rows - TILE], axis=0)]
    concatenate x3 -> x1, other arithmetic: 1.41 us -> 0.08 us  [fast_on_device(): piece = jnp.concatenate([piece[0], piece[1]], axis=1)]
    another operation x1 -> x0, other arithmetic: 1.32 us -> none  [on_device(): jnp.stack([exchange_grad[0] + top[0], exchange_grad[1] + top[1] + side[0]...]
  transfers between devices with their start and end apart: 7 -> 8, of which waited for: 2 -> 1; matrix products, arithmetic and copies ran while one was open for 5% -> 2% of each run, Pallas kernels for 17% -> 19%
where the time goes in v1:
time: 77.1 us; the launch traced here: 76.3 us
  starting transfers between devices  26.8 us (35%)
  Pallas kernels  21.4 us (28%)
  local copies, waits for them, and re-layouts  14.2 us (18%)
  blocking collectives  9.15 us (12%)
  waiting for transfers between devices  3.85 us (5%)
    unnamed x50, local copies, waits for them, and re-layouts  11.3 us
    ppermute x4, starting transfers between devices, shifted(): return lax.ppermute(block, axis, route)  10.2 us
    pallas_call x4, Pallas kernels, call(): pl.pallas_call(body, out_shape=jax.ShapeDtypeStruct(shape, f32), in_specs...  9.42 us
    all_to_all x1, blocking collectives, fast_on_device(): arrived = lax.all_to_all(rows, ('gy', 'gz'), 0, 0, tiled=True)  9.15 us
    pallas_call x1, Pallas kernels, exchange_of(): pl.pallas_call(exchange_kernel, out_shape=jax.ShapeDtypeStruct(magnetizat...  8.36 us
    all_to_all x1, starting transfers between devices, fast_on_device(): arrived = lax.all_to_all(lines, ALL, 0, 0, tiled=True)  5.55 us
    all_to_all x1, starting transfers between devices, fast_on_device(): side_gathered = lax.all_to_all(sent, ('gy', 'gz'), 0, 0, tiled=True)  5.17 us
    all_to_all x1, starting transfers between devices, fast_on_device(): gathered = lax.all_to_all(sent, ALL, 0, 0, tiled=True)  4.14 us
  transfers between devices with their start and end apart: 8, of which 1 were waited for; matrix products, arithmetic and copies ran while one was open for 2% of the time, Pallas kernels for 19%

profile of v1, /device:TPU:0, one launch (start us, length us, event | category | flops | bytes accessed | tf_op | source)
XLA Modules:
  0.0 76.3 jit_solution(5713064454846512389)
XLA Ops:
  0.0 1.3 %broadcast_in_dim.18 = f32[8,16,128]{2,1,0:T(8,128)} broadcast(f32[16,128]{1,0:T(8,128)} %bitcast.5), dimensions={1,2} | broadcast | bytes 73728 | tf_op jit(solution)/shard_map/broadcast_in_dim | solution.py:564
  1.3 5.2 %all-to-all-start.1 = ((f32[8,16,128]{2,1,0:T(8,128)}), f32[8,16,128]{2,1,0:T(8,128)S(1)}, u32[]{:S(2)}, u32[]{:S(2)}) async-start(f32[8,16,128]{2,1,0:T(8,128)} %broadcast_in_dim.18), calls=%async_computation.1 | async-start | bytes 131072 | tf_op jit(solution)/shard_map/all_to_all | solution.py:565
  6.6 0.9 %fusion = (f32[16,64]{1,0:T(8,128)S(1)}, f32[16,64]{1,0:T(8,128)S(1)}) fusion(f32[32,64]{1,0:T(8,128)} %bitcast.4), kind=kLoop, calls=%fused_computation.3 | loop fusion | bytes 16384 | tf_op jit(solution)/shard_map/slice | solution.py:560
  7.5 3.8 %all-to-all-done.1.gathered = f32[8,16,128]{2,1,0:T(8,128)S(1)} async-done(((f32[8,16,128]{2,1,0:T(8,128)}), f32[8,16,128]{2,1,0:T(8,128)S(1)}, u32[]{:S(2)}, u32[]{:S(2)}) %all-to-all-start.1) | async-done | bytes 65568 | tf_op jit(solution)/shard_map/all_to_all | solution.py:565
  11.3 0.7 broadcast_in_dim.8
  12.1 4.1 %all-to-all-start = ((f32[32,16,128]{2,1,0:T(8,128)}), f32[32,16,128]{2,1,0:T(8,128)S(1)}, u32[]{:S(2)}, u32[]{:S(2)}) async-start(f32[32,16,128]{2,1,0:T(8,128)} %broadcast_in_dim.8), calls=%async_computation | async-start | bytes 524288 | tf_op jit(solution)/shard_map/all_to_all | solution.py:562
  16.2 3.6 %faces.1 = (f32[4,64,128]{2,1,0:T(8,128)}, f32[4,64,128]{2,1,0:T(8,128)}, f32[4,16,128]{2,1,0:T(8,128)}, f32[4,16,128]{2,1,0:T(8,128)}, f32[64,128]{1,0:T(8,128)}) custom-call(f32[3,16,64,128]{3,2,1,0:T(8,128)} %magnetization.3, f32[16,64,128]{2,1,0:T(8,128)} %stiffness.3), custom_call_target="tpu_custom_call" | custom-call | tf_op jit(solution)/shard_map/faces/pallas_call | solution.py:315
  19.8 1.8 %collective-permute-start.4 = (f32[64,128]{1,0:T(8,128)}, f32[64,128]{1,0:T(8,128)S(1)}, u32[]{:S(2)}, u32[]{:S(2)}) collective-permute-start(f32[64,128]{1,0:T(8,128)} %get-tuple-element.25), channel_id=1, source_target_pairs={{0,4},{4,0},{1,5},{5,1},{2,6},{6,2},{3,7},{7,3},{8,12},{12,8},{9,1... | collective-permute-start | bytes 98312 | tf_op jit(solution)/shard_map/ppermute | solution.py:329
  21.6 1.3 %collective-permute-start.2 = (f32[4,16,128]{2,1,0:T(8,128)}, f32[4,16,128]{2,1,0:T(8,128)S(1)}, u32[]{:S(2)}, u32[]{:S(2)}) collective-permute-start(f32[4,16,128]{2,1,0:T(8,128)} %get-tuple-element.23), channel_id=1, source_target_pairs={{8,0},{16,8},{24,16},{9,1},{17,9},{25,17},{10,2},{18,10},{26,18},{... | collective-permute-start | bytes 98312 | tf_op jit(solution)/shard_map/ppermute | solution.py:309
  22.9 4.5 %collective-permute-start.3 = (f32[4,16,128]{2,1,0:T(8,128)}, f32[4,16,128]{2,1,0:T(8,128)S(1)}, u32[]{:S(2)}, u32[]{:S(2)}) collective-permute-start(f32[4,16,128]{2,1,0:T(8,128)} %get-tuple-element.24), channel_id=1, source_target_pairs={{0,8},{8,16},{16,24},{1,9},{9,17},{17,25},{2,10},{10,18},{18,26},{... | collective-permute-start | bytes 98312 | tf_op jit(solution)/shard_map/ppermute | solution.py:309
  27.4 1.3 %collective-permute-start = (f32[4,64,128]{2,1,0:T(8,128)}, f32[4,64,128]{2,1,0:T(8,128)S(1)}, u32[]{:S(2)}, u32[]{:S(2)}) collective-permute-start(f32[4,64,128]{2,1,0:T(8,128)} %get-tuple-element.21), channel_id=1, source_target_pairs={{1,0},{2,1},{3,2},{5,4},{6,5},{7,6},{9,8},{10,9},{11,10},{13,12},{... | collective-permute-start | bytes 393224 | tf_op jit(solution)/shard_map/ppermute | solution.py:309
  28.7 3.0 %collective-permute-start.1 = (f32[4,64,128]{2,1,0:T(8,128)}, f32[4,64,128]{2,1,0:T(8,128)S(1)}, u32[]{:S(2)}, u32[]{:S(2)}) collective-permute-start(f32[4,64,128]{2,1,0:T(8,128)} %get-tuple-element.22), channel_id=1, source_target_pairs={{0,1},{1,2},{2,3},{4,5},{5,6},{6,7},{8,9},{9,10},{10,11},{12,13},{... | collective-permute-start | bytes 393224 | tf_op jit(solution)/shard_map/ppermute | solution.py:309
  31.8 0.6 broadcast_select_fusion
  33.6 0.6 copy-done.17
  34.3 0.6 copy-done.19
  34.9 4.0 %lines.1 = f32[32,16,128]{2,1,0:T(8,128)S(1)} custom-call(s32[1]{0:T(128)} %bitcast.here, f32[32,16,128]{2,1,0:T(8,128)S(1)} %all-to-all-done.gathered, f32[4,64,128]{2,1,0:T(8,128)S(1)} %copy-done.16, f32[32,8,128]{2,1,0:T(8,128)S(1)} %copy-done.15, bf16[512,256]{1,0:T(8,128)(2,1)S(1)} %copy-done.2, bf16[512,256]{1,0:T(8,128)(2,1)S(1)} %copy-done.1, ...), custom_call_target="tpu_custom_call" | custom-call | tf_op jit(solution)/shard_map/lines/pallas_call | solution.py:529
  38.9 0.7 copy-done.6
  39.6 5.5 %all-to-all-start.2 = ((f32[32,16,128]{2,1,0:T(8,128)}), f32[32,16,128]{2,1,0:T(8,128)}, u32[]{:S(2)}, u32[]{:S(2)}) async-start(f32[32,16,128]{2,1,0:T(8,128)} %copy-done.6), calls=%async_computation.2 | async-start | bytes 524288 | tf_op jit(solution)/shard_map/all_to_all | solution.py:585
  45.2 1.1 %copy-done.7 = f32[2,2,16,2048]{3,2,1,0:T(8,128)S(1)} copy-done((f32[2,2,16,2048]{3,2,1,0:T(8,128)S(1)}, f32[2,2,16,2048]{3,2,1,0:T(8,128)}, u32[]{:S(2)}) %copy-start.7) | copy-done | bytes 524312
  46.3 0.8 %copy-done.9 = f32[8,16,128]{2,1,0:T(8,128)S(1)} copy-done((f32[8,16,128]{2,1,0:T(8,128)S(1)}, f32[8,16,128]{2,1,0:T(8,128)}, u32[]{:S(2)}) %copy-start.9) | copy-done | bytes 65560
  47.1 0.9 %copy-done.10 = f32[8,64,32]{2,1,0:T(8,128)S(1)} copy-done((f32[8,64,32]{2,1,0:T(8,128)S(1)}, f32[8,64,32]{2,1,0:T(8,128)}, u32[]{:S(2)}) %copy-start.10) | copy-done | bytes 65560
  48.1 0.9 %copy-done.14 = f32[8,32,64]{2,1,0:T(8,128)S(1)} copy-done((f32[8,32,64]{2,1,0:T(8,128)S(1)}, f32[8,32,64]{2,1,0:T(8,128)}, u32[]{:S(2)}) %copy-start.14) | copy-done | bytes 65560
  49.0 2.8 %side.1 = f32[8,32,128]{2,1,0:T(8,128)S(1)} custom-call(s32[1]{0:T(128)} %bitcast.3.here, f32[8,16,128]{2,1,0:T(8,128)S(1)} %copy-done.9, f32[8,32,64]{2,1,0:T(8,128)S(1)} %copy-done.14, f32[8,64,32]{2,1,0:T(8,128)S(1)} %copy-done.10, bf16[512,256]{1,0:T(8,128)(2,1)S(1)} %copy-done.2, bf16[512,256]{1,0:T(8,128)(2,1)S(1)} %copy-done.1, ...), custom_call_target="tpu_custom_call" | custom-call | tf_op jit(solution)/shard_map/side/pallas_call | solution.py:529
  51.9 0.9 %copy-done.18 = f32[4,64,128]{2,1,0:T(8,128)S(1)} copy-done((f32[4,64,128]{2,1,0:T(8,128)S(1)}, f32[4,64,128]{2,1,0:T(8,128)}, u32[]{:S(2)}) %copy-start.18) | copy-done | bytes 131096
  52.8 0.9 %copy-done.20 = f32[4,64,128]{2,1,0:T(8,128)S(1)} copy-done((f32[4,64,128]{2,1,0:T(8,128)S(1)}, f32[4,64,128]{2,1,0:T(8,128)}, u32[]{:S(2)}) %copy-start.20) | copy-done | bytes 131096
  53.7 0.8 copy-done.22
  54.4 0.8 copy-done.24
  55.2 8.4 %exchange.1.exchange_grad = f32[3,16,64,128]{3,2,1,0:T(8,128)S(1)} custom-call(f32[3,16,64,128]{3,2,1,0:T(8,128)S(1)} %copy-done, f32[16,64,128]{2,1,0:T(8,128)S(1)} %copy-done.5, f32[4,64,128]{2,1,0:T(8,128)S(1)} %copy-done.18, f32[4,64,128]{2,1,0:T(8,128)S(1)} %copy-done.20, f32[4,16,128]{2,1,0:T(8,128)S(1)} %copy-done.22, f32[4,16,128]{2,1,0:T(8,128)S(1)} %copy-done.24, ...), custom_call_target="tpu_custom_call" | custom-call | tf_op jit(solution)/shard_map/exchange/pallas_call | solution.py:338
  63.6 0.9 %copy-done.3 = bf16[512,256]{1,0:T(8,128)(2,1)S(1)} copy-done((bf16[512,256]{1,0:T(8,128)(2,1)S(1)}, bf16[512,256]{1,0:T(8,128)(2,1)}, u32[]{:S(2)}) %copy-start.3) | copy-done | bytes 262168
  64.5 1.4 %rows.1 = f32[8,48,128]{2,1,0:T(8,128)S(1)} custom-call(f32[32,16,128]{2,1,0:T(8,128)} %all-to-all-done.2.arrived, f32[8,32,128]{2,1,0:T(8,128)S(1)} %side.1, bf16[512,256]{1,0:T(8,128)(2,1)S(1)} %copy-done.3, bf16[512,256]{1,0:T(8,128)(2,1)S(1)} %copy-done.1, f32[2,8,256]{2,1,0:T(8,128)S(1)} %copy-done.11), custom_call_target="tpu_custom_call" | custom-call | tf_op jit(solution)/shard_map/rows/pallas_call | solution.py:529
  65.9 9.2 %all_to_all.20.arrived = f32[8,48,128]{2,1,0:T(8,128)S(1)} all-to-all(f32[8,48,128]{2,1,0:T(8,128)S(1)} %rows.1), channel_id=1, replica_groups=mesh['gx'=4,'gy'=2,'gz'=4] {'gy','gz'}, dimensions={0} | all-to-all | bytes 393216 | tf_op jit(solution)/shard_map/all_to_all | solution.py:614
  75.1 1.3 %gradient.1 = f32[3,16,64,128]{3,2,1,0:T(8,128)} custom-call(f32[3,16,64,128]{3,2,1,0:T(8,128)S(1)} %exchange.1.exchange_grad, f32[8,48,128]{2,1,0:T(8,128)S(1)} %all_to_all.20.arrived), custom_call_target="tpu_custom_call" | custom-call | tf_op jit(solution)/shard_map/gradient/pallas_call | solution.py:529
  (46 shorter events, 1.4 us)
Async XLA Ops:
  1.3 10.0 %all-to-all-start.1 = ((f32[8,16,128]{2,1,0:T(8,128)}), f32[8,16,128]{2,1,0:T(8,128)S(1)}, u32[]{:S(2)}, u32[]{:S(2)}) async-start(f32[8,16,128]{2,1,0:T(8,128)} %broadcast_in_dim.18), calls=%async_computation.1 | async-start | bytes 131072 | tf_op jit(solution)/shard_map/all_to_all | solution.py:565
  6.5 28.4 %copy-start.1 = (bf16[512,256]{1,0:T(8,128)(2,1)S(1)}, bf16[512,256]{1,0:T(8,128)(2,1)}, u32[]{:S(2)}) copy-start(bf16[512,256]{1,0:T(8,128)(2,1)} %constant.37.clone.low) | copy-start | bytes 786436
  6.5 28.4 %copy-start.2 = (bf16[512,256]{1,0:T(8,128)(2,1)S(1)}, bf16[512,256]{1,0:T(8,128)(2,1)}, u32[]{:S(2)}) copy-start(bf16[512,256]{1,0:T(8,128)(2,1)} %constant.36.clone.high) | copy-start | bytes 786436
  6.5 28.4 %copy-start.4 = (f32[2,2,64,2048]{3,2,1,0:T(8,128)S(1)}, f32[2,2,64,2048]{3,2,1,0:T(8,128)}, u32[]{:S(2)}) copy-start(f32[2,2,64,2048]{3,2,1,0:T(8,128)} %kernel.2) | copy-start | bytes 6291460
  6.5 28.4 %copy-start.11 = (f32[2,8,256]{2,1,0:T(8,128)S(1)}, f32[2,8,256]{2,1,0:T(8,128)}, u32[]{:S(2)}) copy-start(f32[2,8,256]{2,1,0:T(8,128)} %constant.38.clone.turns) | copy-start | bytes 49156
  6.5 28.4 %copy-start.15 = (f32[32,8,128]{2,1,0:T(8,128)S(1)}, f32[32,8,128]{2,1,0:T(8,128)}, u32[]{:S(2)}) copy-start(f32[32,8,128]{2,1,0:T(8,128)} %constant.40.clone.offsets) | copy-start | bytes 393220
  6.6 28.4 %copy-start.16 = (f32[4,64,128]{2,1,0:T(8,128)S(1)}, f32[4,64,128]{2,1,0:T(8,128)}, u32[]{:S(2)}) copy-start(f32[4,64,128]{2,1,0:T(8,128)} %constant.39.clone.steps) | copy-start | bytes 393220
  11.3 0.7 copy-start.8
  12.1 22.8 %all-to-all-start = ((f32[32,16,128]{2,1,0:T(8,128)}), f32[32,16,128]{2,1,0:T(8,128)S(1)}, u32[]{:S(2)}, u32[]{:S(2)}) async-start(f32[32,16,128]{2,1,0:T(8,128)} %broadcast_in_dim.8), calls=%async_computation | async-start | bytes 524288 | tf_op jit(solution)/shard_map/all_to_all | solution.py:562
  19.8 12.0 %collective-permute-start.4 = (f32[64,128]{1,0:T(8,128)}, f32[64,128]{1,0:T(8,128)S(1)}, u32[]{:S(2)}, u32[]{:S(2)}) collective-permute-start(f32[64,128]{1,0:T(8,128)} %get-tuple-element.25), channel_id=1, source_target_pairs={{0,4},{4,0},{1,5},{5,1},{2,6},{6,2},{3,7},{7,3},{8,12},{12,8},{9,1... | collective-permute-start | bytes 98312 | tf_op jit(solution)/shard_map/ppermute | solution.py:329
  21.6 10.8 %collective-permute-start.2 = (f32[4,16,128]{2,1,0:T(8,128)}, f32[4,16,128]{2,1,0:T(8,128)S(1)}, u32[]{:S(2)}, u32[]{:S(2)}) collective-permute-start(f32[4,16,128]{2,1,0:T(8,128)} %get-tuple-element.23), channel_id=1, source_target_pairs={{8,0},{16,8},{24,16},{9,1},{17,9},{25,17},{10,2},{18,10},{26,18},{... | collective-permute-start | bytes 98312 | tf_op jit(solution)/shard_map/ppermute | solution.py:309
  22.9 10.2 %collective-permute-start.3 = (f32[4,16,128]{2,1,0:T(8,128)}, f32[4,16,128]{2,1,0:T(8,128)S(1)}, u32[]{:S(2)}, u32[]{:S(2)}) collective-permute-start(f32[4,16,128]{2,1,0:T(8,128)} %get-tuple-element.24), channel_id=1, source_target_pairs={{0,8},{8,16},{16,24},{1,9},{9,17},{17,25},{2,10},{10,18},{18,26},{... | collective-permute-start | bytes 98312 | tf_op jit(solution)/shard_map/ppermute | solution.py:309
  27.4 6.2 %collective-permute-start = (f32[4,64,128]{2,1,0:T(8,128)}, f32[4,64,128]{2,1,0:T(8,128)S(1)}, u32[]{:S(2)}, u32[]{:S(2)}) collective-permute-start(f32[4,64,128]{2,1,0:T(8,128)} %get-tuple-element.21), channel_id=1, source_target_pairs={{1,0},{2,1},{3,2},{5,4},{6,5},{7,6},{9,8},{10,9},{11,10},{13,12},{... | collective-permute-start | bytes 393224 | tf_op jit(solution)/shard_map/ppermute | solution.py:309
  28.7 5.5 %collective-permute-start.1 = (f32[4,64,128]{2,1,0:T(8,128)}, f32[4,64,128]{2,1,0:T(8,128)S(1)}, u32[]{:S(2)}, u32[]{:S(2)}) collective-permute-start(f32[4,64,128]{2,1,0:T(8,128)} %get-tuple-element.22), channel_id=1, source_target_pairs={{0,1},{1,2},{2,3},{4,5},{5,6},{6,7},{8,9},{9,10},{10,11},{12,13},{... | collective-permute-start | bytes 393224 | tf_op jit(solution)/shard_map/ppermute | solution.py:309
  33.0 0.6 copy-start.23
  33.6 0.6 copy-start.17
  34.3 0.6 copy-start.19
  38.9 0.7 copy-start.6
  39.6 12.2 %copy-start = (f32[3,16,64,128]{3,2,1,0:T(8,128)S(1)}, f32[3,16,64,128]{3,2,1,0:T(8,128)}, u32[]{:S(2)}) copy-start(f32[3,16,64,128]{3,2,1,0:T(8,128)} %magnetization.3) | copy-start | bytes 4718596
  39.6 23.9 %all-to-all-start.2 = ((f32[32,16,128]{2,1,0:T(8,128)}), f32[32,16,128]{2,1,0:T(8,128)}, u32[]{:S(2)}, u32[]{:S(2)}) async-start(f32[32,16,128]{2,1,0:T(8,128)} %copy-done.6), calls=%async_computation.2 | async-start | bytes 524288 | tf_op jit(solution)/shard_map/all_to_all | solution.py:585
  45.2 6.6 %copy-start.5 = (f32[16,64,128]{2,1,0:T(8,128)S(1)}, f32[16,64,128]{2,1,0:T(8,128)}, u32[]{:S(2)}) copy-start(f32[16,64,128]{2,1,0:T(8,128)} %stiffness.3) | copy-start | bytes 1572868
  45.2 1.1 %copy-start.7 = (f32[2,2,16,2048]{3,2,1,0:T(8,128)S(1)}, f32[2,2,16,2048]{3,2,1,0:T(8,128)}, u32[]{:S(2)}) copy-start(f32[2,2,16,2048]{3,2,1,0:T(8,128)} %kernel.3) | copy-start | bytes 1572868
  46.3 0.8 %copy-start.9 = (f32[8,16,128]{2,1,0:T(8,128)S(1)}, f32[8,16,128]{2,1,0:T(8,128)}, u32[]{:S(2)}) copy-start(f32[8,16,128]{2,1,0:T(8,128)} %copy-done.8) | copy-start | bytes 196612
  47.1 0.9 %copy-start.10 = (f32[8,64,32]{2,1,0:T(8,128)S(1)}, f32[8,64,32]{2,1,0:T(8,128)}, u32[]{:S(2)}) copy-start(f32[8,64,32]{2,1,0:T(8,128)} %constant.42.clone.back) | copy-start | bytes 196612
  48.1 0.9 %copy-start.14 = (f32[8,32,64]{2,1,0:T(8,128)S(1)}, f32[8,32,64]{2,1,0:T(8,128)}, u32[]{:S(2)}) copy-start(f32[8,32,64]{2,1,0:T(8,128)} %constant.41.clone.there) | copy-start | bytes 196612
  49.0 2.8 %copy-start.12 = (f32[64,128]{1,0:T(8,128)S(1)}, f32[64,128]{1,0:T(8,128)}, u32[]{:S(2)}) copy-start(f32[64,128]{1,0:T(8,128)} %get-tuple-element.33.y_before) | copy-start | bytes 98308
  49.0 2.8 %copy-start.13 = (f32[64,128]{1,0:T(8,128)S(1)}, f32[64,128]{1,0:T(8,128)}, u32[]{:S(2)}) copy-start(f32[64,128]{1,0:T(8,128)} %get-tuple-element.32.y_next) | copy-start | bytes 98308
  51.8 0.9 %copy-start.18 = (f32[4,64,128]{2,1,0:T(8,128)S(1)}, f32[4,64,128]{2,1,0:T(8,128)}, u32[]{:S(2)}) copy-start(f32[4,64,128]{2,1,0:T(8,128)} %copy-done.17) | copy-start | bytes 393220
  52.7 0.9 %copy-start.20 = (f32[4,64,128]{2,1,0:T(8,128)S(1)}, f32[4,64,128]{2,1,0:T(8,128)}, u32[]{:S(2)}) copy-start(f32[4,64,128]{2,1,0:T(8,128)} %copy-done.19) | copy-start | bytes 393220
  53.7 0.8 copy-start.22
  54.4 0.8 copy-start.24
  63.5 1.0 %copy-start.3 = (bf16[512,256]{1,0:T(8,128)(2,1)S(1)}, bf16[512,256]{1,0:T(8,128)(2,1)}, u32[]{:S(2)}) copy-start(bf16[512,256]{1,0:T(8,128)(2,1)} %constant.36.clone.high) | copy-start | bytes 786436
  (1 other events, 0.6 us)

commit v2 on v1

--- a/solution.py
+++ b/solution.py
@@ -16,6 +16,10 @@
 ALL = ("gx", "gy", "gz")
 f32 = jnp.float32
 bf16 = jnp.bfloat16
+MIB = 1024 * 1024
+SMEM = pl.BlockSpec(memory_space=pltpu.SMEM)
+VMEM = pl.BlockSpec(memory_space=pltpu.VMEM)
+HBM = pl.BlockSpec(memory_space=pltpu.HBM)
 
 
 def split(values):
@@ -228,25 +232,55 @@
     )
 
 
-def faces_kernel(magnetization, stiffness, z_first, z_last, x_first, x_last, y_faces):
+def copies_of(pairs, semaphores):
+    started = [
+        pltpu.make_async_copy(source, target, semaphores.at[i])
+        for i, (source, target) in enumerate(pairs)
+    ]
+    for copy in started:
+        copy.start()
+    return started
+
+
+def faces_kernel(
+    magnetization, stiffness, z_first, z_last, x_first, x_last, y_faces, m, s, semaphores, sent
+):
     depth, across = stiffness.shape[:2]
+    loads = copies_of(
+        [(stiffness, s)] + [(magnetization.at[c], m.at[c]) for c in range(3)], semaphores
+    )
     lane = lax.broadcasted_iota(jnp.int32, (across, LANES), 1)
-    sides = jnp.zeros((across, LANES), f32)
-    for field in range(4):
-        ref = stiffness if field == 3 else magnetization.at[field]
-        z_first[field] = ref[0]
-        z_last[field] = ref[depth - 1]
+    first = jnp.zeros((across, LANES), f32)
+    last = jnp.zeros((across, LANES), f32)
+    stores = []
+    for field, load in ((3, loads[0]), (0, loads[1]), (1, loads[2]), (2, loads[3])):
+        load.wait()
+        ref = s if field == 3 else m.at[field]
+        for k, (target, z) in enumerate(((z_first, 0), (z_last, depth - 1))):
+            store = pltpu.make_async_copy(ref.at[z], target.at[field], sent.at[2 * field + k])
+            store.start()
+            stores.append(store)
         x_first[field] = ref[:, 0, :]
         x_last[field] = ref[:, across - 1, :]
         for z in range(depth):
             column = field * depth + z
-            values = ref[z]
-            sides = jnp.where(lane == column, values[:, 0:1], sides)
-            sides = jnp.where(lane == column + 4 * depth, values[:, LANES - 1 : LANES], sides)
-    y_faces[...] = sides
+            turned = pltpu.roll(ref[z], column, 1) if column else ref[z]
+            first = jnp.where(lane == column, turned, first)
+            last = jnp.where(lane == (column - 1) % LANES, turned, last)
+    y_faces[...] = jnp.where(
+        lane < LANES // 2, first, pltpu.roll(last, LANES // 2 + 1, 1)
+    )
+    for store in stores:
+        store.wait()
+
+
+def twice_weight(a, b):
+    return 4.0 * a * b / (a + b)
 
 
 def exchange_kernel(
+    counts,
+    here,
     magnetization,
     stiffness,
     z_next,
@@ -255,58 +289,96 @@
     x_before,
     y_next,
     y_before,
+    y_faces,
     out,
+    m,
+    s,
+    semaphores,
 ):
     depth, across = stiffness.shape[:2]
+    chunk = depth // 4
+    pairs = []
+    for k in range(4):
+        layers = slice(k * chunk, (k + 1) * chunk)
+        pairs.append((stiffness.at[layers], s.at[layers]))
+        pairs.append((magnetization.at[:, layers], m.at[:, layers]))
+    loads = copies_of(pairs, semaphores)
+
+    count_x, count_y, count_z = counts
+    at_z = here[0] % count_z
+    at_y = here[0] // count_z % count_y
+    at_x = here[0] // (count_z * count_y)
+
+    def inside(condition, values):
+        return jnp.where(condition, values, 0.0)
+
     lane = lax.broadcasted_iota(jnp.int32, (across, LANES), 1)
-    sublane = lax.broadcasted_iota(jnp.int32, (across, LANES), 0)
-    last_lane, first_lane = lane == LANES - 1, lane == 0
-    last_row, first_row = sublane == across - 1, sublane == 0
-
-    def weight(a, b):
-        return 2.0 * a * b / (a + b)
-
-    def one(z, field):
-        ref = stiffness if field == 3 else magnetization.at[field]
-        centre = ref[z]
-        column = field * depth + z
-        along = jnp.where(
-            last_lane, y_next[:, column : column + 1], pltpu.roll(centre, LANES - 1, 1)
-        )
-        across_next = jnp.where(
-            last_row, x_next[field, z : z + 1, :], pltpu.roll(centre, across - 1, 0)
-        )
-        along_before = y_before[:, 4 * depth + column : 4 * depth + column + 1]
-        across_before = x_before[field, z : z + 1, :]
-        return centre, along, across_next, along_before, across_before
-
-    below_weight = weight(z_before[3], stiffness[0])
-    below = [below_weight * (z_before[c] - magnetization[c, 0]) for c in range(3)]
+    row = lax.broadcasted_iota(jnp.int32, (across, LANES), 0)
+    first_lane, last_lane, last_row = lane == 0, lane == LANES - 1, row == across - 1
+    half = LANES // 2
+
+    stiff = (lane >= 3 * depth) & (lane < 4 * depth)
+
+    def y_edge(own, halo, present):
+        halo_stiffness = inside(present, halo)
+        weight = twice_weight(jnp.where(stiff, own, 1.0), jnp.where(stiff, halo_stiffness, 1.0))
+        spread = pltpu.roll(weight, LANES - 3 * depth, 1)
+        for c in (1, 2):
+            spread = jnp.where(
+                lane >= c * depth, pltpu.roll(weight, LANES - (3 - c) * depth, 1), spread
+            )
+        return spread * (own - halo)
+
+    own = y_faces[...]
+    after = y_edge(pltpu.roll(own, half, 1), y_next[...], at_y < count_y - 1)
+    before = y_edge(own, pltpu.roll(y_before[...], half, 1), at_y > 0)
+
+    loads[0].wait()
+    loads[1].wait()
+    below_weight = twice_weight(inside(at_z > 0, z_before[3]), s[0])
+    below = [below_weight * (z_before[c] - m[c, 0]) for c in range(3)]
     for z in range(depth):
-        s, s_along, s_across, s_along_before, s_across_before = one(z, 3)
-        s_above = stiffness[z + 1] if z + 1 < depth else z_next[3]
-        w_along, w_across, w_above = weight(s, s_along), weight(s, s_across), weight(s, s_above)
-        w_along_before = weight(s_along_before, s[:, 0:1])
-        w_across_before = weight(s_across_before, s[0:1, :])
+        if z % chunk == 0 and z + chunk < depth:
+            for load in loads[2 * (z // chunk + 1) : 2 * (z // chunk + 2)]:
+                load.wait()
+        centre = s[z]
+        above = s[z + 1] if z + 1 < depth else inside(at_z < count_z - 1, z_next[3])
+        weight_z = twice_weight(centre, above)
+        weight_x = jnp.where(
+            last_row, 0.0, twice_weight(centre, pltpu.roll(centre, across - 1, 0))
+        )
+        weight_y = jnp.where(
+            last_lane, 0.0, twice_weight(centre, pltpu.roll(centre, LANES - 1, 1))
+        )
         for c in range(3):
-            m, m_along, m_across, m_along_before, m_across_before = one(z, c)
-            m_above = magnetization[c, z + 1] if z + 1 < depth else z_next[c]
-            up = w_above * (m - m_above)
-            flux_along = w_along * (m - m_along)
-            flux_across = w_across * (m - m_across)
-            edge_along = w_along_before * (m_along_before - m[:, 0:1])
-            edge_across = w_across_before * (m_across_before - m[0:1, :])
-            lower_along = jnp.where(first_lane, edge_along, pltpu.roll(flux_along, 1, 1))
-            lower_across = jnp.where(first_row, edge_across, pltpu.roll(flux_across, 1, 0))
-            total = (up - below[c]) + (flux_across - lower_across) + (flux_along - lower_along)
-            out[c, z] = 2.0 * total
+            column = c * depth + z
+            values = m[c, z]
+            upper = m[c, z + 1] if z + 1 < depth else z_next[c]
+            up = weight_z * (values - upper)
+            flux_x = weight_x * (values - pltpu.roll(values, across - 1, 0))
+            flux_y = weight_y * (values - pltpu.roll(values, LANES - 1, 1))
+            total = (up - below[c]) + (flux_x - pltpu.roll(flux_x, 1, 0))
+            total = total + (flux_y - pltpu.roll(flux_y, 1, 1))
+            edge = jnp.where(
+                first_lane,
+                before[:, column : column + 1],
+                jnp.where(last_lane, after[:, column : column + 1], 0.0),
+            )
+            out[c, z] = total + edge
             below[c] = up
 
-
-def shifted(block, axis, distance):
+    for edge_row, halo, present in (
+        (across - 1, x_next, at_x < count_x - 1),
+        (0, x_before, at_x > 0),
+    ):
+        weight = twice_weight(s[:, edge_row, :], inside(present, halo[3]))
+        for c in range(3):
+            out[c, :, edge_row, :] += weight * (m[c, :, edge_row, :] - halo[c])
+
+
+def ring(block, axis, distance):
     count = lax.axis_size(axis)
-    route = [(i, i + distance) for i in range(count) if 0 <= i + distance < count]
-    return lax.ppermute(block, axis, route)
+    return lax.ppermute(block, axis, [(i, (i + distance) % count) for i in range(count)])
 
 
 def exchange_halos(magnetization, stiffness):
@@ -314,6 +386,8 @@
     shape = jax.ShapeDtypeStruct
     z_first, z_last, x_first, x_last, y_faces = pl.pallas_call(
         faces_kernel,
+        in_specs=[HBM, HBM],
+        out_specs=[HBM, HBM, VMEM, VMEM, VMEM],
         out_shape=[
             shape((4, across, along), f32),
             shape((4, across, along), f32),
@@ -321,26 +395,36 @@
             shape((4, depth, along), f32),
             shape((across, LANES), f32),
         ],
+        scratch_shapes=[
+            pltpu.VMEM(magnetization.shape, f32),
+            pltpu.VMEM(stiffness.shape, f32),
+            pltpu.SemaphoreType.DMA((4,)),
+            pltpu.SemaphoreType.DMA((8,)),
+        ],
+        compiler_params=pltpu.CompilerParams(vmem_limit_bytes=8 * MIB),
         name="faces",
     )(magnetization, stiffness)
-    z_next, z_before = shifted(z_first, "gz", -1), shifted(z_last, "gz", 1)
-    x_next, x_before = shifted(x_first, "gx", -1), shifted(x_last, "gx", 1)
-    if lax.axis_size("gy") == 2:
-        other = lax.ppermute(y_faces, "gy", [(0, 1), (1, 0)])
-        at = lax.axis_index("gy")
-        y_next, y_before = jnp.where(at == 0, other, 0.0), jnp.where(at == 1, other, 0.0)
-    else:
-        y_next, y_before = shifted(y_faces, "gy", -1), shifted(y_faces, "gy", 1)
-    return z_next, z_before, x_next, x_before, y_next, y_before
-
-
-def exchange_of(magnetization, stiffness, halos):
+    z_next, z_before = ring(z_first, "gz", -1), ring(z_last, "gz", 1)
+    x_next, x_before = ring(x_first, "gx", -1), ring(x_last, "gx", 1)
+    y_next = ring(y_faces, "gy", -1)
+    y_before = y_next if lax.axis_size("gy") == 2 else ring(y_faces, "gy", 1)
+    return z_next, z_before, x_next, x_before, y_next, y_before, y_faces
+
+
+def exchange_of(counts, index, magnetization, stiffness, halos):
     return pl.pallas_call(
-        exchange_kernel,
+        functools.partial(exchange_kernel, counts),
+        in_specs=[SMEM, HBM, HBM] + [VMEM] * len(halos),
+        out_specs=VMEM,
         out_shape=jax.ShapeDtypeStruct(magnetization.shape, f32),
-        compiler_params=pltpu.CompilerParams(vmem_limit_bytes=32 * 1024 * 1024),
+        scratch_shapes=[
+            pltpu.VMEM(magnetization.shape, f32),
+            pltpu.VMEM(stiffness.shape, f32),
+            pltpu.SemaphoreType.DMA((8,)),
+        ],
+        compiler_params=pltpu.CompilerParams(vmem_limit_bytes=16 * MIB),
         name="exchange",
-    )(magnetization, stiffness, *halos)
+    )(index, magnetization, stiffness, *halos)
 
 
 def line_tables(counts, top_rows, kys, size):
@@ -359,13 +443,21 @@
     return steps, np.pad(offsets, ((0, 0), (0, TILE - 4), (0, 0)))
 
 
-def depth_tables(group, kzs, depth):
-    size = group * kzs
-    kz = np.arange(size).reshape(group, kzs, 1)
-    angle = (kz * np.arange(depth) % size) * (2.0 * math.pi / size)
-    there = np.concatenate([np.cos(angle), -np.sin(angle)], axis=1).astype(np.float32)
-    back = np.swapaxes(there, 1, 2)
-    return there, back
+def depth_tables(counts, kzs, depth_block):
+    count_x, count_y, count_z = counts
+    size = count_y * count_z * kzs
+    share = depth_block // count_x
+    kz = np.arange(size).reshape(count_y * count_z, kzs, 1)
+
+    def table(z):
+        angle = (kz * z % size) * (2.0 * math.pi / size)
+        return np.concatenate([np.cos(angle), -np.sin(angle)], axis=1).astype(np.float32)
+
+    row = np.arange(count_x * count_z * TILE)
+    within = row % TILE
+    z = row // TILE % count_z * depth_block + row // (TILE * count_z) * share + within
+    there = np.where(within < share, table(z), np.float32(0.0))
+    return there, np.swapaxes(table(np.arange(depth_block * count_z)), 1, 2)
 
 
 def stacked_product(real, imag, tables, sign):
@@ -378,8 +470,7 @@
     return dot3(jnp.concatenate([upper, lower], axis=0), tables)
 
 
-def back_and_forth(real, imag, kernel, high, low, turns):
-    tables = (high[...], low[...])
+def back_and_forth(real, imag, columns_of, tables, turns):
     rows = real.shape[0]
     total_real = total_imag = None
     for b in range(turns.shape[1]):
@@ -388,10 +479,10 @@
             real * cosine + imag * sine, imag * cosine - real * sine, tables, -1
         )
         wave_real, wave_imag = waves[:rows], waves[rows:]
-        columns = slice(b * INNER, (b + 1) * INNER)
+        kernel = columns_of(b)
         weighted_real, weighted_imag = [], []
         for c in range(2):
-            kernel_real, kernel_imag = kernel[c, 0, :, columns], kernel[c, 1, :, columns]
+            kernel_real, kernel_imag = kernel[c, 0], kernel[c, 1]
             weighted_real.append(kernel_real * wave_real + kernel_imag * wave_imag)
             weighted_imag.append(kernel_real * wave_imag - kernel_imag * wave_real)
         back = stacked_product(
@@ -412,13 +503,42 @@
     ]
 
 
-def lines_kernel(counts, here, gathered, steps, offsets, high, low, turns, kernel, out):
+def lines_kernel(
+    counts,
+    here,
+    gathered,
+    steps_from,
+    offsets_from,
+    high_from,
+    low_from,
+    turns_from,
+    kernel_from,
+    out,
+    steps,
+    offset,
+    high,
+    low,
+    turns,
+    kernel,
+    semaphores,
+):
     count_x, count_y, count_z = counts
     group = count_y * count_z
-    top_rows = gathered.shape[1]
+    top_rows = LANES // group
     half = LANES // 2
-    kys = kernel.shape[2]
-    offset = offsets[here[0]]
+    kys = kernel_from.shape[2]
+    pairs = [
+        (steps_from, steps),
+        (offsets_from.at[here[0]], offset),
+        (turns_from, turns),
+        (high_from, high),
+        (low_from, low),
+    ]
+    for b in range(kernel.shape[0]):
+        pairs.append((kernel_from.at[:, :, :, pl.ds(b * INNER, INNER)], kernel.at[b]))
+    loads = copies_of(pairs, semaphores)
+    loads[0].wait()
+    loads[1].wait()
     table = []
     for h in range(2):
         step_cos, step_sin = steps[2 * h], steps[2 * h + 1]
@@ -426,7 +546,7 @@
         table.append(step_cos * offset_cos - step_sin * offset_sin)
         table.append(-(step_sin * offset_cos + step_cos * offset_sin))
     blocks = [
-        gathered[g * group : (g + 1) * group].reshape(group * top_rows, LANES)
+        gathered[g * group : (g + 1) * group, 0:top_rows, :].reshape(group * top_rows, LANES)
         for g in range(count_x)
     ]
     mixed = dot3(jnp.concatenate(table, axis=0), split(jnp.concatenate(blocks, axis=1)))
@@ -444,22 +564,42 @@
             )
         )
     lines = jnp.concatenate(pieces, axis=1)
-    images = back_and_forth(lines[:kys], lines[kys:], kernel, high, low, turns)
+    for load in loads[2:5]:
+        load.wait()
+
+    def columns_of(b):
+        loads[5 + b].wait()
+        return kernel.at[b]
+
+    images = back_and_forth(
+        lines[:kys], lines[kys:], columns_of, (high[...], low[...]), turns
+    )
     for c in range(2):
         block = jnp.concatenate(images[c], axis=0).T
         out[:, c * TILE : (c + 1) * TILE, :] = block.reshape(count_x * group, TILE, LANES)
 
 
 def side_kernel_body(counts, here, gathered, there, back, high, low, turns, kernel, out):
-    count_y, count_z = counts[1:]
-    depth_block = gathered.shape[1]
+    count_x, count_y, count_z = counts
+    depth_block = out.shape[1] // 2
+    top_rows = gathered.shape[1] - TILE
     kzs = kernel.shape[2]
-    blocks = [
-        gathered[y * count_z : (y + 1) * count_z].reshape(count_z * depth_block, LANES)
-        for y in range(count_y)
-    ]
+    blocks = []
+    for y in range(count_y):
+        rows = [
+            gathered[(x * count_y + y) * count_z + z, top_rows:, :]
+            for x in range(count_x)
+            for z in range(count_z)
+        ]
+        blocks.append(jnp.concatenate(rows, axis=0))
     lines = dot3(there[here[0]], split(jnp.concatenate(blocks, axis=1)))
-    images = back_and_forth(lines[:kzs], lines[kzs:], kernel, high, low, turns)
+
+    def columns_of(b):
+        return kernel.at[:, :, :, b * INNER : (b + 1) * INNER]
+
+    images = back_and_forth(
+        lines[:kzs], lines[kzs:], columns_of, (high[...], low[...]), turns
+    )
     scale = 1.0 / (count_y * count_z * kzs * kernel.shape[3])
     for c in range(2):
         image = dot3(back[here[0]] * scale, split(jnp.concatenate(images[c], axis=0)))
@@ -520,20 +660,30 @@
         out[2, z] = exchange_grad[2, z] + side[1][z : z + 1]
 
 
-MIB = 1024 * 1024
-SMEM = pl.BlockSpec(memory_space=pltpu.SMEM)
-VMEM = pl.BlockSpec(memory_space=pltpu.VMEM)
-
-
-def call(body, name, shape, limit, *operands, scalars=0):
+def call(body, name, shape, limit, kinds, operands, scratch=()):
     return pl.pallas_call(
         body,
         out_shape=jax.ShapeDtypeStruct(shape, f32),
-        in_specs=[SMEM] * scalars + [VMEM] * (len(operands) - scalars),
+        in_specs=[{"s": SMEM, "v": VMEM, "h": HBM}[kind] for kind in kinds],
         out_specs=VMEM,
+        scratch_shapes=list(scratch),
         compiler_params=pltpu.CompilerParams(vmem_limit_bytes=limit * MIB),
         name=name,
     )(*operands)
+
+
+def residual_blocks(residual_top, residual_side, devices, share):
+    block_x, block_y = residual_top.shape
+    top_rows = block_y // 2
+    top_piece = residual_top.T.reshape(2, top_rows, block_x)
+    top_piece = jnp.concatenate([top_piece[0], top_piece[1]], axis=1)
+    side_piece = lax.dynamic_slice_in_dim(
+        residual_side.T, lax.axis_index("gx") * share, share, axis=0
+    )
+    piece = jnp.concatenate(
+        [top_piece, side_piece, jnp.zeros((TILE - share, LANES), f32)], axis=0
+    )
+    return jnp.broadcast_to(piece[None], (devices,) + piece.shape)
 
 
 def fast_on_device(magnetization, stiffness, residual_top, residual_side, top_kernel, side_kernel):
@@ -554,33 +704,29 @@
     (high, low), _, turns = transform_tables(extent, size)
     high, low, turns = jnp.asarray(high), jnp.asarray(low), jnp.asarray(turns)
     steps, offsets = line_tables(counts, top_rows, kys, size)
-    there, back = depth_tables(group, kzs, depth_block * count_z)
-
-    piece = residual_top.T.reshape(2, top_rows, block_x)
-    piece = jnp.concatenate([piece[0], piece[1]], axis=1)
-    sent = jnp.broadcast_to(piece[None], (devices, top_rows, LANES))
+    there, back = depth_tables(counts, kzs, depth_block)
+
+    sent = residual_blocks(residual_top, residual_side, devices, depth_block // count_x)
     gathered = lax.all_to_all(sent, ALL, 0, 0, tiled=True)
-
-    sent = jnp.broadcast_to(residual_side.T[None], (group, depth_block, LANES))
-    side_gathered = lax.all_to_all(sent, ("gy", "gz"), 0, 0, tiled=True)
-
     halos = exchange_halos(magnetization, stiffness)
-    gathered, side_gathered, halos = lax.optimization_barrier((gathered, side_gathered, halos))
+    gathered, halos = lax.optimization_barrier((gathered, halos))
 
     lines = call(
         functools.partial(lines_kernel, counts),
         "lines",
         (devices, 2 * TILE, LANES),
         24,
-        index,
-        gathered,
-        jnp.asarray(steps),
-        jnp.asarray(offsets),
-        high,
-        low,
-        turns,
-        top_kernel,
-        scalars=1,
+        "svhhhhhh",
+        (index, gathered, jnp.asarray(steps), jnp.asarray(offsets), high, low, turns, top_kernel),
+        [
+            pltpu.VMEM(steps.shape, f32),
+            pltpu.VMEM(offsets.shape[1:], f32),
+            pltpu.VMEM(high.shape, bf16),
+            pltpu.VMEM(low.shape, bf16),
+            pltpu.VMEM(turns.shape, f32),
+            pltpu.VMEM((size // INNER, 2, 2, kys, INNER), f32),
+            pltpu.SemaphoreType.DMA((5 + size // INNER,)),
+        ],
     )
     arrived = lax.all_to_all(lines, ALL, 0, 0, tiled=True)
     side = call(
@@ -588,31 +734,30 @@
         "side",
         (group, 2 * depth_block, LANES),
         16,
-        plane_index,
-        side_gathered,
-        jnp.asarray(there),
-        jnp.asarray(back),
-        high,
-        low,
-        turns,
-        side_kernel,
-        scalars=1,
-    )
-    exchange_grad = exchange_of(magnetization, stiffness, halos)
+        "svvvvvvv",
+        (
+            plane_index,
+            gathered,
+            jnp.asarray(there),
+            jnp.asarray(back),
+            high,
+            low,
+            turns,
+            side_kernel,
+        ),
+    )
+    exchange_grad = exchange_of(counts, index, magnetization, stiffness, halos)
     arrived, side, exchange_grad = lax.optimization_barrier((arrived, side, exchange_grad))
     rows = call(
         functools.partial(rows_kernel, counts),
         "rows",
         (group, 2 * TILE + 2 * depth_block, LANES),
         16,
-        arrived,
-        side,
-        high,
-        low,
-        turns,
+        "vvvvv",
+        (arrived, side, high, low, turns),
     )
     arrived = lax.all_to_all(rows, ("gy", "gz"), 0, 0, tiled=True)
-    return call(sum_kernel, "gradient", magnetization.shape, 16, exchange_grad, arrived)
+    return call(sum_kernel, "gradient", magnetization.shape, 16, "vv", (exchange_grad, arrived))
 
 
 def fits(counts, stiffness, residual_top, residual_side, top_kernel, side_kernel):
@@ -648,20 +793,14 @@
     top_rows = block_y // 2
     share = depth_block // count_x
 
-    top_piece = residual_top.T.reshape(2, top_rows, block_x)
-    top_piece = jnp.concatenate([top_piece[0], top_piece[1]], axis=1)
-    side_piece = lax.dynamic_slice_in_dim(
-        residual_side.T, lax.axis_index("gx") * share, share, axis=0
-    )
-    piece = jnp.concatenate(
-        [top_piece, side_piece, jnp.zeros((TILE - share, LANES), f32)], axis=0
-    )
-    rows = piece.shape[0]
-    sent = jnp.broadcast_to(piece[None], (devices, rows, LANES)).reshape(devices * rows, LANES)
-    gathered = lax.all_to_all(sent, ALL, 0, 0, tiled=True).reshape(devices, rows, LANES)
-
+    sent = residual_blocks(residual_top, residual_side, devices, share)
+    rows = sent.shape[1]
+    gathered = lax.all_to_all(sent, ALL, 0, 0, tiled=True)
+    index = (
+        (lax.axis_index("gx") * count_y + lax.axis_index("gy")) * count_z + lax.axis_index("gz")
+    ).reshape(1)
     exchange_grad = exchange_of(
-        magnetization, stiffness, exchange_halos(magnetization, stiffness)
+        counts, index, magnetization, stiffness, exchange_halos(magnetization, stiffness)
     )
 
     parts = image_parts(

time: 77.1 us -> 60.7 us (0.79)
  starting transfers between devices: 26.8 us -> 17.2 us
  local copies, waits for them, and re-layouts: 14.2 us -> 10.5 us
  Pallas kernels: 21.4 us -> 19.7 us
    ppermute x5, starting transfers between devices: 11.9 us -> 6.42 us  [ring(): lax.ppermute(block, axis, [(i, (i + distance) % count) for i in range(cou...]
    all_to_all x1 -> x0, starting transfers between devices: 5.17 us -> none  [fast_on_device(): side_gathered = lax.all_to_all(sent, ('gy', 'gz'), 0, 0, tiled=True)]
    pallas_call x2, Pallas kernels: 11.9 us -> 7.41 us  [the longest x1 5.96 us: exchange_of(): pl.pallas_call(functools.partial(exchange_kernel, counts), in_specs=[SMEM...]
    all_to_all x1 -> x0, waiting for transfers between devices: 3.83 us -> none  [fast_on_device(): side_gathered = lax.all_to_all(sent, ('gy', 'gz'), 0, 0, tiled=True)]
    all_to_all x1, starting transfers between devices: 4.14 us -> 7.3 us  [fast_on_device(): gathered = lax.all_to_all(sent, ALL, 0, 0, tiled=True)]
    ppermute x5, waiting for transfers between devices: 0.01 us -> 3.06 us  [ring(): lax.ppermute(block, axis, [(i, (i + distance) % count) for i in range(cou...]
    pallas_call x4, Pallas kernels: 9.42 us -> 12.3 us  [call(): pl.pallas_call(body, out_shape=jax.ShapeDtypeStruct(shape, f32), in_specs...]
    unnamed x50 -> x56, local copies, waits for them, and re-layouts: 11.3 us -> 8.82 us
  transfers between devices with their start and end apart: 8 -> 7, of which waited for: 1 -> 2; matrix products, arithmetic and copies ran while one was open for 2% -> 0% of each run, Pallas kernels for 19% -> 17%
where the time goes in v2:
time: 60.7 us; the launch traced here: 60.1 us
  Pallas kernels  19.7 us (32%)
  starting transfers between devices  17.2 us (28%)
  local copies, waits for them, and re-layouts  10.5 us (17%)
  blocking collectives  8.72 us (14%)
  waiting for transfers between devices  3.68 us (6%)
    pallas_call x4, Pallas kernels, call(): pl.pallas_call(body, out_shape=jax.ShapeDtypeStruct(shape, f32), in_specs...  12.3 us
    unnamed x56, local copies, waits for them, and re-layouts  8.82 us
    all_to_all x1, blocking collectives, fast_on_device(): arrived = lax.all_to_all(rows, ('gy', 'gz'), 0, 0, tiled=True)  8.72 us
    all_to_all x1, starting transfers between devices, fast_on_device(): gathered = lax.all_to_all(sent, ALL, 0, 0, tiled=True)  7.3 us
    ppermute x5, starting transfers between devices, ring(): lax.ppermute(block, axis, [(i, (i + distance) % count) for i in range(cou...  6.42 us
    pallas_call x1, Pallas kernels, exchange_of(): pl.pallas_call(functools.partial(exchange_kernel, counts), in_specs=[SMEM...  5.96 us
    all_to_all x1, starting transfers between devices, fast_on_device(): arrived = lax.all_to_all(lines, ALL, 0, 0, tiled=True)  3.51 us
    ppermute x5, waiting for transfers between devices, ring(): lax.ppermute(block, axis, [(i, (i + distance) % count) for i in range(cou...  3.06 us
  transfers between devices with their start and end apart: 7, of which 2 were waited for; matrix products, arithmetic and copies ran while one was open for 0% of the time, Pallas kernels for 17%

profile of v2, /device:TPU:0, one launch (start us, length us, event | category | flops | bytes accessed | tf_op | source)
XLA Modules:
  0.0 60.1 jit_solution(6508148507604977740)
XLA Ops:
  0.0 0.8 %fusion = (f32[16,64]{1,0:T(8,128)S(1)}, f32[16,64]{1,0:T(8,128)S(1)}) fusion(f32[32,64]{1,0:T(8,128)} %bitcast.5), kind=kLoop, calls=%fused_computation.2 | loop fusion | bytes 16384 | tf_op jit(solution)/shard_map/slice | solution.py:679
  0.8 0.1 pad.3.clone
  0.9 0.1 maximum_maximum_fusion
  0.9 0.0 copy-start.11
  1.0 0.0 copy-start.20
  1.0 0.8 %broadcast_in_dim.10 = f32[32,24,128]{2,1,0:T(8,128)} broadcast(f32[24,128]{1,0:T(8,128)S(1)} %maximum_maximum_fusion), dimensions={1,2} | broadcast | bytes 405504 | tf_op jit(solution)/shard_map/broadcast_in_dim | solution.py:686
  1.7 7.3 %all-to-all-start = ((f32[32,24,128]{2,1,0:T(8,128)}), f32[32,24,128]{2,1,0:T(8,128)S(1)}, u32[]{:S(2)}, u32[]{:S(2)}) async-start(f32[32,24,128]{2,1,0:T(8,128)} %broadcast_in_dim.10), calls=%async_computation | async-start | bytes 786432 | tf_op jit(solution)/shard_map/all_to_all | solution.py:710
  9.1 1.4 %copy-done.1 = f32[3,16,64,128]{3,2,1,0:T(8,128)S(1)} copy-done((f32[3,16,64,128]{3,2,1,0:T(8,128)S(1)}, f32[3,16,64,128]{3,2,1,0:T(8,128)}, u32[]{:S(2)}) %copy-start.1) | copy-done | bytes 1572888
  10.5 1.5 %faces.1 = (f32[4,64,128]{2,1,0:T(8,128)S(1)}, f32[4,64,128]{2,1,0:T(8,128)S(1)}, f32[4,16,128]{2,1,0:T(8,128)S(1)}, f32[4,16,128]{2,1,0:T(8,128)S(1)}, f32[64,128]{1,0:T(8,128)S(1)}) custom-call(f32[3,16,64,128]{3,2,1,0:T(8,128)S(1)} %copy-done.1, f32[16,64,128]{2,1,0:T(8,128)S(1)} %copy-done.7), custom_call_target="tpu_custom_call" | custom-call | tf_op jit(solution)/shard_map/faces/pallas_call | solution.py:387
  11.9 1.6 %collective-permute-start = (f32[4,64,128]{2,1,0:T(8,128)S(1)}, f32[4,64,128]{2,1,0:T(8,128)S(1)}, u32[]{:S(2)}, u32[]{:S(2)}) collective-permute-start(f32[4,64,128]{2,1,0:T(8,128)S(1)} %get-tuple-element.21), channel_id=1, source_target_pairs={{0,3},{1,0},{2,1},{3,2},{4,7},{5,4},{6,5},{7,6},{8,11},{9,8},{10,9... | collective-permute-start | bytes 393224 | tf_op jit(solution)/shard_map/ppermute | solution.py:381
  13.5 3.3 %collective-permute-start.2 = (f32[4,16,128]{2,1,0:T(8,128)S(1)}, f32[4,16,128]{2,1,0:T(8,128)S(1)}, u32[]{:S(2)}, u32[]{:S(2)}) collective-permute-start(f32[4,16,128]{2,1,0:T(8,128)S(1)} %get-tuple-element.23), channel_id=1, source_target_pairs={{0,24},{8,0},{16,8},{24,16},{1,25},{9,1},{17,9},{25,17},{2,26},{10... | collective-permute-start | bytes 98312 | tf_op jit(solution)/shard_map/ppermute | solution.py:381
  16.9 1.5 %collective-permute-start.4 = (f32[64,128]{1,0:T(8,128)S(1)}, f32[64,128]{1,0:T(8,128)S(1)}, u32[]{:S(2)}, u32[]{:S(2)}) collective-permute-start(f32[64,128]{1,0:T(8,128)S(1)} %get-tuple-element.33.y_faces), channel_id=1, source_target_pairs={{0,4},{4,0},{1,5},{5,1},{2,6},{6,2},{3,7},{7,3},{8,12},{12,8},{9,1... | collective-permute-start | bytes 98312 | tf_op jit(solution)/shard_map/ppermute | solution.py:381
  18.4 0.6 %copy-done.22 = f32[64,128]{1,0:T(8,128)} copy-done((f32[64,128]{1,0:T(8,128)}, f32[64,128]{1,0:T(8,128)S(1)}, u32[]{:S(2)}) %copy-start.22) | copy-done | bytes 32792
  19.0 0.6 %copy-done.24 = f32[4,16,128]{2,1,0:T(8,128)} copy-done((f32[4,16,128]{2,1,0:T(8,128)}, f32[4,16,128]{2,1,0:T(8,128)S(1)}, u32[]{:S(2)}) %copy-start.24) | copy-done | bytes 32792
  19.6 3.0 %collective-permute-done.3.x_before = f32[4,16,128]{2,1,0:T(8,128)S(1)} collective-permute-done((f32[4,16,128]{2,1,0:T(8,128)S(1)}, f32[4,16,128]{2,1,0:T(8,128)S(1)}, u32[]{:S(2)}, u32[]{:S(2)}) %collective-permute-start.3) | collective-permute-done | bytes 32800 | tf_op jit(solution)/shard_map/ppermute | solution.py:381
  22.6 0.6 %copy-done.26 = f32[4,16,128]{2,1,0:T(8,128)} copy-done((f32[4,16,128]{2,1,0:T(8,128)}, f32[4,16,128]{2,1,0:T(8,128)S(1)}, u32[]{:S(2)}) %copy-start.26) | copy-done | bytes 32792
  23.3 0.7 %copy-done.16 = f32[4,64,128]{2,1,0:T(8,128)} copy-done((f32[4,64,128]{2,1,0:T(8,128)}, f32[4,64,128]{2,1,0:T(8,128)S(1)}, u32[]{:S(2)}) %copy-start.16) | copy-done | bytes 131096
  23.9 0.6 %copy-done.18 = f32[4,64,128]{2,1,0:T(8,128)} copy-done((f32[4,64,128]{2,1,0:T(8,128)}, f32[4,64,128]{2,1,0:T(8,128)S(1)}, u32[]{:S(2)}) %copy-start.18) | copy-done | bytes 131096
  24.6 0.0 copy-start.6
  24.6 1.6 %copy-done.6 = f32[2,2,64,2048]{3,2,1,0:T(8,128)S(1)} copy-done((f32[2,2,64,2048]{3,2,1,0:T(8,128)S(1)}, f32[2,2,64,2048]{3,2,1,0:T(8,128)}, u32[]{:S(2)}) %copy-start.6) | copy-done | bytes 2097176
  26.2 6.7 %lines.1 = f32[32,16,128]{2,1,0:T(8,128)} custom-call(s32[1]{0:T(128)} %bitcast.here, f32[32,24,128]{2,1,0:T(8,128)S(1)} %all-to-all-done.gathered, f32[4,64,128]{2,1,0:T(8,128)S(1)} %copy-done.21, f32[32,8,128]{2,1,0:T(8,128)S(1)} %copy-done.20, bf16[512,256]{1,0:T(8,128)(2,1)S(1)} %copy-done.4, bf16[512,256]{1,0:T(8,128)(2,1)S(1)} %copy-done.3, ...), custom_call_target="tpu_custom_call" | custom-call | tf_op jit(solution)/shard_map/lines/pallas_call | solution.py:664
  33.0 3.5 %all-to-all-start.1 = ((f32[32,16,128]{2,1,0:T(8,128)}), f32[32,16,128]{2,1,0:T(8,128)}, u32[]{:S(2)}, u32[]{:S(2)}) async-start(f32[32,16,128]{2,1,0:T(8,128)} %lines.1), calls=%async_computation.1 | async-start | bytes 524288 | tf_op jit(solution)/shard_map/all_to_all | solution.py:731
  36.5 0.0 copy-start.15
  36.5 0.9 %copy-done.15 = f32[8,32,128]{2,1,0:T(8,128)S(1)} copy-done((f32[8,32,128]{2,1,0:T(8,128)S(1)}, f32[8,32,128]{2,1,0:T(8,128)}, u32[]{:S(2)}) %copy-start.15) | copy-done | bytes 131096
  37.5 2.9 %side.1 = f32[8,32,128]{2,1,0:T(8,128)S(1)} custom-call(s32[1]{0:T(128)} %bitcast.3.here, f32[32,24,128]{2,1,0:T(8,128)S(1)} %all-to-all-done.gathered, f32[8,32,128]{2,1,0:T(8,128)S(1)} %copy-done.15, f32[8,64,32]{2,1,0:T(8,128)S(1)} %copy-done.10, bf16[512,256]{1,0:T(8,128)(2,1)S(1)} %copy-done.4, bf16[512,256]{1,0:T(8,128)(2,1)S(1)} %copy-done.3, ...), custom_call_target="tpu_custom_call" | custom-call | tf_op jit(solution)/shard_map/side/pallas_call | solution.py:664
  40.5 6.0 %exchange.1.exchange_grad = f32[3,16,64,128]{3,2,1,0:T(8,128)S(1)} custom-call(s32[1]{0:T(128)} %bitcast.here, f32[3,16,64,128]{3,2,1,0:T(8,128)S(1)} %copy-done.2, f32[16,64,128]{2,1,0:T(8,128)S(1)} %copy-done.8, f32[4,64,128]{2,1,0:T(8,128)S(1)} %copy-done.17, f32[4,64,128]{2,1,0:T(8,128)S(1)} %copy-done.19, f32[4,16,128]{2,1,0:T(8,128)S(1)} %copy-done.25, ...), custom_call_target="tpu_custom_call" | custom-call | tf_op jit(solution)/shard_map/exchange/pallas_call | solution.py:415
  46.4 0.6 %all-to-all-done.1.arrived = f32[32,16,128]{2,1,0:T(8,128)} async-done(((f32[32,16,128]{2,1,0:T(8,128)}), f32[32,16,128]{2,1,0:T(8,128)}, u32[]{:S(2)}, u32[]{:S(2)}) %all-to-all-start.1) | async-done | bytes 262176 | tf_op jit(solution)/shard_map/all_to_all | solution.py:731
  47.1 0.9 %copy-done.5 = bf16[512,256]{1,0:T(8,128)(2,1)S(1)} copy-done((bf16[512,256]{1,0:T(8,128)(2,1)S(1)}, bf16[512,256]{1,0:T(8,128)(2,1)}, u32[]{:S(2)}) %copy-start.5) | copy-done | bytes 262168
  48.0 0.7 %copy-done.12 = f32[2,8,256]{2,1,0:T(8,128)S(1)} copy-done((f32[2,8,256]{2,1,0:T(8,128)S(1)}, f32[2,8,256]{2,1,0:T(8,128)}, u32[]{:S(2)}) %copy-start.12) | copy-done | bytes 16408
  48.7 1.4 %rows.1 = f32[8,48,128]{2,1,0:T(8,128)S(1)} custom-call(f32[32,16,128]{2,1,0:T(8,128)} %all-to-all-done.1.arrived, f32[8,32,128]{2,1,0:T(8,128)S(1)} %side.1, bf16[512,256]{1,0:T(8,128)(2,1)S(1)} %copy-done.5, bf16[512,256]{1,0:T(8,128)(2,1)S(1)} %copy-done.3, f32[2,8,256]{2,1,0:T(8,128)S(1)} %copy-done.12), custom_call_target="tpu_custom_call" | custom-call | tf_op jit(solution)/shard_map/rows/pallas_call | solution.py:664
  50.1 8.7 %all_to_all.15.arrived = f32[8,48,128]{2,1,0:T(8,128)S(1)} all-to-all(f32[8,48,128]{2,1,0:T(8,128)S(1)} %rows.1), channel_id=1, replica_groups=mesh['gx'=4,'gy'=2,'gz'=4] {'gy','gz'}, dimensions={0} | all-to-all | bytes 393216 | tf_op jit(solution)/shard_map/all_to_all | solution.py:759
  58.9 1.3 %gradient.1 = f32[3,16,64,128]{3,2,1,0:T(8,128)} custom-call(f32[3,16,64,128]{3,2,1,0:T(8,128)S(1)} %exchange.1.exchange_grad, f32[8,48,128]{2,1,0:T(8,128)S(1)} %all_to_all.15.arrived), custom_call_target="tpu_custom_call" | custom-call | tf_op jit(solution)/shard_map/gradient/pallas_call | solution.py:664
  (51 shorter events, 0.1 us)
Async XLA Ops:
  0.0 0.9 %copy-start = (f32[128,16]{0,1:T(8,128)S(1)}, f32[128,16]{0,1:T(8,128)}, u32[]{:S(2)}) copy-start(f32[128,16]{0,1:T(8,128)} %param.16) | copy-start | bytes 24580
  0.0 9.1 %copy-start.7 = (f32[16,64,128]{2,1,0:T(8,128)S(1)}, f32[16,64,128]{2,1,0:T(8,128)}, u32[]{:S(2)}) copy-start(f32[16,64,128]{2,1,0:T(8,128)} %stiffness.3) | copy-start | bytes 1572868
  0.9 23.6 %copy-start.3 = (bf16[512,256]{1,0:T(8,128)(2,1)S(1)}, bf16[512,256]{1,0:T(8,128)(2,1)}, u32[]{:S(2)}) copy-start(bf16[512,256]{1,0:T(8,128)(2,1)} %constant.37.clone.low_from.low) | copy-start | bytes 786436
  0.9 23.6 %copy-start.4 = (bf16[512,256]{1,0:T(8,128)(2,1)S(1)}, bf16[512,256]{1,0:T(8,128)(2,1)}, u32[]{:S(2)}) copy-start(bf16[512,256]{1,0:T(8,128)(2,1)} %constant.36.clone.high_from.high) | copy-start | bytes 786436
  0.9 23.6 %copy-start.11 = (f32[2,8,256]{2,1,0:T(8,128)S(1)}, f32[2,8,256]{2,1,0:T(8,128)}, u32[]{:S(2)}) copy-start(f32[2,8,256]{2,1,0:T(8,128)} %constant.38.clone.turns_from.turns) | copy-start | bytes 49156
  1.0 23.6 %copy-start.20 = (f32[32,8,128]{2,1,0:T(8,128)S(1)}, f32[32,8,128]{2,1,0:T(8,128)}, u32[]{:S(2)}) copy-start(f32[32,8,128]{2,1,0:T(8,128)} %constant.40.clone.offsets_from) | copy-start | bytes 393220
  1.7 22.8 %all-to-all-start = ((f32[32,24,128]{2,1,0:T(8,128)}), f32[32,24,128]{2,1,0:T(8,128)S(1)}, u32[]{:S(2)}, u32[]{:S(2)}) async-start(f32[32,24,128]{2,1,0:T(8,128)} %broadcast_in_dim.10), calls=%async_computation | async-start | bytes 786432 | tf_op jit(solution)/shard_map/all_to_all | solution.py:710
  9.1 1.4 %copy-start.1 = (f32[3,16,64,128]{3,2,1,0:T(8,128)S(1)}, f32[3,16,64,128]{3,2,1,0:T(8,128)}, u32[]{:S(2)}) copy-start(f32[3,16,64,128]{3,2,1,0:T(8,128)} %magnetization.3) | copy-start | bytes 4718596
  10.5 14.1 %copy-start.21 = (f32[4,64,128]{2,1,0:T(8,128)S(1)}, f32[4,64,128]{2,1,0:T(8,128)}, u32[]{:S(2)}) copy-start(f32[4,64,128]{2,1,0:T(8,128)} %constant.39.clone.steps_from) | copy-start | bytes 393220
  11.9 11.3 %collective-permute-start = (f32[4,64,128]{2,1,0:T(8,128)S(1)}, f32[4,64,128]{2,1,0:T(8,128)S(1)}, u32[]{:S(2)}, u32[]{:S(2)}) collective-permute-start(f32[4,64,128]{2,1,0:T(8,128)S(1)} %get-tuple-element.21), channel_id=1, source_target_pairs={{0,3},{1,0},{2,1},{3,2},{4,7},{5,4},{6,5},{7,6},{8,11},{9,8},{10,9... | collective-permute-start | bytes 393224 | tf_op jit(solution)/shard_map/ppermute | solution.py:381
  13.5 10.4 %collective-permute-start.1 = (f32[4,64,128]{2,1,0:T(8,128)S(1)}, f32[4,64,128]{2,1,0:T(8,128)S(1)}, u32[]{:S(2)}, u32[]{:S(2)}) collective-permute-start(f32[4,64,128]{2,1,0:T(8,128)S(1)} %get-tuple-element.22), channel_id=1, source_target_pairs={{0,1},{1,2},{2,3},{3,0},{4,5},{5,6},{6,7},{7,4},{8,9},{9,10},{10,1... | collective-permute-start | bytes 393224 | tf_op jit(solution)/shard_map/ppermute | solution.py:381
  13.5 5.5 %collective-permute-start.2 = (f32[4,16,128]{2,1,0:T(8,128)S(1)}, f32[4,16,128]{2,1,0:T(8,128)S(1)}, u32[]{:S(2)}, u32[]{:S(2)}) collective-permute-start(f32[4,16,128]{2,1,0:T(8,128)S(1)} %get-tuple-element.23), channel_id=1, source_target_pairs={{0,24},{8,0},{16,8},{24,16},{1,25},{9,1},{17,9},{25,17},{2,26},{10... | collective-permute-start | bytes 98312 | tf_op jit(solution)/shard_map/ppermute | solution.py:381
  16.9 5.8 %collective-permute-start.3 = (f32[4,16,128]{2,1,0:T(8,128)S(1)}, f32[4,16,128]{2,1,0:T(8,128)S(1)}, u32[]{:S(2)}, u32[]{:S(2)}) collective-permute-start(f32[4,16,128]{2,1,0:T(8,128)S(1)} %get-tuple-element.24), channel_id=1, source_target_pairs={{0,8},{8,16},{16,24},{24,0},{1,9},{9,17},{17,25},{25,1},{2,10},{10... | collective-permute-start | bytes 98312 | tf_op jit(solution)/shard_map/ppermute | solution.py:381
  16.9 6.4 %collective-permute-start.4 = (f32[64,128]{1,0:T(8,128)S(1)}, f32[64,128]{1,0:T(8,128)S(1)}, u32[]{:S(2)}, u32[]{:S(2)}) collective-permute-start(f32[64,128]{1,0:T(8,128)S(1)} %get-tuple-element.33.y_faces), channel_id=1, source_target_pairs={{0,4},{4,0},{1,5},{5,1},{2,6},{6,2},{3,7},{7,3},{8,12},{12,8},{9,1... | collective-permute-start | bytes 98312 | tf_op jit(solution)/shard_map/ppermute | solution.py:381
  23.3 9.7 %copy-start.13 = (f32[64,128]{1,0:T(8,128)}, f32[64,128]{1,0:T(8,128)S(1)}, u32[]{:S(2)}) copy-start(f32[64,128]{1,0:T(8,128)S(1)} %collective-permute-done.4.y_next.y_before) | copy-start | bytes 98308
  23.3 0.7 %copy-start.16 = (f32[4,64,128]{2,1,0:T(8,128)}, f32[4,64,128]{2,1,0:T(8,128)S(1)}, u32[]{:S(2)}) copy-start(f32[4,64,128]{2,1,0:T(8,128)S(1)} %collective-permute-done.z_next) | copy-start | bytes 393220
  23.9 0.6 %copy-start.18 = (f32[4,64,128]{2,1,0:T(8,128)}, f32[4,64,128]{2,1,0:T(8,128)S(1)}, u32[]{:S(2)}) copy-start(f32[4,64,128]{2,1,0:T(8,128)S(1)} %collective-permute-done.1.z_before) | copy-start | bytes 393220
  24.6 1.6 %copy-start.6 = (f32[2,2,64,2048]{3,2,1,0:T(8,128)S(1)}, f32[2,2,64,2048]{3,2,1,0:T(8,128)}, u32[]{:S(2)}) copy-start(f32[2,2,64,2048]{3,2,1,0:T(8,128)} %kernel_from.1) | copy-start | bytes 6291460
  26.2 10.3 %copy-start.9 = (f32[2,2,16,2048]{3,2,1,0:T(8,128)S(1)}, f32[2,2,16,2048]{3,2,1,0:T(8,128)}, u32[]{:S(2)}) copy-start(f32[2,2,16,2048]{3,2,1,0:T(8,128)} %kernel.1) | copy-start | bytes 1572868
  26.2 10.3 %copy-start.10 = (f32[8,64,32]{2,1,0:T(8,128)S(1)}, f32[8,64,32]{2,1,0:T(8,128)}, u32[]{:S(2)}) copy-start(f32[8,64,32]{2,1,0:T(8,128)} %constant.42.clone.back) | copy-start | bytes 196612
  33.0 7.4 %copy-start.2 = (f32[3,16,64,128]{3,2,1,0:T(8,128)S(1)}, f32[3,16,64,128]{3,2,1,0:T(8,128)}, u32[]{:S(2)}) copy-start(f32[3,16,64,128]{3,2,1,0:T(8,128)} %magnetization.3) | copy-start | bytes 4718596
  33.0 14.1 %all-to-all-start.1 = ((f32[32,16,128]{2,1,0:T(8,128)}), f32[32,16,128]{2,1,0:T(8,128)}, u32[]{:S(2)}, u32[]{:S(2)}) async-start(f32[32,16,128]{2,1,0:T(8,128)} %lines.1), calls=%async_computation.1 | async-start | bytes 524288 | tf_op jit(solution)/shard_map/all_to_all | solution.py:731
  36.5 3.9 %copy-start.8 = (f32[16,64,128]{2,1,0:T(8,128)S(1)}, f32[16,64,128]{2,1,0:T(8,128)}, u32[]{:S(2)}) copy-start(f32[16,64,128]{2,1,0:T(8,128)} %stiffness.3) | copy-start | bytes 1572868
  36.5 3.9 %copy-start.14 = (f32[64,128]{1,0:T(8,128)S(1)}, f32[64,128]{1,0:T(8,128)}, u32[]{:S(2)}) copy-start(f32[64,128]{1,0:T(8,128)} %copy-done.13) | copy-start | bytes 98308
  36.5 1.0 %copy-start.15 = (f32[8,32,128]{2,1,0:T(8,128)S(1)}, f32[8,32,128]{2,1,0:T(8,128)}, u32[]{:S(2)}) copy-start(f32[8,32,128]{2,1,0:T(8,128)} %constant.41.clone.there) | copy-start | bytes 393220
  37.5 2.9 %copy-start.17 = (f32[4,64,128]{2,1,0:T(8,128)S(1)}, f32[4,64,128]{2,1,0:T(8,128)}, u32[]{:S(2)}) copy-start(f32[4,64,128]{2,1,0:T(8,128)} %copy-done.16) | copy-start | bytes 393220
  37.5 2.9 %copy-start.19 = (f32[4,64,128]{2,1,0:T(8,128)S(1)}, f32[4,64,128]{2,1,0:T(8,128)}, u32[]{:S(2)}) copy-start(f32[4,64,128]{2,1,0:T(8,128)} %copy-done.18) | copy-start | bytes 393220
  37.5 3.0 %copy-start.23 = (f32[64,128]{1,0:T(8,128)S(1)}, f32[64,128]{1,0:T(8,128)}, u32[]{:S(2)}) copy-start(f32[64,128]{1,0:T(8,128)} %copy-done.22) | copy-start | bytes 98308
  37.5 3.0 %copy-start.25 = (f32[4,16,128]{2,1,0:T(8,128)S(1)}, f32[4,16,128]{2,1,0:T(8,128)}, u32[]{:S(2)}) copy-start(f32[4,16,128]{2,1,0:T(8,128)} %copy-done.24) | copy-start | bytes 98308
  37.5 3.0 %copy-start.27 = (f32[4,16,128]{2,1,0:T(8,128)S(1)}, f32[4,16,128]{2,1,0:T(8,128)}, u32[]{:S(2)}) copy-start(f32[4,16,128]{2,1,0:T(8,128)} %copy-done.26) | copy-start | bytes 98308
  47.1 1.0 %copy-start.5 = (bf16[512,256]{1,0:T(8,128)(2,1)S(1)}, bf16[512,256]{1,0:T(8,128)(2,1)}, u32[]{:S(2)}) copy-start(bf16[512,256]{1,0:T(8,128)(2,1)} %constant.36.clone.high_from.high) | copy-start | bytes 786436
  48.0 0.7 %copy-start.12 = (f32[2,8,256]{2,1,0:T(8,128)S(1)}, f32[2,8,256]{2,1,0:T(8,128)}, u32[]{:S(2)}) copy-start(f32[2,8,256]{2,1,0:T(8,128)} %constant.38.clone.turns_from.turns) | copy-start | bytes 49156
  (3 other events, 1.8 us)

commit v3 on v2

--- a/solution.py
+++ b/solution.py
@@ -32,6 +32,18 @@
     def one(a, b):
         return lax.dot_general(a, b, (((1,), (0,)), ((), ())), preferred_element_type=f32)
     return one(high, right[0]) + one(low, right[0]) + one(high, right[1])
+
+
+def call(body, name, shape, limit, kinds, operands, scratch=()):
+    return pl.pallas_call(
+        body,
+        out_shape=jax.ShapeDtypeStruct(shape, f32),
+        in_specs=[{"s": SMEM, "v": VMEM, "h": HBM}[kind] for kind in kinds],
+        out_specs=VMEM,
+        scratch_shapes=list(scratch),
+        compiler_params=pltpu.CompilerParams(vmem_limit_bytes=limit * MIB),
+        name=name,
+    )(*operands)
 
 
 def transform_tables(extent, size):
@@ -278,32 +290,25 @@
     return 4.0 * a * b / (a + b)
 
 
-def exchange_kernel(
+def edges_kernel(
     counts,
     here,
-    magnetization,
-    stiffness,
+    z_first,
+    z_last,
+    x_first,
+    x_last,
+    y_faces,
     z_next,
     z_before,
     x_next,
     x_before,
     y_next,
     y_before,
-    y_faces,
     out,
-    m,
-    s,
-    semaphores,
 ):
-    depth, across = stiffness.shape[:2]
-    chunk = depth // 4
-    pairs = []
-    for k in range(4):
-        layers = slice(k * chunk, (k + 1) * chunk)
-        pairs.append((stiffness.at[layers], s.at[layers]))
-        pairs.append((magnetization.at[:, layers], m.at[:, layers]))
-    loads = copies_of(pairs, semaphores)
-
+    across = y_faces.shape[0]
+    depth = x_first.shape[1]
+    half = LANES // 2
     count_x, count_y, count_z = counts
     at_z = here[0] % count_z
     at_y = here[0] // count_z % count_y
@@ -312,16 +317,26 @@
     def inside(condition, values):
         return jnp.where(condition, values, 0.0)
 
+    row = 0
+    for own, halo, present in (
+        (z_last, z_next, at_z < count_z - 1),
+        (z_first, z_before, at_z > 0),
+        (x_last, x_next, at_x < count_x - 1),
+        (x_first, x_before, at_x > 0),
+    ):
+        rows = own.shape[1]
+        weight = twice_weight(own[3], inside(present, halo[3]))
+        for c in range(3):
+            out[row : row + rows, :] = weight * (own[c] - halo[c])
+            row += rows
+
     lane = lax.broadcasted_iota(jnp.int32, (across, LANES), 1)
-    row = lax.broadcasted_iota(jnp.int32, (across, LANES), 0)
-    first_lane, last_lane, last_row = lane == 0, lane == LANES - 1, row == across - 1
-    half = LANES // 2
-
     stiff = (lane >= 3 * depth) & (lane < 4 * depth)
 
     def y_edge(own, halo, present):
-        halo_stiffness = inside(present, halo)
-        weight = twice_weight(jnp.where(stiff, own, 1.0), jnp.where(stiff, halo_stiffness, 1.0))
+        weight = twice_weight(
+            jnp.where(stiff, own, 1.0), jnp.where(stiff, inside(present, halo), 1.0)
+        )
         spread = pltpu.roll(weight, LANES - 3 * depth, 1)
         for c in (1, 2):
             spread = jnp.where(
@@ -332,18 +347,23 @@
     own = y_faces[...]
     after = y_edge(pltpu.roll(own, half, 1), y_next[...], at_y < count_y - 1)
     before = y_edge(own, pltpu.roll(y_before[...], half, 1), at_y > 0)
-
-    loads[0].wait()
-    loads[1].wait()
-    below_weight = twice_weight(inside(at_z > 0, z_before[3]), s[0])
-    below = [below_weight * (z_before[c] - m[c, 0]) for c in range(3)]
+    out[row : row + across, :] = jnp.where(lane < half, after, pltpu.roll(before, half, 1))
+
+
+def exchange_kernel(magnetization, stiffness, edges, out):
+    depth, across = stiffness.shape[:2]
+    half = LANES // 2
+    lane = lax.broadcasted_iota(jnp.int32, (across, LANES), 1)
+    row = lax.broadcasted_iota(jnp.int32, (across, LANES), 0)
+    first_lane, last_lane, last_row = lane == 0, lane == LANES - 1, row == across - 1
+    z_rows, x_rows = 3 * across, 3 * depth
+    y_row = 2 * (z_rows + x_rows)
+    sides = edges[y_row : y_row + across, :]
+    below = [-edges[z_rows + c * across : z_rows + (c + 1) * across, :] for c in range(3)]
     for z in range(depth):
-        if z % chunk == 0 and z + chunk < depth:
-            for load in loads[2 * (z // chunk + 1) : 2 * (z // chunk + 2)]:
-                load.wait()
-        centre = s[z]
-        above = s[z + 1] if z + 1 < depth else inside(at_z < count_z - 1, z_next[3])
-        weight_z = twice_weight(centre, above)
+        centre = stiffness[z]
+        if z + 1 < depth:
+            weight_z = twice_weight(centre, stiffness[z + 1])
         weight_x = jnp.where(
             last_row, 0.0, twice_weight(centre, pltpu.roll(centre, across - 1, 0))
         )
@@ -352,28 +372,25 @@
         )
         for c in range(3):
             column = c * depth + z
-            values = m[c, z]
-            upper = m[c, z + 1] if z + 1 < depth else z_next[c]
-            up = weight_z * (values - upper)
+            values = magnetization[c, z]
+            if z + 1 < depth:
+                up = weight_z * (values - magnetization[c, z + 1])
+            else:
+                up = edges[c * across : (c + 1) * across, :]
             flux_x = weight_x * (values - pltpu.roll(values, across - 1, 0))
             flux_y = weight_y * (values - pltpu.roll(values, LANES - 1, 1))
             total = (up - below[c]) + (flux_x - pltpu.roll(flux_x, 1, 0))
             total = total + (flux_y - pltpu.roll(flux_y, 1, 1))
-            edge = jnp.where(
+            side = jnp.where(
                 first_lane,
-                before[:, column : column + 1],
-                jnp.where(last_lane, after[:, column : column + 1], 0.0),
+                sides[:, half + column : half + column + 1],
+                jnp.where(last_lane, sides[:, column : column + 1], 0.0),
             )
-            out[c, z] = total + edge
+            out[c, z] = total + side
             below[c] = up
-
-    for edge_row, halo, present in (
-        (across - 1, x_next, at_x < count_x - 1),
-        (0, x_before, at_x > 0),
-    ):
-        weight = twice_weight(s[:, edge_row, :], inside(present, halo[3]))
+    for start, edge_row in ((2 * z_rows, across - 1), (2 * z_rows + x_rows, 0)):
         for c in range(3):
-            out[c, :, edge_row, :] += weight * (m[c, :, edge_row, :] - halo[c])
+            out[c, :, edge_row, :] += edges[start + c * depth : start + (c + 1) * depth, :]
 
 
 def ring(block, axis, distance):
@@ -381,10 +398,10 @@
     return lax.ppermute(block, axis, [(i, (i + distance) % count) for i in range(count)])
 
 
-def exchange_halos(magnetization, stiffness):
+def edge_terms(counts, index, magnetization, stiffness):
     depth, across, along = stiffness.shape
     shape = jax.ShapeDtypeStruct
-    z_first, z_last, x_first, x_last, y_faces = pl.pallas_call(
+    faces = pl.pallas_call(
         faces_kernel,
         in_specs=[HBM, HBM],
         out_specs=[HBM, HBM, VMEM, VMEM, VMEM],
@@ -401,30 +418,33 @@
             pltpu.SemaphoreType.DMA((4,)),
             pltpu.SemaphoreType.DMA((8,)),
         ],
-        compiler_params=pltpu.CompilerParams(vmem_limit_bytes=8 * MIB),
+        compiler_params=pltpu.CompilerParams(vmem_limit_bytes=60 * MIB),
         name="faces",
     )(magnetization, stiffness)
+    z_first, z_last, x_first, x_last, y_faces = faces
     z_next, z_before = ring(z_first, "gz", -1), ring(z_last, "gz", 1)
     x_next, x_before = ring(x_first, "gx", -1), ring(x_last, "gx", 1)
     y_next = ring(y_faces, "gy", -1)
     y_before = y_next if lax.axis_size("gy") == 2 else ring(y_faces, "gy", 1)
-    return z_next, z_before, x_next, x_before, y_next, y_before, y_faces
-
-
-def exchange_of(counts, index, magnetization, stiffness, halos):
-    return pl.pallas_call(
-        functools.partial(exchange_kernel, counts),
-        in_specs=[SMEM, HBM, HBM] + [VMEM] * len(halos),
-        out_specs=VMEM,
-        out_shape=jax.ShapeDtypeStruct(magnetization.shape, f32),
-        scratch_shapes=[
-            pltpu.VMEM(magnetization.shape, f32),
-            pltpu.VMEM(stiffness.shape, f32),
-            pltpu.SemaphoreType.DMA((8,)),
-        ],
-        compiler_params=pltpu.CompilerParams(vmem_limit_bytes=16 * MIB),
-        name="exchange",
-    )(index, magnetization, stiffness, *halos)
+    return call(
+        functools.partial(edges_kernel, counts),
+        "edges",
+        (7 * across + 6 * depth, LANES),
+        16,
+        "s" + "v" * 11,
+        (index, *faces, z_next, z_before, x_next, x_before, y_next, y_before),
+    )
+
+
+def exchange_of(magnetization, stiffness, edges):
+    return call(
+        exchange_kernel,
+        "exchange",
+        magnetization.shape,
+        16,
+        "vvv",
+        (magnetization, stiffness, edges),
+    )
 
 
 def line_tables(counts, top_rows, kys, size):
@@ -503,42 +523,13 @@
     ]
 
 
-def lines_kernel(
-    counts,
-    here,
-    gathered,
-    steps_from,
-    offsets_from,
-    high_from,
-    low_from,
-    turns_from,
-    kernel_from,
-    out,
-    steps,
-    offset,
-    high,
-    low,
-    turns,
-    kernel,
-    semaphores,
-):
+def lines_kernel(counts, here, gathered, steps, offsets, high, low, turns, kernel, out):
     count_x, count_y, count_z = counts
     group = count_y * count_z
     top_rows = LANES // group
     half = LANES // 2
-    kys = kernel_from.shape[2]
-    pairs = [
-        (steps_from, steps),
-        (offsets_from.at[here[0]], offset),
-        (turns_from, turns),
-        (high_from, high),
-        (low_from, low),
-    ]
-    for b in range(kernel.shape[0]):
-        pairs.append((kernel_from.at[:, :, :, pl.ds(b * INNER, INNER)], kernel.at[b]))
-    loads = copies_of(pairs, semaphores)
-    loads[0].wait()
-    loads[1].wait()
+    kys = kernel.shape[2]
+    offset = offsets[here[0]]
     table = []
     for h in range(2):
         step_cos, step_sin = steps[2 * h], steps[2 * h + 1]
@@ -564,12 +555,9 @@
             )
         )
     lines = jnp.concatenate(pieces, axis=1)
-    for load in loads[2:5]:
-        load.wait()
 
     def columns_of(b):
-        loads[5 + b].wait()
-        return kernel.at[b]
+        return kernel.at[:, :, :, b * INNER : (b + 1) * INNER]
 
     images = back_and_forth(
         lines[:kys], lines[kys:], columns_of, (high[...], low[...]), turns
@@ -660,30 +648,26 @@
         out[2, z] = exchange_grad[2, z] + side[1][z : z + 1]
 
 
-def call(body, name, shape, limit, kinds, operands, scratch=()):
-    return pl.pallas_call(
-        body,
-        out_shape=jax.ShapeDtypeStruct(shape, f32),
-        in_specs=[{"s": SMEM, "v": VMEM, "h": HBM}[kind] for kind in kinds],
-        out_specs=VMEM,
-        scratch_shapes=list(scratch),
-        compiler_params=pltpu.CompilerParams(vmem_limit_bytes=limit * MIB),
-        name=name,
-    )(*operands)
-
-
 def residual_blocks(residual_top, residual_side, devices, share):
     block_x, block_y = residual_top.shape
     top_rows = block_y // 2
-    top_piece = residual_top.T.reshape(2, top_rows, block_x)
-    top_piece = jnp.concatenate([top_piece[0], top_piece[1]], axis=1)
-    side_piece = lax.dynamic_slice_in_dim(
-        residual_side.T, lax.axis_index("gx") * share, share, axis=0
-    )
-    piece = jnp.concatenate(
-        [top_piece, side_piece, jnp.zeros((TILE - share, LANES), f32)], axis=0
-    )
-    return jnp.broadcast_to(piece[None], (devices,) + piece.shape)
+
+    def body(at_x, top, side, out):
+        piece = jnp.concatenate([top[0:top_rows, :], top[top_rows:, :]], axis=1)
+        part = side[pl.ds(at_x[0] * share, share), :]
+        part = jnp.concatenate([part, jnp.zeros((TILE - share, LANES), f32)], axis=0)
+        for device in range(devices):
+            out[device, 0:top_rows, :] = piece
+            out[device, top_rows:, :] = part
+
+    return call(
+        body,
+        "pack",
+        (devices, top_rows + TILE, LANES),
+        8,
+        "svv",
+        (lax.axis_index("gx").reshape(1), residual_top.T, residual_side.T),
+    )
 
 
 def fast_on_device(magnetization, stiffness, residual_top, residual_side, top_kernel, side_kernel):
@@ -708,25 +692,16 @@
 
     sent = residual_blocks(residual_top, residual_side, devices, depth_block // count_x)
     gathered = lax.all_to_all(sent, ALL, 0, 0, tiled=True)
-    halos = exchange_halos(magnetization, stiffness)
-    gathered, halos = lax.optimization_barrier((gathered, halos))
+    edges = edge_terms(counts, index, magnetization, stiffness)
+    gathered, edges = lax.optimization_barrier((gathered, edges))
 
     lines = call(
         functools.partial(lines_kernel, counts),
         "lines",
         (devices, 2 * TILE, LANES),
         24,
-        "svhhhhhh",
+        "svvvvvvv",
         (index, gathered, jnp.asarray(steps), jnp.asarray(offsets), high, low, turns, top_kernel),
-        [
-            pltpu.VMEM(steps.shape, f32),
-            pltpu.VMEM(offsets.shape[1:], f32),
-            pltpu.VMEM(high.shape, bf16),
-            pltpu.VMEM(low.shape, bf16),
-            pltpu.VMEM(turns.shape, f32),
-            pltpu.VMEM((size // INNER, 2, 2, kys, INNER), f32),
-            pltpu.SemaphoreType.DMA((5 + size // INNER,)),
-        ],
     )
     arrived = lax.all_to_all(lines, ALL, 0, 0, tiled=True)
     side = call(
@@ -746,13 +721,13 @@
             side_kernel,
         ),
     )
-    exchange_grad = exchange_of(counts, index, magnetization, stiffness, halos)
+    exchange_grad = exchange_of(magnetization, stiffness, edges)
     arrived, side, exchange_grad = lax.optimization_barrier((arrived, side, exchange_grad))
     rows = call(
         functools.partial(rows_kernel, counts),
         "rows",
         (group, 2 * TILE + 2 * depth_block, LANES),
-        16,
+        60,
         "vvvvv",
         (arrived, side, high, low, turns),
     )
@@ -800,7 +775,7 @@
         (lax.axis_index("gx") * count_y + lax.axis_index("gy")) * count_z + lax.axis_index("gz")
     ).reshape(1)
     exchange_grad = exchange_of(
-        counts, index, magnetization, stiffness, exchange_halos(magnetization, stiffness)
+        magnetization, stiffness, edge_terms(counts, index, magnetization, stiffness)
     )
 
     parts = image_parts(

time: 60.7 us -> 62.6 us (1.031)
  waiting for transfers between devices: 3.68 us -> 4.54 us
  blocking collectives: 8.72 us -> 9.43 us
    pallas_call x4 -> x7, Pallas kernels: 12.3 us -> 17 us  [call(): pl.pallas_call(body, out_shape=jax.ShapeDtypeStruct(shape, f32), in_specs...]
    pallas_call x2 -> x1, Pallas kernels: 7.41 us -> 3.14 us  [edge_terms(): pl.pallas_call(faces_kernel, in_specs=[HBM, HBM], out_specs=[HBM, HBM, VM...]
    ppermute x5, waiting for transfers between devices: 3.06 us -> 4.45 us  [ring(): lax.ppermute(block, axis, [(i, (i + distance) % count) for i in range(cou...]
    unnamed x56 -> x46, local copies, waits for them, and re-layouts: 8.82 us -> 9.92 us
    broadcast_in_dim x2 -> x0, local copies, waits for them, and re-layouts: 0.77 us -> none  [the longest x1 0.77 us: residual_blocks(): return jnp.broadcast_to(piece[None], (devices,) + piece.shape)]
    slice x1 -> x0, local copies, waits for them, and re-layouts: 0.77 us -> none  [residual_blocks(): top_piece = jnp.concatenate([top_piece[0], top_piece[1]], axis=1)]
    all_to_all x1, blocking collectives: 8.72 us -> 9.43 us  [fast_on_device(): arrived = lax.all_to_all(rows, ('gy', 'gz'), 0, 0, tiled=True)]
  transfers between devices with their start and end apart: 7 -> 7, of which waited for: 2 -> 3; matrix products, arithmetic and copies ran while one was open for 0% -> 0% of each run, Pallas kernels for 17% -> 18%
where the time goes in v3:
time: 62.6 us; the launch traced here: 61.8 us
  Pallas kernels  20.1 us (32%)
  starting transfers between devices  17.5 us (28%)
  local copies, waits for them, and re-layouts  9.92 us (16%)
  blocking collectives  9.43 us (15%)
  waiting for transfers between devices  4.54 us (7%)
    pallas_call x7, Pallas kernels, call(): pl.pallas_call(body, out_shape=jax.ShapeDtypeStruct(shape, f32), in_specs...  17 us
    unnamed x46, local copies, waits for them, and re-layouts  9.92 us
    all_to_all x1, blocking collectives, fast_on_device(): arrived = lax.all_to_all(rows, ('gy', 'gz'), 0, 0, tiled=True)  9.43 us
    all_to_all x1, starting transfers between devices, fast_on_device(): gathered = lax.all_to_all(sent, ALL, 0, 0, tiled=True)  7.3 us
    ppermute x5, starting transfers between devices, ring(): lax.ppermute(block, axis, [(i, (i + distance) % count) for i in range(cou...  6.42 us
    ppermute x5, waiting for transfers between devices, ring(): lax.ppermute(block, axis, [(i, (i + distance) % count) for i in range(cou...  4.45 us
    all_to_all x1, starting transfers between devices, fast_on_device(): arrived = lax.all_to_all(lines, ALL, 0, 0, tiled=True)  3.81 us
    pallas_call x1, Pallas kernels, edge_terms(): pl.pallas_call(faces_kernel, in_specs=[HBM, HBM], out_specs=[HBM, HBM, VM...  3.14 us
  transfers between devices with their start and end apart: 7, of which 3 were waited for; matrix products, arithmetic and copies ran while one was open for 0% of the time, Pallas kernels for 18%

profile of v3, /device:TPU:0, one launch (start us, length us, event | category | flops | bytes accessed | tf_op | source)
XLA Modules:
  0.0 61.8 jit_solution(9865063449926196890)
XLA Ops:
  0.0 0.7 %copy-done.21 = f32[64,32]{0,1:T(8,128)S(1)} copy-done((f32[64,32]{0,1:T(8,128)S(1)}, f32[64,32]{0,1:T(8,128)}, u32[]{:S(2)}) %copy-start.21) | copy-done | bytes 8216
  0.7 0.7 %copy-done.22 = f32[128,16]{0,1:T(8,128)S(1)} copy-done((f32[128,16]{0,1:T(8,128)S(1)}, f32[128,16]{0,1:T(8,128)}, u32[]{:S(2)}) %copy-start.22) | copy-done | bytes 8216
  1.4 0.8 %pack.1 = f32[32,24,128]{2,1,0:T(8,128)} custom-call(s32[1]{0:T(128)} %bitcast.1.at_x, f32[32,64]{1,0:T(8,128)S(1)} %bitcast.5, f32[16,128]{1,0:T(8,128)S(1)} %bitcast.6), custom_call_target="tpu_custom_call" | custom-call | tf_op jit(solution)/shard_map/pack/pallas_call | solution.py:38
  2.2 7.3 %all-to-all-start = ((f32[32,24,128]{2,1,0:T(8,128)}), f32[32,24,128]{2,1,0:T(8,128)S(1)}, u32[]{:S(2)}, u32[]{:S(2)}) async-start(f32[32,24,128]{2,1,0:T(8,128)} %pack.1), calls=%async_computation | async-start | bytes 786432 | tf_op jit(solution)/shard_map/all_to_all | solution.py:694
  9.6 0.0 copy-start.1
  9.6 0.0 copy-start.12
  9.6 0.0 copy-start.16
  9.6 0.0 copy-start.17
  9.6 3.1 %faces.1 = (f32[4,64,128]{2,1,0:T(8,128)}, f32[4,64,128]{2,1,0:T(8,128)}, f32[4,16,128]{2,1,0:T(8,128)}, f32[4,16,128]{2,1,0:T(8,128)}, f32[64,128]{1,0:T(8,128)}) custom-call(f32[3,16,64,128]{3,2,1,0:T(8,128)} %magnetization.3, f32[16,64,128]{2,1,0:T(8,128)} %stiffness.3), custom_call_target="tpu_custom_call" | custom-call | tf_op jit(solution)/shard_map/faces/pallas_call | solution.py:404
  12.8 1.6 %collective-permute-start = (f32[4,64,128]{2,1,0:T(8,128)}, f32[4,64,128]{2,1,0:T(8,128)S(1)}, u32[]{:S(2)}, u32[]{:S(2)}) collective-permute-start(f32[4,64,128]{2,1,0:T(8,128)} %get-tuple-element.15.z_first), channel_id=1, source_target_pairs={{0,3},{1,0},{2,1},{3,2},{4,7},{5,4},{6,5},{7,6},{8,11},{9,8},{10,9... | collective-permute-start | bytes 393224 | tf_op jit(solution)/shard_map/ppermute | solution.py:398
  14.3 3.3 %collective-permute-start.2 = (f32[4,16,128]{2,1,0:T(8,128)}, f32[4,16,128]{2,1,0:T(8,128)S(1)}, u32[]{:S(2)}, u32[]{:S(2)}) collective-permute-start(f32[4,16,128]{2,1,0:T(8,128)} %get-tuple-element.17.x_first), channel_id=1, source_target_pairs={{0,24},{8,0},{16,8},{24,16},{1,25},{9,1},{17,9},{25,17},{2,26},{10... | collective-permute-start | bytes 98312 | tf_op jit(solution)/shard_map/ppermute | solution.py:398
  17.7 1.5 %collective-permute-start.4 = (f32[64,128]{1,0:T(8,128)}, f32[64,128]{1,0:T(8,128)S(1)}, u32[]{:S(2)}, u32[]{:S(2)}) collective-permute-start(f32[64,128]{1,0:T(8,128)} %get-tuple-element.19.y_faces), channel_id=1, source_target_pairs={{0,4},{4,0},{1,5},{5,1},{2,6},{6,2},{3,7},{7,3},{8,12},{12,8},{9,1... | collective-permute-start | bytes 98312 | tf_op jit(solution)/shard_map/ppermute | solution.py:398
  19.2 0.6 collective-permute-done.2.x_next
  19.8 3.8 %collective-permute-done.3.x_before = f32[4,16,128]{2,1,0:T(8,128)S(1)} collective-permute-done((f32[4,16,128]{2,1,0:T(8,128)}, f32[4,16,128]{2,1,0:T(8,128)S(1)}, u32[]{:S(2)}, u32[]{:S(2)}) %collective-permute-start.3) | collective-permute-done | bytes 32800 | tf_op jit(solution)/shard_map/ppermute | solution.py:398
  23.6 0.9 %copy-done.14 = f32[4,64,128]{2,1,0:T(8,128)S(1)} copy-done((f32[4,64,128]{2,1,0:T(8,128)S(1)}, f32[4,64,128]{2,1,0:T(8,128)}, u32[]{:S(2)}) %copy-start.14) | copy-done | bytes 131096
  24.5 0.9 %copy-done.15 = f32[4,64,128]{2,1,0:T(8,128)S(1)} copy-done((f32[4,64,128]{2,1,0:T(8,128)S(1)}, f32[4,64,128]{2,1,0:T(8,128)}, u32[]{:S(2)}) %copy-start.15) | copy-done | bytes 131096
  25.4 0.8 %copy-done.18 = f32[4,16,128]{2,1,0:T(8,128)S(1)} copy-done((f32[4,16,128]{2,1,0:T(8,128)S(1)}, f32[4,16,128]{2,1,0:T(8,128)}, u32[]{:S(2)}) %copy-start.18) | copy-done | bytes 32792
  26.2 0.8 %copy-done.19 = f32[4,16,128]{2,1,0:T(8,128)S(1)} copy-done((f32[4,16,128]{2,1,0:T(8,128)S(1)}, f32[4,16,128]{2,1,0:T(8,128)}, u32[]{:S(2)}) %copy-start.19) | copy-done | bytes 32792
  27.0 0.8 %copy-done.20 = f32[64,128]{1,0:T(8,128)S(1)} copy-done((f32[64,128]{1,0:T(8,128)S(1)}, f32[64,128]{1,0:T(8,128)}, u32[]{:S(2)}) %copy-start.20) | copy-done | bytes 32792
  27.7 0.2 edges.1
  28.0 1.7 %copy-done.5 = f32[2,2,64,2048]{3,2,1,0:T(8,128)S(1)} copy-done((f32[2,2,64,2048]{3,2,1,0:T(8,128)S(1)}, f32[2,2,64,2048]{3,2,1,0:T(8,128)}, u32[]{:S(2)}) %copy-start.5) | copy-done | bytes 2097176
  29.8 4.7 %lines.1 = f32[32,16,128]{2,1,0:T(8,128)} custom-call(s32[1]{0:T(128)} %bitcast.here, f32[32,24,128]{2,1,0:T(8,128)S(1)} %all-to-all-done.gathered, f32[4,64,128]{2,1,0:T(8,128)S(1)} %copy-done.17, f32[32,8,128]{2,1,0:T(8,128)S(1)} %copy-done.16, bf16[512,256]{1,0:T(8,128)(2,1)S(1)} %copy-done.3, bf16[512,256]{1,0:T(8,128)(2,1)S(1)} %copy-done.1, ...), custom_call_target="tpu_custom_call" | custom-call | tf_op jit(solution)/shard_map/lines/pallas_call | solution.py:38
  34.4 3.8 %all-to-all-start.1 = ((f32[32,16,128]{2,1,0:T(8,128)}), f32[32,16,128]{2,1,0:T(8,128)}, u32[]{:S(2)}, u32[]{:S(2)}) async-start(f32[32,16,128]{2,1,0:T(8,128)} %lines.1), calls=%async_computation.1 | async-start | bytes 524288 | tf_op jit(solution)/shard_map/all_to_all | solution.py:706
  38.3 1.0 %copy-done.6 = f32[16,64,128]{2,1,0:T(8,128)S(1)} copy-done((f32[16,64,128]{2,1,0:T(8,128)S(1)}, f32[16,64,128]{2,1,0:T(8,128)}, u32[]{:S(2)}) %copy-start.6) | copy-done | bytes 524312
  39.3 1.0 %copy-done.8 = f32[544,128]{1,0:T(8,128)S(1)} copy-done((f32[544,128]{1,0:T(8,128)S(1)}, f32[544,128]{1,0:T(8,128)}, u32[]{:S(2)}) %copy-start.8) | copy-done | bytes 278552
  40.3 4.9 %exchange.1.exchange_grad = f32[3,16,64,128]{3,2,1,0:T(8,128)S(1)} custom-call(f32[3,16,64,128]{3,2,1,0:T(8,128)S(1)} %copy-done, f32[16,64,128]{2,1,0:T(8,128)S(1)} %copy-done.6, f32[544,128]{1,0:T(8,128)S(1)} %copy-done.8), custom_call_target="tpu_custom_call" | custom-call | tf_op jit(solution)/shard_map/exchange/pallas_call | solution.py:38
  45.2 2.8 %side.1 = f32[8,32,128]{2,1,0:T(8,128)S(1)} custom-call(s32[1]{0:T(128)} %bitcast.4.here, f32[32,24,128]{2,1,0:T(8,128)S(1)} %all-to-all-done.gathered, f32[8,32,128]{2,1,0:T(8,128)S(1)} %copy-done.13, f32[8,64,32]{2,1,0:T(8,128)S(1)} %copy-done.11, bf16[512,256]{1,0:T(8,128)(2,1)S(1)} %copy-done.4, bf16[512,256]{1,0:T(8,128)(2,1)S(1)} %copy-done.2, ...), custom_call_target="tpu_custom_call" | custom-call | tf_op jit(solution)/shard_map/side/pallas_call | solution.py:38
  48.1 0.6 %copy-done.10 = f32[8,32,128]{2,1,0:T(8,128)} copy-done((f32[8,32,128]{2,1,0:T(8,128)}, f32[8,32,128]{2,1,0:T(8,128)S(1)}, u32[]{:S(2)}) %copy-start.10) | copy-done | bytes 131096
  48.7 0.1 all-to-all-done.1.arrived
  48.8 2.3 %rows.1 = f32[8,48,128]{2,1,0:T(8,128)} custom-call(f32[32,16,128]{2,1,0:T(8,128)} %all-to-all-done.1.arrived, f32[8,32,128]{2,1,0:T(8,128)} %copy-done.10, bf16[512,256]{1,0:T(8,128)(2,1)} %constant.30.clone.high, bf16[512,256]{1,0:T(8,128)(2,1)} %constant.31.clone.low, f32[2,8,256]{2,1,0:T(8,128)} %constant.32.clone.turns), custom_call_target="tpu_custom_call" | custom-call | tf_op jit(solution)/shard_map/rows/pallas_call | solution.py:38
  51.1 9.4 %all_to_all.15.arrived = f32[8,48,128]{2,1,0:T(8,128)S(1)} all-to-all(f32[8,48,128]{2,1,0:T(8,128)} %rows.1), channel_id=1, replica_groups=mesh['gx'=4,'gy'=2,'gz'=4] {'gy','gz'}, dimensions={0} | all-to-all | bytes 393216 | tf_op jit(solution)/shard_map/all_to_all | solution.py:734
  60.6 1.3 %gradient.1 = f32[3,16,64,128]{3,2,1,0:T(8,128)} custom-call(f32[3,16,64,128]{3,2,1,0:T(8,128)S(1)} %exchange.1.exchange_grad, f32[8,48,128]{2,1,0:T(8,128)S(1)} %all_to_all.15.arrived), custom_call_target="tpu_custom_call" | custom-call | tf_op jit(solution)/shard_map/gradient/pallas_call | solution.py:38
  (37 shorter events, 0.1 us)
Async XLA Ops:
  0.0 0.7 %copy-start.21 = (f32[64,32]{0,1:T(8,128)S(1)}, f32[64,32]{0,1:T(8,128)}, u32[]{:S(2)}) copy-start(f32[64,32]{0,1:T(8,128)} %param.15) | copy-start | bytes 24580
  0.7 0.7 %copy-start.22 = (f32[128,16]{0,1:T(8,128)S(1)}, f32[128,16]{0,1:T(8,128)}, u32[]{:S(2)}) copy-start(f32[128,16]{0,1:T(8,128)} %param.16) | copy-start | bytes 24580
  2.2 25.7 %all-to-all-start = ((f32[32,24,128]{2,1,0:T(8,128)}), f32[32,24,128]{2,1,0:T(8,128)S(1)}, u32[]{:S(2)}, u32[]{:S(2)}) async-start(f32[32,24,128]{2,1,0:T(8,128)} %pack.1), calls=%async_computation | async-start | bytes 786432 | tf_op jit(solution)/shard_map/all_to_all | solution.py:694
  9.6 18.4 %copy-start.1 = (bf16[512,256]{1,0:T(8,128)(2,1)S(1)}, bf16[512,256]{1,0:T(8,128)(2,1)}, u32[]{:S(2)}) copy-start(bf16[512,256]{1,0:T(8,128)(2,1)} %constant.31.clone.low) | copy-start | bytes 786436
  9.6 18.4 %copy-start.3 = (bf16[512,256]{1,0:T(8,128)(2,1)S(1)}, bf16[512,256]{1,0:T(8,128)(2,1)}, u32[]{:S(2)}) copy-start(bf16[512,256]{1,0:T(8,128)(2,1)} %constant.30.clone.high) | copy-start | bytes 786436
  9.6 18.4 %copy-start.12 = (f32[2,8,256]{2,1,0:T(8,128)S(1)}, f32[2,8,256]{2,1,0:T(8,128)}, u32[]{:S(2)}) copy-start(f32[2,8,256]{2,1,0:T(8,128)} %constant.32.clone.turns) | copy-start | bytes 49156
  9.6 18.4 %copy-start.16 = (f32[32,8,128]{2,1,0:T(8,128)S(1)}, f32[32,8,128]{2,1,0:T(8,128)}, u32[]{:S(2)}) copy-start(f32[32,8,128]{2,1,0:T(8,128)} %constant.34.clone.offsets) | copy-start | bytes 393220
  9.6 18.4 %copy-start.17 = (f32[4,64,128]{2,1,0:T(8,128)S(1)}, f32[4,64,128]{2,1,0:T(8,128)}, u32[]{:S(2)}) copy-start(f32[4,64,128]{2,1,0:T(8,128)} %constant.33.clone.steps) | copy-start | bytes 393220
  12.8 10.9 %collective-permute-start = (f32[4,64,128]{2,1,0:T(8,128)}, f32[4,64,128]{2,1,0:T(8,128)S(1)}, u32[]{:S(2)}, u32[]{:S(2)}) collective-permute-start(f32[4,64,128]{2,1,0:T(8,128)} %get-tuple-element.15.z_first), channel_id=1, source_target_pairs={{0,3},{1,0},{2,1},{3,2},{4,7},{5,4},{6,5},{7,6},{8,11},{9,8},{10,9... | collective-permute-start | bytes 393224 | tf_op jit(solution)/shard_map/ppermute | solution.py:398
  14.3 9.3 %collective-permute-start.1 = (f32[4,64,128]{2,1,0:T(8,128)}, f32[4,64,128]{2,1,0:T(8,128)S(1)}, u32[]{:S(2)}, u32[]{:S(2)}) collective-permute-start(f32[4,64,128]{2,1,0:T(8,128)} %get-tuple-element.16.z_last), channel_id=1, source_target_pairs={{0,1},{1,2},{2,3},{3,0},{4,5},{5,6},{6,7},{7,4},{8,9},{9,10},{10,1... | collective-permute-start | bytes 393224 | tf_op jit(solution)/shard_map/ppermute | solution.py:398
  14.3 5.4 %collective-permute-start.2 = (f32[4,16,128]{2,1,0:T(8,128)}, f32[4,16,128]{2,1,0:T(8,128)S(1)}, u32[]{:S(2)}, u32[]{:S(2)}) collective-permute-start(f32[4,16,128]{2,1,0:T(8,128)} %get-tuple-element.17.x_first), channel_id=1, source_target_pairs={{0,24},{8,0},{16,8},{24,16},{1,25},{9,1},{17,9},{25,17},{2,26},{10... | collective-permute-start | bytes 98312 | tf_op jit(solution)/shard_map/ppermute | solution.py:398
  17.7 5.9 %collective-permute-start.3 = (f32[4,16,128]{2,1,0:T(8,128)}, f32[4,16,128]{2,1,0:T(8,128)S(1)}, u32[]{:S(2)}, u32[]{:S(2)}) collective-permute-start(f32[4,16,128]{2,1,0:T(8,128)} %get-tuple-element.18.x_last), channel_id=1, source_target_pairs={{0,8},{8,16},{16,24},{24,0},{1,9},{9,17},{17,25},{25,1},{2,10},{10... | collective-permute-start | bytes 98312 | tf_op jit(solution)/shard_map/ppermute | solution.py:398
  17.7 5.9 %collective-permute-start.4 = (f32[64,128]{1,0:T(8,128)}, f32[64,128]{1,0:T(8,128)S(1)}, u32[]{:S(2)}, u32[]{:S(2)}) collective-permute-start(f32[64,128]{1,0:T(8,128)} %get-tuple-element.19.y_faces), channel_id=1, source_target_pairs={{0,4},{4,0},{1,5},{5,1},{2,6},{6,2},{3,7},{7,3},{8,12},{12,8},{9,1... | collective-permute-start | bytes 98312 | tf_op jit(solution)/shard_map/ppermute | solution.py:398
  23.6 0.9 %copy-start.14 = (f32[4,64,128]{2,1,0:T(8,128)S(1)}, f32[4,64,128]{2,1,0:T(8,128)}, u32[]{:S(2)}) copy-start(f32[4,64,128]{2,1,0:T(8,128)} %get-tuple-element.15.z_first) | copy-start | bytes 393220
  24.5 0.9 %copy-start.15 = (f32[4,64,128]{2,1,0:T(8,128)S(1)}, f32[4,64,128]{2,1,0:T(8,128)}, u32[]{:S(2)}) copy-start(f32[4,64,128]{2,1,0:T(8,128)} %get-tuple-element.16.z_last) | copy-start | bytes 393220
  25.4 0.8 %copy-start.18 = (f32[4,16,128]{2,1,0:T(8,128)S(1)}, f32[4,16,128]{2,1,0:T(8,128)}, u32[]{:S(2)}) copy-start(f32[4,16,128]{2,1,0:T(8,128)} %get-tuple-element.17.x_first) | copy-start | bytes 98308
  26.2 0.8 %copy-start.19 = (f32[4,16,128]{2,1,0:T(8,128)S(1)}, f32[4,16,128]{2,1,0:T(8,128)}, u32[]{:S(2)}) copy-start(f32[4,16,128]{2,1,0:T(8,128)} %get-tuple-element.18.x_last) | copy-start | bytes 98308
  27.0 0.8 %copy-start.20 = (f32[64,128]{1,0:T(8,128)S(1)}, f32[64,128]{1,0:T(8,128)}, u32[]{:S(2)}) copy-start(f32[64,128]{1,0:T(8,128)} %get-tuple-element.19.y_faces) | copy-start | bytes 98308
  28.0 6.5 %copy-start.7 = (f32[544,128]{1,0:T(8,128)}, f32[544,128]{1,0:T(8,128)S(1)}, u32[]{:S(2)}) copy-start(f32[544,128]{1,0:T(8,128)S(1)} %edges.1) | copy-start | bytes 835588
  28.0 10.3 %copy-start = (f32[3,16,64,128]{3,2,1,0:T(8,128)S(1)}, f32[3,16,64,128]{3,2,1,0:T(8,128)}, u32[]{:S(2)}) copy-start(f32[3,16,64,128]{3,2,1,0:T(8,128)} %magnetization.3) | copy-start | bytes 4718596
  28.0 1.7 %copy-start.5 = (f32[2,2,64,2048]{3,2,1,0:T(8,128)S(1)}, f32[2,2,64,2048]{3,2,1,0:T(8,128)}, u32[]{:S(2)}) copy-start(f32[2,2,64,2048]{3,2,1,0:T(8,128)} %kernel.2) | copy-start | bytes 6291460
  34.4 14.4 %all-to-all-start.1 = ((f32[32,16,128]{2,1,0:T(8,128)}), f32[32,16,128]{2,1,0:T(8,128)}, u32[]{:S(2)}, u32[]{:S(2)}) async-start(f32[32,16,128]{2,1,0:T(8,128)} %lines.1), calls=%async_computation.1 | async-start | bytes 524288 | tf_op jit(solution)/shard_map/all_to_all | solution.py:706
  38.3 1.0 %copy-start.6 = (f32[16,64,128]{2,1,0:T(8,128)S(1)}, f32[16,64,128]{2,1,0:T(8,128)}, u32[]{:S(2)}) copy-start(f32[16,64,128]{2,1,0:T(8,128)} %stiffness.3) | copy-start | bytes 1572868
  39.3 1.0 %copy-start.8 = (f32[544,128]{1,0:T(8,128)S(1)}, f32[544,128]{1,0:T(8,128)}, u32[]{:S(2)}) copy-start(f32[544,128]{1,0:T(8,128)} %copy-done.7) | copy-start | bytes 835588
  40.3 4.9 %copy-start.2 = (bf16[512,256]{1,0:T(8,128)(2,1)S(1)}, bf16[512,256]{1,0:T(8,128)(2,1)}, u32[]{:S(2)}) copy-start(bf16[512,256]{1,0:T(8,128)(2,1)} %constant.31.clone.low) | copy-start | bytes 786436
  40.3 4.9 %copy-start.4 = (bf16[512,256]{1,0:T(8,128)(2,1)S(1)}, bf16[512,256]{1,0:T(8,128)(2,1)}, u32[]{:S(2)}) copy-start(bf16[512,256]{1,0:T(8,128)(2,1)} %constant.30.clone.high) | copy-start | bytes 786436
  40.3 4.9 %copy-start.9 = (f32[2,2,16,2048]{3,2,1,0:T(8,128)S(1)}, f32[2,2,16,2048]{3,2,1,0:T(8,128)}, u32[]{:S(2)}) copy-start(f32[2,2,16,2048]{3,2,1,0:T(8,128)} %kernel.3) | copy-start | bytes 1572868
  40.3 4.9 %copy-start.11 = (f32[8,64,32]{2,1,0:T(8,128)S(1)}, f32[8,64,32]{2,1,0:T(8,128)}, u32[]{:S(2)}) copy-start(f32[8,64,32]{2,1,0:T(8,128)} %constant.36.clone.back) | copy-start | bytes 196612
  40.3 4.9 %copy-start.13 = (f32[8,32,128]{2,1,0:T(8,128)S(1)}, f32[8,32,128]{2,1,0:T(8,128)}, u32[]{:S(2)}) copy-start(f32[8,32,128]{2,1,0:T(8,128)} %constant.35.clone.there) | copy-start | bytes 393220
  48.1 0.7 %copy-start.10 = (f32[8,32,128]{2,1,0:T(8,128)}, f32[8,32,128]{2,1,0:T(8,128)S(1)}, u32[]{:S(2)}) copy-start(f32[8,32,128]{2,1,0:T(8,128)S(1)} %side.1) | copy-start | bytes 393220

commit v4 on v3

--- a/solution.py
+++ b/solution.py
@@ -34,16 +34,33 @@
     return one(high, right[0]) + one(low, right[0]) + one(high, right[1])
 
 
-def call(body, name, shape, limit, kinds, operands, scratch=()):
-    return pl.pallas_call(
+def from_hbm(values):
+    return pltpu.with_memory_space_constraint(values, pltpu.HBM)
+
+
+def call(body, name, shape, limit, microseconds, operands, in_hbm=(), scratch=(), refs=()):
+    shapes = shape if isinstance(shape, list) else [shape]
+    moved = sum(4 * math.prod(each) for each in shapes)
+    moved += sum(x.size * x.dtype.itemsize for x in operands)
+    results = pl.pallas_call(
         body,
-        out_shape=jax.ShapeDtypeStruct(shape, f32),
-        in_specs=[{"s": SMEM, "v": VMEM, "h": HBM}[kind] for kind in kinds],
-        out_specs=VMEM,
+        out_shape=[
+            pltpu.HBM(each, f32) if i in in_hbm else jax.ShapeDtypeStruct(each, f32)
+            for i, each in enumerate(shapes)
+        ],
+        in_specs=[
+            SMEM if x.shape == (1,) else HBM if i in refs else VMEM
+            for i, x in enumerate(operands)
+        ],
+        out_specs=[VMEM] * len(shapes),
         scratch_shapes=list(scratch),
         compiler_params=pltpu.CompilerParams(vmem_limit_bytes=limit * MIB),
+        cost_estimate=pl.CostEstimate(
+            flops=int(microseconds * 1e9), bytes_accessed=moved, transcendentals=0
+        ),
         name=name,
     )(*operands)
+    return results if isinstance(shape, list) else results[0]
 
 
 def transform_tables(extent, size):
@@ -244,7 +261,7 @@
     )
 
 
-def copies_of(pairs, semaphores):
+def begin(semaphores, pairs):
     started = [
         pltpu.make_async_copy(source, target, semaphores.at[i])
         for i, (source, target) in enumerate(pairs)
@@ -255,23 +272,20 @@
 
 
 def faces_kernel(
-    magnetization, stiffness, z_first, z_last, x_first, x_last, y_faces, m, s, semaphores, sent
+    magnetization, stiffness, z_first, z_last, x_first, x_last, y_faces, m, s, loading
 ):
     depth, across = stiffness.shape[:2]
-    loads = copies_of(
-        [(stiffness, s)] + [(magnetization.at[c], m.at[c]) for c in range(3)], semaphores
+    loads = begin(
+        loading, [(stiffness, s)] + [(magnetization.at[c], m.at[c]) for c in range(3)]
     )
     lane = lax.broadcasted_iota(jnp.int32, (across, LANES), 1)
     first = jnp.zeros((across, LANES), f32)
     last = jnp.zeros((across, LANES), f32)
-    stores = []
-    for field, load in ((3, loads[0]), (0, loads[1]), (1, loads[2]), (2, loads[3])):
-        load.wait()
+    for field in (3, 0, 1, 2):
+        loads[(field + 1) % 4].wait()
         ref = s if field == 3 else m.at[field]
-        for k, (target, z) in enumerate(((z_first, 0), (z_last, depth - 1))):
-            store = pltpu.make_async_copy(ref.at[z], target.at[field], sent.at[2 * field + k])
-            store.start()
-            stores.append(store)
+        z_first[field] = ref[0]
+        z_last[field] = ref[depth - 1]
         x_first[field] = ref[:, 0, :]
         x_last[field] = ref[:, across - 1, :]
         for z in range(depth):
@@ -279,36 +293,56 @@
             turned = pltpu.roll(ref[z], column, 1) if column else ref[z]
             first = jnp.where(lane == column, turned, first)
             last = jnp.where(lane == (column - 1) % LANES, turned, last)
-    y_faces[...] = jnp.where(
-        lane < LANES // 2, first, pltpu.roll(last, LANES // 2 + 1, 1)
-    )
-    for store in stores:
-        store.wait()
+    y_faces[...] = jnp.where(lane < LANES // 2, first, pltpu.roll(last, LANES // 2 + 1, 1))
 
 
 def twice_weight(a, b):
     return 4.0 * a * b / (a + b)
 
 
-def edges_kernel(
+def exchange_kernel(
     counts,
     here,
-    z_first,
-    z_last,
-    x_first,
-    x_last,
-    y_faces,
+    magnetization_from,
+    stiffness_from,
+    z_next_from,
+    z_before_from,
+    x_next_from,
+    x_before_from,
+    y_next_from,
+    y_before_from,
+    y_faces_from,
+    out,
+    m,
+    s,
     z_next,
     z_before,
     x_next,
     x_before,
     y_next,
     y_before,
-    out,
+    y_faces,
+    loading,
 ):
-    across = y_faces.shape[0]
-    depth = x_first.shape[1]
-    half = LANES // 2
+    depth, across = s.shape[:2]
+    chunk = depth // 4
+    pairs = [
+        (y_next_from, y_next),
+        (y_before_from, y_before),
+        (y_faces_from, y_faces),
+        (z_before_from, z_before),
+    ]
+    for k in range(4):
+        layers = pl.ds(k * chunk, chunk)
+        pairs.append((stiffness_from.at[layers], s.at[layers]))
+        pairs.append((magnetization_from.at[:, layers], m.at[:, layers]))
+    pairs += [
+        (z_next_from, z_next),
+        (x_next_from, x_next),
+        (x_before_from, x_before),
+    ]
+    loads = begin(loading, pairs)
+
     count_x, count_y, count_z = counts
     at_z = here[0] % count_z
     at_y = here[0] // count_z % count_y
@@ -317,20 +351,11 @@
     def inside(condition, values):
         return jnp.where(condition, values, 0.0)
 
-    row = 0
-    for own, halo, present in (
-        (z_last, z_next, at_z < count_z - 1),
-        (z_first, z_before, at_z > 0),
-        (x_last, x_next, at_x < count_x - 1),
-        (x_first, x_before, at_x > 0),
-    ):
-        rows = own.shape[1]
-        weight = twice_weight(own[3], inside(present, halo[3]))
-        for c in range(3):
-            out[row : row + rows, :] = weight * (own[c] - halo[c])
-            row += rows
-
+    half = LANES // 2
     lane = lax.broadcasted_iota(jnp.int32, (across, LANES), 1)
+    row = lax.broadcasted_iota(jnp.int32, (across, LANES), 0)
+    first_lane, last_lane, last_row = lane == 0, lane == LANES - 1, row == across - 1
+
     stiff = (lane >= 3 * depth) & (lane < 4 * depth)
 
     def y_edge(own, halo, present):
@@ -344,26 +369,24 @@
             )
         return spread * (own - halo)
 
+    for copy in loads[:3]:
+        copy.wait()
     own = y_faces[...]
     after = y_edge(pltpu.roll(own, half, 1), y_next[...], at_y < count_y - 1)
     before = y_edge(own, pltpu.roll(y_before[...], half, 1), at_y > 0)
-    out[row : row + across, :] = jnp.where(lane < half, after, pltpu.roll(before, half, 1))
-
-
-def exchange_kernel(magnetization, stiffness, edges, out):
-    depth, across = stiffness.shape[:2]
-    half = LANES // 2
-    lane = lax.broadcasted_iota(jnp.int32, (across, LANES), 1)
-    row = lax.broadcasted_iota(jnp.int32, (across, LANES), 0)
-    first_lane, last_lane, last_row = lane == 0, lane == LANES - 1, row == across - 1
-    z_rows, x_rows = 3 * across, 3 * depth
-    y_row = 2 * (z_rows + x_rows)
-    sides = edges[y_row : y_row + across, :]
-    below = [-edges[z_rows + c * across : z_rows + (c + 1) * across, :] for c in range(3)]
+
+    for copy in loads[3:6]:
+        copy.wait()
+    below_weight = twice_weight(inside(at_z > 0, z_before[3]), s[0])
+    below = [below_weight * (z_before[c] - m[c, 0]) for c in range(3)]
     for z in range(depth):
-        centre = stiffness[z]
-        if z + 1 < depth:
-            weight_z = twice_weight(centre, stiffness[z + 1])
+        if z % chunk == chunk - 1:
+            k = 4 + 2 * (z // chunk + 1)
+            for copy in loads[k : k + 2] if z + 1 < depth else loads[k:]:
+                copy.wait()
+        centre = s[z]
+        above = s[z + 1] if z + 1 < depth else inside(at_z < count_z - 1, z_next[3])
+        weight_z = twice_weight(centre, above)
         weight_x = jnp.where(
             last_row, 0.0, twice_weight(centre, pltpu.roll(centre, across - 1, 0))
         )
@@ -372,25 +395,27 @@
         )
         for c in range(3):
             column = c * depth + z
-            values = magnetization[c, z]
-            if z + 1 < depth:
-                up = weight_z * (values - magnetization[c, z + 1])
-            else:
-                up = edges[c * across : (c + 1) * across, :]
+            values = m[c, z]
+            upper = m[c, z + 1] if z + 1 < depth else z_next[c]
+            up = weight_z * (values - upper)
             flux_x = weight_x * (values - pltpu.roll(values, across - 1, 0))
             flux_y = weight_y * (values - pltpu.roll(values, LANES - 1, 1))
             total = (up - below[c]) + (flux_x - pltpu.roll(flux_x, 1, 0))
             total = total + (flux_y - pltpu.roll(flux_y, 1, 1))
             side = jnp.where(
                 first_lane,
-                sides[:, half + column : half + column + 1],
-                jnp.where(last_lane, sides[:, column : column + 1], 0.0),
+                before[:, column : column + 1],
+                jnp.where(last_lane, after[:, column : column + 1], 0.0),
             )
             out[c, z] = total + side
             below[c] = up
-    for start, edge_row in ((2 * z_rows, across - 1), (2 * z_rows + x_rows, 0)):
+    for edge_row, halo, present in (
+        (across - 1, x_next, at_x < count_x - 1),
+        (0, x_before, at_x > 0),
+    ):
+        weight = twice_weight(s[:, edge_row, :], inside(present, halo[3]))
         for c in range(3):
-            out[c, :, edge_row, :] += edges[start + c * depth : start + (c + 1) * depth, :]
+            out[c, :, edge_row, :] += weight * (m[c, :, edge_row, :] - halo[c])
 
 
 def ring(block, axis, distance):
@@ -398,86 +423,76 @@
     return lax.ppermute(block, axis, [(i, (i + distance) % count) for i in range(count)])
 
 
-def edge_terms(counts, index, magnetization, stiffness):
+def faces_of(magnetization, stiffness):
     depth, across, along = stiffness.shape
-    shape = jax.ShapeDtypeStruct
-    faces = pl.pallas_call(
+    return call(
         faces_kernel,
-        in_specs=[HBM, HBM],
-        out_specs=[HBM, HBM, VMEM, VMEM, VMEM],
-        out_shape=[
-            shape((4, across, along), f32),
-            shape((4, across, along), f32),
-            shape((4, depth, along), f32),
-            shape((4, depth, along), f32),
-            shape((across, LANES), f32),
+        "faces",
+        [
+            (4, across, along),
+            (4, across, along),
+            (4, depth, along),
+            (4, depth, along),
+            (across, LANES),
         ],
-        scratch_shapes=[
+        8,
+        2.0,
+        (from_hbm(magnetization), from_hbm(stiffness)),
+        in_hbm=(4,),
+        refs=(0, 1),
+        scratch=[
             pltpu.VMEM(magnetization.shape, f32),
             pltpu.VMEM(stiffness.shape, f32),
             pltpu.SemaphoreType.DMA((4,)),
-            pltpu.SemaphoreType.DMA((8,)),
         ],
-        compiler_params=pltpu.CompilerParams(vmem_limit_bytes=60 * MIB),
-        name="faces",
-    )(magnetization, stiffness)
-    z_first, z_last, x_first, x_last, y_faces = faces
-    z_next, z_before = ring(z_first, "gz", -1), ring(z_last, "gz", 1)
-    x_next, x_before = ring(x_first, "gx", -1), ring(x_last, "gx", 1)
+    )
+
+
+def halos_zy(z_first, z_last, y_faces):
     y_next = ring(y_faces, "gy", -1)
     y_before = y_next if lax.axis_size("gy") == 2 else ring(y_faces, "gy", 1)
+    return ring(z_first, "gz", -1), ring(z_last, "gz", 1), y_next, y_before, y_faces
+
+
+def halos_x(x_first, x_last):
+    return ring(x_first, "gx", -1), ring(x_last, "gx", 1)
+
+
+def exchange_of(counts, index, magnetization, stiffness, zy, x):
+    z_next, z_before, y_next, y_before, y_faces = zy
+    arrays = (magnetization, stiffness, z_next, z_before, *x, y_next, y_before, y_faces)
     return call(
-        functools.partial(edges_kernel, counts),
-        "edges",
-        (7 * across + 6 * depth, LANES),
-        16,
-        "s" + "v" * 11,
-        (index, *faces, z_next, z_before, x_next, x_before, y_next, y_before),
-    )
-
-
-def exchange_of(magnetization, stiffness, edges):
-    return call(
-        exchange_kernel,
+        functools.partial(exchange_kernel, counts),
         "exchange",
         magnetization.shape,
-        16,
-        "vvv",
-        (magnetization, stiffness, edges),
-    )
-
-
-def line_tables(counts, top_rows, kys, size):
-    group = counts[1] * counts[2]
-    row = np.arange(group * top_rows)
-    j = np.arange(kys)
-    start = np.arange(counts[0] * group) * kys
-    steps, offsets = [], []
-    for h in range(2):
-        y = row // top_rows * top_rows * 2 + h * top_rows + row % top_rows
-        for values, into in ((j, steps), (start, offsets)):
-            angle = (np.outer(values, y) % size) * (2.0 * math.pi / size)
-            into += [np.cos(angle), np.sin(angle)]
-    steps = np.stack(steps).astype(np.float32)
-    offsets = np.stack(offsets, axis=1).astype(np.float32)
-    return steps, np.pad(offsets, ((0, 0), (0, TILE - 4), (0, 0)))
-
-
-def depth_tables(counts, kzs, depth_block):
-    count_x, count_y, count_z = counts
-    size = count_y * count_z * kzs
-    share = depth_block // count_x
-    kz = np.arange(size).reshape(count_y * count_z, kzs, 1)
-
-    def table(z):
-        angle = (kz * z % size) * (2.0 * math.pi / size)
-        return np.concatenate([np.cos(angle), -np.sin(angle)], axis=1).astype(np.float32)
-
-    row = np.arange(count_x * count_z * TILE)
-    within = row % TILE
-    z = row // TILE % count_z * depth_block + row // (TILE * count_z) * share + within
-    there = np.where(within < share, table(z), np.float32(0.0))
-    return there, np.swapaxes(table(np.arange(depth_block * count_z)), 1, 2)
+        8,
+        5.0,
+        (index, *(from_hbm(array) for array in arrays)),
+        refs=range(1, 10),
+        scratch=[pltpu.VMEM(array.shape, f32) for array in arrays]
+        + [pltpu.SemaphoreType.DMA((15,))],
+    )
+
+
+def whole_log(count):
+    return count.bit_length() - 1
+
+
+def cos_sin(steps, size):
+    quarter = steps >> whole_log(size // 4)
+    angle = ((steps & (size // 4 - 1)) - size // 8).astype(f32) * (2.0 * math.pi / size)
+    square = angle * angle
+    sine = cosine = 0.0
+    for k in range(5, -1, -1):
+        sine = sine * square + (-1) ** k / math.factorial(2 * k + 1)
+        cosine = cosine * square + (-1) ** k / math.factorial(2 * k)
+    sine = sine * angle
+    first, second = (cosine - sine) * math.sqrt(0.5), (cosine + sine) * math.sqrt(0.5)
+    odd = (quarter & 1) == 1
+    real = jnp.where(odd, -second, first)
+    imag = jnp.where(odd, first, second)
+    back = quarter >= 2
+    return jnp.where(back, -real, real), jnp.where(back, -imag, imag)
 
 
 def stacked_product(real, imag, tables, sign):
@@ -523,23 +538,33 @@
     ]
 
 
-def lines_kernel(counts, here, gathered, steps, offsets, high, low, turns, kernel, out):
+def lines_kernel(counts, here, gathered, swapped, high, low, turns, kernel, out):
     count_x, count_y, count_z = counts
     group = count_y * count_z
     top_rows = LANES // group
     half = LANES // 2
-    kys = kernel.shape[2]
-    offset = offsets[here[0]]
+    kys, size = kernel.shape[2:]
+    ky = here[0] * kys + lax.broadcasted_iota(jnp.int32, (kys, LANES), 0)
+    lane = lax.broadcasted_iota(jnp.int32, (kys, LANES), 1)
+    odd = (lane >> whole_log(LANES // 2)) ^ (here[0] & 1)
+    pair = lane >> whole_log(top_rows) & (group // 2 - 1)
     table = []
     for h in range(2):
-        step_cos, step_sin = steps[2 * h], steps[2 * h + 1]
-        offset_cos, offset_sin = offset[2 * h : 2 * h + 1], offset[2 * h + 1 : 2 * h + 2]
-        table.append(step_cos * offset_cos - step_sin * offset_sin)
-        table.append(-(step_sin * offset_cos + step_cos * offset_sin))
-    blocks = [
-        gathered[g * group : (g + 1) * group, 0:top_rows, :].reshape(group * top_rows, LANES)
-        for g in range(count_x)
-    ]
+        y = (2 * pair + odd) * (2 * top_rows) + h * top_rows + (lane & (top_rows - 1))
+        cosine, sine = cos_sin(ky * y & (size - 1), size)
+        table += [cosine, -sine]
+    blocks = []
+    for g in range(count_x):
+        members = slice(g * group // 2, (g + 1) * group // 2)
+        blocks.append(
+            jnp.concatenate(
+                [
+                    part[members, 0:top_rows, :].reshape(half, LANES)
+                    for part in (gathered, swapped)
+                ],
+                axis=0,
+            )
+        )
     mixed = dot3(jnp.concatenate(table, axis=0), split(jnp.concatenate(blocks, axis=1)))
     low_half, high_half = mixed[: 2 * kys], mixed[2 * kys :]
     lane = lax.broadcasted_iota(jnp.int32, (2 * kys, LANES), 1)
@@ -567,30 +592,61 @@
         out[:, c * TILE : (c + 1) * TILE, :] = block.reshape(count_x * group, TILE, LANES)
 
 
-def side_kernel_body(counts, here, gathered, there, back, high, low, turns, kernel, out):
+def side_kernel_body(
+    counts, here, gathered, swapped, high, low, turns, kernel_from, out, kernel, loading
+):
     count_x, count_y, count_z = counts
     depth_block = out.shape[1] // 2
     top_rows = gathered.shape[1] - TILE
-    kzs = kernel.shape[2]
+    kzs, length = kernel_from.shape[2:]
+    loads = begin(
+        loading,
+        [
+            (kernel_from.at[:, :, :, pl.ds(b * INNER, INNER)], kernel.at[b])
+            for b in range(length // INNER)
+        ],
+    )
+    size = kzs * count_y * count_z
+    share = depth_block // count_x
+
+    columns = count_x * count_z * TILE
+    kz = here[0] * kzs + lax.broadcasted_iota(jnp.int32, (kzs, columns), 0)
+    column = lax.broadcasted_iota(jnp.int32, (kzs, columns), 1)
+    within = column & (TILE - 1)
+    pair = column >> whole_log(TILE) & (count_z // 2 - 1)
+    odd = (column >> whole_log(columns // 2)) ^ (here[0] & 1)
+    z = (2 * pair + odd) * depth_block + within
+    z = z + (column >> whole_log(TILE * count_z // 2) & (count_x - 1)) * share
+    cosine, sine = cos_sin(kz * z & (size - 1), size)
+    there = jnp.concatenate([cosine, -sine], axis=0)
+    there = jnp.where(jnp.concatenate([within, within], axis=0) < share, there, 0.0)
+
     blocks = []
     for y in range(count_y):
         rows = [
-            gathered[(x * count_y + y) * count_z + z, top_rows:, :]
+            part[(x * count_y + y) * count_z // 2 + pair, top_rows:, :]
+            for part in (gathered, swapped)
             for x in range(count_x)
-            for z in range(count_z)
+            for pair in range(count_z // 2)
         ]
         blocks.append(jnp.concatenate(rows, axis=0))
-    lines = dot3(there[here[0]], split(jnp.concatenate(blocks, axis=1)))
+    lines = dot3(there, split(jnp.concatenate(blocks, axis=1)))
 
     def columns_of(b):
-        return kernel.at[:, :, :, b * INNER : (b + 1) * INNER]
+        loads[b].wait()
+        return kernel.at[b]
 
     images = back_and_forth(
         lines[:kzs], lines[kzs:], columns_of, (high[...], low[...]), turns
     )
-    scale = 1.0 / (count_y * count_z * kzs * kernel.shape[3])
+
+    rows = depth_block * count_z
+    z = lax.broadcasted_iota(jnp.int32, (rows, 2 * kzs), 0)
+    column = lax.broadcasted_iota(jnp.int32, (rows, 2 * kzs), 1)
+    cosine, sine = cos_sin((here[0] * kzs + (column & (kzs - 1))) * z & (size - 1), size)
+    back = jnp.where(column < kzs, cosine, -sine) * (1.0 / (size * length))
     for c in range(2):
-        image = dot3(back[here[0]] * scale, split(jnp.concatenate(images[c], axis=0)))
+        image = dot3(back, split(jnp.concatenate(images[c], axis=0)))
         for y in range(count_y):
             for z in range(count_z):
                 out[y * count_z + z, c * depth_block : (c + 1) * depth_block, :] = image[
@@ -598,8 +654,9 @@
                 ]
 
 
-def rows_kernel(counts, arrived, side, high, low, turns, out):
+def rows_kernel(counts, arrived, side, high, low, turns, out, loading):
     count_y, count_z = counts[1:]
+    loads = begin(loading, [(side, out.at[:, 2 * TILE :, :])])
     per_turn = arrived.shape[0] // turns.shape[1]
     half = LANES // 2
     lane = lax.broadcasted_iota(jnp.int32, (2 * TILE, LANES), 1)
@@ -627,7 +684,7 @@
     for y in range(count_y):
         for z in range(count_z):
             out[y * count_z + z, 0 : 2 * TILE, :] = total[:, y * LANES : (y + 1) * LANES]
-    out[:, 2 * TILE :, :] = side[...]
+    loads[0].wait()
 
 
 def sum_kernel(exchange_grad, arrived, out):
@@ -664,8 +721,8 @@
         body,
         "pack",
         (devices, top_rows + TILE, LANES),
-        8,
-        "svv",
+        60,
+        0.8,
         (lax.axis_index("gx").reshape(1), residual_top.T, residual_side.T),
     )
 
@@ -687,52 +744,59 @@
     plane_index = plane_index.reshape(1)
     (high, low), _, turns = transform_tables(extent, size)
     high, low, turns = jnp.asarray(high), jnp.asarray(low), jnp.asarray(turns)
-    steps, offsets = line_tables(counts, top_rows, kys, size)
-    there, back = depth_tables(counts, kzs, depth_block)
-
-    sent = residual_blocks(residual_top, residual_side, devices, depth_block // count_x)
-    gathered = lax.all_to_all(sent, ALL, 0, 0, tiled=True)
-    edges = edge_terms(counts, index, magnetization, stiffness)
-    gathered, edges = lax.optimization_barrier((gathered, edges))
+
+    parities = [range(parity, devices, 2) for parity in range(2)]
+    sent = residual_blocks(residual_top, residual_side, devices // 2, depth_block // count_x)
+    gathered = lax.all_to_all(
+        sent, ALL, 0, 0, tiled=True, axis_index_groups=[list(each) for each in parities]
+    )
+    z_first, z_last, x_first, x_last, y_faces = faces_of(magnetization, stiffness)
+    gathered, x_first, x_last, y_faces = lax.optimization_barrier(
+        (gathered, x_first, x_last, y_faces)
+    )
+    swapped = lax.ppermute(gathered, "gz", [(i, i ^ 1) for i in range(count_z)])
+    zy = halos_zy(z_first, z_last, y_faces)
 
     lines = call(
         functools.partial(lines_kernel, counts),
         "lines",
         (devices, 2 * TILE, LANES),
-        24,
-        "svvvvvvv",
-        (index, gathered, jnp.asarray(steps), jnp.asarray(offsets), high, low, turns, top_kernel),
+        16,
+        4.0,
+        (index, gathered, swapped, high, low, turns, top_kernel),
     )
     arrived = lax.all_to_all(lines, ALL, 0, 0, tiled=True)
+    lines, x_first, x_last = lax.optimization_barrier((lines, x_first, x_last))
+    x = halos_x(x_first, x_last)
     side = call(
         functools.partial(side_kernel_body, counts),
         "side",
         (group, 2 * depth_block, LANES),
-        16,
-        "svvvvvvv",
-        (
-            plane_index,
-            gathered,
-            jnp.asarray(there),
-            jnp.asarray(back),
-            high,
-            low,
-            turns,
-            side_kernel,
-        ),
-    )
-    exchange_grad = exchange_of(magnetization, stiffness, edges)
-    arrived, side, exchange_grad = lax.optimization_barrier((arrived, side, exchange_grad))
+        8,
+        2.8,
+        (plane_index, gathered, swapped, high, low, turns, from_hbm(side_kernel)),
+        in_hbm=(0,),
+        refs=(6,),
+        scratch=[
+            pltpu.VMEM((size // INNER, 2, 2, kzs, INNER), f32),
+            pltpu.SemaphoreType.DMA((size // INNER,)),
+        ],
+    )
+    arrived, side = lax.optimization_barrier((arrived, side))
     rows = call(
         functools.partial(rows_kernel, counts),
         "rows",
         (group, 2 * TILE + 2 * depth_block, LANES),
-        60,
-        "vvvvv",
-        (arrived, side, high, low, turns),
-    )
+        8,
+        1.4,
+        (arrived, from_hbm(side), high, low, turns),
+        refs=(1,),
+        scratch=[pltpu.SemaphoreType.DMA((1,))],
+    )
+    rows, zy, x = lax.optimization_barrier((rows, zy, x))
     arrived = lax.all_to_all(rows, ("gy", "gz"), 0, 0, tiled=True)
-    return call(sum_kernel, "gradient", magnetization.shape, 16, "vv", (exchange_grad, arrived))
+    exchange_grad = exchange_of(counts, index, magnetization, stiffness, zy, x)
+    return call(sum_kernel, "gradient", magnetization.shape, 16, 1.2, (exchange_grad, arrived))
 
 
 def fits(counts, stiffness, residual_top, residual_side, top_kernel, side_kernel):
@@ -748,10 +812,15 @@
         and count_y * LANES == INNER
         and block_y % 16 == 0
         and count_x % 2 == 0
+        and count_z % 2 == 0
         and (count_x * group) % (2 * top_kernel.shape[3] // INNER) == 0
         and INNER == top_kernel.shape[2] * count_z
         and stiffness.shape[0] % 16 == 0
         and side_kernel.shape[2] % 16 == 0
+        and all(
+            count & (count - 1) == 0
+            for count in (group, count_x, count_z, top_kernel.shape[3], side_kernel.shape[2])
+        )
     )
 
 
@@ -774,8 +843,14 @@
     index = (
         (lax.axis_index("gx") * count_y + lax.axis_index("gy")) * count_z + lax.axis_index("gz")
     ).reshape(1)
+    z_first, z_last, x_first, x_last, y_faces = faces_of(magnetization, stiffness)
     exchange_grad = exchange_of(
-        magnetization, stiffness, edge_terms(counts, index, magnetization, stiffness)
+        counts,
+        index,
+        magnetization,
+        stiffness,
+        halos_zy(z_first, z_last, y_faces),
+        halos_x(x_first, x_last),
     )
 
     parts = image_parts(

time: 62.6 us -> 52.6 us (0.84)
  blocking collectives: 9.43 us -> 0 us
  local copies, waits for them, and re-layouts: 9.92 us -> 1.01 us
  starting transfers between devices: 17.5 us -> 20.7 us
  waiting for transfers between devices: 4.54 us -> 7.32 us
  Pallas kernels: 20.1 us -> 22.8 us
    all_to_all x1 -> x0, blocking collectives: 9.43 us -> none  [fast_on_device(): arrived = lax.all_to_all(rows, ('gy', 'gz'), 0, 0, tiled=True)]
    unnamed x46 -> x24, local copies, waits for them, and re-layouts: 9.92 us -> 1.01 us
    all_to_all x1 -> x2, waiting for transfers between devices: 0.01 us -> 5.86 us  [the longest x1 5.86 us: fast_on_device(): lax.all_to_all(sent, ALL, 0, 0, tiled=True, axis_index_groups=[list(each)...]
    ppermute x5, waiting for transfers between devices: 4.45 us -> 0.01 us  [ring(): lax.ppermute(block, axis, [(i, (i + distance) % count) for i in range(cou...]
    all_to_all x1 -> x2, starting transfers between devices: 7.3 us -> 11.7 us  [the longest x1 8.31 us: fast_on_device(): lax.all_to_all(sent, ALL, 0, 0, tiled=True, axis_index_groups=[list(each)...]
    pallas_call x8 -> x7, Pallas kernels: 20.1 us -> 22.8 us  [call(): pl.pallas_call(body, out_shape=[pltpu.HBM(each, f32) if i in in_hbm else...]
    ppermute x0 -> x1, waiting for transfers between devices: none -> 1.44 us  [fast_on_device(): swapped = lax.ppermute(gathered, 'gz', [(i, i ^ 1) for i in range(count_z)])]
    all_to_all x1, starting transfers between devices: 3.81 us -> 2.59 us  [fast_on_device(): arrived = lax.all_to_all(lines, ALL, 0, 0, tiled=True)]
  transfers between devices with their start and end apart: 7 -> 9, of which waited for: 3 -> 2; matrix products, arithmetic and copies ran while one was open for 0% -> 0% of each run, Pallas kernels for 18% -> 29%
where the time goes in v4:
time: 52.6 us; the launch traced here: 52.1 us
  Pallas kernels  22.8 us (43%)
  starting transfers between devices  20.7 us (39%)
  waiting for transfers between devices  7.32 us (14%)
  local copies, waits for them, and re-layouts  1.01 us (2%)
    pallas_call x7, Pallas kernels, call(): pl.pallas_call(body, out_shape=[pltpu.HBM(each, f32) if i in in_hbm else...  22.8 us
    all_to_all x1, starting transfers between devices, fast_on_device(): lax.all_to_all(sent, ALL, 0, 0, tiled=True, axis_index_groups=[list(each)...  8.31 us
    ppermute x5, starting transfers between devices, ring(): lax.ppermute(block, axis, [(i, (i + distance) % count) for i in range(cou...  6.42 us
    all_to_all x1, waiting for transfers between devices, fast_on_device(): lax.all_to_all(sent, ALL, 0, 0, tiled=True, axis_index_groups=[list(each)...  5.86 us
    all_to_all x1, starting transfers between devices, fast_on_device(): arrived = lax.all_to_all(rows, ('gy', 'gz'), 0, 0, tiled=True)  3.4 us
    all_to_all x1, starting transfers between devices, fast_on_device(): arrived = lax.all_to_all(lines, ALL, 0, 0, tiled=True)  2.59 us
    ppermute x1, waiting for transfers between devices, fast_on_device(): swapped = lax.ppermute(gathered, 'gz', [(i, i ^ 1) for i in range(count_z)])  1.44 us
  transfers between devices with their start and end apart: 9, of which 2 were waited for; matrix products, arithmetic and copies ran while one was open for 0% of the time, Pallas kernels for 29%

profile of v4, /device:TPU:0, one launch (start us, length us, event | category | flops | bytes accessed | tf_op | source)
XLA Modules:
  0.0 52.1 jit_solution(3314786141624937609)
XLA Ops:
  0.0 1.5 %pack.1 = f32[16,24,128]{2,1,0:T(8,128)} custom-call(s32[1]{0:T(128)} %bitcast.1.at_x, f32[32,64]{1,0:T(8,128)} %bitcast.5, f32[16,128]{1,0:T(8,128)} %bitcast.6), custom_call_target="tpu_custom_call" | custom-call | flops 800000000 | bytes 212996 | tf_op jit(solution)/shard_map/pack/pallas_call | solution.py:45
  1.5 8.3 %all-to-all-start = ((f32[16,24,128]{2,1,0:T(8,128)}), f32[16,24,128]{2,1,0:T(8,128)S(1)}, u32[]{:S(2)}, u32[]{:S(2)}) async-start(f32[16,24,128]{2,1,0:T(8,128)} %pack.1), calls=%async_computation | async-start | bytes 393216 | tf_op jit(solution)/shard_map/all_to_all | solution.py:750
  9.8 0.0 copy-start
  9.8 0.0 copy-start.1
  9.8 0.0 copy-start.2
  9.8 0.0 copy-start.5
  9.8 2.7 %faces.1 = (f32[4,64,128]{2,1,0:T(8,128)S(1)}, f32[4,64,128]{2,1,0:T(8,128)S(1)}, f32[4,16,128]{2,1,0:T(8,128)S(1)}, f32[4,16,128]{2,1,0:T(8,128)S(1)}, f32[64,128]{1,0:T(8,128)}) custom-call(f32[3,16,64,128]{3,2,1,0:T(8,128)} %magnetization_from.1, f32[16,64,128]{2,1,0:T(8,128)} %stiffness_from.1), custom_call_target="tpu_custom_call" | custom-call | flops 2000000000 | bytes 2457600 | tf_op jit(solution)/shard_map/faces/pallas_call | solution.py:45
  12.6 5.9 %all-to-all-done.gathered = f32[16,24,128]{2,1,0:T(8,128)S(1)} async-done(((f32[16,24,128]{2,1,0:T(8,128)}), f32[16,24,128]{2,1,0:T(8,128)S(1)}, u32[]{:S(2)}, u32[]{:S(2)}) %all-to-all-start) | async-done | bytes 196640 | tf_op jit(solution)/shard_map/all_to_all | solution.py:750
  18.4 0.0 collective-permute-start
  18.4 1.4 %collective-permute-done.swapped = f32[16,24,128]{2,1,0:T(8,128)S(1)} collective-permute-done((f32[16,24,128]{2,1,0:T(8,128)S(1)}, f32[16,24,128]{2,1,0:T(8,128)S(1)}, u32[]{:S(2)}, u32[]{:S(2)}) %collective-permute-start) | collective-permute-done | bytes 196640 | tf_op jit(solution)/shard_map/ppermute | solution.py:757
  19.9 0.0 copy-done
  19.9 0.0 copy-done.2
  19.9 4.7 %lines.1 = f32[32,16,128]{2,1,0:T(8,128)} custom-call(s32[1]{0:T(128)} %bitcast.here, f32[16,24,128]{2,1,0:T(8,128)S(1)} %all-to-all-done.gathered, f32[16,24,128]{2,1,0:T(8,128)S(1)} %collective-permute-done.swapped, bf16[512,256]{1,0:T(8,128)(2,1)S(1)} %copy-done.2, bf16[512,256]{1,0:T(8,128)(2,1)S(1)} %copy-done.1, f32[2,8,256]{2,1,0:T(8,128)S(1)} %copy-done.5, ...), custom_call_target="tpu_custom_call" | custom-call | flops 4000000000 | bytes 3293188 | tf_op jit(solution)/shard_map/lines/pallas_call | solution.py:45
  24.6 2.6 %all-to-all-start.1 = ((f32[32,16,128]{2,1,0:T(8,128)}), f32[32,16,128]{2,1,0:T(8,128)S(1)}, u32[]{:S(2)}, u32[]{:S(2)}) async-start(f32[32,16,128]{2,1,0:T(8,128)} %lines.1), calls=%async_computation.1 | async-start | bytes 524288 | tf_op jit(solution)/shard_map/all_to_all | solution.py:768
  27.2 1.5 %collective-permute-start.1 = (f32[4,64,128]{2,1,0:T(8,128)S(1)}, f32[4,64,128]{2,1,0:T(8,128)S(1)}, u32[]{:S(2)}, u32[]{:S(2)}) collective-permute-start(f32[4,64,128]{2,1,0:T(8,128)S(1)} %get-tuple-element.32), channel_id=1, source_target_pairs={{0,3},{1,0},{2,1},{3,2},{4,7},{5,4},{6,5},{7,6},{8,11},{9,8},{10,9... | collective-permute-start | bytes 393224 | tf_op jit(solution)/shard_map/ppermute | solution.py:423
  28.7 0.0 collective-permute-start.2
  28.7 1.5 %collective-permute-start.3 = (f32[64,128]{1,0:T(8,128)S(1)}, f32[64,128]{1,0:T(8,128)S(1)}, u32[]{:S(2)}, u32[]{:S(2)}) collective-permute-start(f32[64,128]{1,0:T(8,128)S(1)} %copy-done.8), channel_id=1, source_target_pairs={{0,4},{4,0},{1,5},{5,1},{2,6},{6,2},{3,7},{7,3},{8,12},{12,8},{9,1... | collective-permute-start | bytes 98312 | tf_op jit(solution)/shard_map/ppermute | solution.py:423
  30.2 3.5 %collective-permute-start.4 = (f32[4,16,128]{2,1,0:T(8,128)S(1)}, f32[4,16,128]{2,1,0:T(8,128)S(1)}, u32[]{:S(2)}, u32[]{:S(2)}) collective-permute-start(f32[4,16,128]{2,1,0:T(8,128)S(1)} %get-tuple-element.37), channel_id=1, source_target_pairs={{0,24},{8,0},{16,8},{24,16},{1,25},{9,1},{17,9},{25,17},{2,26},{10... | collective-permute-start | bytes 98312 | tf_op jit(solution)/shard_map/ppermute | solution.py:423
  33.7 0.0 collective-permute-start.5
  33.7 0.9 %copy-done.3 = bf16[512,256]{1,0:T(8,128)(2,1)S(1)} copy-done((bf16[512,256]{1,0:T(8,128)(2,1)S(1)}, bf16[512,256]{1,0:T(8,128)(2,1)}, u32[]{:S(2)}) %copy-start.3) | copy-done | bytes 262168
  34.6 4.9 %side.1 = f32[8,32,128]{2,1,0:T(8,128)} custom-call(s32[1]{0:T(128)} %bitcast.4.here, f32[16,24,128]{2,1,0:T(8,128)S(1)} %all-to-all-done.gathered, f32[16,24,128]{2,1,0:T(8,128)S(1)} %collective-permute-done.swapped, bf16[512,256]{1,0:T(8,128)(2,1)S(1)} %copy-done.3, bf16[512,256]{1,0:T(8,128)(2,1)S(1)} %copy-done.1, f32[2,8,256]{2,1,0:T(8,128)S(1)} %copy-done.5, ...), custom_call_target="tpu_custom_call" | custom-call | flops 2800000000 | bytes 1589252 | tf_op jit(solution)/shard_map/side/pallas_call | solution.py:45
  39.5 0.0 all-to-all-done.1.arrived
  39.5 1.8 %rows.1 = f32[8,48,128]{2,1,0:T(8,128)} custom-call(f32[32,16,128]{2,1,0:T(8,128)S(1)} %all-to-all-done.1.arrived, f32[8,32,128]{2,1,0:T(8,128)} %side.1, bf16[512,256]{1,0:T(8,128)(2,1)S(1)} %copy-done.4, bf16[512,256]{1,0:T(8,128)(2,1)S(1)} %copy-done.1, f32[2,8,256]{2,1,0:T(8,128)S(1)} %copy-done.5), custom_call_target="tpu_custom_call" | custom-call | flops 1400000000 | bytes 1130496 | tf_op jit(solution)/shard_map/rows/pallas_call | solution.py:45
  41.3 0.0 collective-permute-done.1.z_next_from
  41.4 0.0 collective-permute-done.2.z_before_from
  41.4 0.0 collective-permute-done.3.y_next_from.y_before_from
  41.4 0.0 collective-permute-done.4.x_next_from
  41.4 0.0 collective-permute-done.5.x_before_from
  41.4 3.4 %all-to-all-start.2 = ((f32[8,48,128]{2,1,0:T(8,128)}), f32[8,48,128]{2,1,0:T(8,128)S(1)}, u32[]{:S(2)}, u32[]{:S(2)}) async-start(f32[8,48,128]{2,1,0:T(8,128)} %rows.1), calls=%async_computation.2 | async-start | bytes 393216 | tf_op jit(solution)/shard_map/all_to_all | solution.py:797
  44.9 5.9 %exchange.1.exchange_grad = f32[3,16,64,128]{3,2,1,0:T(8,128)S(1)} custom-call(s32[1]{0:T(128)} %bitcast.here, f32[3,16,64,128]{3,2,1,0:T(8,128)} %magnetization_from.1, f32[16,64,128]{2,1,0:T(8,128)} %stiffness_from.1, f32[4,64,128]{2,1,0:T(8,128)} %copy-done.6, f32[4,64,128]{2,1,0:T(8,128)} %copy-done.7, f32[4,16,128]{2,1,0:T(8,128)} %copy-done.10, ...), custom_call_target="tpu_custom_call" | custom-call | flops 5000000000 | bytes 4096004 | tf_op jit(solution)/shard_map/exchange/pallas_call | solution.py:45
  50.9 0.0 all-to-all-done.2.arrived
  50.9 1.3 %gradient.1 = f32[3,16,64,128]{3,2,1,0:T(8,128)} custom-call(f32[3,16,64,128]{3,2,1,0:T(8,128)S(1)} %exchange.1.exchange_grad, f32[8,48,128]{2,1,0:T(8,128)S(1)} %all-to-all-done.2.arrived), custom_call_target="tpu_custom_call" | custom-call | flops 1200000000 | bytes 3342336 | tf_op jit(solution)/shard_map/gradient/pallas_call | solution.py:45
  (17 shorter events, 0.0 us)
Async XLA Ops:
  1.5 17.0 %all-to-all-start = ((f32[16,24,128]{2,1,0:T(8,128)}), f32[16,24,128]{2,1,0:T(8,128)S(1)}, u32[]{:S(2)}, u32[]{:S(2)}) async-start(f32[16,24,128]{2,1,0:T(8,128)} %pack.1), calls=%async_computation | async-start | bytes 393216 | tf_op jit(solution)/shard_map/all_to_all | solution.py:750
  9.8 10.1 %copy-start = (f32[2,2,64,2048]{3,2,1,0:T(8,128)S(1)}, f32[2,2,64,2048]{3,2,1,0:T(8,128)}, u32[]{:S(2)}) copy-start(f32[2,2,64,2048]{3,2,1,0:T(8,128)} %kernel.1) | copy-start | bytes 6291460
  9.8 10.1 %copy-start.1 = (bf16[512,256]{1,0:T(8,128)(2,1)S(1)}, bf16[512,256]{1,0:T(8,128)(2,1)}, u32[]{:S(2)}) copy-start(bf16[512,256]{1,0:T(8,128)(2,1)} %constant.23.clone.low) | copy-start | bytes 786436
  9.8 10.1 %copy-start.2 = (bf16[512,256]{1,0:T(8,128)(2,1)S(1)}, bf16[512,256]{1,0:T(8,128)(2,1)}, u32[]{:S(2)}) copy-start(bf16[512,256]{1,0:T(8,128)(2,1)} %constant.22.clone.high) | copy-start | bytes 786436
  9.8 10.1 %copy-start.5 = (f32[2,8,256]{2,1,0:T(8,128)S(1)}, f32[2,8,256]{2,1,0:T(8,128)}, u32[]{:S(2)}) copy-start(f32[2,8,256]{2,1,0:T(8,128)} %constant.24.clone.turns) | copy-start | bytes 49156
  18.4 1.4 %collective-permute-start = (f32[16,24,128]{2,1,0:T(8,128)S(1)}, f32[16,24,128]{2,1,0:T(8,128)S(1)}, u32[]{:S(2)}, u32[]{:S(2)}) collective-permute-start(f32[16,24,128]{2,1,0:T(8,128)S(1)} %all-to-all-done.gathered), channel_id=1, source_target_pairs={{0,1},{1,0},{2,3},{3,2},{4,5},{5,4},{6,7},{7,6},{8,9},{9,8},{10,11... | collective-permute-start | bytes 589832 | tf_op jit(solution)/shard_map/ppermute | solution.py:757
  19.9 8.8 %copy-start.8 = (f32[64,128]{1,0:T(8,128)S(1)}, f32[64,128]{1,0:T(8,128)}, u32[]{:S(2)}) copy-start(f32[64,128]{1,0:T(8,128)} %get-tuple-element.45.y_faces_from) | copy-start | bytes 98308
  24.6 14.9 %all-to-all-start.1 = ((f32[32,16,128]{2,1,0:T(8,128)}), f32[32,16,128]{2,1,0:T(8,128)S(1)}, u32[]{:S(2)}, u32[]{:S(2)}) async-start(f32[32,16,128]{2,1,0:T(8,128)} %lines.1), calls=%async_computation.1 | async-start | bytes 524288 | tf_op jit(solution)/shard_map/all_to_all | solution.py:768
  27.2 14.1 %collective-permute-start.1 = (f32[4,64,128]{2,1,0:T(8,128)S(1)}, f32[4,64,128]{2,1,0:T(8,128)S(1)}, u32[]{:S(2)}, u32[]{:S(2)}) collective-permute-start(f32[4,64,128]{2,1,0:T(8,128)S(1)} %get-tuple-element.32), channel_id=1, source_target_pairs={{0,3},{1,0},{2,1},{3,2},{4,7},{5,4},{6,5},{7,6},{8,11},{9,8},{10,9... | collective-permute-start | bytes 393224 | tf_op jit(solution)/shard_map/ppermute | solution.py:423
  28.7 12.7 %collective-permute-start.2 = (f32[4,64,128]{2,1,0:T(8,128)S(1)}, f32[4,64,128]{2,1,0:T(8,128)S(1)}, u32[]{:S(2)}, u32[]{:S(2)}) collective-permute-start(f32[4,64,128]{2,1,0:T(8,128)S(1)} %get-tuple-element.33), channel_id=1, source_target_pairs={{0,1},{1,2},{2,3},{3,0},{4,5},{5,6},{6,7},{7,4},{8,9},{9,10},{10,1... | collective-permute-start | bytes 393224 | tf_op jit(solution)/shard_map/ppermute | solution.py:423
  28.7 12.7 %collective-permute-start.3 = (f32[64,128]{1,0:T(8,128)S(1)}, f32[64,128]{1,0:T(8,128)S(1)}, u32[]{:S(2)}, u32[]{:S(2)}) collective-permute-start(f32[64,128]{1,0:T(8,128)S(1)} %copy-done.8), channel_id=1, source_target_pairs={{0,4},{4,0},{1,5},{5,1},{2,6},{6,2},{3,7},{7,3},{8,12},{12,8},{9,1... | collective-permute-start | bytes 98312 | tf_op jit(solution)/shard_map/ppermute | solution.py:423
  30.2 11.2 %collective-permute-start.4 = (f32[4,16,128]{2,1,0:T(8,128)S(1)}, f32[4,16,128]{2,1,0:T(8,128)S(1)}, u32[]{:S(2)}, u32[]{:S(2)}) collective-permute-start(f32[4,16,128]{2,1,0:T(8,128)S(1)} %get-tuple-element.37), channel_id=1, source_target_pairs={{0,24},{8,0},{16,8},{24,16},{1,25},{9,1},{17,9},{25,17},{2,26},{10... | collective-permute-start | bytes 98312 | tf_op jit(solution)/shard_map/ppermute | solution.py:423
  33.7 7.8 %collective-permute-start.5 = (f32[4,16,128]{2,1,0:T(8,128)S(1)}, f32[4,16,128]{2,1,0:T(8,128)S(1)}, u32[]{:S(2)}, u32[]{:S(2)}) collective-permute-start(f32[4,16,128]{2,1,0:T(8,128)S(1)} %get-tuple-element.38), channel_id=1, source_target_pairs={{0,8},{8,16},{16,24},{24,0},{1,9},{9,17},{17,25},{25,1},{2,10},{10... | collective-permute-start | bytes 98312 | tf_op jit(solution)/shard_map/ppermute | solution.py:423
  33.7 1.0 %copy-start.3 = (bf16[512,256]{1,0:T(8,128)(2,1)S(1)}, bf16[512,256]{1,0:T(8,128)(2,1)}, u32[]{:S(2)}) copy-start(bf16[512,256]{1,0:T(8,128)(2,1)} %constant.22.clone.high) | copy-start | bytes 786436
  34.6 4.9 %copy-start.4 = (bf16[512,256]{1,0:T(8,128)(2,1)S(1)}, bf16[512,256]{1,0:T(8,128)(2,1)}, u32[]{:S(2)}) copy-start(bf16[512,256]{1,0:T(8,128)(2,1)} %constant.22.clone.high) | copy-start | bytes 786436
  41.3 3.5 %copy-start.6 = (f32[4,64,128]{2,1,0:T(8,128)}, f32[4,64,128]{2,1,0:T(8,128)S(1)}, u32[]{:S(2)}) copy-start(f32[4,64,128]{2,1,0:T(8,128)S(1)} %collective-permute-done.1.z_next_from) | copy-start | bytes 393220
  41.4 3.5 %copy-start.7 = (f32[4,64,128]{2,1,0:T(8,128)}, f32[4,64,128]{2,1,0:T(8,128)S(1)}, u32[]{:S(2)}) copy-start(f32[4,64,128]{2,1,0:T(8,128)S(1)} %collective-permute-done.2.z_before_from) | copy-start | bytes 393220
  41.4 3.5 %copy-start.9 = (f32[64,128]{1,0:T(8,128)}, f32[64,128]{1,0:T(8,128)S(1)}, u32[]{:S(2)}) copy-start(f32[64,128]{1,0:T(8,128)S(1)} %collective-permute-done.3.y_next_from.y_before_from) | copy-start | bytes 98308
  41.4 3.5 %copy-start.10 = (f32[4,16,128]{2,1,0:T(8,128)}, f32[4,16,128]{2,1,0:T(8,128)S(1)}, u32[]{:S(2)}) copy-start(f32[4,16,128]{2,1,0:T(8,128)S(1)} %collective-permute-done.4.x_next_from) | copy-start | bytes 98308
  41.4 3.5 %copy-start.11 = (f32[4,16,128]{2,1,0:T(8,128)}, f32[4,16,128]{2,1,0:T(8,128)S(1)}, u32[]{:S(2)}) copy-start(f32[4,16,128]{2,1,0:T(8,128)S(1)} %collective-permute-done.5.x_before_from) | copy-start | bytes 98308
  41.4 9.4 %all-to-all-start.2 = ((f32[8,48,128]{2,1,0:T(8,128)}), f32[8,48,128]{2,1,0:T(8,128)S(1)}, u32[]{:S(2)}, u32[]{:S(2)}) async-start(f32[8,48,128]{2,1,0:T(8,128)} %rows.1), calls=%async_computation.2 | async-start | bytes 393216 | tf_op jit(solution)/shard_map/all_to_all | solution.py:797

commit v5 on v4

--- a/solution.py
+++ b/solution.py
@@ -505,40 +505,137 @@
     return dot3(jnp.concatenate([upper, lower], axis=0), tables)
 
 
-def back_and_forth(real, imag, columns_of, tables, turns):
-    rows = real.shape[0]
-    total_real = total_imag = None
-    for b in range(turns.shape[1]):
-        cosine, sine = turns[0, b : b + 1, :], turns[1, b : b + 1, :]
-        waves = stacked_product(
-            real * cosine + imag * sine, imag * cosine - real * sine, tables, -1
-        )
-        wave_real, wave_imag = waves[:rows], waves[rows:]
-        kernel = columns_of(b)
-        weighted_real, weighted_imag = [], []
-        for c in range(2):
-            kernel_real, kernel_imag = kernel[c, 0], kernel[c, 1]
-            weighted_real.append(kernel_real * wave_real + kernel_imag * wave_imag)
-            weighted_imag.append(kernel_real * wave_imag - kernel_imag * wave_real)
-        back = stacked_product(
-            jnp.concatenate(weighted_real, axis=0),
-            jnp.concatenate(weighted_imag, axis=0),
-            tables,
-            1,
-        )
-        back_real, back_imag = back[: 2 * rows], back[2 * rows :]
-        if b == 0:
-            total_real, total_imag = back_real, back_imag
-        else:
-            total_real = total_real + (back_real * cosine - back_imag * sine)
-            total_imag = total_imag + (back_real * sine + back_imag * cosine)
-    return [
-        (total_real[c * rows : (c + 1) * rows], total_imag[c * rows : (c + 1) * rows])
-        for c in range(2)
-    ]
-
-
-def lines_kernel(counts, here, gathered, swapped, high, low, turns, kernel, out):
+def add(a, b):
+    return a[0] + b[0], a[1] + b[1]
+
+
+def subtract(a, b):
+    return a[0] - b[0], a[1] - b[1]
+
+
+def eight_points(z, sign):
+    def quarter_turn(a):
+        return (-a[1], a[0]) if sign > 0 else (a[1], -a[0])
+
+    def four_points(p, q, r, s):
+        e, f, g, h = add(p, r), subtract(p, r), add(q, s), quarter_turn(subtract(q, s))
+        return add(e, g), add(f, h), subtract(e, g), subtract(f, h)
+
+    even = four_points(z[0], z[2], z[4], z[6])
+    odd = four_points(z[1], z[3], z[5], z[7])
+    root = math.sqrt(0.5)
+    first, third = add(odd[1], quarter_turn(odd[1])), subtract(quarter_turn(odd[3]), odd[3])
+    odd = (
+        odd[0],
+        (first[0] * root, first[1] * root),
+        quarter_turn(odd[2]),
+        (third[0] * root, third[1] * root),
+    )
+    return [add(a, b) for a, b in zip(even, odd)] + [subtract(a, b) for a, b in zip(even, odd)]
+
+
+def spread_tables(extent, size):
+    step = size // INNER
+    count = extent // step
+    angle = np.outer(np.arange(count), np.arange(INNER)) * (2.0 * math.pi / INNER)
+    cosine, sine = np.cos(angle), np.sin(angle)
+
+    def parts(table):
+        table = table.astype(np.float32)
+        high = table.astype(ml_dtypes.bfloat16)
+        return high, (table - high.astype(np.float32)).astype(ml_dtypes.bfloat16)
+
+    high, low = parts(np.block([[cosine, -sine], [sine, cosine]]))
+    there = np.concatenate([high, high, low, np.zeros_like(low)], axis=0)
+    high, low = parts(np.block([[cosine.T, sine.T], [-sine.T, cosine.T]]))
+    back = np.concatenate([high, low], axis=1)
+    angle = np.outer(np.arange(step), np.arange(INNER)) * (2.0 * math.pi / size)
+    return there, back, np.stack([np.cos(angle), np.sin(angle)]).astype(np.float32)
+
+
+def regrouping(extent, step, transposed):
+    x = lax.broadcasted_iota(jnp.int32, (extent, extent), int(transposed))
+    place = lax.broadcasted_iota(jnp.int32, (extent, extent), 1 - int(transposed))
+    count = extent // step
+    moved = (x & (step - 1)) * count + (x >> whole_log(step))
+    return jnp.where(moved == place, 1.0, 0.0).astype(bf16)
+
+
+def product(left, right):
+    return lax.dot_general(left, right, (((1,), (0,)), ((), ())), preferred_element_type=f32)
+
+
+def there_and_back(real, imag, columns_of, there, back, turns):
+    rows, extent = real.shape
+    step = turns.shape[1]
+    count = extent // step
+    per = LANES // count
+    high, low = split(jnp.concatenate([real, imag], axis=0))
+    moved = product(jnp.concatenate([high, low], axis=0), regrouping(extent, step, False))
+    lane = lax.broadcasted_iota(jnp.int32, (rows, LANES), 1)
+    lines = []
+    for v in range(step):
+        column = v // per * LANES
+        first = None
+        for k in range(4):
+            piece = moved[k * rows : (k + 1) * rows, column : column + LANES]
+            shift = (k - v) * count % LANES
+            piece = pltpu.roll(piece, shift, 1) if shift else piece
+            first = piece if k == 0 else jnp.where(lane < k * count, first, piece)
+        second = jnp.where(lane < 2 * count, first, 0.0)
+        lines.append(jnp.concatenate([first, second], axis=1))
+    waves = product(jnp.concatenate(lines, axis=0).astype(bf16), there)
+
+    results = []
+    for start in range(0, rows, 16):
+        halves = [[], []]
+        for half in range(INNER // LANES):
+            lanes = slice(half * LANES, (half + 1) * LANES)
+            turn = [(turns[0, v : v + 1, lanes], turns[1, v : v + 1, lanes]) for v in range(step)]
+            z = []
+            for v in range(step):
+                part = waves[v * rows + start : v * rows + start + 16]
+                a = part[:, lanes]
+                b = part[:, INNER + half * LANES : INNER + (half + 1) * LANES]
+                if v:
+                    cosine, sine = turn[v]
+                    a, b = a * cosine + b * sine, b * cosine - a * sine
+                z.append((a, b))
+            z = eight_points(z, -1)
+            for c in range(2):
+                weighted = []
+                for k in range(step):
+                    kernel = columns_of(k)
+                    kernel_real = kernel[c, 0, start : start + 16, lanes]
+                    kernel_imag = kernel[c, 1, start : start + 16, lanes]
+                    weighted.append(
+                        (
+                            kernel_real * z[k][0] + kernel_imag * z[k][1],
+                            kernel_real * z[k][1] - kernel_imag * z[k][0],
+                        )
+                    )
+                weighted = eight_points(weighted, 1)
+                for v in range(1, step):
+                    (a, b), (cosine, sine) = weighted[v], turn[v]
+                    weighted[v] = (a * cosine - b * sine, a * sine + b * cosine)
+                halves[c].append(weighted)
+        parts = ([], [])
+        for v in range(step):
+            for c in range(2):
+                pieces = [
+                    split(halves[c][half][v][k])
+                    for k in range(2)
+                    for half in range(INNER // LANES)
+                ]
+                for k in range(2):
+                    parts[k].append(jnp.concatenate([piece[k] for piece in pieces], axis=1))
+        both = product(jnp.concatenate(parts[0] + parts[1], axis=0), back)
+        middle = both.shape[0] // 2
+        results.append(both[:middle] + pltpu.roll(both[:middle], LANES // 2, 1) + both[middle:])
+    return results
+
+
+def lines_kernel(counts, here, gathered, swapped, there, back, turns, kernel, out):
     count_x, count_y, count_z = counts
     group = count_y * count_z
     top_rows = LANES // group
@@ -584,16 +681,21 @@
     def columns_of(b):
         return kernel.at[:, :, :, b * INNER : (b + 1) * INNER]
 
-    images = back_and_forth(
-        lines[:kys], lines[kys:], columns_of, (high[...], low[...]), turns
-    )
-    for c in range(2):
-        block = jnp.concatenate(images[c], axis=0).T
-        out[:, c * TILE : (c + 1) * TILE, :] = block.reshape(count_x * group, TILE, LANES)
+    results = there_and_back(
+        lines[:kys], lines[kys:], columns_of, there[...], back[...], turns
+    )
+    count = count_x * group
+    for v in range(turns.shape[1]):
+        block = jnp.concatenate(
+            [result[(2 * v + c) * 16 : (2 * v + c + 1) * 16] for c in range(2) for result in results],
+            axis=0,
+        ).T
+        out[:, v, :] = block[:count]
+        out[:, TILE + v, :] = block[count : 2 * count]
 
 
 def side_kernel_body(
-    counts, here, gathered, swapped, high, low, turns, kernel_from, out, kernel, loading
+    counts, here, gathered, swapped, there, back, turns, kernel_from, out, kernel, loading
 ):
     count_x, count_y, count_z = counts
     depth_block = out.shape[1] // 2
@@ -618,8 +720,8 @@
     z = (2 * pair + odd) * depth_block + within
     z = z + (column >> whole_log(TILE * count_z // 2) & (count_x - 1)) * share
     cosine, sine = cos_sin(kz * z & (size - 1), size)
-    there = jnp.concatenate([cosine, -sine], axis=0)
-    there = jnp.where(jnp.concatenate([within, within], axis=0) < share, there, 0.0)
+    table = jnp.concatenate([cosine, -sine], axis=0)
+    table = jnp.where(jnp.concatenate([within, within], axis=0) < share, table, 0.0)
 
     blocks = []
     for y in range(count_y):
@@ -630,23 +732,51 @@
             for pair in range(count_z // 2)
         ]
         blocks.append(jnp.concatenate(rows, axis=0))
-    lines = dot3(there, split(jnp.concatenate(blocks, axis=1)))
+    lines = dot3(table, split(jnp.concatenate(blocks, axis=1)))
+
+    waiting = dict(enumerate(loads))
 
     def columns_of(b):
-        loads[b].wait()
+        if b in waiting:
+            waiting.pop(b).wait()
         return kernel.at[b]
 
-    images = back_and_forth(
-        lines[:kzs], lines[kzs:], columns_of, (high[...], low[...]), turns
-    )
+    result = there_and_back(
+        lines[:kzs], lines[kzs:], columns_of, there[...], back[...], turns
+    )[0]
+    step = turns.shape[1]
+    extent = count_y * LANES
+    count = extent // step
+    per = LANES // count
+    lane = lax.broadcasted_iota(jnp.int32, (kzs, LANES), 1)
+    images = []
+    for c in range(2):
+        for k in range(2):
+            columns = []
+            for first in range(0, step, per):
+                column = None
+                for v in range(first, first + per):
+                    piece = result[(2 * v + c) * 16 : (2 * v + c + 1) * 16]
+                    shift = (v - first - k) * count % LANES
+                    piece = pltpu.roll(piece, shift, 1) if shift else piece
+                    column = (
+                        piece
+                        if v == first
+                        else jnp.where(lane < (v - first) * count, column, piece)
+                    )
+                columns.append(column)
+            images.append(jnp.concatenate(columns, axis=1))
+    high, low = split(jnp.concatenate(images, axis=0))
+    order = regrouping(extent, step, True)
+    images = product(high, order) + product(low, order)
 
     rows = depth_block * count_z
     z = lax.broadcasted_iota(jnp.int32, (rows, 2 * kzs), 0)
     column = lax.broadcasted_iota(jnp.int32, (rows, 2 * kzs), 1)
     cosine, sine = cos_sin((here[0] * kzs + (column & (kzs - 1))) * z & (size - 1), size)
-    back = jnp.where(column < kzs, cosine, -sine) * (1.0 / (size * length))
+    table = jnp.where(column < kzs, cosine, -sine) * (1.0 / (size * length))
     for c in range(2):
-        image = dot3(back, split(jnp.concatenate(images[c], axis=0)))
+        image = dot3(table, split(images[2 * kzs * c : 2 * kzs * (c + 1)]))
         for y in range(count_y):
             for z in range(count_z):
                 out[y * count_z + z, c * depth_block : (c + 1) * depth_block, :] = image[
@@ -660,15 +790,17 @@
     per_turn = arrived.shape[0] // turns.shape[1]
     half = LANES // 2
     lane = lax.broadcasted_iota(jnp.int32, (2 * TILE, LANES), 1)
-    real, imag = [], []
+    parts = [[], []]
     for b in range(turns.shape[1]):
-        real_pieces, imag_pieces = [], []
+        spectra = ([], [])
         for g in range(b * per_turn, (b + 1) * per_turn, 2):
             first, second = arrived[g], arrived[g + 1]
-            real_pieces.append(jnp.where(lane < half, first, pltpu.roll(second, half, 1)))
-            imag_pieces.append(jnp.where(lane < half, pltpu.roll(first, half, 1), second))
-        real.append(jnp.concatenate(real_pieces, axis=1))
-        imag.append(jnp.concatenate(imag_pieces, axis=1))
+            spectra[0].append(jnp.where(lane < half, first, pltpu.roll(second, half, 1)))
+            spectra[1].append(jnp.where(lane < half, pltpu.roll(first, half, 1), second))
+        spectra = [jnp.concatenate(pieces, axis=1) for pieces in spectra]
+        for k in range(2):
+            parts[k] += [spectrum[k * TILE : (k + 1) * TILE] for spectrum in spectra]
+    real, imag = parts
     back = stacked_product(
         jnp.concatenate(real, axis=0), jnp.concatenate(imag, axis=0), (high[...], low[...]), 1
     )
@@ -744,6 +876,7 @@
     plane_index = plane_index.reshape(1)
     (high, low), _, turns = transform_tables(extent, size)
     high, low, turns = jnp.asarray(high), jnp.asarray(low), jnp.asarray(turns)
+    there, back, spread_turns = (jnp.asarray(table) for table in spread_tables(extent, size))
 
     parities = [range(parity, devices, 2) for parity in range(2)]
     sent = residual_blocks(residual_top, residual_side, devices // 2, depth_block // count_x)
@@ -763,7 +896,7 @@
         (devices, 2 * TILE, LANES),
         16,
         4.0,
-        (index, gathered, swapped, high, low, turns, top_kernel),
+        (index, gathered, swapped, there, back, spread_turns, top_kernel),
     )
     arrived = lax.all_to_all(lines, ALL, 0, 0, tiled=True)
     lines, x_first, x_last = lax.optimization_barrier((lines, x_first, x_last))
@@ -774,7 +907,7 @@
         (group, 2 * depth_block, LANES),
         8,
         2.8,
-        (plane_index, gathered, swapped, high, low, turns, from_hbm(side_kernel)),
+        (plane_index, gathered, swapped, there, back, spread_turns, from_hbm(side_kernel)),
         in_hbm=(0,),
         refs=(6,),
         scratch=[
@@ -815,6 +948,8 @@
         and count_z % 2 == 0
         and (count_x * group) % (2 * top_kernel.shape[3] // INNER) == 0
         and INNER == top_kernel.shape[2] * count_z
+        and top_kernel.shape[3] == TILE * INNER == side_kernel.shape[3]
+        and INNER == 2 * LANES
         and stiffness.shape[0] % 16 == 0
         and side_kernel.shape[2] % 16 == 0
         and all(

time: 52.6 us -> 49.4 us (0.939)
  Pallas kernels: 22.8 us -> 19.4 us
  waiting for transfers between devices: 7.32 us -> 8.45 us
  local copies, waits for them, and re-layouts: 1.01 us -> 0.06 us
    pallas_call x7, Pallas kernels: 22.8 us -> 19.4 us  [call(): pl.pallas_call(body, out_shape=[pltpu.HBM(each, f32) if i in in_hbm else...]
    all_to_all x1, waiting for transfers between devices: 0.01 us -> 1.14 us  [fast_on_device(): arrived = lax.all_to_all(lines, ALL, 0, 0, tiled=True)]
    unnamed x24 -> x26, local copies, waits for them, and re-layouts: 1.01 us -> 0.06 us
  transfers between devices with their start and end apart: 9 -> 9, of which waited for: 2 -> 3; matrix products, arithmetic and copies ran while one was open for 0% -> 0% of each run, Pallas kernels for 29% -> 27%
where the time goes in v5:
time: 49.4 us; the launch traced here: 48.9 us
  starting transfers between devices  20.7 us (42%)
  Pallas kernels  19.4 us (39%)
  waiting for transfers between devices  8.45 us (17%)
    pallas_call x7, Pallas kernels, call(): pl.pallas_call(body, out_shape=[pltpu.HBM(each, f32) if i in in_hbm else...  19.4 us
    all_to_all x1, starting transfers between devices, fast_on_device(): lax.all_to_all(sent, ALL, 0, 0, tiled=True, axis_index_groups=[list(each)...  8.31 us
    ppermute x5, starting transfers between devices, ring(): lax.ppermute(block, axis, [(i, (i + distance) % count) for i in range(cou...  6.42 us
    all_to_all x1, waiting for transfers between devices, fast_on_device(): lax.all_to_all(sent, ALL, 0, 0, tiled=True, axis_index_groups=[list(each)...  5.86 us
    all_to_all x1, starting transfers between devices, fast_on_device(): arrived = lax.all_to_all(rows, ('gy', 'gz'), 0, 0, tiled=True)  3.4 us
    all_to_all x1, starting transfers between devices, fast_on_device(): arrived = lax.all_to_all(lines, ALL, 0, 0, tiled=True)  2.59 us
    ppermute x1, waiting for transfers between devices, fast_on_device(): swapped = lax.ppermute(gathered, 'gz', [(i, i ^ 1) for i in range(count_z)])  1.44 us
    all_to_all x1, waiting for transfers between devices, fast_on_device(): arrived = lax.all_to_all(lines, ALL, 0, 0, tiled=True)  1.14 us
  transfers between devices with their start and end apart: 9, of which 3 were waited for; matrix products, arithmetic and copies ran while one was open for 0% of the time, Pallas kernels for 27%

profile of v5, /device:TPU:0, one launch (start us, length us, event | category | flops | bytes accessed | tf_op | source)
XLA Modules:
  0.0 48.9 jit_solution(15707701223097776944)
XLA Ops:
  0.0 1.5 %pack.1 = f32[16,24,128]{2,1,0:T(8,128)} custom-call(s32[1]{0:T(128)} %bitcast.1.at_x, f32[32,64]{1,0:T(8,128)} %bitcast.5, f32[16,128]{1,0:T(8,128)} %bitcast.6), custom_call_target="tpu_custom_call" | custom-call | flops 800000000 | bytes 212996 | tf_op jit(solution)/shard_map/pack/pallas_call | solution.py:45
  1.5 8.3 %all-to-all-start = ((f32[16,24,128]{2,1,0:T(8,128)}), f32[16,24,128]{2,1,0:T(8,128)S(1)}, u32[]{:S(2)}, u32[]{:S(2)}) async-start(f32[16,24,128]{2,1,0:T(8,128)} %pack.1), calls=%async_computation | async-start | bytes 393216 | tf_op jit(solution)/shard_map/all_to_all | solution.py:883
  9.8 0.0 copy-start
  9.8 0.0 copy-start.3
  9.8 0.0 copy-start.4
  9.8 0.0 copy-start.6
  9.8 2.7 %faces.1 = (f32[4,64,128]{2,1,0:T(8,128)S(1)}, f32[4,64,128]{2,1,0:T(8,128)S(1)}, f32[4,16,128]{2,1,0:T(8,128)S(1)}, f32[4,16,128]{2,1,0:T(8,128)S(1)}, f32[64,128]{1,0:T(8,128)}) custom-call(f32[3,16,64,128]{3,2,1,0:T(8,128)} %magnetization_from.1, f32[16,64,128]{2,1,0:T(8,128)} %stiffness_from.1), custom_call_target="tpu_custom_call" | custom-call | flops 2000000000 | bytes 2457600 | tf_op jit(solution)/shard_map/faces/pallas_call | solution.py:45
  12.6 5.9 %all-to-all-done.gathered = f32[16,24,128]{2,1,0:T(8,128)S(1)} async-done(((f32[16,24,128]{2,1,0:T(8,128)}), f32[16,24,128]{2,1,0:T(8,128)S(1)}, u32[]{:S(2)}, u32[]{:S(2)}) %all-to-all-start) | async-done | bytes 196640 | tf_op jit(solution)/shard_map/all_to_all | solution.py:883
  18.4 0.0 collective-permute-start
  18.4 1.4 %collective-permute-done.swapped = f32[16,24,128]{2,1,0:T(8,128)S(1)} collective-permute-done((f32[16,24,128]{2,1,0:T(8,128)S(1)}, f32[16,24,128]{2,1,0:T(8,128)S(1)}, u32[]{:S(2)}, u32[]{:S(2)}) %collective-permute-start) | collective-permute-done | bytes 196640 | tf_op jit(solution)/shard_map/ppermute | solution.py:890
  19.9 0.0 copy-done.3
  19.9 3.3 %lines.1 = f32[32,16,128]{2,1,0:T(8,128)} custom-call(s32[1]{0:T(128)} %bitcast.here, f32[16,24,128]{2,1,0:T(8,128)S(1)} %all-to-all-done.gathered, f32[16,24,128]{2,1,0:T(8,128)S(1)} %collective-permute-done.swapped, bf16[256,512]{1,0:T(8,128)(2,1)S(1)} %copy-done.3, bf16[512,128]{1,0:T(8,128)(2,1)S(1)} %copy-done.4, f32[2,8,256]{2,1,0:T(8,128)S(1)} %copy-done.6, ...), custom_call_target="tpu_custom_call" | custom-call | flops 4000000000 | bytes 3162116 | tf_op jit(solution)/shard_map/lines/pallas_call | solution.py:45
  23.2 2.6 %all-to-all-start.1 = ((f32[32,16,128]{2,1,0:T(8,128)}), f32[32,16,128]{2,1,0:T(8,128)S(1)}, u32[]{:S(2)}, u32[]{:S(2)}) async-start(f32[32,16,128]{2,1,0:T(8,128)} %lines.1), calls=%async_computation.1 | async-start | bytes 524288 | tf_op jit(solution)/shard_map/all_to_all | solution.py:901
  25.8 1.5 %collective-permute-start.1 = (f32[4,64,128]{2,1,0:T(8,128)S(1)}, f32[4,64,128]{2,1,0:T(8,128)S(1)}, u32[]{:S(2)}, u32[]{:S(2)}) collective-permute-start(f32[4,64,128]{2,1,0:T(8,128)S(1)} %get-tuple-element.32), channel_id=1, source_target_pairs={{0,3},{1,0},{2,1},{3,2},{4,7},{5,4},{6,5},{7,6},{8,11},{9,8},{10,9... | collective-permute-start | bytes 393224 | tf_op jit(solution)/shard_map/ppermute | solution.py:423
  27.2 0.0 collective-permute-start.2
  27.2 0.0 copy-done.9
  27.3 1.5 %collective-permute-start.3 = (f32[64,128]{1,0:T(8,128)S(1)}, f32[64,128]{1,0:T(8,128)S(1)}, u32[]{:S(2)}, u32[]{:S(2)}) collective-permute-start(f32[64,128]{1,0:T(8,128)S(1)} %copy-done.9), channel_id=1, source_target_pairs={{0,4},{4,0},{1,5},{5,1},{2,6},{6,2},{3,7},{7,3},{8,12},{12,8},{9,1... | collective-permute-start | bytes 98312 | tf_op jit(solution)/shard_map/ppermute | solution.py:423
  28.7 3.5 %collective-permute-start.4 = (f32[4,16,128]{2,1,0:T(8,128)S(1)}, f32[4,16,128]{2,1,0:T(8,128)S(1)}, u32[]{:S(2)}, u32[]{:S(2)}) collective-permute-start(f32[4,16,128]{2,1,0:T(8,128)S(1)} %get-tuple-element.37), channel_id=1, source_target_pairs={{0,24},{8,0},{16,8},{24,16},{1,25},{9,1},{17,9},{25,17},{2,26},{10... | collective-permute-start | bytes 98312 | tf_op jit(solution)/shard_map/ppermute | solution.py:423
  32.2 0.0 collective-permute-start.5
  32.2 2.9 %side.1 = f32[8,32,128]{2,1,0:T(8,128)} custom-call(s32[1]{0:T(128)} %bitcast.4.here, f32[16,24,128]{2,1,0:T(8,128)S(1)} %all-to-all-done.gathered, f32[16,24,128]{2,1,0:T(8,128)S(1)} %collective-permute-done.swapped, bf16[256,512]{1,0:T(8,128)(2,1)S(1)} %copy-done.3, bf16[512,128]{1,0:T(8,128)(2,1)S(1)} %copy-done.4, f32[2,8,256]{2,1,0:T(8,128)S(1)} %copy-done.6, ...), custom_call_target="tpu_custom_call" | custom-call | flops 2800000000 | bytes 1458180 | tf_op jit(solution)/shard_map/side/pallas_call | solution.py:45
  35.2 1.1 %all-to-all-done.1.arrived = f32[32,16,128]{2,1,0:T(8,128)S(1)} async-done(((f32[32,16,128]{2,1,0:T(8,128)}), f32[32,16,128]{2,1,0:T(8,128)S(1)}, u32[]{:S(2)}, u32[]{:S(2)}) %all-to-all-start.1) | async-done | bytes 262176 | tf_op jit(solution)/shard_map/all_to_all | solution.py:901
  36.3 0.0 copy-done.1
  36.3 1.8 %rows.1 = f32[8,48,128]{2,1,0:T(8,128)} custom-call(f32[32,16,128]{2,1,0:T(8,128)S(1)} %all-to-all-done.1.arrived, f32[8,32,128]{2,1,0:T(8,128)} %side.1, bf16[512,256]{1,0:T(8,128)(2,1)S(1)} %copy-done.2, bf16[512,256]{1,0:T(8,128)(2,1)S(1)} %copy-done.1, f32[2,8,256]{2,1,0:T(8,128)S(1)} %copy-done.5), custom_call_target="tpu_custom_call" | custom-call | flops 1400000000 | bytes 1130496 | tf_op jit(solution)/shard_map/rows/pallas_call | solution.py:45
  38.1 0.0 collective-permute-done.1.z_next_from
  38.2 0.0 collective-permute-done.2.z_before_from
  38.2 0.0 collective-permute-done.3.y_next_from.y_before_from
  38.2 0.0 collective-permute-done.4.x_next_from
  38.2 0.0 collective-permute-done.5.x_before_from
  38.2 3.4 %all-to-all-start.2 = ((f32[8,48,128]{2,1,0:T(8,128)}), f32[8,48,128]{2,1,0:T(8,128)S(1)}, u32[]{:S(2)}, u32[]{:S(2)}) async-start(f32[8,48,128]{2,1,0:T(8,128)} %rows.1), calls=%async_computation.2 | async-start | bytes 393216 | tf_op jit(solution)/shard_map/all_to_all | solution.py:930
  41.7 5.9 %exchange.1.exchange_grad = f32[3,16,64,128]{3,2,1,0:T(8,128)S(1)} custom-call(s32[1]{0:T(128)} %bitcast.here, f32[3,16,64,128]{3,2,1,0:T(8,128)} %magnetization_from.1, f32[16,64,128]{2,1,0:T(8,128)} %stiffness_from.1, f32[4,64,128]{2,1,0:T(8,128)} %copy-done.7, f32[4,64,128]{2,1,0:T(8,128)} %copy-done.8, f32[4,16,128]{2,1,0:T(8,128)} %copy-done.11, ...), custom_call_target="tpu_custom_call" | custom-call | flops 5000000000 | bytes 4096004 | tf_op jit(solution)/shard_map/exchange/pallas_call | solution.py:45
  47.7 0.0 all-to-all-done.2.arrived
  47.7 1.3 %gradient.1 = f32[3,16,64,128]{3,2,1,0:T(8,128)} custom-call(f32[3,16,64,128]{3,2,1,0:T(8,128)S(1)} %exchange.1.exchange_grad, f32[8,48,128]{2,1,0:T(8,128)S(1)} %all-to-all-done.2.arrived), custom_call_target="tpu_custom_call" | custom-call | flops 1200000000 | bytes 3342336 | tf_op jit(solution)/shard_map/gradient/pallas_call | solution.py:45
  (19 shorter events, 0.0 us)
Async XLA Ops:
  1.5 17.0 %all-to-all-start = ((f32[16,24,128]{2,1,0:T(8,128)}), f32[16,24,128]{2,1,0:T(8,128)S(1)}, u32[]{:S(2)}, u32[]{:S(2)}) async-start(f32[16,24,128]{2,1,0:T(8,128)} %pack.1), calls=%async_computation | async-start | bytes 393216 | tf_op jit(solution)/shard_map/all_to_all | solution.py:883
  9.8 10.1 %copy-start = (f32[2,2,64,2048]{3,2,1,0:T(8,128)S(1)}, f32[2,2,64,2048]{3,2,1,0:T(8,128)}, u32[]{:S(2)}) copy-start(f32[2,2,64,2048]{3,2,1,0:T(8,128)} %kernel.1) | copy-start | bytes 6291460
  9.8 10.1 %copy-start.3 = (bf16[256,512]{1,0:T(8,128)(2,1)S(1)}, bf16[256,512]{1,0:T(8,128)(2,1)}, u32[]{:S(2)}) copy-start(bf16[256,512]{1,0:T(8,128)(2,1)} %constant.31.clone.there) | copy-start | bytes 786436
  9.8 10.1 %copy-start.4 = (bf16[512,128]{1,0:T(8,128)(2,1)S(1)}, bf16[512,128]{1,0:T(8,128)(2,1)}, u32[]{:S(2)}) copy-start(bf16[512,128]{1,0:T(8,128)(2,1)} %constant.32.clone.back) | copy-start | bytes 393220
  9.8 10.1 %copy-start.6 = (f32[2,8,256]{2,1,0:T(8,128)S(1)}, f32[2,8,256]{2,1,0:T(8,128)}, u32[]{:S(2)}) copy-start(f32[2,8,256]{2,1,0:T(8,128)} %constant.33.clone.turns) | copy-start | bytes 49156
  18.4 1.4 %collective-permute-start = (f32[16,24,128]{2,1,0:T(8,128)S(1)}, f32[16,24,128]{2,1,0:T(8,128)S(1)}, u32[]{:S(2)}, u32[]{:S(2)}) collective-permute-start(f32[16,24,128]{2,1,0:T(8,128)S(1)} %all-to-all-done.gathered), channel_id=1, source_target_pairs={{0,1},{1,0},{2,3},{3,2},{4,5},{5,4},{6,7},{7,6},{8,9},{9,8},{10,11... | collective-permute-start | bytes 589832 | tf_op jit(solution)/shard_map/ppermute | solution.py:890
  19.9 7.4 %copy-start.9 = (f32[64,128]{1,0:T(8,128)S(1)}, f32[64,128]{1,0:T(8,128)}, u32[]{:S(2)}) copy-start(f32[64,128]{1,0:T(8,128)} %get-tuple-element.45.y_faces_from) | copy-start | bytes 98308
  23.2 13.1 %all-to-all-start.1 = ((f32[32,16,128]{2,1,0:T(8,128)}), f32[32,16,128]{2,1,0:T(8,128)S(1)}, u32[]{:S(2)}, u32[]{:S(2)}) async-start(f32[32,16,128]{2,1,0:T(8,128)} %lines.1), calls=%async_computation.1 | async-start | bytes 524288 | tf_op jit(solution)/shard_map/all_to_all | solution.py:901
  25.8 12.4 %collective-permute-start.1 = (f32[4,64,128]{2,1,0:T(8,128)S(1)}, f32[4,64,128]{2,1,0:T(8,128)S(1)}, u32[]{:S(2)}, u32[]{:S(2)}) collective-permute-start(f32[4,64,128]{2,1,0:T(8,128)S(1)} %get-tuple-element.32), channel_id=1, source_target_pairs={{0,3},{1,0},{2,1},{3,2},{4,7},{5,4},{6,5},{7,6},{8,11},{9,8},{10,9... | collective-permute-start | bytes 393224 | tf_op jit(solution)/shard_map/ppermute | solution.py:423
  27.2 10.9 %collective-permute-start.2 = (f32[4,64,128]{2,1,0:T(8,128)S(1)}, f32[4,64,128]{2,1,0:T(8,128)S(1)}, u32[]{:S(2)}, u32[]{:S(2)}) collective-permute-start(f32[4,64,128]{2,1,0:T(8,128)S(1)} %get-tuple-element.33), channel_id=1, source_target_pairs={{0,1},{1,2},{2,3},{3,0},{4,5},{5,6},{6,7},{7,4},{8,9},{9,10},{10,1... | collective-permute-start | bytes 393224 | tf_op jit(solution)/shard_map/ppermute | solution.py:423
  27.3 10.9 %collective-permute-start.3 = (f32[64,128]{1,0:T(8,128)S(1)}, f32[64,128]{1,0:T(8,128)S(1)}, u32[]{:S(2)}, u32[]{:S(2)}) collective-permute-start(f32[64,128]{1,0:T(8,128)S(1)} %copy-done.9), channel_id=1, source_target_pairs={{0,4},{4,0},{1,5},{5,1},{2,6},{6,2},{3,7},{7,3},{8,12},{12,8},{9,1... | collective-permute-start | bytes 98312 | tf_op jit(solution)/shard_map/ppermute | solution.py:423
  28.7 9.5 %collective-permute-start.4 = (f32[4,16,128]{2,1,0:T(8,128)S(1)}, f32[4,16,128]{2,1,0:T(8,128)S(1)}, u32[]{:S(2)}, u32[]{:S(2)}) collective-permute-start(f32[4,16,128]{2,1,0:T(8,128)S(1)} %get-tuple-element.37), channel_id=1, source_target_pairs={{0,24},{8,0},{16,8},{24,16},{1,25},{9,1},{17,9},{25,17},{2,26},{10... | collective-permute-start | bytes 98312 | tf_op jit(solution)/shard_map/ppermute | solution.py:423
  32.2 6.0 %collective-permute-start.5 = (f32[4,16,128]{2,1,0:T(8,128)S(1)}, f32[4,16,128]{2,1,0:T(8,128)S(1)}, u32[]{:S(2)}, u32[]{:S(2)}) collective-permute-start(f32[4,16,128]{2,1,0:T(8,128)S(1)} %get-tuple-element.38), channel_id=1, source_target_pairs={{0,8},{8,16},{16,24},{24,0},{1,9},{9,17},{17,25},{25,1},{2,10},{10... | collective-permute-start | bytes 98312 | tf_op jit(solution)/shard_map/ppermute | solution.py:423
  32.2 4.1 %copy-start.1 = (bf16[512,256]{1,0:T(8,128)(2,1)S(1)}, bf16[512,256]{1,0:T(8,128)(2,1)}, u32[]{:S(2)}) copy-start(bf16[512,256]{1,0:T(8,128)(2,1)} %constant.29.clone.low) | copy-start | bytes 786436
  32.2 4.1 %copy-start.2 = (bf16[512,256]{1,0:T(8,128)(2,1)S(1)}, bf16[512,256]{1,0:T(8,128)(2,1)}, u32[]{:S(2)}) copy-start(bf16[512,256]{1,0:T(8,128)(2,1)} %constant.28.clone.high) | copy-start | bytes 786436
  32.2 4.1 %copy-start.5 = (f32[2,8,256]{2,1,0:T(8,128)S(1)}, f32[2,8,256]{2,1,0:T(8,128)}, u32[]{:S(2)}) copy-start(f32[2,8,256]{2,1,0:T(8,128)} %constant.30.clone.turns) | copy-start | bytes 49156
  38.1 3.5 %copy-start.7 = (f32[4,64,128]{2,1,0:T(8,128)}, f32[4,64,128]{2,1,0:T(8,128)S(1)}, u32[]{:S(2)}) copy-start(f32[4,64,128]{2,1,0:T(8,128)S(1)} %collective-permute-done.1.z_next_from) | copy-start | bytes 393220
  38.2 3.5 %copy-start.8 = (f32[4,64,128]{2,1,0:T(8,128)}, f32[4,64,128]{2,1,0:T(8,128)S(1)}, u32[]{:S(2)}) copy-start(f32[4,64,128]{2,1,0:T(8,128)S(1)} %collective-permute-done.2.z_before_from) | copy-start | bytes 393220
  38.2 3.5 %copy-start.10 = (f32[64,128]{1,0:T(8,128)}, f32[64,128]{1,0:T(8,128)S(1)}, u32[]{:S(2)}) copy-start(f32[64,128]{1,0:T(8,128)S(1)} %collective-permute-done.3.y_next_from.y_before_from) | copy-start | bytes 98308
  38.2 3.5 %copy-start.11 = (f32[4,16,128]{2,1,0:T(8,128)}, f32[4,16,128]{2,1,0:T(8,128)S(1)}, u32[]{:S(2)}) copy-start(f32[4,16,128]{2,1,0:T(8,128)S(1)} %collective-permute-done.4.x_next_from) | copy-start | bytes 98308
  38.2 3.5 %copy-start.12 = (f32[4,16,128]{2,1,0:T(8,128)}, f32[4,16,128]{2,1,0:T(8,128)S(1)}, u32[]{:S(2)}) copy-start(f32[4,16,128]{2,1,0:T(8,128)S(1)} %collective-permute-done.5.x_before_from) | copy-start | bytes 98308
  38.2 9.4 %all-to-all-start.2 = ((f32[8,48,128]{2,1,0:T(8,128)}), f32[8,48,128]{2,1,0:T(8,128)S(1)}, u32[]{:S(2)}, u32[]{:S(2)}) async-start(f32[8,48,128]{2,1,0:T(8,128)} %rows.1), calls=%async_computation.2 | async-start | bytes 393216 | tf_op jit(solution)/shard_map/all_to_all | solution.py:930

commit v6 on v5

--- a/solution.py
+++ b/solution.py
@@ -22,6 +22,10 @@
 HBM = pl.BlockSpec(memory_space=pltpu.HBM)
 
 
+def whole_log(count):
+    return count.bit_length() - 1
+
+
 def split(values):
     high = values.astype(bf16)
     return high, (values - high.astype(f32)).astype(bf16)
@@ -38,7 +42,7 @@
     return pltpu.with_memory_space_constraint(values, pltpu.HBM)
 
 
-def call(body, name, shape, limit, microseconds, operands, in_hbm=(), scratch=(), refs=()):
+def call(body, name, shape, limit, microseconds, operands, in_hbm=(), scratch=(), refs=(), out_refs=(), aliases=()):
     shapes = shape if isinstance(shape, list) else [shape]
     moved = sum(4 * math.prod(each) for each in shapes)
     moved += sum(x.size * x.dtype.itemsize for x in operands)
@@ -52,7 +56,8 @@
             SMEM if x.shape == (1,) else HBM if i in refs else VMEM
             for i, x in enumerate(operands)
         ],
-        out_specs=[VMEM] * len(shapes),
+        out_specs=[HBM if i in out_refs else VMEM for i in range(len(shapes))],
+        input_output_aliases=dict(aliases),
         scratch_shapes=list(scratch),
         compiler_params=pltpu.CompilerParams(vmem_limit_bytes=limit * MIB),
         cost_estimate=pl.CostEstimate(
@@ -279,8 +284,8 @@
         loading, [(stiffness, s)] + [(magnetization.at[c], m.at[c]) for c in range(3)]
     )
     lane = lax.broadcasted_iota(jnp.int32, (across, LANES), 1)
-    first = jnp.zeros((across, LANES), f32)
-    last = jnp.zeros((across, LANES), f32)
+    pair = (lane + 1 & (LANES - 1)) >> 1
+    sides = jnp.zeros((across, LANES), f32)
     for field in (3, 0, 1, 2):
         loads[(field + 1) % 4].wait()
         ref = s if field == 3 else m.at[field]
@@ -290,14 +295,15 @@
         x_last[field] = ref[:, across - 1, :]
         for z in range(depth):
             column = field * depth + z
-            turned = pltpu.roll(ref[z], column, 1) if column else ref[z]
-            first = jnp.where(lane == column, turned, first)
-            last = jnp.where(lane == (column - 1) % LANES, turned, last)
-    y_faces[...] = jnp.where(lane < LANES // 2, first, pltpu.roll(last, LANES // 2 + 1, 1))
+            turned = pltpu.roll(ref[z], 2 * column, 1) if column else ref[z]
+            sides = jnp.where(pair == column, turned, sides)
+    y_faces[...] = sides
 
 
 def twice_weight(a, b):
-    return 4.0 * a * b / (a + b)
+    total = a + b
+    inverse = pl.reciprocal(total, approx=True)
+    return 4.0 * a * b * (inverse * (2.0 - total * inverse))
 
 
 def exchange_kernel(
@@ -351,29 +357,30 @@
     def inside(condition, values):
         return jnp.where(condition, values, 0.0)
 
-    half = LANES // 2
     lane = lax.broadcasted_iota(jnp.int32, (across, LANES), 1)
     row = lax.broadcasted_iota(jnp.int32, (across, LANES), 0)
     first_lane, last_lane, last_row = lane == 0, lane == LANES - 1, row == across - 1
 
-    stiff = (lane >= 3 * depth) & (lane < 4 * depth)
-
-    def y_edge(own, halo, present):
-        weight = twice_weight(
-            jnp.where(stiff, own, 1.0), jnp.where(stiff, inside(present, halo), 1.0)
-        )
-        spread = pltpu.roll(weight, LANES - 3 * depth, 1)
-        for c in (1, 2):
-            spread = jnp.where(
-                lane >= c * depth, pltpu.roll(weight, LANES - (3 - c) * depth, 1), spread
-            )
-        return spread * (own - halo)
-
     for copy in loads[:3]:
         copy.wait()
     own = y_faces[...]
-    after = y_edge(pltpu.roll(own, half, 1), y_next[...], at_y < count_y - 1)
-    before = y_edge(own, pltpu.roll(y_before[...], half, 1), at_y > 0)
+    even = (lane & 1) == 0
+    field = (lane + 1 & (LANES - 1)) >> whole_log(2 * depth)
+    halo = jnp.where(
+        even, pltpu.roll(y_before[...], 1, 1), pltpu.roll(y_next[...], LANES - 1, 1)
+    )
+    present = jnp.where(even, at_y, count_y - 1 - at_y) > 0
+    weight = twice_weight(
+        jnp.where(field == 3, own, 1.0),
+        jnp.where(field == 3, jnp.where(present, halo, 0.0), 1.0),
+    )
+    spread = pltpu.roll(weight, LANES - 6 * depth, 1)
+    for c in (1, 2):
+        spread = jnp.where(
+            field == c, pltpu.roll(weight, LANES - (3 - c) * 2 * depth, 1), spread
+        )
+    sides = spread * (own - halo)
+    outer = first_lane | last_lane
 
     for copy in loads[3:6]:
         copy.wait()
@@ -402,12 +409,8 @@
             flux_y = weight_y * (values - pltpu.roll(values, LANES - 1, 1))
             total = (up - below[c]) + (flux_x - pltpu.roll(flux_x, 1, 0))
             total = total + (flux_y - pltpu.roll(flux_y, 1, 1))
-            side = jnp.where(
-                first_lane,
-                before[:, column : column + 1],
-                jnp.where(last_lane, after[:, column : column + 1], 0.0),
-            )
-            out[c, z] = total + side
+            both = pltpu.roll(sides, LANES - 2 * column, 1) if column else sides
+            out[c, z] = jnp.where(outer, total + both, total)
             below[c] = up
     for edge_row, halo, present in (
         (across - 1, x_next, at_x < count_x - 1),
@@ -474,10 +477,6 @@
     )
 
 
-def whole_log(count):
-    return count.bit_length() - 1
-
-
 def cos_sin(steps, size):
     quarter = steps >> whole_log(size // 4)
     angle = ((steps & (size // 4 - 1)) - size // 8).astype(f32) * (2.0 * math.pi / size)
@@ -495,16 +494,6 @@
     return jnp.where(back, -real, real), jnp.where(back, -imag, imag)
 
 
-def stacked_product(real, imag, tables, sign):
-    if sign < 0:
-        upper = jnp.concatenate([real, imag], axis=1)
-        lower = jnp.concatenate([imag, -real], axis=1)
-    else:
-        upper = jnp.concatenate([real, -imag], axis=1)
-        lower = jnp.concatenate([imag, real], axis=1)
-    return dot3(jnp.concatenate([upper, lower], axis=0), tables)
-
-
 def add(a, b):
     return a[0] + b[0], a[1] + b[1]
 
@@ -536,21 +525,14 @@
 
 def spread_tables(extent, size):
     step = size // INNER
-    count = extent // step
-    angle = np.outer(np.arange(count), np.arange(INNER)) * (2.0 * math.pi / INNER)
+    angle = np.outer(np.arange(INNER), np.arange(extent // step)) * (2.0 * math.pi / INNER)
     cosine, sine = np.cos(angle), np.sin(angle)
-
-    def parts(table):
-        table = table.astype(np.float32)
-        high = table.astype(ml_dtypes.bfloat16)
-        return high, (table - high.astype(np.float32)).astype(ml_dtypes.bfloat16)
-
-    high, low = parts(np.block([[cosine, -sine], [sine, cosine]]))
-    there = np.concatenate([high, high, low, np.zeros_like(low)], axis=0)
-    high, low = parts(np.block([[cosine.T, sine.T], [-sine.T, cosine.T]]))
-    back = np.concatenate([high, low], axis=1)
+    table = np.block([[cosine, sine], [-sine, cosine]]).astype(np.float32)
+    high = table.astype(ml_dtypes.bfloat16)
+    low = (table - high.astype(np.float32)).astype(ml_dtypes.bfloat16)
     angle = np.outer(np.arange(step), np.arange(INNER)) * (2.0 * math.pi / size)
-    return there, back, np.stack([np.cos(angle), np.sin(angle)]).astype(np.float32)
+    turns = np.stack([np.cos(angle), np.sin(angle)]).astype(np.float32)
+    return np.concatenate([high, low], axis=1), turns
 
 
 def regrouping(extent, step, transposed):
@@ -561,11 +543,40 @@
     return jnp.where(moved == place, 1.0, 0.0).astype(bf16)
 
 
-def product(left, right):
-    return lax.dot_general(left, right, (((1,), (0,)), ((), ())), preferred_element_type=f32)
-
-
-def there_and_back(real, imag, columns_of, there, back, turns):
+def product(left, right, contracted=0):
+    return lax.dot_general(
+        left, right, (((1,), (contracted,)), ((), ())), preferred_element_type=f32
+    )
+
+
+def regrouped(values, step, transposed):
+    high, low = split(values)
+    rest = (values - high.astype(f32) - low.astype(f32)).astype(bf16)
+    order = regrouping(values.shape[1], step, transposed)
+    return product(high, order) + product(low, order) + product(rest, order)
+
+
+def beside(pieces, count):
+    per = LANES // count
+    lane = lax.broadcasted_iota(jnp.int32, pieces[0].shape, 1)
+    columns = []
+    for start in range(0, len(pieces), per):
+        column = pieces[start]
+        for i in range(1, per):
+            piece = pltpu.roll(pieces[start + i], i * count, 1)
+            column = jnp.where(lane < i * count, column, piece)
+        columns.append(column)
+    return jnp.concatenate(columns, axis=1)
+
+
+def back_product(turned, back):
+    high, low = split(turned)
+    both = product(jnp.concatenate([high, low], axis=0), back)
+    middle = both.shape[0] // 2
+    return both[:middle] + pltpu.roll(both[:middle], LANES // 2, 1) + both[middle:]
+
+
+def there_and_back(real, imag, columns_of, back, turns):
     rows, extent = real.shape
     step = turns.shape[1]
     count = extent // step
@@ -576,15 +587,20 @@
     lines = []
     for v in range(step):
         column = v // per * LANES
-        first = None
-        for k in range(4):
-            piece = moved[k * rows : (k + 1) * rows, column : column + LANES]
-            shift = (k - v) * count % LANES
-            piece = pltpu.roll(piece, shift, 1) if shift else piece
-            first = piece if k == 0 else jnp.where(lane < k * count, first, piece)
-        second = jnp.where(lane < 2 * count, first, 0.0)
+
+        def piece(k, to):
+            block = moved[k * rows : (k + 1) * rows, column : column + LANES]
+            shift = (to - v) * count % LANES
+            return pltpu.roll(block, shift, 1) if shift else block
+
+        first = jnp.where(lane < count, piece(0, 0), piece(1, 1))
+        first = jnp.where(lane < 2 * count, first, pltpu.roll(first, 2 * count, 1))
+        second = jnp.where(lane < count, piece(2, 0), piece(3, 1))
+        second = jnp.where(lane < 2 * count, second, 0.0)
         lines.append(jnp.concatenate([first, second], axis=1))
-    waves = product(jnp.concatenate(lines, axis=0).astype(bf16), there)
+    waves = product(
+        jnp.concatenate(lines, axis=0).astype(bf16), jnp.concatenate([back, back], axis=1), 1
+    )
 
     results = []
     for start in range(0, rows, 16):
@@ -619,23 +635,19 @@
                     (a, b), (cosine, sine) = weighted[v], turn[v]
                     weighted[v] = (a * cosine - b * sine, a * sine + b * cosine)
                 halves[c].append(weighted)
-        parts = ([], [])
-        for v in range(step):
-            for c in range(2):
-                pieces = [
-                    split(halves[c][half][v][k])
-                    for k in range(2)
-                    for half in range(INNER // LANES)
-                ]
-                for k in range(2):
-                    parts[k].append(jnp.concatenate([piece[k] for piece in pieces], axis=1))
-        both = product(jnp.concatenate(parts[0] + parts[1], axis=0), back)
-        middle = both.shape[0] // 2
-        results.append(both[:middle] + pltpu.roll(both[:middle], LANES // 2, 1) + both[middle:])
+        turned = [
+            jnp.concatenate(
+                [halves[c][half][v][k] for k in range(2) for half in range(INNER // LANES)],
+                axis=1,
+            )
+            for v in range(step)
+            for c in range(2)
+        ]
+        results.append(back_product(jnp.concatenate(turned, axis=0), back))
     return results
 
 
-def lines_kernel(counts, here, gathered, swapped, there, back, turns, kernel, out):
+def lines_kernel(counts, here, gathered, swapped, back, turns, kernel, out):
     count_x, count_y, count_z = counts
     group = count_y * count_z
     top_rows = LANES // group
@@ -681,9 +693,7 @@
     def columns_of(b):
         return kernel.at[:, :, :, b * INNER : (b + 1) * INNER]
 
-    results = there_and_back(
-        lines[:kys], lines[kys:], columns_of, there[...], back[...], turns
-    )
+    results = there_and_back(lines[:kys], lines[kys:], columns_of, back[...], turns)
     count = count_x * group
     for v in range(turns.shape[1]):
         block = jnp.concatenate(
@@ -695,10 +705,10 @@
 
 
 def side_kernel_body(
-    counts, here, gathered, swapped, there, back, turns, kernel_from, out, kernel, loading
+    counts, here, gathered, swapped, back, turns, kernel_from, out, kernel, loading
 ):
     count_x, count_y, count_z = counts
-    depth_block = out.shape[1] // 2
+    depth_block = (out.shape[1] - 2 * TILE) // 2
     top_rows = gathered.shape[1] - TILE
     kzs, length = kernel_from.shape[2:]
     loads = begin(
@@ -741,34 +751,15 @@
             waiting.pop(b).wait()
         return kernel.at[b]
 
-    result = there_and_back(
-        lines[:kzs], lines[kzs:], columns_of, there[...], back[...], turns
-    )[0]
+    result = there_and_back(lines[:kzs], lines[kzs:], columns_of, back[...], turns)[0]
     step = turns.shape[1]
-    extent = count_y * LANES
-    count = extent // step
-    per = LANES // count
-    lane = lax.broadcasted_iota(jnp.int32, (kzs, LANES), 1)
+    count = count_y * LANES // step
     images = []
     for c in range(2):
-        for k in range(2):
-            columns = []
-            for first in range(0, step, per):
-                column = None
-                for v in range(first, first + per):
-                    piece = result[(2 * v + c) * 16 : (2 * v + c + 1) * 16]
-                    shift = (v - first - k) * count % LANES
-                    piece = pltpu.roll(piece, shift, 1) if shift else piece
-                    column = (
-                        piece
-                        if v == first
-                        else jnp.where(lane < (v - first) * count, column, piece)
-                    )
-                columns.append(column)
-            images.append(jnp.concatenate(columns, axis=1))
-    high, low = split(jnp.concatenate(images, axis=0))
-    order = regrouping(extent, step, True)
-    images = product(high, order) + product(low, order)
+        pieces = [result[(2 * v + c) * 16 : (2 * v + c + 1) * 16] for v in range(step)]
+        images.append(beside(pieces, count))
+        images.append(beside([pltpu.roll(piece, LANES - count, 1) for piece in pieces], count))
+    images = regrouped(jnp.concatenate(images, axis=0), step, True)
 
     rows = depth_block * count_z
     z = lax.broadcasted_iota(jnp.int32, (rows, 2 * kzs), 0)
@@ -779,62 +770,99 @@
         image = dot3(table, split(images[2 * kzs * c : 2 * kzs * (c + 1)]))
         for y in range(count_y):
             for z in range(count_z):
-                out[y * count_z + z, c * depth_block : (c + 1) * depth_block, :] = image[
+                start = 2 * TILE + c * depth_block
+                out[y * count_z + z, start : start + depth_block, :] = image[
                     z * depth_block : (z + 1) * depth_block, y * LANES : (y + 1) * LANES
                 ]
-
-
-def rows_kernel(counts, arrived, side, high, low, turns, out, loading):
+    out[:, 0 : 2 * TILE, :] = jnp.zeros((out.shape[0], 2 * TILE, LANES), f32)
+
+
+def rows_kernel(counts, arrived, side, back, turns, out, result, sending):
+    del side
     count_y, count_z = counts[1:]
-    loads = begin(loading, [(side, out.at[:, 2 * TILE :, :])])
-    per_turn = arrived.shape[0] // turns.shape[1]
+    step = turns.shape[1]
+    size = step * INNER
+    per_turn = arrived.shape[0] // step
     half = LANES // 2
     lane = lax.broadcasted_iota(jnp.int32, (2 * TILE, LANES), 1)
-    parts = [[], []]
-    for b in range(turns.shape[1]):
-        spectra = ([], [])
-        for g in range(b * per_turn, (b + 1) * per_turn, 2):
-            first, second = arrived[g], arrived[g + 1]
-            spectra[0].append(jnp.where(lane < half, first, pltpu.roll(second, half, 1)))
-            spectra[1].append(jnp.where(lane < half, pltpu.roll(first, half, 1), second))
-        spectra = [jnp.concatenate(pieces, axis=1) for pieces in spectra]
-        for k in range(2):
-            parts[k] += [spectrum[k * TILE : (k + 1) * TILE] for spectrum in spectra]
-    real, imag = parts
-    back = stacked_product(
-        jnp.concatenate(real, axis=0), jnp.concatenate(imag, axis=0), (high[...], low[...]), 1
-    )
-    middle = back.shape[0] // 2
-    size = turns.shape[1] * INNER
-    total = None
-    for b in range(turns.shape[1]):
-        part = slice(b * 2 * TILE, (b + 1) * 2 * TILE)
-        term = back[:middle][part] * turns[0, b : b + 1, :]
-        term = term - back[middle:][part] * turns[1, b : b + 1, :]
-        total = term if b == 0 else total + term
+    halves = []
+    for pair in range(0, per_turn, 2):
+        z = []
+        for b in range(step):
+            first, second = arrived[b * per_turn + pair], arrived[b * per_turn + pair + 1]
+            spectra = (
+                jnp.where(lane < half, first, pltpu.roll(second, half, 1)),
+                jnp.where(lane < half, pltpu.roll(first, half, 1), second),
+            )
+            z.append(
+                tuple(
+                    jnp.concatenate(
+                        [spectrum[k * TILE : (k + 1) * TILE] for spectrum in spectra], axis=0
+                    )
+                    for k in range(2)
+                )
+            )
+        z = eight_points(z, 1)
+        lanes = slice(pair // 2 * LANES, (pair // 2 + 1) * LANES)
+        for v in range(1, step):
+            cosine, sine = turns[0, v : v + 1, lanes], turns[1, v : v + 1, lanes]
+            a, b = z[v]
+            z[v] = (a * cosine - b * sine, a * sine + b * cosine)
+        halves.append(z)
+    turned = [
+        jnp.concatenate([z[v][k] for k in range(2) for z in halves], axis=1) for v in range(step)
+    ]
+    lines = back_product(jnp.concatenate(turned, axis=0), back[...])
+    pieces = [lines[v * 2 * TILE : (v + 1) * 2 * TILE] for v in range(step)]
+    total = regrouped(beside(pieces, count_y * LANES // step), step, True)
     total = total * (1.0 / (size * size))
     for y in range(count_y):
-        for z in range(count_z):
-            out[y * count_z + z, 0 : 2 * TILE, :] = total[:, y * LANES : (y + 1) * LANES]
-    loads[0].wait()
-
-
-def sum_kernel(exchange_grad, arrived, out):
+        result[y] = total[:, y * LANES : (y + 1) * LANES]
+    sends = begin(
+        sending,
+        [
+            (result.at[y], out.at[y * count_z + z, 0 : 2 * TILE, :])
+            for y in range(count_y)
+            for z in range(count_z)
+        ],
+    )
+    for copy in sends:
+        copy.wait()
+
+
+def sum_kernel(exchange_grad, arrived, out, result, sending):
     depth = exchange_grad.shape[1]
     group = arrived.shape[0]
-    side = [None, None]
-    top = [None, None]
-    for c in range(2):
+    sends = []
+
+    def send(c):
+        sends.append(pltpu.make_async_copy(result.at[c], out.at[c], sending.at[c]))
+        sends[-1].start()
+
+    def top(c):
+        return arrived[:, c * TILE : (c + 1) * TILE, :].reshape(group * TILE, LANES)
+
+    def side(c):
         rows = slice(2 * TILE + c * depth, 2 * TILE + (c + 1) * depth)
         total = arrived[0, rows, :]
         for p in range(1, group):
             total = total + arrived[p, rows, :]
-        side[c] = total
-        top[c] = arrived[:, c * TILE : (c + 1) * TILE, :].reshape(group * TILE, LANES)
+        return total
+
+    image = top(0)
     for z in range(depth):
-        out[0, z] = exchange_grad[0, z] + top[0]
-        out[1, z] = exchange_grad[1, z] + top[1] + side[0][z : z + 1]
-        out[2, z] = exchange_grad[2, z] + side[1][z : z + 1]
+        result[0, z] = exchange_grad[0, z] + image
+    send(0)
+    column = side(1)
+    for z in range(depth):
+        result[2, z] = exchange_grad[2, z] + column[z : z + 1]
+    send(2)
+    image, column = top(1), side(0)
+    for z in range(depth):
+        result[1, z] = exchange_grad[1, z] + image + column[z : z + 1]
+    send(1)
+    for copy in sends:
+        copy.wait()
 
 
 def residual_blocks(residual_top, residual_side, devices, share):
@@ -874,9 +902,7 @@
     plane_index = here[1] * count_z + here[2]
     index = (here[0] * group + plane_index).reshape(1)
     plane_index = plane_index.reshape(1)
-    (high, low), _, turns = transform_tables(extent, size)
-    high, low, turns = jnp.asarray(high), jnp.asarray(low), jnp.asarray(turns)
-    there, back, spread_turns = (jnp.asarray(table) for table in spread_tables(extent, size))
+    back, turns = (jnp.asarray(table) for table in spread_tables(extent, size))
 
     parities = [range(parity, devices, 2) for parity in range(2)]
     sent = residual_blocks(residual_top, residual_side, devices // 2, depth_block // count_x)
@@ -896,7 +922,7 @@
         (devices, 2 * TILE, LANES),
         16,
         4.0,
-        (index, gathered, swapped, there, back, spread_turns, top_kernel),
+        (index, gathered, swapped, back, turns, top_kernel),
     )
     arrived = lax.all_to_all(lines, ALL, 0, 0, tiled=True)
     lines, x_first, x_last = lax.optimization_barrier((lines, x_first, x_last))
@@ -904,12 +930,12 @@
     side = call(
         functools.partial(side_kernel_body, counts),
         "side",
-        (group, 2 * depth_block, LANES),
+        (group, 2 * TILE + 2 * depth_block, LANES),
         8,
         2.8,
-        (plane_index, gathered, swapped, there, back, spread_turns, from_hbm(side_kernel)),
+        (plane_index, gathered, swapped, back, turns, from_hbm(side_kernel)),
         in_hbm=(0,),
-        refs=(6,),
+        refs=(5,),
         scratch=[
             pltpu.VMEM((size // INNER, 2, 2, kzs, INNER), f32),
             pltpu.SemaphoreType.DMA((size // INNER,)),
@@ -922,14 +948,29 @@
         (group, 2 * TILE + 2 * depth_block, LANES),
         8,
         1.4,
-        (arrived, from_hbm(side), high, low, turns),
+        (arrived, from_hbm(side), back, turns),
+        in_hbm=(0,),
         refs=(1,),
-        scratch=[pltpu.SemaphoreType.DMA((1,))],
+        scratch=[
+            pltpu.VMEM((count_y, 2 * TILE, LANES), f32),
+            pltpu.SemaphoreType.DMA((group,)),
+        ],
+        out_refs=(0,),
+        aliases={1: 0},
     )
     rows, zy, x = lax.optimization_barrier((rows, zy, x))
     arrived = lax.all_to_all(rows, ("gy", "gz"), 0, 0, tiled=True)
     exchange_grad = exchange_of(counts, index, magnetization, stiffness, zy, x)
-    return call(sum_kernel, "gradient", magnetization.shape, 16, 1.2, (exchange_grad, arrived))
+    return call(
+        sum_kernel,
+        "gradient",
+        magnetization.shape,
+        16,
+        1.2,
+        (exchange_grad, arrived),
+        out_refs=(0,),
+        scratch=[pltpu.VMEM(magnetization.shape, f32), pltpu.SemaphoreType.DMA((3,))],
+    )
 
 
 def fits(counts, stiffness, residual_top, residual_side, top_kernel, side_kernel):

time: 49.4 us -> 48.7 us (0.986)
  Pallas kernels: 19.4 us -> 18 us
  waiting for transfers between devices: 8.45 us -> 9.28 us
    pallas_call x7, Pallas kernels: 19.4 us -> 18 us  [call(): pl.pallas_call(body, out_shape=[pltpu.HBM(each, f32) if i in in_hbm else...]
    all_to_all x1, waiting for transfers between devices: 0.01 us -> 0.81 us  [fast_on_device(): arrived = lax.all_to_all(rows, ('gy', 'gz'), 0, 0, tiled=True)]
  transfers between devices with their start and end apart: 9 -> 9, of which waited for: 3 -> 5; matrix products, arithmetic and copies ran while one was open for 0% -> 0% of each run, Pallas kernels for 27% -> 25%
where the time goes in v6:
time: 48.7 us; the launch traced here: 48.2 us
  starting transfers between devices  20.7 us (43%)
  Pallas kernels  18 us (37%)
  waiting for transfers between devices  9.28 us (19%)
    pallas_call x7, Pallas kernels, call(): pl.pallas_call(body, out_shape=[pltpu.HBM(each, f32) if i in in_hbm else...  18 us
    all_to_all x1, starting transfers between devices, fast_on_device(): lax.all_to_all(sent, ALL, 0, 0, tiled=True, axis_index_groups=[list(each)...  8.31 us
    ppermute x5, starting transfers between devices, ring(): lax.ppermute(block, axis, [(i, (i + distance) % count) for i in range(cou...  6.42 us
    all_to_all x1, waiting for transfers between devices, fast_on_device(): lax.all_to_all(sent, ALL, 0, 0, tiled=True, axis_index_groups=[list(each)...  5.94 us
    all_to_all x1, starting transfers between devices, fast_on_device(): arrived = lax.all_to_all(rows, ('gy', 'gz'), 0, 0, tiled=True)  3.39 us
    all_to_all x1, starting transfers between devices, fast_on_device(): arrived = lax.all_to_all(lines, ALL, 0, 0, tiled=True)  2.59 us
    ppermute x1, waiting for transfers between devices, fast_on_device(): swapped = lax.ppermute(gathered, 'gz', [(i, i ^ 1) for i in range(count_z)])  1.44 us
  transfers between devices with their start and end apart: 9, of which 5 were waited for; matrix products, arithmetic and copies ran while one was open for 0% of the time, Pallas kernels for 25%

profile of v6, /device:TPU:0, one launch (start us, length us, event | category | flops | bytes accessed | tf_op | source)
XLA Modules:
  0.0 48.2 jit_solution(6937892093651299054)
XLA Ops:
  0.0 1.5 %pack.1 = f32[16,24,128]{2,1,0:T(8,128)} custom-call(s32[1]{0:T(128)} %bitcast.1.at_x, f32[32,64]{1,0:T(8,128)} %bitcast.5, f32[16,128]{1,0:T(8,128)} %bitcast.6), custom_call_target="tpu_custom_call" | custom-call | flops 800000000 | bytes 212996 | tf_op jit(solution)/shard_map/pack/pallas_call | solution.py:49
  1.5 8.3 %all-to-all-start = ((f32[16,24,128]{2,1,0:T(8,128)}), f32[16,24,128]{2,1,0:T(8,128)S(1)}, u32[]{:S(2)}, u32[]{:S(2)}) async-start(f32[16,24,128]{2,1,0:T(8,128)} %pack.1), calls=%async_computation | async-start | bytes 393216 | tf_op jit(solution)/shard_map/all_to_all | solution.py:909
  9.8 0.0 copy-start
  9.8 0.0 copy-start.1
  9.8 0.0 copy-start.2
  9.8 2.7 %faces.1 = (f32[4,64,128]{2,1,0:T(8,128)S(1)}, f32[4,64,128]{2,1,0:T(8,128)S(1)}, f32[4,16,128]{2,1,0:T(8,128)S(1)}, f32[4,16,128]{2,1,0:T(8,128)S(1)}, f32[64,128]{1,0:T(8,128)}) custom-call(f32[3,16,64,128]{3,2,1,0:T(8,128)} %magnetization_from.1, f32[16,64,128]{2,1,0:T(8,128)} %stiffness_from.1), custom_call_target="tpu_custom_call" | custom-call | flops 2000000000 | bytes 2457600 | tf_op jit(solution)/shard_map/faces/pallas_call | solution.py:49
  12.5 5.9 %all-to-all-done.gathered = f32[16,24,128]{2,1,0:T(8,128)S(1)} async-done(((f32[16,24,128]{2,1,0:T(8,128)}), f32[16,24,128]{2,1,0:T(8,128)S(1)}, u32[]{:S(2)}, u32[]{:S(2)}) %all-to-all-start) | async-done | bytes 196640 | tf_op jit(solution)/shard_map/all_to_all | solution.py:909
  18.4 0.0 collective-permute-start
  18.4 1.4 %collective-permute-done.swapped = f32[16,24,128]{2,1,0:T(8,128)S(1)} collective-permute-done((f32[16,24,128]{2,1,0:T(8,128)S(1)}, f32[16,24,128]{2,1,0:T(8,128)S(1)}, u32[]{:S(2)}, u32[]{:S(2)}) %collective-permute-start) | collective-permute-done | bytes 196640 | tf_op jit(solution)/shard_map/ppermute | solution.py:916
  19.9 0.0 copy-done
  19.9 3.4 %lines.1 = f32[32,16,128]{2,1,0:T(8,128)} custom-call(s32[1]{0:T(128)} %bitcast.here, f32[16,24,128]{2,1,0:T(8,128)S(1)} %all-to-all-done.gathered, f32[16,24,128]{2,1,0:T(8,128)S(1)} %collective-permute-done.swapped, bf16[512,128]{1,0:T(8,128)(2,1)S(1)} %copy-done.1, f32[2,8,256]{2,1,0:T(8,128)S(1)} %copy-done.2, f32[2,2,64,2048]{3,2,1,0:T(8,128)S(1)} %copy-done), custom_call_target="tpu_custom_call" | custom-call | flops 4000000000 | bytes 2899972 | tf_op jit(solution)/shard_map/lines/pallas_call | solution.py:49
  23.3 2.6 %all-to-all-start.1 = ((f32[32,16,128]{2,1,0:T(8,128)}), f32[32,16,128]{2,1,0:T(8,128)S(1)}, u32[]{:S(2)}, u32[]{:S(2)}) async-start(f32[32,16,128]{2,1,0:T(8,128)} %lines.1), calls=%async_computation.1 | async-start | bytes 524288 | tf_op jit(solution)/shard_map/all_to_all | solution.py:927
  25.9 1.5 %collective-permute-start.1 = (f32[4,64,128]{2,1,0:T(8,128)S(1)}, f32[4,64,128]{2,1,0:T(8,128)S(1)}, u32[]{:S(2)}, u32[]{:S(2)}) collective-permute-start(f32[4,64,128]{2,1,0:T(8,128)S(1)} %get-tuple-element.32), channel_id=1, source_target_pairs={{0,3},{1,0},{2,1},{3,2},{4,7},{5,4},{6,5},{7,6},{8,11},{9,8},{10,9... | collective-permute-start | bytes 393224 | tf_op jit(solution)/shard_map/ppermute | solution.py:426
  27.4 0.0 collective-permute-start.2
  27.4 1.5 %collective-permute-start.3 = (f32[64,128]{1,0:T(8,128)S(1)}, f32[64,128]{1,0:T(8,128)S(1)}, u32[]{:S(2)}, u32[]{:S(2)}) collective-permute-start(f32[64,128]{1,0:T(8,128)S(1)} %copy-done.5), channel_id=1, source_target_pairs={{0,4},{4,0},{1,5},{5,1},{2,6},{6,2},{3,7},{7,3},{8,12},{12,8},{9,1... | collective-permute-start | bytes 98312 | tf_op jit(solution)/shard_map/ppermute | solution.py:426
  28.8 3.5 %collective-permute-start.4 = (f32[4,16,128]{2,1,0:T(8,128)S(1)}, f32[4,16,128]{2,1,0:T(8,128)S(1)}, u32[]{:S(2)}, u32[]{:S(2)}) collective-permute-start(f32[4,16,128]{2,1,0:T(8,128)S(1)} %get-tuple-element.37), channel_id=1, source_target_pairs={{0,24},{8,0},{16,8},{24,16},{1,25},{9,1},{17,9},{25,17},{2,26},{10... | collective-permute-start | bytes 98312 | tf_op jit(solution)/shard_map/ppermute | solution.py:426
  32.3 0.0 collective-permute-start.5
  32.3 3.2 %side.1 = f32[8,48,128]{2,1,0:T(8,128)} custom-call(s32[1]{0:T(128)} %bitcast.4.here, f32[16,24,128]{2,1,0:T(8,128)S(1)} %all-to-all-done.gathered, f32[16,24,128]{2,1,0:T(8,128)S(1)} %collective-permute-done.swapped, bf16[512,128]{1,0:T(8,128)(2,1)S(1)} %copy-done.1, f32[2,8,256]{2,1,0:T(8,128)S(1)} %copy-done.2, f32[2,2,16,2048]{3,2,1,0:T(8,128)} %kernel_from.1), custom_call_target="tpu_custom_call" | custom-call | flops 2800000000 | bytes 1261572 | tf_op jit(solution)/shard_map/side/pallas_call | solution.py:49
  35.5 0.9 %all-to-all-done.1.arrived = f32[32,16,128]{2,1,0:T(8,128)S(1)} async-done(((f32[32,16,128]{2,1,0:T(8,128)}), f32[32,16,128]{2,1,0:T(8,128)S(1)}, u32[]{:S(2)}, u32[]{:S(2)}) %all-to-all-start.1) | async-done | bytes 262176 | tf_op jit(solution)/shard_map/all_to_all | solution.py:927
  36.4 1.4 %rows.1 = f32[8,48,128]{2,1,0:T(8,128)} custom-call(f32[32,16,128]{2,1,0:T(8,128)S(1)} %all-to-all-done.1.arrived, f32[8,48,128]{2,1,0:T(8,128)} %side.1, bf16[512,128]{1,0:T(8,128)(2,1)S(1)} %copy-done.1, f32[2,8,256]{2,1,0:T(8,128)S(1)} %copy-done.2), custom_call_target="tpu_custom_call", output_to_operand_aliasing={{}: (1, {})} | custom-call | flops 1400000000 | bytes 802816 | tf_op jit(solution)/shard_map/rows/pallas_call | solution.py:49
  37.8 0.0 collective-permute-done.1.z_next_from
  37.8 0.0 copy-start.3
  37.8 0.0 collective-permute-done.2.z_before_from
  37.9 0.0 collective-permute-done.3.y_next_from.y_before_from
  37.9 0.0 copy-start.6
  37.9 0.0 collective-permute-done.4.x_next_from
  37.9 0.1 collective-permute-done.5.x_before_from
  38.0 3.4 %all-to-all-start.2 = ((f32[8,48,128]{2,1,0:T(8,128)}), f32[8,48,128]{2,1,0:T(8,128)S(1)}, u32[]{:S(2)}, u32[]{:S(2)}) async-start(f32[8,48,128]{2,1,0:T(8,128)} %rows.1), calls=%async_computation.2 | async-start | bytes 393216 | tf_op jit(solution)/shard_map/all_to_all | solution.py:962
  41.4 0.0 copy-done.3
  41.5 4.7 %exchange.1.exchange_grad = f32[3,16,64,128]{3,2,1,0:T(8,128)S(1)} custom-call(s32[1]{0:T(128)} %bitcast.here, f32[3,16,64,128]{3,2,1,0:T(8,128)} %magnetization_from.1, f32[16,64,128]{2,1,0:T(8,128)} %stiffness_from.1, f32[4,64,128]{2,1,0:T(8,128)} %copy-done.3, f32[4,64,128]{2,1,0:T(8,128)} %copy-done.4, f32[4,16,128]{2,1,0:T(8,128)} %copy-done.7, ...), custom_call_target="tpu_custom_call" | custom-call | flops 5000000000 | bytes 4096004 | tf_op jit(solution)/shard_map/exchange/pallas_call | solution.py:49
  46.2 0.8 %all-to-all-done.2.arrived = f32[8,48,128]{2,1,0:T(8,128)S(1)} async-done(((f32[8,48,128]{2,1,0:T(8,128)}), f32[8,48,128]{2,1,0:T(8,128)S(1)}, u32[]{:S(2)}, u32[]{:S(2)}) %all-to-all-start.2) | async-done | bytes 196640 | tf_op jit(solution)/shard_map/all_to_all | solution.py:962
  47.0 1.2 %gradient.1 = f32[3,16,64,128]{3,2,1,0:T(8,128)} custom-call(f32[3,16,64,128]{3,2,1,0:T(8,128)S(1)} %exchange.1.exchange_grad, f32[8,48,128]{2,1,0:T(8,128)S(1)} %all-to-all-done.2.arrived), custom_call_target="tpu_custom_call" | custom-call | flops 1200000000 | bytes 3342336 | tf_op jit(solution)/shard_map/gradient/pallas_call | solution.py:49
  (11 shorter events, 0.0 us)
Async XLA Ops:
  1.5 17.0 %all-to-all-start = ((f32[16,24,128]{2,1,0:T(8,128)}), f32[16,24,128]{2,1,0:T(8,128)S(1)}, u32[]{:S(2)}, u32[]{:S(2)}) async-start(f32[16,24,128]{2,1,0:T(8,128)} %pack.1), calls=%async_computation | async-start | bytes 393216 | tf_op jit(solution)/shard_map/all_to_all | solution.py:909
  9.8 10.1 %copy-start = (f32[2,2,64,2048]{3,2,1,0:T(8,128)S(1)}, f32[2,2,64,2048]{3,2,1,0:T(8,128)}, u32[]{:S(2)}) copy-start(f32[2,2,64,2048]{3,2,1,0:T(8,128)} %kernel.1) | copy-start | bytes 6291460
  9.8 10.1 %copy-start.1 = (bf16[512,128]{1,0:T(8,128)(2,1)S(1)}, bf16[512,128]{1,0:T(8,128)(2,1)}, u32[]{:S(2)}) copy-start(bf16[512,128]{1,0:T(8,128)(2,1)} %constant.20.clone.back) | copy-start | bytes 393220
  9.8 10.1 %copy-start.2 = (f32[2,8,256]{2,1,0:T(8,128)S(1)}, f32[2,8,256]{2,1,0:T(8,128)}, u32[]{:S(2)}) copy-start(f32[2,8,256]{2,1,0:T(8,128)} %constant.21.clone.turns) | copy-start | bytes 49156
  18.4 1.4 %collective-permute-start = (f32[16,24,128]{2,1,0:T(8,128)S(1)}, f32[16,24,128]{2,1,0:T(8,128)S(1)}, u32[]{:S(2)}, u32[]{:S(2)}) collective-permute-start(f32[16,24,128]{2,1,0:T(8,128)S(1)} %all-to-all-done.gathered), channel_id=1, source_target_pairs={{0,1},{1,0},{2,3},{3,2},{4,5},{5,4},{6,7},{7,6},{8,9},{9,8},{10,11... | collective-permute-start | bytes 589832 | tf_op jit(solution)/shard_map/ppermute | solution.py:916
  19.9 7.5 %copy-start.5 = (f32[64,128]{1,0:T(8,128)S(1)}, f32[64,128]{1,0:T(8,128)}, u32[]{:S(2)}) copy-start(f32[64,128]{1,0:T(8,128)} %get-tuple-element.45.y_faces_from) | copy-start | bytes 98308
  23.3 13.1 %all-to-all-start.1 = ((f32[32,16,128]{2,1,0:T(8,128)}), f32[32,16,128]{2,1,0:T(8,128)S(1)}, u32[]{:S(2)}, u32[]{:S(2)}) async-start(f32[32,16,128]{2,1,0:T(8,128)} %lines.1), calls=%async_computation.1 | async-start | bytes 524288 | tf_op jit(solution)/shard_map/all_to_all | solution.py:927
  25.9 11.9 %collective-permute-start.1 = (f32[4,64,128]{2,1,0:T(8,128)S(1)}, f32[4,64,128]{2,1,0:T(8,128)S(1)}, u32[]{:S(2)}, u32[]{:S(2)}) collective-permute-start(f32[4,64,128]{2,1,0:T(8,128)S(1)} %get-tuple-element.32), channel_id=1, source_target_pairs={{0,3},{1,0},{2,1},{3,2},{4,7},{5,4},{6,5},{7,6},{8,11},{9,8},{10,9... | collective-permute-start | bytes 393224 | tf_op jit(solution)/shard_map/ppermute | solution.py:426
  27.4 10.5 %collective-permute-start.2 = (f32[4,64,128]{2,1,0:T(8,128)S(1)}, f32[4,64,128]{2,1,0:T(8,128)S(1)}, u32[]{:S(2)}, u32[]{:S(2)}) collective-permute-start(f32[4,64,128]{2,1,0:T(8,128)S(1)} %get-tuple-element.33), channel_id=1, source_target_pairs={{0,1},{1,2},{2,3},{3,0},{4,5},{5,6},{6,7},{7,4},{8,9},{9,10},{10,1... | collective-permute-start | bytes 393224 | tf_op jit(solution)/shard_map/ppermute | solution.py:426
  27.4 10.5 %collective-permute-start.3 = (f32[64,128]{1,0:T(8,128)S(1)}, f32[64,128]{1,0:T(8,128)S(1)}, u32[]{:S(2)}, u32[]{:S(2)}) collective-permute-start(f32[64,128]{1,0:T(8,128)S(1)} %copy-done.5), channel_id=1, source_target_pairs={{0,4},{4,0},{1,5},{5,1},{2,6},{6,2},{3,7},{7,3},{8,12},{12,8},{9,1... | collective-permute-start | bytes 98312 | tf_op jit(solution)/shard_map/ppermute | solution.py:426
  28.8 9.0 %collective-permute-start.4 = (f32[4,16,128]{2,1,0:T(8,128)S(1)}, f32[4,16,128]{2,1,0:T(8,128)S(1)}, u32[]{:S(2)}, u32[]{:S(2)}) collective-permute-start(f32[4,16,128]{2,1,0:T(8,128)S(1)} %get-tuple-element.37), channel_id=1, source_target_pairs={{0,24},{8,0},{16,8},{24,16},{1,25},{9,1},{17,9},{25,17},{2,26},{10... | collective-permute-start | bytes 98312 | tf_op jit(solution)/shard_map/ppermute | solution.py:426
  32.3 5.7 %collective-permute-start.5 = (f32[4,16,128]{2,1,0:T(8,128)S(1)}, f32[4,16,128]{2,1,0:T(8,128)S(1)}, u32[]{:S(2)}, u32[]{:S(2)}) collective-permute-start(f32[4,16,128]{2,1,0:T(8,128)S(1)} %get-tuple-element.38), channel_id=1, source_target_pairs={{0,8},{8,16},{16,24},{24,0},{1,9},{9,17},{17,25},{25,1},{2,10},{10... | collective-permute-start | bytes 98312 | tf_op jit(solution)/shard_map/ppermute | solution.py:426
  37.8 3.6 %copy-start.3 = (f32[4,64,128]{2,1,0:T(8,128)}, f32[4,64,128]{2,1,0:T(8,128)S(1)}, u32[]{:S(2)}) copy-start(f32[4,64,128]{2,1,0:T(8,128)S(1)} %collective-permute-done.1.z_next_from) | copy-start | bytes 393220
  37.8 3.6 %copy-start.4 = (f32[4,64,128]{2,1,0:T(8,128)}, f32[4,64,128]{2,1,0:T(8,128)S(1)}, u32[]{:S(2)}) copy-start(f32[4,64,128]{2,1,0:T(8,128)S(1)} %collective-permute-done.2.z_before_from) | copy-start | bytes 393220
  37.9 3.6 %copy-start.6 = (f32[64,128]{1,0:T(8,128)}, f32[64,128]{1,0:T(8,128)S(1)}, u32[]{:S(2)}) copy-start(f32[64,128]{1,0:T(8,128)S(1)} %collective-permute-done.3.y_next_from.y_before_from) | copy-start | bytes 98308
  37.9 3.6 %copy-start.7 = (f32[4,16,128]{2,1,0:T(8,128)}, f32[4,16,128]{2,1,0:T(8,128)S(1)}, u32[]{:S(2)}) copy-start(f32[4,16,128]{2,1,0:T(8,128)S(1)} %collective-permute-done.4.x_next_from) | copy-start | bytes 98308
  38.0 3.4 %copy-start.8 = (f32[4,16,128]{2,1,0:T(8,128)}, f32[4,16,128]{2,1,0:T(8,128)S(1)}, u32[]{:S(2)}) copy-start(f32[4,16,128]{2,1,0:T(8,128)S(1)} %collective-permute-done.5.x_before_from) | copy-start | bytes 98308
  38.0 9.0 %all-to-all-start.2 = ((f32[8,48,128]{2,1,0:T(8,128)}), f32[8,48,128]{2,1,0:T(8,128)S(1)}, u32[]{:S(2)}, u32[]{:S(2)}) async-start(f32[8,48,128]{2,1,0:T(8,128)} %rows.1), calls=%async_computation.2 | async-start | bytes 393216 | tf_op jit(solution)/shard_map/all_to_all | solution.py:962

commit v7 on v6

--- a/solution.py
+++ b/solution.py
@@ -17,6 +17,7 @@
 f32 = jnp.float32
 bf16 = jnp.bfloat16
 MIB = 1024 * 1024
+QUAD = 4
 SMEM = pl.BlockSpec(memory_space=pltpu.SMEM)
 VMEM = pl.BlockSpec(memory_space=pltpu.VMEM)
 HBM = pl.BlockSpec(memory_space=pltpu.HBM)
@@ -647,7 +648,7 @@
     return results
 
 
-def lines_kernel(counts, here, gathered, swapped, back, turns, kernel, out):
+def lines_kernel(counts, here, gathered, swapped, back, turns, kernel, out, received):
     count_x, count_y, count_z = counts
     group = count_y * count_z
     top_rows = LANES // group
@@ -662,18 +663,13 @@
         y = (2 * pair + odd) * (2 * top_rows) + h * top_rows + (lane & (top_rows - 1))
         cosine, sine = cos_sin(ky * y & (size - 1), size)
         table += [cosine, -sine]
-    blocks = []
-    for g in range(count_x):
-        members = slice(g * group // 2, (g + 1) * group // 2)
-        blocks.append(
-            jnp.concatenate(
-                [
-                    part[members, 0:top_rows, :].reshape(half, LANES)
-                    for part in (gathered, swapped)
-                ],
-                axis=0,
-            )
-        )
+    for k, part in enumerate((gathered, swapped)):
+        for member in range(part.shape[0]):
+            g, place = divmod(member, group // 2)
+            for j in range(top_rows // QUAD):
+                row = (k * group // 2 + place) * top_rows + j * QUAD
+                received[g, row : row + QUAD, :] = part[member, j]
+    blocks = [received[g] for g in range(count_x)]
     mixed = dot3(jnp.concatenate(table, axis=0), split(jnp.concatenate(blocks, axis=1)))
     low_half, high_half = mixed[: 2 * kys], mixed[2 * kys :]
     lane = lax.broadcasted_iota(jnp.int32, (2 * kys, LANES), 1)
@@ -705,11 +701,11 @@
 
 
 def side_kernel_body(
-    counts, here, gathered, swapped, back, turns, kernel_from, out, kernel, loading
+    counts, here, gathered, swapped, back, turns, kernel_from, out, kernel, received, loading
 ):
     count_x, count_y, count_z = counts
     depth_block = (out.shape[1] - 2 * TILE) // 2
-    top_rows = gathered.shape[1] - TILE
+    last = gathered.shape[1] - 1
     kzs, length = kernel_from.shape[2:]
     loads = begin(
         loading,
@@ -719,29 +715,23 @@
         ],
     )
     size = kzs * count_y * count_z
-    share = depth_block // count_x
-
-    columns = count_x * count_z * TILE
+    columns = count_x * count_z * QUAD
     kz = here[0] * kzs + lax.broadcasted_iota(jnp.int32, (kzs, columns), 0)
     column = lax.broadcasted_iota(jnp.int32, (kzs, columns), 1)
-    within = column & (TILE - 1)
-    pair = column >> whole_log(TILE) & (count_z // 2 - 1)
+    pair = column >> whole_log(QUAD) & (count_z // 2 - 1)
     odd = (column >> whole_log(columns // 2)) ^ (here[0] & 1)
-    z = (2 * pair + odd) * depth_block + within
-    z = z + (column >> whole_log(TILE * count_z // 2) & (count_x - 1)) * share
+    z = (2 * pair + odd) * depth_block + (column & (QUAD - 1))
+    z = z + (column >> whole_log(QUAD * count_z // 2) & (count_x - 1)) * QUAD
     cosine, sine = cos_sin(kz * z & (size - 1), size)
     table = jnp.concatenate([cosine, -sine], axis=0)
-    table = jnp.where(jnp.concatenate([within, within], axis=0) < share, table, 0.0)
-
-    blocks = []
-    for y in range(count_y):
-        rows = [
-            part[(x * count_y + y) * count_z // 2 + pair, top_rows:, :]
-            for part in (gathered, swapped)
-            for x in range(count_x)
-            for pair in range(count_z // 2)
-        ]
-        blocks.append(jnp.concatenate(rows, axis=0))
+    for k, part in enumerate((gathered, swapped)):
+        for x in range(count_x):
+            for y in range(count_y):
+                for pair in range(count_z // 2):
+                    row = ((k * count_x + x) * count_z // 2 + pair) * QUAD
+                    member = (x * count_y + y) * count_z // 2 + pair
+                    received[y, row : row + QUAD, :] = part[member, last]
+    blocks = [received[y] for y in range(count_y)]
     lines = dot3(table, split(jnp.concatenate(blocks, axis=1)))
 
     waiting = dict(enumerate(loads))
@@ -865,22 +855,29 @@
         copy.wait()
 
 
-def residual_blocks(residual_top, residual_side, devices, share):
+def residual_blocks(residual_top, residual_side, copies, share, quads):
     block_x, block_y = residual_top.shape
     top_rows = block_y // 2
 
     def body(at_x, top, side, out):
         piece = jnp.concatenate([top[0:top_rows, :], top[top_rows:, :]], axis=1)
         part = side[pl.ds(at_x[0] * share, share), :]
-        part = jnp.concatenate([part, jnp.zeros((TILE - share, LANES), f32)], axis=0)
-        for device in range(devices):
-            out[device, 0:top_rows, :] = piece
-            out[device, top_rows:, :] = part
-
+        if not quads:
+            part = jnp.concatenate([part, jnp.zeros((TILE - share, LANES), f32)], axis=0)
+        for copy in range(copies):
+            if quads:
+                for j in range(top_rows // QUAD):
+                    out[copy, j] = piece[j * QUAD : (j + 1) * QUAD]
+                out[copy, top_rows // QUAD] = part
+            else:
+                out[copy, 0:top_rows, :] = piece
+                out[copy, top_rows:, :] = part
+
+    shape = (top_rows // QUAD + 1, QUAD) if quads else (top_rows + TILE,)
     return call(
         body,
         "pack",
-        (devices, top_rows + TILE, LANES),
+        (copies, *shape, LANES),
         60,
         0.8,
         (lax.axis_index("gx").reshape(1), residual_top.T, residual_side.T),
@@ -905,7 +902,9 @@
     back, turns = (jnp.asarray(table) for table in spread_tables(extent, size))
 
     parities = [range(parity, devices, 2) for parity in range(2)]
-    sent = residual_blocks(residual_top, residual_side, devices // 2, depth_block // count_x)
+    sent = residual_blocks(
+        residual_top, residual_side, devices // 2, depth_block // count_x, True
+    )
     gathered = lax.all_to_all(
         sent, ALL, 0, 0, tiled=True, axis_index_groups=[list(each) for each in parities]
     )
@@ -923,6 +922,7 @@
         16,
         4.0,
         (index, gathered, swapped, back, turns, top_kernel),
+        scratch=[pltpu.VMEM((count_x, LANES, LANES), f32)],
     )
     arrived = lax.all_to_all(lines, ALL, 0, 0, tiled=True)
     lines, x_first, x_last = lax.optimization_barrier((lines, x_first, x_last))
@@ -938,6 +938,7 @@
         refs=(5,),
         scratch=[
             pltpu.VMEM((size // INNER, 2, 2, kzs, INNER), f32),
+            pltpu.VMEM((count_y, count_x * count_z * QUAD, LANES), f32),
             pltpu.SemaphoreType.DMA((size // INNER,)),
         ],
     )
@@ -992,6 +993,7 @@
         and top_kernel.shape[3] == TILE * INNER == side_kernel.shape[3]
         and INNER == 2 * LANES
         and stiffness.shape[0] % 16 == 0
+        and stiffness.shape[0] == count_x * QUAD
         and side_kernel.shape[2] % 16 == 0
         and all(
             count & (count - 1) == 0
@@ -1013,7 +1015,7 @@
     top_rows = block_y // 2
     share = depth_block // count_x
 
-    sent = residual_blocks(residual_top, residual_side, devices, share)
+    sent = residual_blocks(residual_top, residual_side, devices, share, False)
     rows = sent.shape[1]
     gathered = lax.all_to_all(sent, ALL, 0, 0, tiled=True)
     index = (

time: 48.7 us -> 48 us (0.986)
  waiting for transfers between devices: 9.28 us -> 8.56 us
    all_to_all x1, waiting for transfers between devices: 5.94 us -> 5.23 us  [fast_on_device(): lax.all_to_all(sent, ALL, 0, 0, tiled=True, axis_index_groups=[list(each)...]
where the time goes in v7:
time: 48 us; the launch traced here: 47.5 us
  starting transfers between devices  20.7 us (43%)
  Pallas kernels  17.9 us (37%)
  waiting for transfers between devices  8.56 us (18%)
    pallas_call x7, Pallas kernels, call(): pl.pallas_call(body, out_shape=[pltpu.HBM(each, f32) if i in in_hbm else...  17.9 us
    all_to_all x1, starting transfers between devices, fast_on_device(): lax.all_to_all(sent, ALL, 0, 0, tiled=True, axis_index_groups=[list(each)...  8.31 us
    ppermute x5, starting transfers between devices, ring(): lax.ppermute(block, axis, [(i, (i + distance) % count) for i in range(cou...  6.42 us
    all_to_all x1, waiting for transfers between devices, fast_on_device(): lax.all_to_all(sent, ALL, 0, 0, tiled=True, axis_index_groups=[list(each)...  5.23 us
    all_to_all x1, starting transfers between devices, fast_on_device(): arrived = lax.all_to_all(rows, ('gy', 'gz'), 0, 0, tiled=True)  3.39 us
    all_to_all x1, starting transfers between devices, fast_on_device(): arrived = lax.all_to_all(lines, ALL, 0, 0, tiled=True)  2.59 us
    ppermute x1, waiting for transfers between devices, fast_on_device(): swapped = lax.ppermute(gathered, 'gz', [(i, i ^ 1) for i in range(count_z)])  1.39 us
    all_to_all x1, waiting for transfers between devices, fast_on_device(): arrived = lax.all_to_all(lines, ALL, 0, 0, tiled=True)  0.98 us
  transfers between devices with their start and end apart: 9, of which 5 were waited for; matrix products, arithmetic and copies ran while one was open for 0% of the time, Pallas kernels for 25%

profile of v7, /device:TPU:0, one launch (start us, length us, event | category | flops | bytes accessed | tf_op | source)
XLA Modules:
  0.0 47.5 jit_solution(2624827839645812802)
XLA Ops:
  0.0 1.5 %pack.1 = f32[16,5,4,128]{3,2,1,0:T(4,128)} custom-call(s32[1]{0:T(128)} %bitcast.1.at_x, f32[32,64]{1,0:T(8,128)} %bitcast.5, f32[16,128]{1,0:T(8,128)} %bitcast.6), custom_call_target="tpu_custom_call" | custom-call | flops 800000000 | bytes 180228 | tf_op jit(solution)/shard_map/pack/pallas_call | solution.py:50
  1.5 8.3 %all-to-all-start = ((f32[16,5,4,128]{3,2,1,0:T(4,128)}), f32[16,5,4,128]{3,2,1,0:T(4,128)S(1)}, u32[]{:S(2)}, u32[]{:S(2)}) async-start(f32[16,5,4,128]{3,2,1,0:T(4,128)} %pack.1), calls=%async_computation | async-start | bytes 327680 | tf_op jit(solution)/shard_map/all_to_all | solution.py:908
  9.8 0.0 copy-start
  9.8 0.0 copy-start.1
  9.8 0.0 copy-start.2
  9.8 2.7 %faces.1 = (f32[4,64,128]{2,1,0:T(8,128)S(1)}, f32[4,64,128]{2,1,0:T(8,128)S(1)}, f32[4,16,128]{2,1,0:T(8,128)S(1)}, f32[4,16,128]{2,1,0:T(8,128)S(1)}, f32[64,128]{1,0:T(8,128)}) custom-call(f32[3,16,64,128]{3,2,1,0:T(8,128)} %magnetization_from.1, f32[16,64,128]{2,1,0:T(8,128)} %stiffness_from.1), custom_call_target="tpu_custom_call" | custom-call | flops 2000000000 | bytes 2457600 | tf_op jit(solution)/shard_map/faces/pallas_call | solution.py:50
  12.5 5.2 %all-to-all-done.gathered = f32[16,5,4,128]{3,2,1,0:T(4,128)S(1)} async-done(((f32[16,5,4,128]{3,2,1,0:T(4,128)}), f32[16,5,4,128]{3,2,1,0:T(4,128)S(1)}, u32[]{:S(2)}, u32[]{:S(2)}) %all-to-all-start) | async-done | bytes 163872 | tf_op jit(solution)/shard_map/all_to_all | solution.py:908
  17.7 0.0 collective-permute-start
  17.7 1.4 %collective-permute-done.swapped = f32[16,5,4,128]{3,2,1,0:T(4,128)S(1)} collective-permute-done((f32[16,5,4,128]{3,2,1,0:T(4,128)S(1)}, f32[16,5,4,128]{3,2,1,0:T(4,128)S(1)}, u32[]{:S(2)}, u32[]{:S(2)}) %collective-permute-start) | collective-permute-done | bytes 163872 | tf_op jit(solution)/shard_map/ppermute | solution.py:915
  19.1 0.0 copy-done
  19.1 0.0 copy-done.1
  19.1 3.4 %lines.1 = f32[32,16,128]{2,1,0:T(8,128)} custom-call(s32[1]{0:T(128)} %bitcast.here, f32[16,5,4,128]{3,2,1,0:T(4,128)S(1)} %all-to-all-done.gathered, f32[16,5,4,128]{3,2,1,0:T(4,128)S(1)} %collective-permute-done.swapped, bf16[512,128]{1,0:T(8,128)(2,1)S(1)} %copy-done.1, f32[2,8,256]{2,1,0:T(8,128)S(1)} %copy-done.2, f32[2,2,64,2048]{3,2,1,0:T(8,128)S(1)} %copy-done), custom_call_target="tpu_custom_call" | custom-call | flops 4000000000 | bytes 2834436 | tf_op jit(solution)/shard_map/lines/pallas_call | solution.py:50
  22.5 2.6 %all-to-all-start.1 = ((f32[32,16,128]{2,1,0:T(8,128)}), f32[32,16,128]{2,1,0:T(8,128)S(1)}, u32[]{:S(2)}, u32[]{:S(2)}) async-start(f32[32,16,128]{2,1,0:T(8,128)} %lines.1), calls=%async_computation.1 | async-start | bytes 524288 | tf_op jit(solution)/shard_map/all_to_all | solution.py:927
  25.1 1.5 %collective-permute-start.1 = (f32[4,64,128]{2,1,0:T(8,128)S(1)}, f32[4,64,128]{2,1,0:T(8,128)S(1)}, u32[]{:S(2)}, u32[]{:S(2)}) collective-permute-start(f32[4,64,128]{2,1,0:T(8,128)S(1)} %get-tuple-element.32), channel_id=1, source_target_pairs={{0,3},{1,0},{2,1},{3,2},{4,7},{5,4},{6,5},{7,6},{8,11},{9,8},{10,9... | collective-permute-start | bytes 393224 | tf_op jit(solution)/shard_map/ppermute | solution.py:427
  26.6 0.0 collective-permute-start.2
  26.6 1.5 %collective-permute-start.3 = (f32[64,128]{1,0:T(8,128)S(1)}, f32[64,128]{1,0:T(8,128)S(1)}, u32[]{:S(2)}, u32[]{:S(2)}) collective-permute-start(f32[64,128]{1,0:T(8,128)S(1)} %copy-done.5), channel_id=1, source_target_pairs={{0,4},{4,0},{1,5},{5,1},{2,6},{6,2},{3,7},{7,3},{8,12},{12,8},{9,1... | collective-permute-start | bytes 98312 | tf_op jit(solution)/shard_map/ppermute | solution.py:427
  28.1 3.5 %collective-permute-start.4 = (f32[4,16,128]{2,1,0:T(8,128)S(1)}, f32[4,16,128]{2,1,0:T(8,128)S(1)}, u32[]{:S(2)}, u32[]{:S(2)}) collective-permute-start(f32[4,16,128]{2,1,0:T(8,128)S(1)} %get-tuple-element.37), channel_id=1, source_target_pairs={{0,24},{8,0},{16,8},{24,16},{1,25},{9,1},{17,9},{25,17},{2,26},{10... | collective-permute-start | bytes 98312 | tf_op jit(solution)/shard_map/ppermute | solution.py:427
  31.6 0.0 collective-permute-start.5
  31.6 3.1 %side.1 = f32[8,48,128]{2,1,0:T(8,128)} custom-call(s32[1]{0:T(128)} %bitcast.4.here, f32[16,5,4,128]{3,2,1,0:T(4,128)S(1)} %all-to-all-done.gathered, f32[16,5,4,128]{3,2,1,0:T(4,128)S(1)} %collective-permute-done.swapped, bf16[512,128]{1,0:T(8,128)(2,1)S(1)} %copy-done.1, f32[2,8,256]{2,1,0:T(8,128)S(1)} %copy-done.2, f32[2,2,16,2048]{3,2,1,0:T(8,128)} %kernel_from.1), custom_call_target="tpu_custom_call" | custom-call | flops 2800000000 | bytes 1196036 | tf_op jit(solution)/shard_map/side/pallas_call | solution.py:50
  34.7 1.0 %all-to-all-done.1.arrived = f32[32,16,128]{2,1,0:T(8,128)S(1)} async-done(((f32[32,16,128]{2,1,0:T(8,128)}), f32[32,16,128]{2,1,0:T(8,128)S(1)}, u32[]{:S(2)}, u32[]{:S(2)}) %all-to-all-start.1) | async-done | bytes 262176 | tf_op jit(solution)/shard_map/all_to_all | solution.py:927
  35.7 1.4 %rows.1 = f32[8,48,128]{2,1,0:T(8,128)} custom-call(f32[32,16,128]{2,1,0:T(8,128)S(1)} %all-to-all-done.1.arrived, f32[8,48,128]{2,1,0:T(8,128)} %side.1, bf16[512,128]{1,0:T(8,128)(2,1)S(1)} %copy-done.1, f32[2,8,256]{2,1,0:T(8,128)S(1)} %copy-done.2), custom_call_target="tpu_custom_call", output_to_operand_aliasing={{}: (1, {})} | custom-call | flops 1400000000 | bytes 802816 | tf_op jit(solution)/shard_map/rows/pallas_call | solution.py:50
  37.0 0.0 collective-permute-done.1.z_next_from
  37.1 0.0 copy-start.3
  37.1 0.0 collective-permute-done.2.z_before_from
  37.1 0.0 copy-start.4
  37.1 0.0 collective-permute-done.3.y_next_from.y_before_from
  37.1 0.0 collective-permute-done.4.x_next_from
  37.1 0.1 collective-permute-done.5.x_before_from
  37.3 3.4 %all-to-all-start.2 = ((f32[8,48,128]{2,1,0:T(8,128)}), f32[8,48,128]{2,1,0:T(8,128)S(1)}, u32[]{:S(2)}, u32[]{:S(2)}) async-start(f32[8,48,128]{2,1,0:T(8,128)} %rows.1), calls=%async_computation.2 | async-start | bytes 393216 | tf_op jit(solution)/shard_map/all_to_all | solution.py:963
  40.7 4.7 %exchange.1.exchange_grad = f32[3,16,64,128]{3,2,1,0:T(8,128)S(1)} custom-call(s32[1]{0:T(128)} %bitcast.here, f32[3,16,64,128]{3,2,1,0:T(8,128)} %magnetization_from.1, f32[16,64,128]{2,1,0:T(8,128)} %stiffness_from.1, f32[4,64,128]{2,1,0:T(8,128)} %copy-done.3, f32[4,64,128]{2,1,0:T(8,128)} %copy-done.4, f32[4,16,128]{2,1,0:T(8,128)} %copy-done.7, ...), custom_call_target="tpu_custom_call" | custom-call | flops 5000000000 | bytes 4096004 | tf_op jit(solution)/shard_map/exchange/pallas_call | solution.py:50
  45.4 0.8 %all-to-all-done.2.arrived = f32[8,48,128]{2,1,0:T(8,128)S(1)} async-done(((f32[8,48,128]{2,1,0:T(8,128)}), f32[8,48,128]{2,1,0:T(8,128)S(1)}, u32[]{:S(2)}, u32[]{:S(2)}) %all-to-all-start.2) | async-done | bytes 196640 | tf_op jit(solution)/shard_map/all_to_all | solution.py:963
  46.3 1.2 %gradient.1 = f32[3,16,64,128]{3,2,1,0:T(8,128)} custom-call(f32[3,16,64,128]{3,2,1,0:T(8,128)S(1)} %exchange.1.exchange_grad, f32[8,48,128]{2,1,0:T(8,128)S(1)} %all-to-all-done.2.arrived), custom_call_target="tpu_custom_call" | custom-call | flops 1200000000 | bytes 3342336 | tf_op jit(solution)/shard_map/gradient/pallas_call | solution.py:50
  (11 shorter events, 0.0 us)
Async XLA Ops:
  1.5 16.3 %all-to-all-start = ((f32[16,5,4,128]{3,2,1,0:T(4,128)}), f32[16,5,4,128]{3,2,1,0:T(4,128)S(1)}, u32[]{:S(2)}, u32[]{:S(2)}) async-start(f32[16,5,4,128]{3,2,1,0:T(4,128)} %pack.1), calls=%async_computation | async-start | bytes 327680 | tf_op jit(solution)/shard_map/all_to_all | solution.py:908
  9.8 9.3 %copy-start = (f32[2,2,64,2048]{3,2,1,0:T(8,128)S(1)}, f32[2,2,64,2048]{3,2,1,0:T(8,128)}, u32[]{:S(2)}) copy-start(f32[2,2,64,2048]{3,2,1,0:T(8,128)} %kernel.1) | copy-start | bytes 6291460
  9.8 9.3 %copy-start.1 = (bf16[512,128]{1,0:T(8,128)(2,1)S(1)}, bf16[512,128]{1,0:T(8,128)(2,1)}, u32[]{:S(2)}) copy-start(bf16[512,128]{1,0:T(8,128)(2,1)} %constant.20.clone.back) | copy-start | bytes 393220
  9.8 9.3 %copy-start.2 = (f32[2,8,256]{2,1,0:T(8,128)S(1)}, f32[2,8,256]{2,1,0:T(8,128)}, u32[]{:S(2)}) copy-start(f32[2,8,256]{2,1,0:T(8,128)} %constant.21.clone.turns) | copy-start | bytes 49156
  17.7 1.4 %collective-permute-start = (f32[16,5,4,128]{3,2,1,0:T(4,128)S(1)}, f32[16,5,4,128]{3,2,1,0:T(4,128)S(1)}, u32[]{:S(2)}, u32[]{:S(2)}) collective-permute-start(f32[16,5,4,128]{3,2,1,0:T(4,128)S(1)} %all-to-all-done.gathered), channel_id=1, source_target_pairs={{0,1},{1,0},{2,3},{3,2},{4,5},{5,4},{6,7},{7,6},{8,9},{9,8},{10,11... | collective-permute-start | bytes 491528 | tf_op jit(solution)/shard_map/ppermute | solution.py:915
  19.1 7.5 %copy-start.5 = (f32[64,128]{1,0:T(8,128)S(1)}, f32[64,128]{1,0:T(8,128)}, u32[]{:S(2)}) copy-start(f32[64,128]{1,0:T(8,128)} %get-tuple-element.45.y_faces_from) | copy-start | bytes 98308
  22.5 13.1 %all-to-all-start.1 = ((f32[32,16,128]{2,1,0:T(8,128)}), f32[32,16,128]{2,1,0:T(8,128)S(1)}, u32[]{:S(2)}, u32[]{:S(2)}) async-start(f32[32,16,128]{2,1,0:T(8,128)} %lines.1), calls=%async_computation.1 | async-start | bytes 524288 | tf_op jit(solution)/shard_map/all_to_all | solution.py:927
  25.1 11.9 %collective-permute-start.1 = (f32[4,64,128]{2,1,0:T(8,128)S(1)}, f32[4,64,128]{2,1,0:T(8,128)S(1)}, u32[]{:S(2)}, u32[]{:S(2)}) collective-permute-start(f32[4,64,128]{2,1,0:T(8,128)S(1)} %get-tuple-element.32), channel_id=1, source_target_pairs={{0,3},{1,0},{2,1},{3,2},{4,7},{5,4},{6,5},{7,6},{8,11},{9,8},{10,9... | collective-permute-start | bytes 393224 | tf_op jit(solution)/shard_map/ppermute | solution.py:427
  26.6 10.5 %collective-permute-start.2 = (f32[4,64,128]{2,1,0:T(8,128)S(1)}, f32[4,64,128]{2,1,0:T(8,128)S(1)}, u32[]{:S(2)}, u32[]{:S(2)}) collective-permute-start(f32[4,64,128]{2,1,0:T(8,128)S(1)} %get-tuple-element.33), channel_id=1, source_target_pairs={{0,1},{1,2},{2,3},{3,0},{4,5},{5,6},{6,7},{7,4},{8,9},{9,10},{10,1... | collective-permute-start | bytes 393224 | tf_op jit(solution)/shard_map/ppermute | solution.py:427
  26.6 10.5 %collective-permute-start.3 = (f32[64,128]{1,0:T(8,128)S(1)}, f32[64,128]{1,0:T(8,128)S(1)}, u32[]{:S(2)}, u32[]{:S(2)}) collective-permute-start(f32[64,128]{1,0:T(8,128)S(1)} %copy-done.5), channel_id=1, source_target_pairs={{0,4},{4,0},{1,5},{5,1},{2,6},{6,2},{3,7},{7,3},{8,12},{12,8},{9,1... | collective-permute-start | bytes 98312 | tf_op jit(solution)/shard_map/ppermute | solution.py:427
  28.1 9.0 %collective-permute-start.4 = (f32[4,16,128]{2,1,0:T(8,128)S(1)}, f32[4,16,128]{2,1,0:T(8,128)S(1)}, u32[]{:S(2)}, u32[]{:S(2)}) collective-permute-start(f32[4,16,128]{2,1,0:T(8,128)S(1)} %get-tuple-element.37), channel_id=1, source_target_pairs={{0,24},{8,0},{16,8},{24,16},{1,25},{9,1},{17,9},{25,17},{2,26},{10... | collective-permute-start | bytes 98312 | tf_op jit(solution)/shard_map/ppermute | solution.py:427
  31.6 5.7 %collective-permute-start.5 = (f32[4,16,128]{2,1,0:T(8,128)S(1)}, f32[4,16,128]{2,1,0:T(8,128)S(1)}, u32[]{:S(2)}, u32[]{:S(2)}) collective-permute-start(f32[4,16,128]{2,1,0:T(8,128)S(1)} %get-tuple-element.38), channel_id=1, source_target_pairs={{0,8},{8,16},{16,24},{24,0},{1,9},{9,17},{17,25},{25,1},{2,10},{10... | collective-permute-start | bytes 98312 | tf_op jit(solution)/shard_map/ppermute | solution.py:427
  37.1 3.6 %copy-start.3 = (f32[4,64,128]{2,1,0:T(8,128)}, f32[4,64,128]{2,1,0:T(8,128)S(1)}, u32[]{:S(2)}) copy-start(f32[4,64,128]{2,1,0:T(8,128)S(1)} %collective-permute-done.1.z_next_from) | copy-start | bytes 393220
  37.1 3.6 %copy-start.4 = (f32[4,64,128]{2,1,0:T(8,128)}, f32[4,64,128]{2,1,0:T(8,128)S(1)}, u32[]{:S(2)}) copy-start(f32[4,64,128]{2,1,0:T(8,128)S(1)} %collective-permute-done.2.z_before_from) | copy-start | bytes 393220
  37.1 3.6 %copy-start.6 = (f32[64,128]{1,0:T(8,128)}, f32[64,128]{1,0:T(8,128)S(1)}, u32[]{:S(2)}) copy-start(f32[64,128]{1,0:T(8,128)S(1)} %collective-permute-done.3.y_next_from.y_before_from) | copy-start | bytes 98308
  37.1 3.6 %copy-start.7 = (f32[4,16,128]{2,1,0:T(8,128)}, f32[4,16,128]{2,1,0:T(8,128)S(1)}, u32[]{:S(2)}) copy-start(f32[4,16,128]{2,1,0:T(8,128)S(1)} %collective-permute-done.4.x_next_from) | copy-start | bytes 98308
  37.3 3.4 %copy-start.8 = (f32[4,16,128]{2,1,0:T(8,128)}, f32[4,16,128]{2,1,0:T(8,128)S(1)}, u32[]{:S(2)}) copy-start(f32[4,16,128]{2,1,0:T(8,128)S(1)} %collective-permute-done.5.x_before_from) | copy-start | bytes 98308
  37.3 9.0 %all-to-all-start.2 = ((f32[8,48,128]{2,1,0:T(8,128)}), f32[8,48,128]{2,1,0:T(8,128)S(1)}, u32[]{:S(2)}, u32[]{:S(2)}) async-start(f32[8,48,128]{2,1,0:T(8,128)} %rows.1), calls=%async_computation.2 | async-start | bytes 393216 | tf_op jit(solution)/shard_map/all_to_all | solution.py:963

commit v8 on v7

--- a/solution.py
+++ b/solution.py
@@ -536,6 +536,54 @@
     return np.concatenate([high, low], axis=1), turns
 
 
+def halves_of(table):
+    table = table.astype(np.float32)
+    high = table.astype(ml_dtypes.bfloat16)
+    return high, (table - high.astype(np.float32)).astype(ml_dtypes.bfloat16)
+
+
+def narrow_tables(extent, size):
+    length = 2 * extent
+    ratio = size // length
+    m = np.arange(size)
+    lags = np.arange(1, extent)
+    window = 1.0 + 2.0 * np.cos(np.outer(m, lags) % size * (2.0 * math.pi / size)).sum(axis=1)
+    i = np.arange(INNER)
+    place = np.arange(0, size, INNER)[:, None, None] + i[:, None] - ratio * i[None, :]
+    high, low = halves_of(window[place % size] / length)
+    tiles = np.stack([high, low], axis=1)
+    angle = np.outer(i, i) * (2.0 * math.pi / length)
+    table = np.stack(halves_of(np.concatenate([np.cos(angle), np.sin(angle)], axis=0)))
+    return tiles, table
+
+
+def narrow_kernel(top, side, tiles, top_out, side_out):
+    count = tiles.shape[0]
+    parts = top_out.shape[3] // INNER
+    step = count // parts
+    top_rows, side_rows = top.shape[2], side.shape[2]
+    totals = [None] * parts
+    for k in range(count):
+        columns = slice(k * INNER, (k + 1) * INNER)
+        lines = jnp.concatenate(
+            [
+                top[:, :, :, columns].reshape(4 * top_rows, INNER),
+                side[:, :, :, columns].reshape(4 * side_rows, INNER),
+            ],
+            axis=0,
+        )
+        high, low = split(lines)
+        lines = jnp.concatenate([high, low, high], axis=1)
+        for part in range(parts):
+            tile = tiles[(k - part * step) % count]
+            term = product(lines, jnp.concatenate([tile[0], tile[0], tile[1]], axis=0))
+            totals[part] = term if k == 0 else totals[part] + term
+    for part in range(parts):
+        columns = slice(part * INNER, (part + 1) * INNER)
+        top_out[:, :, :, columns] = totals[part][: 4 * top_rows].reshape(2, 2, top_rows, INNER)
+        side_out[:, :, :, columns] = totals[part][4 * top_rows :].reshape(2, 2, side_rows, INNER)
+
+
 def regrouping(extent, step, transposed):
     x = lax.broadcasted_iota(jnp.int32, (extent, extent), int(transposed))
     place = lax.broadcasted_iota(jnp.int32, (extent, extent), 1 - int(transposed))
@@ -577,92 +625,55 @@
     return both[:middle] + pltpu.roll(both[:middle], LANES // 2, 1) + both[middle:]
 
 
-def there_and_back(real, imag, columns_of, back, turns):
+def dot3_with(values, table):
+    high, low = split(values)
+    lines = jnp.concatenate([high, low, high], axis=1)
+    return product(lines, jnp.concatenate([table[0], table[0], table[1]], axis=0))
+
+
+def there_and_back(real, imag, kernel, table):
     rows, extent = real.shape
-    step = turns.shape[1]
-    count = extent // step
-    per = LANES // count
-    high, low = split(jnp.concatenate([real, imag], axis=0))
-    moved = product(jnp.concatenate([high, low], axis=0), regrouping(extent, step, False))
-    lane = lax.broadcasted_iota(jnp.int32, (rows, LANES), 1)
-    lines = []
-    for v in range(step):
-        column = v // per * LANES
-
-        def piece(k, to):
-            block = moved[k * rows : (k + 1) * rows, column : column + LANES]
-            shift = (to - v) * count % LANES
-            return pltpu.roll(block, shift, 1) if shift else block
-
-        first = jnp.where(lane < count, piece(0, 0), piece(1, 1))
-        first = jnp.where(lane < 2 * count, first, pltpu.roll(first, 2 * count, 1))
-        second = jnp.where(lane < count, piece(2, 0), piece(3, 1))
-        second = jnp.where(lane < 2 * count, second, 0.0)
-        lines.append(jnp.concatenate([first, second], axis=1))
-    waves = product(
-        jnp.concatenate(lines, axis=0).astype(bf16), jnp.concatenate([back, back], axis=1), 1
-    )
-
-    results = []
-    for start in range(0, rows, 16):
-        halves = [[], []]
-        for half in range(INNER // LANES):
-            lanes = slice(half * LANES, (half + 1) * LANES)
-            turn = [(turns[0, v : v + 1, lanes], turns[1, v : v + 1, lanes]) for v in range(step)]
-            z = []
-            for v in range(step):
-                part = waves[v * rows + start : v * rows + start + 16]
-                a = part[:, lanes]
-                b = part[:, INNER + half * LANES : INNER + (half + 1) * LANES]
-                if v:
-                    cosine, sine = turn[v]
-                    a, b = a * cosine + b * sine, b * cosine - a * sine
-                z.append((a, b))
-            z = eight_points(z, -1)
-            for c in range(2):
-                weighted = []
-                for k in range(step):
-                    kernel = columns_of(k)
-                    kernel_real = kernel[c, 0, start : start + 16, lanes]
-                    kernel_imag = kernel[c, 1, start : start + 16, lanes]
-                    weighted.append(
-                        (
-                            kernel_real * z[k][0] + kernel_imag * z[k][1],
-                            kernel_real * z[k][1] - kernel_imag * z[k][0],
-                        )
-                    )
-                weighted = eight_points(weighted, 1)
-                for v in range(1, step):
-                    (a, b), (cosine, sine) = weighted[v], turn[v]
-                    weighted[v] = (a * cosine - b * sine, a * sine + b * cosine)
-                halves[c].append(weighted)
-        turned = [
-            jnp.concatenate(
-                [halves[c][half][v][k] for k in range(2) for half in range(INNER // LANES)],
-                axis=1,
-            )
-            for v in range(step)
-            for c in range(2)
-        ]
-        results.append(back_product(jnp.concatenate(turned, axis=0), back))
-    return results
-
-
-def lines_kernel(counts, here, gathered, swapped, back, turns, kernel, out, received):
+    sign = jnp.where(lax.broadcasted_iota(jnp.int32, (1, extent), 1) & 1 == 0, 1.0, -1.0)
+    lines = jnp.concatenate(
+        [jnp.concatenate([real, imag], axis=1), jnp.concatenate([imag, -real], axis=1)], axis=0
+    )
+    signs = jnp.concatenate([sign, sign], axis=1)
+    waves = dot3_with(jnp.concatenate([lines, lines * signs], axis=0), table)
+    totals = []
+    for b in range(2):
+        wave_real, wave_imag = (
+            waves[(2 * b + k) * rows : (2 * b + k + 1) * rows] for k in range(2)
+        )
+        columns = slice(b * INNER, (b + 1) * INNER)
+        weighted = ([], [])
+        for c in range(2):
+            kernel_real, kernel_imag = kernel[c, 0, :, columns], kernel[c, 1, :, columns]
+            weighted[0].append(kernel_real * wave_real + kernel_imag * wave_imag)
+            weighted[1].append(kernel_real * wave_imag - kernel_imag * wave_real)
+        a, b = (jnp.concatenate(part, axis=0) for part in weighted)
+        lines = jnp.concatenate(
+            [jnp.concatenate([a, -b], axis=1), jnp.concatenate([b, a], axis=1)], axis=0
+        )
+        totals.append(dot3_with(lines, table))
+    total = totals[0] + totals[1] * sign
+    return total[: 2 * rows], total[2 * rows :]
+
+
+def lines_kernel(counts, here, gathered, swapped, table, kernel, out, received):
     count_x, count_y, count_z = counts
     group = count_y * count_z
     top_rows = LANES // group
     half = LANES // 2
-    kys, size = kernel.shape[2:]
+    kys, size = kernel.shape[2], INNER * TILE
     ky = here[0] * kys + lax.broadcasted_iota(jnp.int32, (kys, LANES), 0)
     lane = lax.broadcasted_iota(jnp.int32, (kys, LANES), 1)
     odd = (lane >> whole_log(LANES // 2)) ^ (here[0] & 1)
     pair = lane >> whole_log(top_rows) & (group // 2 - 1)
-    table = []
+    phases_of = []
     for h in range(2):
         y = (2 * pair + odd) * (2 * top_rows) + h * top_rows + (lane & (top_rows - 1))
         cosine, sine = cos_sin(ky * y & (size - 1), size)
-        table += [cosine, -sine]
+        phases_of += [cosine, -sine]
     for k, part in enumerate((gathered, swapped)):
         for member in range(part.shape[0]):
             g, place = divmod(member, group // 2)
@@ -670,7 +681,7 @@
                 row = (k * group // 2 + place) * top_rows + j * QUAD
                 received[g, row : row + QUAD, :] = part[member, j]
     blocks = [received[g] for g in range(count_x)]
-    mixed = dot3(jnp.concatenate(table, axis=0), split(jnp.concatenate(blocks, axis=1)))
+    mixed = dot3(jnp.concatenate(phases_of, axis=0), split(jnp.concatenate(blocks, axis=1)))
     low_half, high_half = mixed[: 2 * kys], mixed[2 * kys :]
     lane = lax.broadcasted_iota(jnp.int32, (2 * kys, LANES), 1)
     pieces = []
@@ -685,35 +696,17 @@
             )
         )
     lines = jnp.concatenate(pieces, axis=1)
-
-    def columns_of(b):
-        return kernel.at[:, :, :, b * INNER : (b + 1) * INNER]
-
-    results = there_and_back(lines[:kys], lines[kys:], columns_of, back[...], turns)
-    count = count_x * group
-    for v in range(turns.shape[1]):
-        block = jnp.concatenate(
-            [result[(2 * v + c) * 16 : (2 * v + c + 1) * 16] for c in range(2) for result in results],
-            axis=0,
-        ).T
-        out[:, v, :] = block[:count]
-        out[:, TILE + v, :] = block[count : 2 * count]
+    for k, part in enumerate(there_and_back(lines[:kys], lines[kys:], kernel, table)):
+        out[:, k * TILE : (k + 1) * TILE, :] = part.T.reshape(count_x * group, TILE, LANES)
 
 
 def side_kernel_body(
-    counts, here, gathered, swapped, back, turns, kernel_from, out, kernel, received, loading
+    counts, here, gathered, swapped, spectrum, kernel, out, received
 ):
     count_x, count_y, count_z = counts
     depth_block = (out.shape[1] - 2 * TILE) // 2
     last = gathered.shape[1] - 1
-    kzs, length = kernel_from.shape[2:]
-    loads = begin(
-        loading,
-        [
-            (kernel_from.at[:, :, :, pl.ds(b * INNER, INNER)], kernel.at[b])
-            for b in range(length // INNER)
-        ],
-    )
+    kzs, length = kernel.shape[2], INNER * TILE
     size = kzs * count_y * count_z
     columns = count_x * count_z * QUAD
     kz = here[0] * kzs + lax.broadcasted_iota(jnp.int32, (kzs, columns), 0)
@@ -734,22 +727,7 @@
     blocks = [received[y] for y in range(count_y)]
     lines = dot3(table, split(jnp.concatenate(blocks, axis=1)))
 
-    waiting = dict(enumerate(loads))
-
-    def columns_of(b):
-        if b in waiting:
-            waiting.pop(b).wait()
-        return kernel.at[b]
-
-    result = there_and_back(lines[:kzs], lines[kzs:], columns_of, back[...], turns)[0]
-    step = turns.shape[1]
-    count = count_y * LANES // step
-    images = []
-    for c in range(2):
-        pieces = [result[(2 * v + c) * 16 : (2 * v + c + 1) * 16] for v in range(step)]
-        images.append(beside(pieces, count))
-        images.append(beside([pltpu.roll(piece, LANES - count, 1) for piece in pieces], count))
-    images = regrouped(jnp.concatenate(images, axis=0), step, True)
+    real, imag = there_and_back(lines[:kzs], lines[kzs:], kernel, spectrum)
 
     rows = depth_block * count_z
     z = lax.broadcasted_iota(jnp.int32, (rows, 2 * kzs), 0)
@@ -757,7 +735,8 @@
     cosine, sine = cos_sin((here[0] * kzs + (column & (kzs - 1))) * z & (size - 1), size)
     table = jnp.where(column < kzs, cosine, -sine) * (1.0 / (size * length))
     for c in range(2):
-        image = dot3(table, split(images[2 * kzs * c : 2 * kzs * (c + 1)]))
+        part = slice(c * kzs, (c + 1) * kzs)
+        image = dot3(table, split(jnp.concatenate([real[part], imag[part]], axis=0)))
         for y in range(count_y):
             for z in range(count_z):
                 start = 2 * TILE + c * depth_block
@@ -900,6 +879,7 @@
     index = (here[0] * group + plane_index).reshape(1)
     plane_index = plane_index.reshape(1)
     back, turns = (jnp.asarray(table) for table in spread_tables(extent, size))
+    tiles, table = (jnp.asarray(values) for values in narrow_tables(extent, size))
 
     parities = [range(parity, devices, 2) for parity in range(2)]
     sent = residual_blocks(
@@ -909,8 +889,16 @@
         sent, ALL, 0, 0, tiled=True, axis_index_groups=[list(each) for each in parities]
     )
     z_first, z_last, x_first, x_last, y_faces = faces_of(magnetization, stiffness)
-    gathered, x_first, x_last, y_faces = lax.optimization_barrier(
-        (gathered, x_first, x_last, y_faces)
+    top_spectra, side_spectra = call(
+        narrow_kernel,
+        "narrow",
+        [(2, 2, kys, 2 * extent), (2, 2, kzs, 2 * extent)],
+        16,
+        2.5,
+        (top_kernel, side_kernel, tiles),
+    )
+    gathered, x_first, x_last, y_faces, top_spectra, side_spectra = lax.optimization_barrier(
+        (gathered, x_first, x_last, y_faces, top_spectra, side_spectra)
     )
     swapped = lax.ppermute(gathered, "gz", [(i, i ^ 1) for i in range(count_z)])
     zy = halos_zy(z_first, z_last, y_faces)
@@ -920,8 +908,8 @@
         "lines",
         (devices, 2 * TILE, LANES),
         16,
-        4.0,
-        (index, gathered, swapped, back, turns, top_kernel),
+        2.2,
+        (index, gathered, swapped, table, top_spectra),
         scratch=[pltpu.VMEM((count_x, LANES, LANES), f32)],
     )
     arrived = lax.all_to_all(lines, ALL, 0, 0, tiled=True)
@@ -932,15 +920,10 @@
         "side",
         (group, 2 * TILE + 2 * depth_block, LANES),
         8,
-        2.8,
-        (plane_index, gathered, swapped, back, turns, from_hbm(side_kernel)),
+        2.0,
+        (plane_index, gathered, swapped, table, side_spectra),
         in_hbm=(0,),
-        refs=(5,),
-        scratch=[
-            pltpu.VMEM((size // INNER, 2, 2, kzs, INNER), f32),
-            pltpu.VMEM((count_y, count_x * count_z * QUAD, LANES), f32),
-            pltpu.SemaphoreType.DMA((size // INNER,)),
-        ],
+        scratch=[pltpu.VMEM((count_y, count_x * count_z * QUAD, LANES), f32)],
     )
     arrived, side = lax.optimization_barrier((arrived, side))
     rows = call(

time: 48 us -> 47.6 us (level)
  waiting for transfers between devices: 8.56 us -> 7.44 us
  starting transfers between devices: 20.7 us -> 21.4 us
    all_to_all x1, waiting for transfers between devices: 5.23 us -> 2.72 us  [fast_on_device(): lax.all_to_all(sent, ALL, 0, 0, tiled=True, axis_index_groups=[list(each)...]
    all_to_all x1, waiting for transfers between devices: 0.98 us -> 2.37 us  [fast_on_device(): arrived = lax.all_to_all(lines, ALL, 0, 0, tiled=True)]
    all_to_all x1, starting transfers between devices: 2.59 us -> 3.24 us  [fast_on_device(): arrived = lax.all_to_all(lines, ALL, 0, 0, tiled=True)]
    pallas_call x7 -> x8, Pallas kernels: 17.9 us -> 17.7 us  [call(): pl.pallas_call(body, out_shape=[pltpu.HBM(each, f32) if i in in_hbm else...]
  transfers between devices with their start and end apart: 9 -> 9, of which waited for: 5 -> 5; matrix products, arithmetic and copies ran while one was open for 0% -> 0% of each run, Pallas kernels for 25% -> 27%
where the time goes in v8:
time: 47.6 us; the launch traced here: 47.1 us
  starting transfers between devices  21.4 us (45%)
  Pallas kernels  17.7 us (37%)
  waiting for transfers between devices  7.44 us (16%)
    pallas_call x8, Pallas kernels, call(): pl.pallas_call(body, out_shape=[pltpu.HBM(each, f32) if i in in_hbm else...  17.7 us
    all_to_all x1, starting transfers between devices, fast_on_device(): lax.all_to_all(sent, ALL, 0, 0, tiled=True, axis_index_groups=[list(each)...  8.31 us
    ppermute x5, starting transfers between devices, ring(): lax.ppermute(block, axis, [(i, (i + distance) % count) for i in range(cou...  6.42 us
    all_to_all x1, starting transfers between devices, fast_on_device(): arrived = lax.all_to_all(rows, ('gy', 'gz'), 0, 0, tiled=True)  3.39 us
    all_to_all x1, starting transfers between devices, fast_on_device(): arrived = lax.all_to_all(lines, ALL, 0, 0, tiled=True)  3.24 us
    all_to_all x1, waiting for transfers between devices, fast_on_device(): lax.all_to_all(sent, ALL, 0, 0, tiled=True, axis_index_groups=[list(each)...  2.72 us
    all_to_all x1, waiting for transfers between devices, fast_on_device(): arrived = lax.all_to_all(lines, ALL, 0, 0, tiled=True)  2.37 us
    ppermute x1, waiting for transfers between devices, fast_on_device(): swapped = lax.ppermute(gathered, 'gz', [(i, i ^ 1) for i in range(count_z)])  1.39 us
  transfers between devices with their start and end apart: 9, of which 5 were waited for; matrix products, arithmetic and copies ran while one was open for 0% of the time, Pallas kernels for 27%

profile of v8, /device:TPU:0, one launch (start us, length us, event | category | flops | bytes accessed | tf_op | source)
XLA Modules:
  0.0 47.1 jit_solution(14289339361641854735)
XLA Ops:
  0.0 1.5 %pack.1 = f32[16,5,4,128]{3,2,1,0:T(4,128)} custom-call(s32[1]{0:T(128)} %bitcast.1.at_x, f32[32,64]{1,0:T(8,128)} %bitcast.5, f32[16,128]{1,0:T(8,128)} %bitcast.6), custom_call_target="tpu_custom_call" | custom-call | flops 800000000 | bytes 180228 | tf_op jit(solution)/shard_map/pack/pallas_call | solution.py:50
  1.5 8.3 %all-to-all-start = ((f32[16,5,4,128]{3,2,1,0:T(4,128)}), f32[16,5,4,128]{3,2,1,0:T(4,128)S(1)}, u32[]{:S(2)}, u32[]{:S(2)}) async-start(f32[16,5,4,128]{3,2,1,0:T(4,128)} %pack.1), calls=%async_computation | async-start | bytes 327680 | tf_op jit(solution)/shard_map/all_to_all | solution.py:888
  9.8 0.0 copy-start
  9.8 0.0 copy-start.1
  9.8 0.0 copy-start.2
  9.8 2.6 %faces.1 = (f32[4,64,128]{2,1,0:T(8,128)S(1)}, f32[4,64,128]{2,1,0:T(8,128)S(1)}, f32[4,16,128]{2,1,0:T(8,128)S(1)}, f32[4,16,128]{2,1,0:T(8,128)S(1)}, f32[64,128]{1,0:T(8,128)}) custom-call(f32[3,16,64,128]{3,2,1,0:T(8,128)} %magnetization_from.1, f32[16,64,128]{2,1,0:T(8,128)} %stiffness_from.1), custom_call_target="tpu_custom_call" | custom-call | flops 2000000000 | bytes 2457600 | tf_op jit(solution)/shard_map/faces/pallas_call | solution.py:50
  12.5 0.0 copy-done
  12.5 0.3 copy-done.2
  12.8 2.2 %narrow.1 = (f32[2,2,64,512]{3,2,1,0:T(8,128)S(1)}, f32[2,2,16,512]{3,2,1,0:T(8,128)S(1)}) custom-call(f32[2,2,64,2048]{3,2,1,0:T(8,128)S(1)} %copy-done, f32[2,2,16,2048]{3,2,1,0:T(8,128)S(1)} %copy-done.1, bf16[8,2,256,256]{3,2,1,0:T(8,128)(2,1)S(1)} %copy-done.2), custom_call_target="tpu_custom_call" | custom-call | flops 2500000000 | bytes 5373952 | tf_op jit(solution)/shard_map/narrow/pallas_call | solution.py:50
  15.0 2.7 %all-to-all-done.gathered = f32[16,5,4,128]{3,2,1,0:T(4,128)S(1)} async-done(((f32[16,5,4,128]{3,2,1,0:T(4,128)}), f32[16,5,4,128]{3,2,1,0:T(4,128)S(1)}, u32[]{:S(2)}, u32[]{:S(2)}) %all-to-all-start) | async-done | bytes 163872 | tf_op jit(solution)/shard_map/all_to_all | solution.py:888
  17.7 0.0 collective-permute-start
  17.7 1.4 %collective-permute-done.swapped = f32[16,5,4,128]{3,2,1,0:T(4,128)S(1)} collective-permute-done((f32[16,5,4,128]{3,2,1,0:T(4,128)S(1)}, f32[16,5,4,128]{3,2,1,0:T(4,128)S(1)}, u32[]{:S(2)}, u32[]{:S(2)}) %collective-permute-start) | collective-permute-done | bytes 163872 | tf_op jit(solution)/shard_map/ppermute | solution.py:903
  19.1 2.4 %lines.1 = f32[32,16,128]{2,1,0:T(8,128)} custom-call(s32[1]{0:T(128)} %bitcast.here, f32[16,5,4,128]{3,2,1,0:T(4,128)S(1)} %all-to-all-done.gathered, f32[16,5,4,128]{3,2,1,0:T(4,128)S(1)} %collective-permute-done.swapped, bf16[2,512,256]{2,1,0:T(8,128)(2,1)S(1)} %copy-done.3, f32[2,2,64,512]{3,2,1,0:T(8,128)S(1)} %get-tuple-element.36.kernel), custom_call_target="tpu_custom_call" | custom-call | flops 2200000000 | bytes 1638404 | tf_op jit(solution)/shard_map/lines/pallas_call | solution.py:50
  21.5 3.2 %all-to-all-start.1 = ((f32[32,16,128]{2,1,0:T(8,128)}), f32[32,16,128]{2,1,0:T(8,128)S(1)}, u32[]{:S(2)}, u32[]{:S(2)}) async-start(f32[32,16,128]{2,1,0:T(8,128)} %lines.1), calls=%async_computation.1 | async-start | bytes 524288 | tf_op jit(solution)/shard_map/all_to_all | solution.py:915
  24.8 1.6 %collective-permute-start.1 = (f32[4,64,128]{2,1,0:T(8,128)S(1)}, f32[4,64,128]{2,1,0:T(8,128)S(1)}, u32[]{:S(2)}, u32[]{:S(2)}) collective-permute-start(f32[4,64,128]{2,1,0:T(8,128)S(1)} %get-tuple-element.40), channel_id=1, source_target_pairs={{0,3},{1,0},{2,1},{3,2},{4,7},{5,4},{6,5},{7,6},{8,11},{9,8},{10,9... | collective-permute-start | bytes 393224 | tf_op jit(solution)/shard_map/ppermute | solution.py:427
  26.3 0.0 collective-permute-start.2
  26.3 1.5 %collective-permute-start.3 = (f32[64,128]{1,0:T(8,128)S(1)}, f32[64,128]{1,0:T(8,128)S(1)}, u32[]{:S(2)}, u32[]{:S(2)}) collective-permute-start(f32[64,128]{1,0:T(8,128)S(1)} %copy-done.8), channel_id=1, source_target_pairs={{0,4},{4,0},{1,5},{5,1},{2,6},{6,2},{3,7},{7,3},{8,12},{12,8},{9,1... | collective-permute-start | bytes 98312 | tf_op jit(solution)/shard_map/ppermute | solution.py:427
  27.8 3.4 %collective-permute-start.4 = (f32[4,16,128]{2,1,0:T(8,128)S(1)}, f32[4,16,128]{2,1,0:T(8,128)S(1)}, u32[]{:S(2)}, u32[]{:S(2)}) collective-permute-start(f32[4,16,128]{2,1,0:T(8,128)S(1)} %get-tuple-element.45), channel_id=1, source_target_pairs={{0,24},{8,0},{16,8},{24,16},{1,25},{9,1},{17,9},{25,17},{2,26},{10... | collective-permute-start | bytes 98312 | tf_op jit(solution)/shard_map/ppermute | solution.py:427
  31.2 0.0 collective-permute-start.5
  31.2 1.7 %side.3 = f32[8,48,128]{2,1,0:T(8,128)} custom-call(s32[1]{0:T(128)} %bitcast.4.here, f32[16,5,4,128]{3,2,1,0:T(4,128)S(1)} %all-to-all-done.gathered, f32[16,5,4,128]{3,2,1,0:T(4,128)S(1)} %collective-permute-done.swapped, bf16[2,512,256]{2,1,0:T(8,128)(2,1)S(1)} %copy-done.3, f32[2,2,16,512]{3,2,1,0:T(8,128)S(1)} %get-tuple-element.37.kernel), custom_call_target="tpu_custom_call" | custom-call | flops 2000000000 | bytes 1179652 | tf_op jit(solution)/shard_map/side/pallas_call | solution.py:50
  32.9 2.4 %all-to-all-done.1.arrived = f32[32,16,128]{2,1,0:T(8,128)S(1)} async-done(((f32[32,16,128]{2,1,0:T(8,128)}), f32[32,16,128]{2,1,0:T(8,128)S(1)}, u32[]{:S(2)}, u32[]{:S(2)}) %all-to-all-start.1) | async-done | bytes 262176 | tf_op jit(solution)/shard_map/all_to_all | solution.py:915
  35.3 1.4 %rows.1 = f32[8,48,128]{2,1,0:T(8,128)} custom-call(f32[32,16,128]{2,1,0:T(8,128)S(1)} %all-to-all-done.1.arrived, f32[8,48,128]{2,1,0:T(8,128)} %side.3, bf16[512,128]{1,0:T(8,128)(2,1)S(1)} %copy-done.4, f32[2,8,256]{2,1,0:T(8,128)S(1)} %copy-done.5), custom_call_target="tpu_custom_call", output_to_operand_aliasing={{}: (1, {})} | custom-call | flops 1400000000 | bytes 802816 | tf_op jit(solution)/shard_map/rows/pallas_call | solution.py:50
  36.7 0.0 collective-permute-done.1.z_next_from
  36.7 0.0 copy-start.6
  36.7 0.0 collective-permute-done.2.z_before_from
  36.7 0.0 collective-permute-done.3.y_next_from.y_before_from
  36.7 0.0 collective-permute-done.4.x_next_from
  36.8 0.1 collective-permute-done.5.x_before_from
  36.9 3.4 %all-to-all-start.2 = ((f32[8,48,128]{2,1,0:T(8,128)}), f32[8,48,128]{2,1,0:T(8,128)S(1)}, u32[]{:S(2)}, u32[]{:S(2)}) async-start(f32[8,48,128]{2,1,0:T(8,128)} %rows.1), calls=%async_computation.2 | async-start | bytes 393216 | tf_op jit(solution)/shard_map/all_to_all | solution.py:946
  40.3 4.7 %exchange.1.exchange_grad = f32[3,16,64,128]{3,2,1,0:T(8,128)S(1)} custom-call(s32[1]{0:T(128)} %bitcast.here, f32[3,16,64,128]{3,2,1,0:T(8,128)} %magnetization_from.1, f32[16,64,128]{2,1,0:T(8,128)} %stiffness_from.1, f32[4,64,128]{2,1,0:T(8,128)} %copy-done.6, f32[4,64,128]{2,1,0:T(8,128)} %copy-done.7, f32[4,16,128]{2,1,0:T(8,128)} %copy-done.10, ...), custom_call_target="tpu_custom_call" | custom-call | flops 5000000000 | bytes 4096004 | tf_op jit(solution)/shard_map/exchange/pallas_call | solution.py:50
  45.1 0.8 %all-to-all-done.2.arrived = f32[8,48,128]{2,1,0:T(8,128)S(1)} async-done(((f32[8,48,128]{2,1,0:T(8,128)}), f32[8,48,128]{2,1,0:T(8,128)S(1)}, u32[]{:S(2)}, u32[]{:S(2)}) %all-to-all-start.2) | async-done | bytes 196640 | tf_op jit(solution)/shard_map/all_to_all | solution.py:946
  45.9 1.2 %gradient.1 = f32[3,16,64,128]{3,2,1,0:T(8,128)} custom-call(f32[3,16,64,128]{3,2,1,0:T(8,128)S(1)} %exchange.1.exchange_grad, f32[8,48,128]{2,1,0:T(8,128)S(1)} %all-to-all-done.2.arrived), custom_call_target="tpu_custom_call" | custom-call | flops 1200000000 | bytes 3342336 | tf_op jit(solution)/shard_map/gradient/pallas_call | solution.py:50
  (18 shorter events, 0.0 us)
Async XLA Ops:
  1.5 16.3 %all-to-all-start = ((f32[16,5,4,128]{3,2,1,0:T(4,128)}), f32[16,5,4,128]{3,2,1,0:T(4,128)S(1)}, u32[]{:S(2)}, u32[]{:S(2)}) async-start(f32[16,5,4,128]{3,2,1,0:T(4,128)} %pack.1), calls=%async_computation | async-start | bytes 327680 | tf_op jit(solution)/shard_map/all_to_all | solution.py:888
  9.8 2.7 %copy-start = (f32[2,2,64,2048]{3,2,1,0:T(8,128)S(1)}, f32[2,2,64,2048]{3,2,1,0:T(8,128)}, u32[]{:S(2)}) copy-start(f32[2,2,64,2048]{3,2,1,0:T(8,128)} %top.1) | copy-start | bytes 6291460
  9.8 2.7 %copy-start.1 = (f32[2,2,16,2048]{3,2,1,0:T(8,128)S(1)}, f32[2,2,16,2048]{3,2,1,0:T(8,128)}, u32[]{:S(2)}) copy-start(f32[2,2,16,2048]{3,2,1,0:T(8,128)} %side.2) | copy-start | bytes 1572868
  9.8 3.0 %copy-start.2 = (bf16[8,2,256,256]{3,2,1,0:T(8,128)(2,1)S(1)}, bf16[8,2,256,256]{3,2,1,0:T(8,128)(2,1)}, u32[]{:S(2)}) copy-start(bf16[8,2,256,256]{3,2,1,0:T(8,128)(2,1)} %constant.26.clone.tiles) | copy-start | bytes 6291460
  12.8 6.3 %copy-start.3 = (bf16[2,512,256]{2,1,0:T(8,128)(2,1)S(1)}, bf16[2,512,256]{2,1,0:T(8,128)(2,1)}, u32[]{:S(2)}) copy-start(bf16[2,512,256]{2,1,0:T(8,128)(2,1)} %constant.27.clone.table.spectrum) | copy-start | bytes 1572868
  17.7 1.4 %collective-permute-start = (f32[16,5,4,128]{3,2,1,0:T(4,128)S(1)}, f32[16,5,4,128]{3,2,1,0:T(4,128)S(1)}, u32[]{:S(2)}, u32[]{:S(2)}) collective-permute-start(f32[16,5,4,128]{3,2,1,0:T(4,128)S(1)} %all-to-all-done.gathered), channel_id=1, source_target_pairs={{0,1},{1,0},{2,3},{3,2},{4,5},{5,4},{6,7},{7,6},{8,9},{9,8},{10,11... | collective-permute-start | bytes 491528 | tf_op jit(solution)/shard_map/ppermute | solution.py:903
  19.1 7.2 %copy-start.8 = (f32[64,128]{1,0:T(8,128)S(1)}, f32[64,128]{1,0:T(8,128)}, u32[]{:S(2)}) copy-start(f32[64,128]{1,0:T(8,128)} %get-tuple-element.53.y_faces_from) | copy-start | bytes 98308
  21.5 13.8 %all-to-all-start.1 = ((f32[32,16,128]{2,1,0:T(8,128)}), f32[32,16,128]{2,1,0:T(8,128)S(1)}, u32[]{:S(2)}, u32[]{:S(2)}) async-start(f32[32,16,128]{2,1,0:T(8,128)} %lines.1), calls=%async_computation.1 | async-start | bytes 524288 | tf_op jit(solution)/shard_map/all_to_all | solution.py:915
  24.8 11.9 %collective-permute-start.1 = (f32[4,64,128]{2,1,0:T(8,128)S(1)}, f32[4,64,128]{2,1,0:T(8,128)S(1)}, u32[]{:S(2)}, u32[]{:S(2)}) collective-permute-start(f32[4,64,128]{2,1,0:T(8,128)S(1)} %get-tuple-element.40), channel_id=1, source_target_pairs={{0,3},{1,0},{2,1},{3,2},{4,7},{5,4},{6,5},{7,6},{8,11},{9,8},{10,9... | collective-permute-start | bytes 393224 | tf_op jit(solution)/shard_map/ppermute | solution.py:427
  26.3 10.4 %collective-permute-start.2 = (f32[4,64,128]{2,1,0:T(8,128)S(1)}, f32[4,64,128]{2,1,0:T(8,128)S(1)}, u32[]{:S(2)}, u32[]{:S(2)}) collective-permute-start(f32[4,64,128]{2,1,0:T(8,128)S(1)} %get-tuple-element.41), channel_id=1, source_target_pairs={{0,1},{1,2},{2,3},{3,0},{4,5},{5,6},{6,7},{7,4},{8,9},{9,10},{10,1... | collective-permute-start | bytes 393224 | tf_op jit(solution)/shard_map/ppermute | solution.py:427
  26.3 10.4 %collective-permute-start.3 = (f32[64,128]{1,0:T(8,128)S(1)}, f32[64,128]{1,0:T(8,128)S(1)}, u32[]{:S(2)}, u32[]{:S(2)}) collective-permute-start(f32[64,128]{1,0:T(8,128)S(1)} %copy-done.8), channel_id=1, source_target_pairs={{0,4},{4,0},{1,5},{5,1},{2,6},{6,2},{3,7},{7,3},{8,12},{12,8},{9,1... | collective-permute-start | bytes 98312 | tf_op jit(solution)/shard_map/ppermute | solution.py:427
  27.8 8.9 %collective-permute-start.4 = (f32[4,16,128]{2,1,0:T(8,128)S(1)}, f32[4,16,128]{2,1,0:T(8,128)S(1)}, u32[]{:S(2)}, u32[]{:S(2)}) collective-permute-start(f32[4,16,128]{2,1,0:T(8,128)S(1)} %get-tuple-element.45), channel_id=1, source_target_pairs={{0,24},{8,0},{16,8},{24,16},{1,25},{9,1},{17,9},{25,17},{2,26},{10... | collective-permute-start | bytes 98312 | tf_op jit(solution)/shard_map/ppermute | solution.py:427
  31.2 5.7 %collective-permute-start.5 = (f32[4,16,128]{2,1,0:T(8,128)S(1)}, f32[4,16,128]{2,1,0:T(8,128)S(1)}, u32[]{:S(2)}, u32[]{:S(2)}) collective-permute-start(f32[4,16,128]{2,1,0:T(8,128)S(1)} %get-tuple-element.46), channel_id=1, source_target_pairs={{0,8},{8,16},{16,24},{24,0},{1,9},{9,17},{17,25},{25,1},{2,10},{10... | collective-permute-start | bytes 98312 | tf_op jit(solution)/shard_map/ppermute | solution.py:427
  31.2 4.1 %copy-start.4 = (bf16[512,128]{1,0:T(8,128)(2,1)S(1)}, bf16[512,128]{1,0:T(8,128)(2,1)}, u32[]{:S(2)}) copy-start(bf16[512,128]{1,0:T(8,128)(2,1)} %constant.24.clone.back) | copy-start | bytes 393220
  31.2 4.1 %copy-start.5 = (f32[2,8,256]{2,1,0:T(8,128)S(1)}, f32[2,8,256]{2,1,0:T(8,128)}, u32[]{:S(2)}) copy-start(f32[2,8,256]{2,1,0:T(8,128)} %constant.25.clone.turns) | copy-start | bytes 49156
  36.7 3.6 %copy-start.6 = (f32[4,64,128]{2,1,0:T(8,128)}, f32[4,64,128]{2,1,0:T(8,128)S(1)}, u32[]{:S(2)}) copy-start(f32[4,64,128]{2,1,0:T(8,128)S(1)} %collective-permute-done.1.z_next_from) | copy-start | bytes 393220
  36.7 3.6 %copy-start.7 = (f32[4,64,128]{2,1,0:T(8,128)}, f32[4,64,128]{2,1,0:T(8,128)S(1)}, u32[]{:S(2)}) copy-start(f32[4,64,128]{2,1,0:T(8,128)S(1)} %collective-permute-done.2.z_before_from) | copy-start | bytes 393220
  36.7 3.6 %copy-start.9 = (f32[64,128]{1,0:T(8,128)}, f32[64,128]{1,0:T(8,128)S(1)}, u32[]{:S(2)}) copy-start(f32[64,128]{1,0:T(8,128)S(1)} %collective-permute-done.3.y_next_from.y_before_from) | copy-start | bytes 98308
  36.8 3.6 %copy-start.10 = (f32[4,16,128]{2,1,0:T(8,128)}, f32[4,16,128]{2,1,0:T(8,128)S(1)}, u32[]{:S(2)}) copy-start(f32[4,16,128]{2,1,0:T(8,128)S(1)} %collective-permute-done.4.x_next_from) | copy-start | bytes 98308
  36.9 3.4 %copy-start.11 = (f32[4,16,128]{2,1,0:T(8,128)}, f32[4,16,128]{2,1,0:T(8,128)S(1)}, u32[]{:S(2)}) copy-start(f32[4,16,128]{2,1,0:T(8,128)S(1)} %collective-permute-done.5.x_before_from) | copy-start | bytes 98308
  36.9 9.0 %all-to-all-start.2 = ((f32[8,48,128]{2,1,0:T(8,128)}), f32[8,48,128]{2,1,0:T(8,128)S(1)}, u32[]{:S(2)}, u32[]{:S(2)}) async-start(f32[8,48,128]{2,1,0:T(8,128)} %rows.1), calls=%async_computation.2 | async-start | bytes 393216 | tf_op jit(solution)/shard_map/all_to_all | solution.py:946

commit v9 on v8

--- a/solution.py
+++ b/solution.py
@@ -43,14 +43,31 @@
     return pltpu.with_memory_space_constraint(values, pltpu.HBM)
 
 
-def call(body, name, shape, limit, microseconds, operands, in_hbm=(), scratch=(), refs=(), out_refs=(), aliases=()):
+def call(
+    body,
+    name,
+    shape,
+    limit,
+    microseconds,
+    operands,
+    in_hbm=(),
+    in_vmem=(),
+    scratch=(),
+    refs=(),
+    out_refs=(),
+    aliases=(),
+):
     shapes = shape if isinstance(shape, list) else [shape]
     moved = sum(4 * math.prod(each) for each in shapes)
     moved += sum(x.size * x.dtype.itemsize for x in operands)
     results = pl.pallas_call(
         body,
         out_shape=[
-            pltpu.HBM(each, f32) if i in in_hbm else jax.ShapeDtypeStruct(each, f32)
+            pltpu.HBM(each, f32)
+            if i in in_hbm
+            else pltpu.VMEM(each, bf16)
+            if i in in_vmem
+            else jax.ShapeDtypeStruct(each, f32)
             for i, each in enumerate(shapes)
         ],
         in_specs=[
@@ -312,42 +329,26 @@
     here,
     magnetization_from,
     stiffness_from,
-    z_next_from,
-    z_before_from,
-    x_next_from,
-    x_before_from,
-    y_next_from,
-    y_before_from,
     y_faces_from,
-    out,
-    m,
-    s,
     z_next,
     z_before,
     x_next,
     x_before,
     y_next,
     y_before,
+    out,
+    m,
+    s,
     y_faces,
     loading,
 ):
     depth, across = s.shape[:2]
     chunk = depth // 4
-    pairs = [
-        (y_next_from, y_next),
-        (y_before_from, y_before),
-        (y_faces_from, y_faces),
-        (z_before_from, z_before),
-    ]
+    pairs = [(y_faces_from, y_faces)]
     for k in range(4):
         layers = pl.ds(k * chunk, chunk)
         pairs.append((stiffness_from.at[layers], s.at[layers]))
         pairs.append((magnetization_from.at[:, layers], m.at[:, layers]))
-    pairs += [
-        (z_next_from, z_next),
-        (x_next_from, x_next),
-        (x_before_from, x_before),
-    ]
     loads = begin(loading, pairs)
 
     count_x, count_y, count_z = counts
@@ -362,8 +363,7 @@
     row = lax.broadcasted_iota(jnp.int32, (across, LANES), 0)
     first_lane, last_lane, last_row = lane == 0, lane == LANES - 1, row == across - 1
 
-    for copy in loads[:3]:
-        copy.wait()
+    loads[0].wait()
     own = y_faces[...]
     even = (lane & 1) == 0
     field = (lane + 1 & (LANES - 1)) >> whole_log(2 * depth)
@@ -383,14 +383,14 @@
     sides = spread * (own - halo)
     outer = first_lane | last_lane
 
-    for copy in loads[3:6]:
+    for copy in loads[1:3]:
         copy.wait()
     below_weight = twice_weight(inside(at_z > 0, z_before[3]), s[0])
     below = [below_weight * (z_before[c] - m[c, 0]) for c in range(3)]
     for z in range(depth):
         if z % chunk == chunk - 1:
-            k = 4 + 2 * (z // chunk + 1)
-            for copy in loads[k : k + 2] if z + 1 < depth else loads[k:]:
+            k = 1 + 2 * (z // chunk + 1)
+            for copy in loads[k : k + 2]:
                 copy.wait()
         centre = s[z]
         above = s[z + 1] if z + 1 < depth else inside(at_z < count_z - 1, z_next[3])
@@ -464,17 +464,25 @@
 
 def exchange_of(counts, index, magnetization, stiffness, zy, x):
     z_next, z_before, y_next, y_before, y_faces = zy
-    arrays = (magnetization, stiffness, z_next, z_before, *x, y_next, y_before, y_faces)
+    fetched = (magnetization, stiffness, y_faces)
     return call(
         functools.partial(exchange_kernel, counts),
         "exchange",
         magnetization.shape,
         8,
         5.0,
-        (index, *(from_hbm(array) for array in arrays)),
-        refs=range(1, 10),
-        scratch=[pltpu.VMEM(array.shape, f32) for array in arrays]
-        + [pltpu.SemaphoreType.DMA((15,))],
+        (
+            index,
+            *(from_hbm(array) for array in fetched),
+            z_next,
+            z_before,
+            *x,
+            y_next,
+            y_before,
+        ),
+        refs=(1, 2, 3),
+        scratch=[pltpu.VMEM(array.shape, f32) for array in fetched]
+        + [pltpu.SemaphoreType.DMA((9,))],
     )
 
 
@@ -495,47 +503,6 @@
     return jnp.where(back, -real, real), jnp.where(back, -imag, imag)
 
 
-def add(a, b):
-    return a[0] + b[0], a[1] + b[1]
-
-
-def subtract(a, b):
-    return a[0] - b[0], a[1] - b[1]
-
-
-def eight_points(z, sign):
-    def quarter_turn(a):
-        return (-a[1], a[0]) if sign > 0 else (a[1], -a[0])
-
-    def four_points(p, q, r, s):
-        e, f, g, h = add(p, r), subtract(p, r), add(q, s), quarter_turn(subtract(q, s))
-        return add(e, g), add(f, h), subtract(e, g), subtract(f, h)
-
-    even = four_points(z[0], z[2], z[4], z[6])
-    odd = four_points(z[1], z[3], z[5], z[7])
-    root = math.sqrt(0.5)
-    first, third = add(odd[1], quarter_turn(odd[1])), subtract(quarter_turn(odd[3]), odd[3])
-    odd = (
-        odd[0],
-        (first[0] * root, first[1] * root),
-        quarter_turn(odd[2]),
-        (third[0] * root, third[1] * root),
-    )
-    return [add(a, b) for a, b in zip(even, odd)] + [subtract(a, b) for a, b in zip(even, odd)]
-
-
-def spread_tables(extent, size):
-    step = size // INNER
-    angle = np.outer(np.arange(INNER), np.arange(extent // step)) * (2.0 * math.pi / INNER)
-    cosine, sine = np.cos(angle), np.sin(angle)
-    table = np.block([[cosine, sine], [-sine, cosine]]).astype(np.float32)
-    high = table.astype(ml_dtypes.bfloat16)
-    low = (table - high.astype(np.float32)).astype(ml_dtypes.bfloat16)
-    angle = np.outer(np.arange(step), np.arange(INNER)) * (2.0 * math.pi / size)
-    turns = np.stack([np.cos(angle), np.sin(angle)]).astype(np.float32)
-    return np.concatenate([high, low], axis=1), turns
-
-
 def halves_of(table):
     table = table.astype(np.float32)
     high = table.astype(ml_dtypes.bfloat16)
@@ -552,9 +519,29 @@
     place = np.arange(0, size, INNER)[:, None, None] + i[:, None] - ratio * i[None, :]
     high, low = halves_of(window[place % size] / length)
     tiles = np.stack([high, low], axis=1)
-    angle = np.outer(i, i) * (2.0 * math.pi / length)
-    table = np.stack(halves_of(np.concatenate([np.cos(angle), np.sin(angle)], axis=0)))
-    return tiles, table
+    return tiles, transform_table(length)
+
+
+def transform_table(size):
+    i = np.arange(INNER)
+    angle = np.outer(i, i) * (2.0 * math.pi / size)
+    return np.stack(halves_of(np.concatenate([np.cos(angle), np.sin(angle)], axis=0)))
+
+
+def y_table_of(counts, here, kys, size):
+    group = counts[1] * counts[2]
+    top_rows = LANES // group
+    ky = here[0] * kys + lax.broadcasted_iota(jnp.int32, (kys, LANES), 0)
+    lane = lax.broadcasted_iota(jnp.int32, (kys, LANES), 1)
+    odd = (lane >> whole_log(LANES // 2)) ^ (here[0] & 1)
+    pair = lane >> whole_log(top_rows) & (group // 2 - 1)
+    phases_of = []
+    for h in range(2):
+        y = (2 * pair + odd) * (2 * top_rows) + h * top_rows + (lane & (top_rows - 1))
+        cosine, sine = cos_sin(ky * y & (size - 1), size)
+        phases_of += [cosine, -sine]
+    high, low = split(jnp.concatenate(phases_of, axis=0))
+    return jnp.concatenate([high, low, high], axis=1)
 
 
 def narrow_kernel(top, side, tiles, top_out, side_out):
@@ -584,45 +571,10 @@
         side_out[:, :, :, columns] = totals[part][4 * top_rows :].reshape(2, 2, side_rows, INNER)
 
 
-def regrouping(extent, step, transposed):
-    x = lax.broadcasted_iota(jnp.int32, (extent, extent), int(transposed))
-    place = lax.broadcasted_iota(jnp.int32, (extent, extent), 1 - int(transposed))
-    count = extent // step
-    moved = (x & (step - 1)) * count + (x >> whole_log(step))
-    return jnp.where(moved == place, 1.0, 0.0).astype(bf16)
-
-
 def product(left, right, contracted=0):
     return lax.dot_general(
         left, right, (((1,), (contracted,)), ((), ())), preferred_element_type=f32
     )
-
-
-def regrouped(values, step, transposed):
-    high, low = split(values)
-    rest = (values - high.astype(f32) - low.astype(f32)).astype(bf16)
-    order = regrouping(values.shape[1], step, transposed)
-    return product(high, order) + product(low, order) + product(rest, order)
-
-
-def beside(pieces, count):
-    per = LANES // count
-    lane = lax.broadcasted_iota(jnp.int32, pieces[0].shape, 1)
-    columns = []
-    for start in range(0, len(pieces), per):
-        column = pieces[start]
-        for i in range(1, per):
-            piece = pltpu.roll(pieces[start + i], i * count, 1)
-            column = jnp.where(lane < i * count, column, piece)
-        columns.append(column)
-    return jnp.concatenate(columns, axis=1)
-
-
-def back_product(turned, back):
-    high, low = split(turned)
-    both = product(jnp.concatenate([high, low], axis=0), back)
-    middle = both.shape[0] // 2
-    return both[:middle] + pltpu.roll(both[:middle], LANES // 2, 1) + both[middle:]
 
 
 def dot3_with(values, table):
@@ -664,16 +616,8 @@
     group = count_y * count_z
     top_rows = LANES // group
     half = LANES // 2
-    kys, size = kernel.shape[2], INNER * TILE
-    ky = here[0] * kys + lax.broadcasted_iota(jnp.int32, (kys, LANES), 0)
-    lane = lax.broadcasted_iota(jnp.int32, (kys, LANES), 1)
-    odd = (lane >> whole_log(LANES // 2)) ^ (here[0] & 1)
-    pair = lane >> whole_log(top_rows) & (group // 2 - 1)
-    phases_of = []
-    for h in range(2):
-        y = (2 * pair + odd) * (2 * top_rows) + h * top_rows + (lane & (top_rows - 1))
-        cosine, sine = cos_sin(ky * y & (size - 1), size)
-        phases_of += [cosine, -sine]
+    kys = kernel.shape[2]
+    y_table = y_table_of(counts, here, kys, INNER * TILE)
     for k, part in enumerate((gathered, swapped)):
         for member in range(part.shape[0]):
             g, place = divmod(member, group // 2)
@@ -681,7 +625,8 @@
                 row = (k * group // 2 + place) * top_rows + j * QUAD
                 received[g, row : row + QUAD, :] = part[member, j]
     blocks = [received[g] for g in range(count_x)]
-    mixed = dot3(jnp.concatenate(phases_of, axis=0), split(jnp.concatenate(blocks, axis=1)))
+    high, low = split(jnp.concatenate(blocks, axis=1))
+    mixed = product(y_table, jnp.concatenate([high, high, low], axis=0))
     low_half, high_half = mixed[: 2 * kys], mixed[2 * kys :]
     lane = lax.broadcasted_iota(jnp.int32, (2 * kys, LANES), 1)
     pieces = []
@@ -701,8 +646,9 @@
 
 
 def side_kernel_body(
-    counts, here, gathered, swapped, spectrum, kernel, out, received
+    counts, here, gathered, swapped, spectrum, kernel, later_from, out, later, received, loading
 ):
+    copies = begin(loading, [(later_from, later)])
     count_x, count_y, count_z = counts
     depth_block = (out.shape[1] - 2 * TILE) // 2
     last = gathered.shape[1] - 1
@@ -744,46 +690,45 @@
                     z * depth_block : (z + 1) * depth_block, y * LANES : (y + 1) * LANES
                 ]
     out[:, 0 : 2 * TILE, :] = jnp.zeros((out.shape[0], 2 * TILE, LANES), f32)
-
-
-def rows_kernel(counts, arrived, side, back, turns, out, result, sending):
+    copies[0].wait()
+
+
+def rows_kernel(counts, arrived, side, table, out, result, sending):
     del side
     count_y, count_z = counts[1:]
-    step = turns.shape[1]
+    per_turn = INNER * 2 // LANES
+    step = arrived.shape[0] // per_turn
     size = step * INNER
-    per_turn = arrived.shape[0] // step
     half = LANES // 2
     lane = lax.broadcasted_iota(jnp.int32, (2 * TILE, LANES), 1)
-    halves = []
-    for pair in range(0, per_turn, 2):
-        z = []
-        for b in range(step):
-            first, second = arrived[b * per_turn + pair], arrived[b * per_turn + pair + 1]
+    upper, lower = [], []
+    for b in range(step):
+        parts = ([], [])
+        for pair in range(b * per_turn, (b + 1) * per_turn, 2):
+            first, second = arrived[pair], arrived[pair + 1]
             spectra = (
                 jnp.where(lane < half, first, pltpu.roll(second, half, 1)),
                 jnp.where(lane < half, pltpu.roll(first, half, 1), second),
             )
-            z.append(
-                tuple(
+            for k in range(2):
+                parts[k].append(
                     jnp.concatenate(
                         [spectrum[k * TILE : (k + 1) * TILE] for spectrum in spectra], axis=0
                     )
-                    for k in range(2)
                 )
-            )
-        z = eight_points(z, 1)
-        lanes = slice(pair // 2 * LANES, (pair // 2 + 1) * LANES)
-        for v in range(1, step):
-            cosine, sine = turns[0, v : v + 1, lanes], turns[1, v : v + 1, lanes]
-            a, b = z[v]
-            z[v] = (a * cosine - b * sine, a * sine + b * cosine)
-        halves.append(z)
-    turned = [
-        jnp.concatenate([z[v][k] for k in range(2) for z in halves], axis=1) for v in range(step)
-    ]
-    lines = back_product(jnp.concatenate(turned, axis=0), back[...])
-    pieces = [lines[v * 2 * TILE : (v + 1) * 2 * TILE] for v in range(step)]
-    total = regrouped(beside(pieces, count_y * LANES // step), step, True)
+        real, imag = (jnp.concatenate(part, axis=1) for part in parts)
+        upper.append(jnp.concatenate([real, -imag], axis=1))
+        lower.append(jnp.concatenate([imag, real], axis=1))
+    lines = dot3_with(jnp.concatenate(upper + lower, axis=0), table)
+    y = lax.broadcasted_iota(jnp.int32, (1, INNER), 1) & (step - 1)
+    total = None
+    for b in range(step):
+        cosine, sine = cos_sin(y * b & (step - 1), step)
+        real, imag = (
+            lines[(k * step + b) * 2 * TILE : (k * step + b + 1) * 2 * TILE] for k in range(2)
+        )
+        term = real * cosine - imag * sine if b else real
+        total = term if b == 0 else total + term
     total = total * (1.0 / (size * size))
     for y in range(count_y):
         result[y] = total[:, y * LANES : (y + 1) * LANES]
@@ -878,8 +823,8 @@
     plane_index = here[1] * count_z + here[2]
     index = (here[0] * group + plane_index).reshape(1)
     plane_index = plane_index.reshape(1)
-    back, turns = (jnp.asarray(table) for table in spread_tables(extent, size))
     tiles, table = (jnp.asarray(values) for values in narrow_tables(extent, size))
+    rows_table = jnp.asarray(transform_table(size))
 
     parities = [range(parity, devices, 2) for parity in range(2)]
     sent = residual_blocks(
@@ -889,7 +834,7 @@
         sent, ALL, 0, 0, tiled=True, axis_index_groups=[list(each) for each in parities]
     )
     z_first, z_last, x_first, x_last, y_faces = faces_of(magnetization, stiffness)
-    top_spectra, side_spectra = call(
+    narrowed = call(
         narrow_kernel,
         "narrow",
         [(2, 2, kys, 2 * extent), (2, 2, kzs, 2 * extent)],
@@ -897,9 +842,10 @@
         2.5,
         (top_kernel, side_kernel, tiles),
     )
-    gathered, x_first, x_last, y_faces, top_spectra, side_spectra = lax.optimization_barrier(
-        (gathered, x_first, x_last, y_faces, top_spectra, side_spectra)
-    )
+    gathered, x_first, x_last, y_faces, narrowed = lax.optimization_barrier(
+        (gathered, x_first, x_last, y_faces, narrowed)
+    )
+    top_spectra, side_spectra = narrowed
     swapped = lax.ppermute(gathered, "gz", [(i, i ^ 1) for i in range(count_z)])
     zy = halos_zy(z_first, z_last, y_faces)
 
@@ -915,24 +861,29 @@
     arrived = lax.all_to_all(lines, ALL, 0, 0, tiled=True)
     lines, x_first, x_last = lax.optimization_barrier((lines, x_first, x_last))
     x = halos_x(x_first, x_last)
-    side = call(
+    side, rows_table = call(
         functools.partial(side_kernel_body, counts),
         "side",
-        (group, 2 * TILE + 2 * depth_block, LANES),
+        [(group, 2 * TILE + 2 * depth_block, LANES), rows_table.shape],
         8,
         2.0,
-        (plane_index, gathered, swapped, table, side_spectra),
+        (plane_index, gathered, swapped, table, side_spectra, from_hbm(rows_table)),
         in_hbm=(0,),
-        scratch=[pltpu.VMEM((count_y, count_x * count_z * QUAD, LANES), f32)],
-    )
-    arrived, side = lax.optimization_barrier((arrived, side))
+        in_vmem=(1,),
+        refs=(5,),
+        scratch=[
+            pltpu.VMEM((count_y, count_x * count_z * QUAD, LANES), f32),
+            pltpu.SemaphoreType.DMA((1,)),
+        ],
+    )
+    arrived, side, rows_table = lax.optimization_barrier((arrived, side, rows_table))
     rows = call(
         functools.partial(rows_kernel, counts),
         "rows",
         (group, 2 * TILE + 2 * depth_block, LANES),
         8,
         1.4,
-        (arrived, from_hbm(side), back, turns),
+        (arrived, from_hbm(side), rows_table),
         in_hbm=(0,),
         refs=(1,),
         scratch=[
@@ -942,7 +893,7 @@
         out_refs=(0,),
         aliases={1: 0},
     )
-    rows, zy, x = lax.optimization_barrier((rows, zy, x))
+    _, zy, x = lax.optimization_barrier((rows, zy, x))
     arrived = lax.all_to_all(rows, ("gy", "gz"), 0, 0, tiled=True)
     exchange_grad = exchange_of(counts, index, magnetization, stiffness, zy, x)
     return call(

time: 47.6 us -> 47.1 us (0.989)
  transfers between devices with their start and end apart: 9 -> 9, of which waited for: 5 -> 4; matrix products, arithmetic and copies ran while one was open for 0% -> 0% of each run, Pallas kernels for 27% -> 27%
where the time goes in v9:
time: 47.1 us; the launch traced here: 46.6 us
  starting transfers between devices  21.4 us (45%)
  Pallas kernels  17.4 us (37%)
  waiting for transfers between devices  7.33 us (16%)
    pallas_call x8, Pallas kernels, call(): pl.pallas_call(body, out_shape=[pltpu.HBM(each, f32) if i in in_hbm else...  17.4 us
    all_to_all x1, starting transfers between devices, fast_on_device(): lax.all_to_all(sent, ALL, 0, 0, tiled=True, axis_index_groups=[list(each)...  8.31 us
    ppermute x5, starting transfers between devices, ring(): lax.ppermute(block, axis, [(i, (i + distance) % count) for i in range(cou...  6.42 us
    all_to_all x1, starting transfers between devices, fast_on_device(): arrived = lax.all_to_all(rows, ('gy', 'gz'), 0, 0, tiled=True)  3.4 us
    all_to_all x1, starting transfers between devices, fast_on_device(): arrived = lax.all_to_all(lines, ALL, 0, 0, tiled=True)  3.24 us
    all_to_all x1, waiting for transfers between devices, fast_on_device(): lax.all_to_all(sent, ALL, 0, 0, tiled=True, axis_index_groups=[list(each)...  2.72 us
    all_to_all x1, waiting for transfers between devices, fast_on_device(): arrived = lax.all_to_all(lines, ALL, 0, 0, tiled=True)  2.31 us
    ppermute x1, waiting for transfers between devices, fast_on_device(): swapped = lax.ppermute(gathered, 'gz', [(i, i ^ 1) for i in range(count_z)])  1.39 us
  transfers between devices with their start and end apart: 9, of which 4 were waited for; matrix products, arithmetic and copies ran while one was open for 0% of the time, Pallas kernels for 27%

profile of v9, /device:TPU:0, one launch (start us, length us, event | category | flops | bytes accessed | tf_op | source)
XLA Modules:
  0.0 46.6 jit_solution(17923385682525660046)
XLA Ops:
  0.0 1.5 %pack.1 = f32[16,5,4,128]{3,2,1,0:T(4,128)} custom-call(s32[1]{0:T(128)} %bitcast.1.at_x, f32[32,64]{1,0:T(8,128)} %bitcast.5, f32[16,128]{1,0:T(8,128)} %bitcast.6), custom_call_target="tpu_custom_call" | custom-call | flops 800000000 | bytes 180228 | tf_op jit(solution)/shard_map/pack/pallas_call | solution.py:63
  1.5 8.3 %all-to-all-start = ((f32[16,5,4,128]{3,2,1,0:T(4,128)}), f32[16,5,4,128]{3,2,1,0:T(4,128)S(1)}, u32[]{:S(2)}, u32[]{:S(2)}) async-start(f32[16,5,4,128]{3,2,1,0:T(4,128)} %pack.1), calls=%async_computation | async-start | bytes 327680 | tf_op jit(solution)/shard_map/all_to_all | solution.py:833
  9.8 0.0 copy-start
  9.8 0.0 copy-start.1
  9.8 0.0 copy-start.2
  9.8 2.7 %faces.1 = (f32[4,64,128]{2,1,0:T(8,128)S(1)}, f32[4,64,128]{2,1,0:T(8,128)S(1)}, f32[4,16,128]{2,1,0:T(8,128)S(1)}, f32[4,16,128]{2,1,0:T(8,128)S(1)}, f32[64,128]{1,0:T(8,128)}) custom-call(f32[3,16,64,128]{3,2,1,0:T(8,128)} %magnetization_from.1, f32[16,64,128]{2,1,0:T(8,128)} %stiffness_from.1), custom_call_target="tpu_custom_call" | custom-call | flops 2000000000 | bytes 2457600 | tf_op jit(solution)/shard_map/faces/pallas_call | solution.py:63
  12.5 0.0 copy-done
  12.5 0.0 copy-done.1
  12.5 0.3 copy-done.2
  12.8 2.2 %narrow.1 = (f32[2,2,64,512]{3,2,1,0:T(8,128)S(1)}, f32[2,2,16,512]{3,2,1,0:T(8,128)S(1)}) custom-call(f32[2,2,64,2048]{3,2,1,0:T(8,128)S(1)} %copy-done, f32[2,2,16,2048]{3,2,1,0:T(8,128)S(1)} %copy-done.1, bf16[8,2,256,256]{3,2,1,0:T(8,128)(2,1)S(1)} %copy-done.2), custom_call_target="tpu_custom_call" | custom-call | flops 2500000000 | bytes 5373952 | tf_op jit(solution)/shard_map/narrow/pallas_call | solution.py:63
  15.0 2.7 %all-to-all-done.gathered = f32[16,5,4,128]{3,2,1,0:T(4,128)S(1)} async-done(((f32[16,5,4,128]{3,2,1,0:T(4,128)}), f32[16,5,4,128]{3,2,1,0:T(4,128)S(1)}, u32[]{:S(2)}, u32[]{:S(2)}) %all-to-all-start) | async-done | bytes 163872 | tf_op jit(solution)/shard_map/all_to_all | solution.py:833
  17.7 0.0 collective-permute-start
  17.7 1.4 %collective-permute-done.swapped = f32[16,5,4,128]{3,2,1,0:T(4,128)S(1)} collective-permute-done((f32[16,5,4,128]{3,2,1,0:T(4,128)S(1)}, f32[16,5,4,128]{3,2,1,0:T(4,128)S(1)}, u32[]{:S(2)}, u32[]{:S(2)}) %collective-permute-start) | collective-permute-done | bytes 163872 | tf_op jit(solution)/shard_map/ppermute | solution.py:849
  19.1 2.3 %lines.1 = f32[32,16,128]{2,1,0:T(8,128)} custom-call(s32[1]{0:T(128)} %bitcast.here, f32[16,5,4,128]{3,2,1,0:T(4,128)S(1)} %all-to-all-done.gathered, f32[16,5,4,128]{3,2,1,0:T(4,128)S(1)} %collective-permute-done.swapped, bf16[2,512,256]{2,1,0:T(8,128)(2,1)S(1)} %copy-done.3, f32[2,2,64,512]{3,2,1,0:T(8,128)S(1)} %get-tuple-element.38.kernel), custom_call_target="tpu_custom_call" | custom-call | flops 2200000000 | bytes 1638404 | tf_op jit(solution)/shard_map/lines/pallas_call | solution.py:63
  21.5 3.2 %all-to-all-start.1 = ((f32[32,16,128]{2,1,0:T(8,128)}), f32[32,16,128]{2,1,0:T(8,128)S(1)}, u32[]{:S(2)}, u32[]{:S(2)}) async-start(f32[32,16,128]{2,1,0:T(8,128)} %lines.1), calls=%async_computation.1 | async-start | bytes 524288 | tf_op jit(solution)/shard_map/all_to_all | solution.py:861
  24.7 1.6 %collective-permute-start.1 = (f32[4,64,128]{2,1,0:T(8,128)S(1)}, f32[4,64,128]{2,1,0:T(8,128)S(1)}, u32[]{:S(2)}, u32[]{:S(2)}) collective-permute-start(f32[4,64,128]{2,1,0:T(8,128)S(1)} %get-tuple-element.45), channel_id=1, source_target_pairs={{0,3},{1,0},{2,1},{3,2},{4,7},{5,4},{6,5},{7,6},{8,11},{9,8},{10,9... | collective-permute-start | bytes 393224 | tf_op jit(solution)/shard_map/ppermute | solution.py:427
  26.3 0.0 collective-permute-start.2
  26.3 1.5 %collective-permute-start.3 = (f32[64,128]{1,0:T(8,128)S(1)}, f32[64,128]{1,0:T(8,128)S(1)}, u32[]{:S(2)}, u32[]{:S(2)}) collective-permute-start(f32[64,128]{1,0:T(8,128)S(1)} %copy-done.4), channel_id=1, source_target_pairs={{0,4},{4,0},{1,5},{5,1},{2,6},{6,2},{3,7},{7,3},{8,12},{12,8},{9,1... | collective-permute-start | bytes 98312 | tf_op jit(solution)/shard_map/ppermute | solution.py:427
  27.8 3.4 %collective-permute-start.4 = (f32[4,16,128]{2,1,0:T(8,128)S(1)}, f32[4,16,128]{2,1,0:T(8,128)S(1)}, u32[]{:S(2)}, u32[]{:S(2)}) collective-permute-start(f32[4,16,128]{2,1,0:T(8,128)S(1)} %get-tuple-element.50), channel_id=1, source_target_pairs={{0,24},{8,0},{16,8},{24,16},{1,25},{9,1},{17,9},{25,17},{2,26},{10... | collective-permute-start | bytes 98312 | tf_op jit(solution)/shard_map/ppermute | solution.py:427
  31.1 0.0 collective-permute-start.5
  31.1 1.8 %side.3 = (f32[8,48,128]{2,1,0:T(8,128)}, bf16[2,512,256]{2,1,0:T(8,128)(2,1)S(1)}) custom-call(s32[1]{0:T(128)} %bitcast.4.here, f32[16,5,4,128]{3,2,1,0:T(4,128)S(1)} %all-to-all-done.gathered, f32[16,5,4,128]{3,2,1,0:T(4,128)S(1)} %collective-permute-done.swapped, bf16[2,512,256]{2,1,0:T(8,128)(2,1)S(1)} %copy-done.3, ...), custom_call_target="tpu_custom_call" | custom-call | flops 2000000000 | bytes 2752516 | tf_op jit(solution)/shard_map/side/pallas_call | solution.py:63
  32.9 2.3 %all-to-all-done.1.arrived = f32[32,16,128]{2,1,0:T(8,128)S(1)} async-done(((f32[32,16,128]{2,1,0:T(8,128)}), f32[32,16,128]{2,1,0:T(8,128)S(1)}, u32[]{:S(2)}, u32[]{:S(2)}) %all-to-all-start.1) | async-done | bytes 262176 | tf_op jit(solution)/shard_map/all_to_all | solution.py:861
  35.2 1.2 %rows.1 = f32[8,48,128]{2,1,0:T(8,128)} custom-call(f32[32,16,128]{2,1,0:T(8,128)S(1)} %all-to-all-done.1.arrived, f32[8,48,128]{2,1,0:T(8,128)} %get-tuple-element.43.side, bf16[2,512,256]{2,1,0:T(8,128)(2,1)S(1)} %get-tuple-element.44.table), custom_call_target="tpu_custom_call", output_to_operand_aliasing={{}: (1, {})} | custom-call | flops 1400000000 | bytes 1179648 | tf_op jit(solution)/shard_map/rows/pallas_call | solution.py:63
  36.4 3.4 %all-to-all-start.2 = ((f32[8,48,128]{2,1,0:T(8,128)}), f32[8,48,128]{2,1,0:T(8,128)S(1)}, u32[]{:S(2)}, u32[]{:S(2)}) async-start(f32[8,48,128]{2,1,0:T(8,128)} %rows.1), calls=%async_computation.2 | async-start | bytes 393216 | tf_op jit(solution)/shard_map/all_to_all | solution.py:897
  39.8 0.0 collective-permute-done.1.z_next
  39.8 0.0 collective-permute-done.2.z_before
  39.8 0.0 collective-permute-done.3.y_next.y_before
  39.8 0.0 collective-permute-done.4.x_next
  39.9 0.0 collective-permute-done.5.x_before
  39.9 4.6 %exchange.1.exchange_grad = f32[3,16,64,128]{3,2,1,0:T(8,128)S(1)} custom-call(s32[1]{0:T(128)} %bitcast.here, f32[3,16,64,128]{3,2,1,0:T(8,128)} %magnetization_from.1, f32[16,64,128]{2,1,0:T(8,128)} %stiffness_from.1, f32[64,128]{1,0:T(8,128)} %get-tuple-element.52.y_faces_from, f32[4,64,128]{2,1,0:T(8,128)S(1)} %collective-permute-done.1.z_next, ...), custom_call_target="tpu_custom_call" | custom-call | flops 5000000000 | bytes 4096004 | tf_op jit(solution)/shard_map/exchange/pallas_call | solution.py:63
  44.5 0.9 %all-to-all-done.2.arrived = f32[8,48,128]{2,1,0:T(8,128)S(1)} async-done(((f32[8,48,128]{2,1,0:T(8,128)}), f32[8,48,128]{2,1,0:T(8,128)S(1)}, u32[]{:S(2)}, u32[]{:S(2)}) %all-to-all-start.2) | async-done | bytes 196640 | tf_op jit(solution)/shard_map/all_to_all | solution.py:897
  45.4 1.2 %gradient.1 = f32[3,16,64,128]{3,2,1,0:T(8,128)} custom-call(f32[3,16,64,128]{3,2,1,0:T(8,128)S(1)} %exchange.1.exchange_grad, f32[8,48,128]{2,1,0:T(8,128)S(1)} %all-to-all-done.2.arrived), custom_call_target="tpu_custom_call" | custom-call | flops 1200000000 | bytes 3342336 | tf_op jit(solution)/shard_map/gradient/pallas_call | solution.py:63
  (4 shorter events, 0.0 us)
Async XLA Ops:
  1.5 16.3 %all-to-all-start = ((f32[16,5,4,128]{3,2,1,0:T(4,128)}), f32[16,5,4,128]{3,2,1,0:T(4,128)S(1)}, u32[]{:S(2)}, u32[]{:S(2)}) async-start(f32[16,5,4,128]{3,2,1,0:T(4,128)} %pack.1), calls=%async_computation | async-start | bytes 327680 | tf_op jit(solution)/shard_map/all_to_all | solution.py:833
  9.8 2.7 %copy-start = (f32[2,2,64,2048]{3,2,1,0:T(8,128)S(1)}, f32[2,2,64,2048]{3,2,1,0:T(8,128)}, u32[]{:S(2)}) copy-start(f32[2,2,64,2048]{3,2,1,0:T(8,128)} %top.1) | copy-start | bytes 6291460
  9.8 2.7 %copy-start.1 = (f32[2,2,16,2048]{3,2,1,0:T(8,128)S(1)}, f32[2,2,16,2048]{3,2,1,0:T(8,128)}, u32[]{:S(2)}) copy-start(f32[2,2,16,2048]{3,2,1,0:T(8,128)} %side.2) | copy-start | bytes 1572868
  9.8 3.0 %copy-start.2 = (bf16[8,2,256,256]{3,2,1,0:T(8,128)(2,1)S(1)}, bf16[8,2,256,256]{3,2,1,0:T(8,128)(2,1)}, u32[]{:S(2)}) copy-start(bf16[8,2,256,256]{3,2,1,0:T(8,128)(2,1)} %constant.22.clone.tiles) | copy-start | bytes 6291460
  12.8 6.3 %copy-start.3 = (bf16[2,512,256]{2,1,0:T(8,128)(2,1)S(1)}, bf16[2,512,256]{2,1,0:T(8,128)(2,1)}, u32[]{:S(2)}) copy-start(bf16[2,512,256]{2,1,0:T(8,128)(2,1)} %constant.23.clone.table.spectrum) | copy-start | bytes 1572868
  17.7 1.4 %collective-permute-start = (f32[16,5,4,128]{3,2,1,0:T(4,128)S(1)}, f32[16,5,4,128]{3,2,1,0:T(4,128)S(1)}, u32[]{:S(2)}, u32[]{:S(2)}) collective-permute-start(f32[16,5,4,128]{3,2,1,0:T(4,128)S(1)} %all-to-all-done.gathered), channel_id=1, source_target_pairs={{0,1},{1,0},{2,3},{3,2},{4,5},{5,4},{6,7},{7,6},{8,9},{9,8},{10,11... | collective-permute-start | bytes 491528 | tf_op jit(solution)/shard_map/ppermute | solution.py:849
  19.1 7.2 %copy-start.4 = (f32[64,128]{1,0:T(8,128)S(1)}, f32[64,128]{1,0:T(8,128)}, u32[]{:S(2)}) copy-start(f32[64,128]{1,0:T(8,128)} %get-tuple-element.52.y_faces_from) | copy-start | bytes 98308
  21.5 13.8 %all-to-all-start.1 = ((f32[32,16,128]{2,1,0:T(8,128)}), f32[32,16,128]{2,1,0:T(8,128)S(1)}, u32[]{:S(2)}, u32[]{:S(2)}) async-start(f32[32,16,128]{2,1,0:T(8,128)} %lines.1), calls=%async_computation.1 | async-start | bytes 524288 | tf_op jit(solution)/shard_map/all_to_all | solution.py:861
  24.7 15.1 %collective-permute-start.1 = (f32[4,64,128]{2,1,0:T(8,128)S(1)}, f32[4,64,128]{2,1,0:T(8,128)S(1)}, u32[]{:S(2)}, u32[]{:S(2)}) collective-permute-start(f32[4,64,128]{2,1,0:T(8,128)S(1)} %get-tuple-element.45), channel_id=1, source_target_pairs={{0,3},{1,0},{2,1},{3,2},{4,7},{5,4},{6,5},{7,6},{8,11},{9,8},{10,9... | collective-permute-start | bytes 393224 | tf_op jit(solution)/shard_map/ppermute | solution.py:427
  26.3 13.5 %collective-permute-start.2 = (f32[4,64,128]{2,1,0:T(8,128)S(1)}, f32[4,64,128]{2,1,0:T(8,128)S(1)}, u32[]{:S(2)}, u32[]{:S(2)}) collective-permute-start(f32[4,64,128]{2,1,0:T(8,128)S(1)} %get-tuple-element.46), channel_id=1, source_target_pairs={{0,1},{1,2},{2,3},{3,0},{4,5},{5,6},{6,7},{7,4},{8,9},{9,10},{10,1... | collective-permute-start | bytes 393224 | tf_op jit(solution)/shard_map/ppermute | solution.py:427
  26.3 13.5 %collective-permute-start.3 = (f32[64,128]{1,0:T(8,128)S(1)}, f32[64,128]{1,0:T(8,128)S(1)}, u32[]{:S(2)}, u32[]{:S(2)}) collective-permute-start(f32[64,128]{1,0:T(8,128)S(1)} %copy-done.4), channel_id=1, source_target_pairs={{0,4},{4,0},{1,5},{5,1},{2,6},{6,2},{3,7},{7,3},{8,12},{12,8},{9,1... | collective-permute-start | bytes 98312 | tf_op jit(solution)/shard_map/ppermute | solution.py:427
  27.8 12.1 %collective-permute-start.4 = (f32[4,16,128]{2,1,0:T(8,128)S(1)}, f32[4,16,128]{2,1,0:T(8,128)S(1)}, u32[]{:S(2)}, u32[]{:S(2)}) collective-permute-start(f32[4,16,128]{2,1,0:T(8,128)S(1)} %get-tuple-element.50), channel_id=1, source_target_pairs={{0,24},{8,0},{16,8},{24,16},{1,25},{9,1},{17,9},{25,17},{2,26},{10... | collective-permute-start | bytes 98312 | tf_op jit(solution)/shard_map/ppermute | solution.py:427
  31.1 8.7 %collective-permute-start.5 = (f32[4,16,128]{2,1,0:T(8,128)S(1)}, f32[4,16,128]{2,1,0:T(8,128)S(1)}, u32[]{:S(2)}, u32[]{:S(2)}) collective-permute-start(f32[4,16,128]{2,1,0:T(8,128)S(1)} %get-tuple-element.51), channel_id=1, source_target_pairs={{0,8},{8,16},{16,24},{24,0},{1,9},{9,17},{17,25},{25,1},{2,10},{10... | collective-permute-start | bytes 98312 | tf_op jit(solution)/shard_map/ppermute | solution.py:427
  36.4 9.0 %all-to-all-start.2 = ((f32[8,48,128]{2,1,0:T(8,128)}), f32[8,48,128]{2,1,0:T(8,128)S(1)}, u32[]{:S(2)}, u32[]{:S(2)}) async-start(f32[8,48,128]{2,1,0:T(8,128)} %rows.1), calls=%async_computation.2 | async-start | bytes 393216 | tf_op jit(solution)/shard_map/all_to_all | solution.py:897

commit v10 on v9

--- a/solution.py
+++ b/solution.py
@@ -646,11 +646,22 @@
 
 
 def side_kernel_body(
-    counts, here, gathered, swapped, spectrum, kernel, later_from, out, later, received, loading
+    counts,
+    here,
+    gathered,
+    swapped,
+    spectrum,
+    kernel,
+    later_from,
+    mine,
+    other,
+    later,
+    received,
+    loading,
 ):
     copies = begin(loading, [(later_from, later)])
     count_x, count_y, count_z = counts
-    depth_block = (out.shape[1] - 2 * TILE) // 2
+    depth_block = mine.shape[1]
     last = gathered.shape[1] - 1
     kzs, length = kernel.shape[2], INNER * TILE
     size = kzs * count_y * count_z
@@ -680,22 +691,22 @@
     column = lax.broadcasted_iota(jnp.int32, (rows, 2 * kzs), 1)
     cosine, sine = cos_sin((here[0] * kzs + (column & (kzs - 1))) * z & (size - 1), size)
     table = jnp.where(column < kzs, cosine, -sine) * (1.0 / (size * length))
-    for c in range(2):
-        part = slice(c * kzs, (c + 1) * kzs)
-        image = dot3(table, split(jnp.concatenate([real[part], imag[part]], axis=0)))
+    even = (here[0] & 1) == 0
+    lines = [jnp.concatenate([part[:kzs] for part in (real, imag)], axis=0)]
+    lines.append(jnp.concatenate([part[kzs:] for part in (real, imag)], axis=0))
+    for out, (a, b) in ((mine, lines), (other, lines[::-1])):
+        image = dot3(table, split(jnp.where(even, a, b)))
         for y in range(count_y):
             for z in range(count_z):
-                start = 2 * TILE + c * depth_block
-                out[y * count_z + z, start : start + depth_block, :] = image[
+                out[y * count_z + z] = image[
                     z * depth_block : (z + 1) * depth_block, y * LANES : (y + 1) * LANES
                 ]
-    out[:, 0 : 2 * TILE, :] = jnp.zeros((out.shape[0], 2 * TILE, LANES), f32)
     copies[0].wait()
 
 
-def rows_kernel(counts, arrived, side, table, out, result, sending):
-    del side
+def rows_kernel(counts, arrived, mine, other, table, out):
     count_y, count_z = counts[1:]
+    out[:, 2 * TILE :, :] = mine[...] + other[...]
     per_turn = INNER * 2 // LANES
     step = arrived.shape[0] // per_turn
     size = step * INNER
@@ -731,17 +742,8 @@
         total = term if b == 0 else total + term
     total = total * (1.0 / (size * size))
     for y in range(count_y):
-        result[y] = total[:, y * LANES : (y + 1) * LANES]
-    sends = begin(
-        sending,
-        [
-            (result.at[y], out.at[y * count_z + z, 0 : 2 * TILE, :])
-            for y in range(count_y)
-            for z in range(count_z)
-        ],
-    )
-    for copy in sends:
-        copy.wait()
+        for z in range(count_z):
+            out[y * count_z + z, 0 : 2 * TILE, :] = total[:, y * LANES : (y + 1) * LANES]
 
 
 def sum_kernel(exchange_grad, arrived, out, result, sending):
@@ -757,10 +759,9 @@
         return arrived[:, c * TILE : (c + 1) * TILE, :].reshape(group * TILE, LANES)
 
     def side(c):
-        rows = slice(2 * TILE + c * depth, 2 * TILE + (c + 1) * depth)
-        total = arrived[0, rows, :]
-        for p in range(1, group):
-            total = total + arrived[p, rows, :]
+        total = arrived[c, 2 * TILE :, :]
+        for p in range(c + 2, group, 2):
+            total = total + arrived[p, 2 * TILE :, :]
         return total
 
     image = top(0)
@@ -861,37 +862,31 @@
     arrived = lax.all_to_all(lines, ALL, 0, 0, tiled=True)
     lines, x_first, x_last = lax.optimization_barrier((lines, x_first, x_last))
     x = halos_x(x_first, x_last)
-    side, rows_table = call(
+    mine, other, rows_table = call(
         functools.partial(side_kernel_body, counts),
         "side",
-        [(group, 2 * TILE + 2 * depth_block, LANES), rows_table.shape],
+        [(group, depth_block, LANES), (group, depth_block, LANES), rows_table.shape],
         8,
         2.0,
         (plane_index, gathered, swapped, table, side_spectra, from_hbm(rows_table)),
-        in_hbm=(0,),
-        in_vmem=(1,),
+        in_vmem=(2,),
         refs=(5,),
         scratch=[
             pltpu.VMEM((count_y, count_x * count_z * QUAD, LANES), f32),
             pltpu.SemaphoreType.DMA((1,)),
         ],
     )
-    arrived, side, rows_table = lax.optimization_barrier((arrived, side, rows_table))
+    other = lax.ppermute(other, "gz", [(i, i ^ 1) for i in range(count_z)])
+    arrived, mine, other, rows_table = lax.optimization_barrier(
+        (arrived, mine, other, rows_table)
+    )
     rows = call(
         functools.partial(rows_kernel, counts),
         "rows",
-        (group, 2 * TILE + 2 * depth_block, LANES),
+        (group, 2 * TILE + depth_block, LANES),
         8,
-        1.4,
-        (arrived, from_hbm(side), rows_table),
-        in_hbm=(0,),
-        refs=(1,),
-        scratch=[
-            pltpu.VMEM((count_y, 2 * TILE, LANES), f32),
-            pltpu.SemaphoreType.DMA((group,)),
-        ],
-        out_refs=(0,),
-        aliases={1: 0},
+        1.1,
+        (arrived, mine, other, rows_table),
     )
     _, zy, x = lax.optimization_barrier((rows, zy, x))
     arrived = lax.all_to_all(rows, ("gy", "gz"), 0, 0, tiled=True)

time: 47.1 us -> 46.6 us (0.989)
  Pallas kernels: 17.4 us -> 16.6 us
    pallas_call x8, Pallas kernels: 17.4 us -> 16.6 us  [call(): pl.pallas_call(body, out_shape=[pltpu.HBM(each, f32) if i in in_hbm else...]
    all_to_all x1, waiting for transfers between devices: 0.89 us -> 0.42 us  [fast_on_device(): arrived = lax.all_to_all(rows, ('gy', 'gz'), 0, 0, tiled=True)]
  transfers between devices with their start and end apart: 9 -> 10, of which waited for: 4 -> 4; matrix products, arithmetic and copies ran while one was open for 0% -> 0% of each run, Pallas kernels for 27% -> 25%
where the time goes in v10:
time: 46.6 us; the launch traced here: 46 us
  starting transfers between devices  21.7 us (47%)
  Pallas kernels  16.6 us (36%)
  waiting for transfers between devices  7.19 us (15%)
    pallas_call x8, Pallas kernels, call(): pl.pallas_call(body, out_shape=[pltpu.HBM(each, f32) if i in in_hbm else...  16.6 us
    all_to_all x1, starting transfers between devices, fast_on_device(): lax.all_to_all(sent, ALL, 0, 0, tiled=True, axis_index_groups=[list(each)...  8.31 us
    ppermute x5, starting transfers between devices, ring(): lax.ppermute(block, axis, [(i, (i + distance) % count) for i in range(cou...  6.48 us
    all_to_all x1, starting transfers between devices, fast_on_device(): arrived = lax.all_to_all(rows, ('gy', 'gz'), 0, 0, tiled=True)  3.37 us
    all_to_all x1, starting transfers between devices, fast_on_device(): arrived = lax.all_to_all(lines, ALL, 0, 0, tiled=True)  3.24 us
    all_to_all x1, waiting for transfers between devices, fast_on_device(): lax.all_to_all(sent, ALL, 0, 0, tiled=True, axis_index_groups=[list(each)...  2.72 us
    all_to_all x1, waiting for transfers between devices, fast_on_device(): arrived = lax.all_to_all(lines, ALL, 0, 0, tiled=True)  2.64 us
    ppermute x1, waiting for transfers between devices, fast_on_device(): swapped = lax.ppermute(gathered, 'gz', [(i, i ^ 1) for i in range(count_z)])  1.39 us
  transfers between devices with their start and end apart: 10, of which 4 were waited for; matrix products, arithmetic and copies ran while one was open for 0% of the time, Pallas kernels for 25%

profile of v10, /device:TPU:0, one launch (start us, length us, event | category | flops | bytes accessed | tf_op | source)
XLA Modules:
  0.0 46.0 jit_solution(4468331461802774712)
XLA Ops:
  0.0 1.5 %pack.1 = f32[16,5,4,128]{3,2,1,0:T(4,128)} custom-call(s32[1]{0:T(128)} %bitcast.1.at_x, f32[32,64]{1,0:T(8,128)} %bitcast.5, f32[16,128]{1,0:T(8,128)} %bitcast.6), custom_call_target="tpu_custom_call" | custom-call | flops 800000000 | bytes 180228 | tf_op jit(solution)/shard_map/pack/pallas_call | solution.py:63
  1.5 8.3 %all-to-all-start = ((f32[16,5,4,128]{3,2,1,0:T(4,128)}), f32[16,5,4,128]{3,2,1,0:T(4,128)S(1)}, u32[]{:S(2)}, u32[]{:S(2)}) async-start(f32[16,5,4,128]{3,2,1,0:T(4,128)} %pack.1), calls=%async_computation | async-start | bytes 327680 | tf_op jit(solution)/shard_map/all_to_all | solution.py:834
  9.8 0.0 copy-start
  9.8 0.0 copy-start.1
  9.8 0.0 copy-start.2
  9.8 2.7 %faces.1 = (f32[4,64,128]{2,1,0:T(8,128)S(1)}, f32[4,64,128]{2,1,0:T(8,128)S(1)}, f32[4,16,128]{2,1,0:T(8,128)S(1)}, f32[4,16,128]{2,1,0:T(8,128)S(1)}, f32[64,128]{1,0:T(8,128)}) custom-call(f32[3,16,64,128]{3,2,1,0:T(8,128)} %magnetization_from.1, f32[16,64,128]{2,1,0:T(8,128)} %stiffness_from.1), custom_call_target="tpu_custom_call" | custom-call | flops 2000000000 | bytes 2457600 | tf_op jit(solution)/shard_map/faces/pallas_call | solution.py:63
  12.5 0.3 copy-done.2
  12.8 2.2 %narrow.1 = (f32[2,2,64,512]{3,2,1,0:T(8,128)S(1)}, f32[2,2,16,512]{3,2,1,0:T(8,128)S(1)}) custom-call(f32[2,2,64,2048]{3,2,1,0:T(8,128)S(1)} %copy-done, f32[2,2,16,2048]{3,2,1,0:T(8,128)S(1)} %copy-done.1, bf16[8,2,256,256]{3,2,1,0:T(8,128)(2,1)S(1)} %copy-done.2), custom_call_target="tpu_custom_call" | custom-call | flops 2500000000 | bytes 5373952 | tf_op jit(solution)/shard_map/narrow/pallas_call | solution.py:63
  15.0 2.7 %all-to-all-done.gathered = f32[16,5,4,128]{3,2,1,0:T(4,128)S(1)} async-done(((f32[16,5,4,128]{3,2,1,0:T(4,128)}), f32[16,5,4,128]{3,2,1,0:T(4,128)S(1)}, u32[]{:S(2)}, u32[]{:S(2)}) %all-to-all-start) | async-done | bytes 163872 | tf_op jit(solution)/shard_map/all_to_all | solution.py:834
  17.7 0.0 collective-permute-start
  17.7 1.4 %collective-permute-done.swapped = f32[16,5,4,128]{3,2,1,0:T(4,128)S(1)} collective-permute-done((f32[16,5,4,128]{3,2,1,0:T(4,128)S(1)}, f32[16,5,4,128]{3,2,1,0:T(4,128)S(1)}, u32[]{:S(2)}, u32[]{:S(2)}) %collective-permute-start) | collective-permute-done | bytes 163872 | tf_op jit(solution)/shard_map/ppermute | solution.py:850
  19.1 2.3 %lines.1 = f32[32,16,128]{2,1,0:T(8,128)} custom-call(s32[1]{0:T(128)} %bitcast.here, f32[16,5,4,128]{3,2,1,0:T(4,128)S(1)} %all-to-all-done.gathered, f32[16,5,4,128]{3,2,1,0:T(4,128)S(1)} %collective-permute-done.swapped, bf16[2,512,256]{2,1,0:T(8,128)(2,1)S(1)} %copy-done.3, f32[2,2,64,512]{3,2,1,0:T(8,128)S(1)} %get-tuple-element.40.kernel), custom_call_target="tpu_custom_call" | custom-call | flops 2200000000 | bytes 1638404 | tf_op jit(solution)/shard_map/lines/pallas_call | solution.py:63
  21.5 3.2 %all-to-all-start.1 = ((f32[32,16,128]{2,1,0:T(8,128)}), f32[32,16,128]{2,1,0:T(8,128)S(1)}, u32[]{:S(2)}, u32[]{:S(2)}) async-start(f32[32,16,128]{2,1,0:T(8,128)} %lines.1), calls=%async_computation.1 | async-start | bytes 524288 | tf_op jit(solution)/shard_map/all_to_all | solution.py:862
  24.7 1.1 %side.3 = (f32[8,16,128]{2,1,0:T(8,128)S(1)}, f32[8,16,128]{2,1,0:T(8,128)S(1)}, bf16[2,512,256]{2,1,0:T(8,128)(2,1)S(1)}) custom-call(s32[1]{0:T(128)} %bitcast.4.here, f32[16,5,4,128]{3,2,1,0:T(4,128)S(1)} %all-to-all-done.gathered, f32[16,5,4,128]{3,2,1,0:T(4,128)S(1)} %collective-permute-done.swapped, bf16[2,512,256]{2,1,0:T(8,128)(2,1)S(1)} %copy-done.3, ...), custom_call_target="tpu_custom_call" | custom-call | flops 2000000000 | bytes 2686980 | tf_op jit(solution)/shard_map/side/pallas_call | solution.py:63
  25.8 0.3 collective-permute-start.1
  26.1 1.6 %collective-permute-start.2 = (f32[4,64,128]{2,1,0:T(8,128)S(1)}, f32[4,64,128]{2,1,0:T(8,128)S(1)}, u32[]{:S(2)}, u32[]{:S(2)}) collective-permute-start(f32[4,64,128]{2,1,0:T(8,128)S(1)} %get-tuple-element.49), channel_id=1, source_target_pairs={{0,3},{1,0},{2,1},{3,2},{4,7},{5,4},{6,5},{7,6},{8,11},{9,8},{10,9... | collective-permute-start | bytes 393224 | tf_op jit(solution)/shard_map/ppermute | solution.py:427
  27.7 0.0 collective-permute-start.3
  27.8 1.5 %collective-permute-start.4 = (f32[64,128]{1,0:T(8,128)S(1)}, f32[64,128]{1,0:T(8,128)S(1)}, u32[]{:S(2)}, u32[]{:S(2)}) collective-permute-start(f32[64,128]{1,0:T(8,128)S(1)} %copy-done.4), channel_id=1, source_target_pairs={{0,4},{4,0},{1,5},{5,1},{2,6},{6,2},{3,7},{7,3},{8,12},{12,8},{9,1... | collective-permute-start | bytes 98312 | tf_op jit(solution)/shard_map/ppermute | solution.py:427
  29.2 3.4 %collective-permute-start.5 = (f32[4,16,128]{2,1,0:T(8,128)S(1)}, f32[4,16,128]{2,1,0:T(8,128)S(1)}, u32[]{:S(2)}, u32[]{:S(2)}) collective-permute-start(f32[4,16,128]{2,1,0:T(8,128)S(1)} %get-tuple-element.54), channel_id=1, source_target_pairs={{0,24},{8,0},{16,8},{24,16},{1,25},{9,1},{17,9},{25,17},{2,26},{10... | collective-permute-start | bytes 98312 | tf_op jit(solution)/shard_map/ppermute | solution.py:427
  32.6 0.0 collective-permute-done.1.other
  32.6 0.0 collective-permute-start.6
  32.6 2.6 %all-to-all-done.1.arrived = f32[32,16,128]{2,1,0:T(8,128)S(1)} async-done(((f32[32,16,128]{2,1,0:T(8,128)}), f32[32,16,128]{2,1,0:T(8,128)S(1)}, u32[]{:S(2)}, u32[]{:S(2)}) %all-to-all-start.1) | async-done | bytes 262176 | tf_op jit(solution)/shard_map/all_to_all | solution.py:862
  35.2 1.1 %rows.1 = f32[8,32,128]{2,1,0:T(8,128)} custom-call(f32[32,16,128]{2,1,0:T(8,128)S(1)} %all-to-all-done.1.arrived, f32[8,16,128]{2,1,0:T(8,128)S(1)} %get-tuple-element.46.mine, f32[8,16,128]{2,1,0:T(8,128)S(1)} %collective-permute-done.1.other, bf16[2,512,256]{2,1,0:T(8,128)(2,1)S(1)} %get-tuple-element.48.table), custom_call_target="tpu_custom_call" | custom-call | flops 1100000000 | bytes 1048576 | tf_op jit(solution)/shard_map/rows/pallas_call | solution.py:63
  36.3 3.4 %all-to-all-start.2 = ((f32[8,32,128]{2,1,0:T(8,128)}), f32[8,32,128]{2,1,0:T(8,128)S(1)}, u32[]{:S(2)}, u32[]{:S(2)}) async-start(f32[8,32,128]{2,1,0:T(8,128)} %rows.1), calls=%async_computation.2 | async-start | bytes 262144 | tf_op jit(solution)/shard_map/all_to_all | solution.py:892
  39.7 0.0 collective-permute-done.2.z_next
  39.7 0.0 collective-permute-done.3.z_before
  39.7 0.0 collective-permute-done.4.y_next.y_before
  39.7 0.0 collective-permute-done.5.x_next
  39.8 0.0 collective-permute-done.6.x_before
  39.8 4.6 %exchange.1.exchange_grad = f32[3,16,64,128]{3,2,1,0:T(8,128)S(1)} custom-call(s32[1]{0:T(128)} %bitcast.here, f32[3,16,64,128]{3,2,1,0:T(8,128)} %magnetization_from.1, f32[16,64,128]{2,1,0:T(8,128)} %stiffness_from.1, f32[64,128]{1,0:T(8,128)} %get-tuple-element.56.y_faces_from, f32[4,64,128]{2,1,0:T(8,128)S(1)} %collective-permute-done.2.z_next, ...), custom_call_target="tpu_custom_call" | custom-call | flops 5000000000 | bytes 4096004 | tf_op jit(solution)/shard_map/exchange/pallas_call | solution.py:63
  44.4 0.4 all-to-all-done.2.arrived
  44.8 1.2 %gradient.1 = f32[3,16,64,128]{3,2,1,0:T(8,128)} custom-call(f32[3,16,64,128]{3,2,1,0:T(8,128)S(1)} %exchange.1.exchange_grad, f32[8,32,128]{2,1,0:T(8,128)S(1)} %all-to-all-done.2.arrived), custom_call_target="tpu_custom_call" | custom-call | flops 1200000000 | bytes 3276800 | tf_op jit(solution)/shard_map/gradient/pallas_call | solution.py:63
  (6 shorter events, 0.0 us)
Async XLA Ops:
  1.5 16.3 %all-to-all-start = ((f32[16,5,4,128]{3,2,1,0:T(4,128)}), f32[16,5,4,128]{3,2,1,0:T(4,128)S(1)}, u32[]{:S(2)}, u32[]{:S(2)}) async-start(f32[16,5,4,128]{3,2,1,0:T(4,128)} %pack.1), calls=%async_computation | async-start | bytes 327680 | tf_op jit(solution)/shard_map/all_to_all | solution.py:834
  9.8 2.7 %copy-start = (f32[2,2,64,2048]{3,2,1,0:T(8,128)S(1)}, f32[2,2,64,2048]{3,2,1,0:T(8,128)}, u32[]{:S(2)}) copy-start(f32[2,2,64,2048]{3,2,1,0:T(8,128)} %top.1) | copy-start | bytes 6291460
  9.8 2.7 %copy-start.1 = (f32[2,2,16,2048]{3,2,1,0:T(8,128)S(1)}, f32[2,2,16,2048]{3,2,1,0:T(8,128)}, u32[]{:S(2)}) copy-start(f32[2,2,16,2048]{3,2,1,0:T(8,128)} %side.2) | copy-start | bytes 1572868
  9.8 3.0 %copy-start.2 = (bf16[8,2,256,256]{3,2,1,0:T(8,128)(2,1)S(1)}, bf16[8,2,256,256]{3,2,1,0:T(8,128)(2,1)}, u32[]{:S(2)}) copy-start(bf16[8,2,256,256]{3,2,1,0:T(8,128)(2,1)} %constant.22.clone.tiles) | copy-start | bytes 6291460
  12.8 6.3 %copy-start.3 = (bf16[2,512,256]{2,1,0:T(8,128)(2,1)S(1)}, bf16[2,512,256]{2,1,0:T(8,128)(2,1)}, u32[]{:S(2)}) copy-start(bf16[2,512,256]{2,1,0:T(8,128)(2,1)} %constant.23.clone.table.spectrum) | copy-start | bytes 1572868
  17.7 1.4 %collective-permute-start = (f32[16,5,4,128]{3,2,1,0:T(4,128)S(1)}, f32[16,5,4,128]{3,2,1,0:T(4,128)S(1)}, u32[]{:S(2)}, u32[]{:S(2)}) collective-permute-start(f32[16,5,4,128]{3,2,1,0:T(4,128)S(1)} %all-to-all-done.gathered), channel_id=1, source_target_pairs={{0,1},{1,0},{2,3},{3,2},{4,5},{5,4},{6,7},{7,6},{8,9},{9,8},{10,11... | collective-permute-start | bytes 491528 | tf_op jit(solution)/shard_map/ppermute | solution.py:850
  21.5 13.8 %all-to-all-start.1 = ((f32[32,16,128]{2,1,0:T(8,128)}), f32[32,16,128]{2,1,0:T(8,128)S(1)}, u32[]{:S(2)}, u32[]{:S(2)}) async-start(f32[32,16,128]{2,1,0:T(8,128)} %lines.1), calls=%async_computation.1 | async-start | bytes 524288 | tf_op jit(solution)/shard_map/all_to_all | solution.py:862
  24.7 3.0 %copy-start.4 = (f32[64,128]{1,0:T(8,128)S(1)}, f32[64,128]{1,0:T(8,128)}, u32[]{:S(2)}) copy-start(f32[64,128]{1,0:T(8,128)} %get-tuple-element.56.y_faces_from) | copy-start | bytes 98308
  25.8 6.8 %collective-permute-start.1 = (f32[8,16,128]{2,1,0:T(8,128)S(1)}, f32[8,16,128]{2,1,0:T(8,128)S(1)}, u32[]{:S(2)}, u32[]{:S(2)}) collective-permute-start(f32[8,16,128]{2,1,0:T(8,128)S(1)} %get-tuple-element.43), channel_id=1, source_target_pairs={{0,1},{1,0},{2,3},{3,2},{4,5},{5,4},{6,7},{7,6},{8,9},{9,8},{10,11... | collective-permute-start | bytes 196616 | tf_op jit(solution)/shard_map/ppermute | solution.py:879
  26.1 13.6 %collective-permute-start.2 = (f32[4,64,128]{2,1,0:T(8,128)S(1)}, f32[4,64,128]{2,1,0:T(8,128)S(1)}, u32[]{:S(2)}, u32[]{:S(2)}) collective-permute-start(f32[4,64,128]{2,1,0:T(8,128)S(1)} %get-tuple-element.49), channel_id=1, source_target_pairs={{0,3},{1,0},{2,1},{3,2},{4,7},{5,4},{6,5},{7,6},{8,11},{9,8},{10,9... | collective-permute-start | bytes 393224 | tf_op jit(solution)/shard_map/ppermute | solution.py:427
  27.7 12.0 %collective-permute-start.3 = (f32[4,64,128]{2,1,0:T(8,128)S(1)}, f32[4,64,128]{2,1,0:T(8,128)S(1)}, u32[]{:S(2)}, u32[]{:S(2)}) collective-permute-start(f32[4,64,128]{2,1,0:T(8,128)S(1)} %get-tuple-element.50), channel_id=1, source_target_pairs={{0,1},{1,2},{2,3},{3,0},{4,5},{5,6},{6,7},{7,4},{8,9},{9,10},{10,1... | collective-permute-start | bytes 393224 | tf_op jit(solution)/shard_map/ppermute | solution.py:427
  27.8 12.0 %collective-permute-start.4 = (f32[64,128]{1,0:T(8,128)S(1)}, f32[64,128]{1,0:T(8,128)S(1)}, u32[]{:S(2)}, u32[]{:S(2)}) collective-permute-start(f32[64,128]{1,0:T(8,128)S(1)} %copy-done.4), channel_id=1, source_target_pairs={{0,4},{4,0},{1,5},{5,1},{2,6},{6,2},{3,7},{7,3},{8,12},{12,8},{9,1... | collective-permute-start | bytes 98312 | tf_op jit(solution)/shard_map/ppermute | solution.py:427
  29.2 10.5 %collective-permute-start.5 = (f32[4,16,128]{2,1,0:T(8,128)S(1)}, f32[4,16,128]{2,1,0:T(8,128)S(1)}, u32[]{:S(2)}, u32[]{:S(2)}) collective-permute-start(f32[4,16,128]{2,1,0:T(8,128)S(1)} %get-tuple-element.54), channel_id=1, source_target_pairs={{0,24},{8,0},{16,8},{24,16},{1,25},{9,1},{17,9},{25,17},{2,26},{10... | collective-permute-start | bytes 98312 | tf_op jit(solution)/shard_map/ppermute | solution.py:427
  32.6 7.2 %collective-permute-start.6 = (f32[4,16,128]{2,1,0:T(8,128)S(1)}, f32[4,16,128]{2,1,0:T(8,128)S(1)}, u32[]{:S(2)}, u32[]{:S(2)}) collective-permute-start(f32[4,16,128]{2,1,0:T(8,128)S(1)} %get-tuple-element.55), channel_id=1, source_target_pairs={{0,8},{8,16},{16,24},{24,0},{1,9},{9,17},{17,25},{25,1},{2,10},{10... | collective-permute-start | bytes 98312 | tf_op jit(solution)/shard_map/ppermute | solution.py:427
  36.3 8.5 %all-to-all-start.2 = ((f32[8,32,128]{2,1,0:T(8,128)}), f32[8,32,128]{2,1,0:T(8,128)S(1)}, u32[]{:S(2)}, u32[]{:S(2)}) async-start(f32[8,32,128]{2,1,0:T(8,128)} %rows.1), calls=%async_computation.2 | async-start | bytes 262144 | tf_op jit(solution)/shard_map/all_to_all | solution.py:892

commit v11 on v10

--- a/solution.py
+++ b/solution.py
@@ -528,6 +528,10 @@
     return np.stack(halves_of(np.concatenate([np.cos(angle), np.sin(angle)], axis=0)))
 
 
+def pair_order(planes, per_plane):
+    return [plane * per_plane + p for p in range(per_plane) for plane in reversed(range(planes))]
+
+
 def y_table_of(counts, here, kys, size):
     group = counts[1] * counts[2]
     top_rows = LANES // group
@@ -618,12 +622,13 @@
     half = LANES // 2
     kys = kernel.shape[2]
     y_table = y_table_of(counts, here, kys, INNER * TILE)
+    pairs = pair_order(count_x, group // 2)
     for k, part in enumerate((gathered, swapped)):
         for member in range(part.shape[0]):
             g, place = divmod(member, group // 2)
             for j in range(top_rows // QUAD):
                 row = (k * group // 2 + place) * top_rows + j * QUAD
-                received[g, row : row + QUAD, :] = part[member, j]
+                received[g, row : row + QUAD, :] = part[pairs.index(member), j]
     blocks = [received[g] for g in range(count_x)]
     high, low = split(jnp.concatenate(blocks, axis=1))
     mixed = product(y_table, jnp.concatenate([high, high, low], axis=0))
@@ -674,13 +679,14 @@
     z = z + (column >> whole_log(QUAD * count_z // 2) & (count_x - 1)) * QUAD
     cosine, sine = cos_sin(kz * z & (size - 1), size)
     table = jnp.concatenate([cosine, -sine], axis=0)
+    pairs = pair_order(count_x, count_y * count_z // 2)
     for k, part in enumerate((gathered, swapped)):
         for x in range(count_x):
             for y in range(count_y):
                 for pair in range(count_z // 2):
                     row = ((k * count_x + x) * count_z // 2 + pair) * QUAD
                     member = (x * count_y + y) * count_z // 2 + pair
-                    received[y, row : row + QUAD, :] = part[member, last]
+                    received[y, row : row + QUAD, :] = part[pairs.index(member), last]
     blocks = [received[y] for y in range(count_y)]
     lines = dot3(table, split(jnp.concatenate(blocks, axis=1)))
 
@@ -827,12 +833,13 @@
     tiles, table = (jnp.asarray(values) for values in narrow_tables(extent, size))
     rows_table = jnp.asarray(transform_table(size))
 
-    parities = [range(parity, devices, 2) for parity in range(2)]
+    pairs = pair_order(count_x, group // 2)
+    parities = [[2 * pair + parity for pair in pairs] for parity in range(2)]
     sent = residual_blocks(
         residual_top, residual_side, devices // 2, depth_block // count_x, True
     )
     gathered = lax.all_to_all(
-        sent, ALL, 0, 0, tiled=True, axis_index_groups=[list(each) for each in parities]
+        sent, ALL, 0, 0, tiled=True, axis_index_groups=parities
     )
     z_first, z_last, x_first, x_last, y_faces = faces_of(magnetization, stiffness)
     narrowed = call(

time: 46.6 us -> 44.8 us (0.961)
  waiting for transfers between devices: 7.19 us -> 4.45 us
  starting transfers between devices: 21.7 us -> 22.7 us
    all_to_all x1, waiting for transfers between devices: 2.72 us -> 0.01 us  [fast_on_device(): lax.all_to_all(sent, ALL, 0, 0, tiled=True, axis_index_groups=parities)]
    all_to_all x1, starting transfers between devices: 8.31 us -> 8.78 us  [fast_on_device(): lax.all_to_all(sent, ALL, 0, 0, tiled=True, axis_index_groups=parities)]
  transfers between devices with their start and end apart: 10 -> 10, of which waited for: 4 -> 3; matrix products, arithmetic and copies ran while one was open for 0% -> 0% of each run, Pallas kernels for 25% -> 26%
where the time goes in v11:
time: 44.8 us; the launch traced here: 44.2 us
  starting transfers between devices  22.7 us (51%)
  Pallas kernels  16.6 us (37%)
  waiting for transfers between devices  4.45 us (10%)
    pallas_call x8, Pallas kernels, call(): pl.pallas_call(body, out_shape=[pltpu.HBM(each, f32) if i in in_hbm else...  16.6 us
    all_to_all x1, starting transfers between devices, fast_on_device(): lax.all_to_all(sent, ALL, 0, 0, tiled=True, axis_index_groups=parities)  8.78 us
    ppermute x5, starting transfers between devices, ring(): lax.ppermute(block, axis, [(i, (i + distance) % count) for i in range(cou...  6.48 us
    all_to_all x1, starting transfers between devices, fast_on_device(): arrived = lax.all_to_all(lines, ALL, 0, 0, tiled=True)  3.64 us
    all_to_all x1, starting transfers between devices, fast_on_device(): arrived = lax.all_to_all(rows, ('gy', 'gz'), 0, 0, tiled=True)  3.37 us
    all_to_all x1, waiting for transfers between devices, fast_on_device(): arrived = lax.all_to_all(lines, ALL, 0, 0, tiled=True)  2.64 us
    ppermute x1, waiting for transfers between devices, fast_on_device(): swapped = lax.ppermute(gathered, 'gz', [(i, i ^ 1) for i in range(count_z)])  1.37 us
  transfers between devices with their start and end apart: 10, of which 3 were waited for; matrix products, arithmetic and copies ran while one was open for 0% of the time, Pallas kernels for 26%

profile of v11, /device:TPU:0, one launch (start us, length us, event | category | flops | bytes accessed | tf_op | source)
XLA Modules:
  0.0 44.2 jit_solution(4054572425894953901)
XLA Ops:
  0.0 1.5 %pack.1 = f32[16,5,4,128]{3,2,1,0:T(4,128)} custom-call(s32[1]{0:T(128)} %bitcast.1.at_x, f32[32,64]{1,0:T(8,128)} %bitcast.5, f32[16,128]{1,0:T(8,128)} %bitcast.6), custom_call_target="tpu_custom_call" | custom-call | flops 800000000 | bytes 180228 | tf_op jit(solution)/shard_map/pack/pallas_call | solution.py:63
  1.5 8.8 %all-to-all-start = ((f32[16,5,4,128]{3,2,1,0:T(4,128)}), f32[16,5,4,128]{3,2,1,0:T(4,128)S(1)}, u32[]{:S(2)}, u32[]{:S(2)}) async-start(f32[16,5,4,128]{3,2,1,0:T(4,128)} %pack.1), calls=%async_computation | async-start | bytes 327680 | tf_op jit(solution)/shard_map/all_to_all | solution.py:841
  10.3 0.0 copy-start.1
  10.3 0.0 copy-start.2
  10.3 2.7 %faces.1 = (f32[4,64,128]{2,1,0:T(8,128)S(1)}, f32[4,64,128]{2,1,0:T(8,128)S(1)}, f32[4,16,128]{2,1,0:T(8,128)S(1)}, f32[4,16,128]{2,1,0:T(8,128)S(1)}, f32[64,128]{1,0:T(8,128)}) custom-call(f32[3,16,64,128]{3,2,1,0:T(8,128)} %magnetization_from.1, f32[16,64,128]{2,1,0:T(8,128)} %stiffness_from.1), custom_call_target="tpu_custom_call" | custom-call | flops 2000000000 | bytes 2457600 | tf_op jit(solution)/shard_map/faces/pallas_call | solution.py:63
  13.0 0.3 copy-done.2
  13.3 2.2 %narrow.1 = (f32[2,2,64,512]{3,2,1,0:T(8,128)S(1)}, f32[2,2,16,512]{3,2,1,0:T(8,128)S(1)}) custom-call(f32[2,2,64,2048]{3,2,1,0:T(8,128)S(1)} %copy-done, f32[2,2,16,2048]{3,2,1,0:T(8,128)S(1)} %copy-done.1, bf16[8,2,256,256]{3,2,1,0:T(8,128)(2,1)S(1)} %copy-done.2), custom_call_target="tpu_custom_call" | custom-call | flops 2500000000 | bytes 5373952 | tf_op jit(solution)/shard_map/narrow/pallas_call | solution.py:63
  15.5 0.0 all-to-all-done.gathered
  15.5 0.1 collective-permute-start
  15.6 1.4 %collective-permute-done.swapped = f32[16,5,4,128]{3,2,1,0:T(4,128)S(1)} collective-permute-done((f32[16,5,4,128]{3,2,1,0:T(4,128)S(1)}, f32[16,5,4,128]{3,2,1,0:T(4,128)S(1)}, u32[]{:S(2)}, u32[]{:S(2)}) %collective-permute-start) | collective-permute-done | bytes 163872 | tf_op jit(solution)/shard_map/ppermute | solution.py:857
  16.9 0.0 copy-done.3
  16.9 2.3 %lines.1 = f32[32,16,128]{2,1,0:T(8,128)} custom-call(s32[1]{0:T(128)} %bitcast.here, f32[16,5,4,128]{3,2,1,0:T(4,128)S(1)} %all-to-all-done.gathered, f32[16,5,4,128]{3,2,1,0:T(4,128)S(1)} %collective-permute-done.swapped, bf16[2,512,256]{2,1,0:T(8,128)(2,1)S(1)} %copy-done.3, f32[2,2,64,512]{3,2,1,0:T(8,128)S(1)} %get-tuple-element.40.kernel), custom_call_target="tpu_custom_call" | custom-call | flops 2200000000 | bytes 1638404 | tf_op jit(solution)/shard_map/lines/pallas_call | solution.py:63
  19.3 3.6 %all-to-all-start.1 = ((f32[32,16,128]{2,1,0:T(8,128)}), f32[32,16,128]{2,1,0:T(8,128)S(1)}, u32[]{:S(2)}, u32[]{:S(2)}) async-start(f32[32,16,128]{2,1,0:T(8,128)} %lines.1), calls=%async_computation.1 | async-start | bytes 524288 | tf_op jit(solution)/shard_map/all_to_all | solution.py:869
  22.9 1.1 %side.3 = (f32[8,16,128]{2,1,0:T(8,128)S(1)}, f32[8,16,128]{2,1,0:T(8,128)S(1)}, bf16[2,512,256]{2,1,0:T(8,128)(2,1)S(1)}) custom-call(s32[1]{0:T(128)} %bitcast.4.here, f32[16,5,4,128]{3,2,1,0:T(4,128)S(1)} %all-to-all-done.gathered, f32[16,5,4,128]{3,2,1,0:T(4,128)S(1)} %collective-permute-done.swapped, bf16[2,512,256]{2,1,0:T(8,128)(2,1)S(1)} %copy-done.3, ...), custom_call_target="tpu_custom_call" | custom-call | flops 2000000000 | bytes 2686980 | tf_op jit(solution)/shard_map/side/pallas_call | solution.py:63
  24.0 0.3 collective-permute-start.1
  24.3 1.6 %collective-permute-start.2 = (f32[4,64,128]{2,1,0:T(8,128)S(1)}, f32[4,64,128]{2,1,0:T(8,128)S(1)}, u32[]{:S(2)}, u32[]{:S(2)}) collective-permute-start(f32[4,64,128]{2,1,0:T(8,128)S(1)} %get-tuple-element.49), channel_id=1, source_target_pairs={{0,3},{1,0},{2,1},{3,2},{4,7},{5,4},{6,5},{7,6},{8,11},{9,8},{10,9... | collective-permute-start | bytes 393224 | tf_op jit(solution)/shard_map/ppermute | solution.py:427
  26.0 0.0 collective-permute-start.3
  26.0 1.5 %collective-permute-start.4 = (f32[64,128]{1,0:T(8,128)S(1)}, f32[64,128]{1,0:T(8,128)S(1)}, u32[]{:S(2)}, u32[]{:S(2)}) collective-permute-start(f32[64,128]{1,0:T(8,128)S(1)} %copy-done.4), channel_id=1, source_target_pairs={{0,4},{4,0},{1,5},{5,1},{2,6},{6,2},{3,7},{7,3},{8,12},{12,8},{9,1... | collective-permute-start | bytes 98312 | tf_op jit(solution)/shard_map/ppermute | solution.py:427
  27.4 3.4 %collective-permute-start.5 = (f32[4,16,128]{2,1,0:T(8,128)S(1)}, f32[4,16,128]{2,1,0:T(8,128)S(1)}, u32[]{:S(2)}, u32[]{:S(2)}) collective-permute-start(f32[4,16,128]{2,1,0:T(8,128)S(1)} %get-tuple-element.54), channel_id=1, source_target_pairs={{0,24},{8,0},{16,8},{24,16},{1,25},{9,1},{17,9},{25,17},{2,26},{10... | collective-permute-start | bytes 98312 | tf_op jit(solution)/shard_map/ppermute | solution.py:427
  30.8 0.0 collective-permute-done.1.other
  30.8 0.0 collective-permute-start.6
  30.8 2.6 %all-to-all-done.1.arrived = f32[32,16,128]{2,1,0:T(8,128)S(1)} async-done(((f32[32,16,128]{2,1,0:T(8,128)}), f32[32,16,128]{2,1,0:T(8,128)S(1)}, u32[]{:S(2)}, u32[]{:S(2)}) %all-to-all-start.1) | async-done | bytes 262176 | tf_op jit(solution)/shard_map/all_to_all | solution.py:869
  33.4 1.1 %rows.1 = f32[8,32,128]{2,1,0:T(8,128)} custom-call(f32[32,16,128]{2,1,0:T(8,128)S(1)} %all-to-all-done.1.arrived, f32[8,16,128]{2,1,0:T(8,128)S(1)} %get-tuple-element.46.mine, f32[8,16,128]{2,1,0:T(8,128)S(1)} %collective-permute-done.1.other, bf16[2,512,256]{2,1,0:T(8,128)(2,1)S(1)} %get-tuple-element.48.table), custom_call_target="tpu_custom_call" | custom-call | flops 1100000000 | bytes 1048576 | tf_op jit(solution)/shard_map/rows/pallas_call | solution.py:63
  34.5 3.4 %all-to-all-start.2 = ((f32[8,32,128]{2,1,0:T(8,128)}), f32[8,32,128]{2,1,0:T(8,128)S(1)}, u32[]{:S(2)}, u32[]{:S(2)}) async-start(f32[8,32,128]{2,1,0:T(8,128)} %rows.1), calls=%async_computation.2 | async-start | bytes 262144 | tf_op jit(solution)/shard_map/all_to_all | solution.py:899
  37.9 0.0 collective-permute-done.2.z_next
  37.9 0.0 collective-permute-done.3.z_before
  37.9 0.0 collective-permute-done.4.y_next.y_before
  38.0 0.0 collective-permute-done.5.x_next
  38.0 0.0 collective-permute-done.6.x_before
  38.0 4.6 %exchange.1.exchange_grad = f32[3,16,64,128]{3,2,1,0:T(8,128)S(1)} custom-call(s32[1]{0:T(128)} %bitcast.here, f32[3,16,64,128]{3,2,1,0:T(8,128)} %magnetization_from.1, f32[16,64,128]{2,1,0:T(8,128)} %stiffness_from.1, f32[64,128]{1,0:T(8,128)} %get-tuple-element.56.y_faces_from, f32[4,64,128]{2,1,0:T(8,128)S(1)} %collective-permute-done.2.z_next, ...), custom_call_target="tpu_custom_call" | custom-call | flops 5000000000 | bytes 4096004 | tf_op jit(solution)/shard_map/exchange/pallas_call | solution.py:63
  42.6 0.4 all-to-all-done.2.arrived
  43.0 1.2 %gradient.1 = f32[3,16,64,128]{3,2,1,0:T(8,128)} custom-call(f32[3,16,64,128]{3,2,1,0:T(8,128)S(1)} %exchange.1.exchange_grad, f32[8,32,128]{2,1,0:T(8,128)S(1)} %all-to-all-done.2.arrived), custom_call_target="tpu_custom_call" | custom-call | flops 1200000000 | bytes 3276800 | tf_op jit(solution)/shard_map/gradient/pallas_call | solution.py:63
  (6 shorter events, 0.0 us)
Async XLA Ops:
  1.5 14.0 %all-to-all-start = ((f32[16,5,4,128]{3,2,1,0:T(4,128)}), f32[16,5,4,128]{3,2,1,0:T(4,128)S(1)}, u32[]{:S(2)}, u32[]{:S(2)}) async-start(f32[16,5,4,128]{3,2,1,0:T(4,128)} %pack.1), calls=%async_computation | async-start | bytes 327680 | tf_op jit(solution)/shard_map/all_to_all | solution.py:841
  10.2 2.7 %copy-start = (f32[2,2,64,2048]{3,2,1,0:T(8,128)S(1)}, f32[2,2,64,2048]{3,2,1,0:T(8,128)}, u32[]{:S(2)}) copy-start(f32[2,2,64,2048]{3,2,1,0:T(8,128)} %top.1) | copy-start | bytes 6291460
  10.3 2.7 %copy-start.1 = (f32[2,2,16,2048]{3,2,1,0:T(8,128)S(1)}, f32[2,2,16,2048]{3,2,1,0:T(8,128)}, u32[]{:S(2)}) copy-start(f32[2,2,16,2048]{3,2,1,0:T(8,128)} %side.2) | copy-start | bytes 1572868
  10.3 3.0 %copy-start.2 = (bf16[8,2,256,256]{3,2,1,0:T(8,128)(2,1)S(1)}, bf16[8,2,256,256]{3,2,1,0:T(8,128)(2,1)}, u32[]{:S(2)}) copy-start(bf16[8,2,256,256]{3,2,1,0:T(8,128)(2,1)} %constant.22.clone.tiles) | copy-start | bytes 6291460
  13.3 3.7 %copy-start.3 = (bf16[2,512,256]{2,1,0:T(8,128)(2,1)S(1)}, bf16[2,512,256]{2,1,0:T(8,128)(2,1)}, u32[]{:S(2)}) copy-start(bf16[2,512,256]{2,1,0:T(8,128)(2,1)} %constant.23.clone.table.spectrum) | copy-start | bytes 1572868
  15.5 1.5 %collective-permute-start = (f32[16,5,4,128]{3,2,1,0:T(4,128)S(1)}, f32[16,5,4,128]{3,2,1,0:T(4,128)S(1)}, u32[]{:S(2)}, u32[]{:S(2)}) collective-permute-start(f32[16,5,4,128]{3,2,1,0:T(4,128)S(1)} %all-to-all-done.gathered), channel_id=1, source_target_pairs={{0,1},{1,0},{2,3},{3,2},{4,5},{5,4},{6,7},{7,6},{8,9},{9,8},{10,11... | collective-permute-start | bytes 491528 | tf_op jit(solution)/shard_map/ppermute | solution.py:857
  19.3 14.2 %all-to-all-start.1 = ((f32[32,16,128]{2,1,0:T(8,128)}), f32[32,16,128]{2,1,0:T(8,128)S(1)}, u32[]{:S(2)}, u32[]{:S(2)}) async-start(f32[32,16,128]{2,1,0:T(8,128)} %lines.1), calls=%async_computation.1 | async-start | bytes 524288 | tf_op jit(solution)/shard_map/all_to_all | solution.py:869
  22.9 3.0 %copy-start.4 = (f32[64,128]{1,0:T(8,128)S(1)}, f32[64,128]{1,0:T(8,128)}, u32[]{:S(2)}) copy-start(f32[64,128]{1,0:T(8,128)} %get-tuple-element.56.y_faces_from) | copy-start | bytes 98308
  24.0 6.8 %collective-permute-start.1 = (f32[8,16,128]{2,1,0:T(8,128)S(1)}, f32[8,16,128]{2,1,0:T(8,128)S(1)}, u32[]{:S(2)}, u32[]{:S(2)}) collective-permute-start(f32[8,16,128]{2,1,0:T(8,128)S(1)} %get-tuple-element.43), channel_id=1, source_target_pairs={{0,1},{1,0},{2,3},{3,2},{4,5},{5,4},{6,7},{7,6},{8,9},{9,8},{10,11... | collective-permute-start | bytes 196616 | tf_op jit(solution)/shard_map/ppermute | solution.py:886
  24.3 13.6 %collective-permute-start.2 = (f32[4,64,128]{2,1,0:T(8,128)S(1)}, f32[4,64,128]{2,1,0:T(8,128)S(1)}, u32[]{:S(2)}, u32[]{:S(2)}) collective-permute-start(f32[4,64,128]{2,1,0:T(8,128)S(1)} %get-tuple-element.49), channel_id=1, source_target_pairs={{0,3},{1,0},{2,1},{3,2},{4,7},{5,4},{6,5},{7,6},{8,11},{9,8},{10,9... | collective-permute-start | bytes 393224 | tf_op jit(solution)/shard_map/ppermute | solution.py:427
  26.0 12.0 %collective-permute-start.3 = (f32[4,64,128]{2,1,0:T(8,128)S(1)}, f32[4,64,128]{2,1,0:T(8,128)S(1)}, u32[]{:S(2)}, u32[]{:S(2)}) collective-permute-start(f32[4,64,128]{2,1,0:T(8,128)S(1)} %get-tuple-element.50), channel_id=1, source_target_pairs={{0,1},{1,2},{2,3},{3,0},{4,5},{5,6},{6,7},{7,4},{8,9},{9,10},{10,1... | collective-permute-start | bytes 393224 | tf_op jit(solution)/shard_map/ppermute | solution.py:427
  26.0 12.0 %collective-permute-start.4 = (f32[64,128]{1,0:T(8,128)S(1)}, f32[64,128]{1,0:T(8,128)S(1)}, u32[]{:S(2)}, u32[]{:S(2)}) collective-permute-start(f32[64,128]{1,0:T(8,128)S(1)} %copy-done.4), channel_id=1, source_target_pairs={{0,4},{4,0},{1,5},{5,1},{2,6},{6,2},{3,7},{7,3},{8,12},{12,8},{9,1... | collective-permute-start | bytes 98312 | tf_op jit(solution)/shard_map/ppermute | solution.py:427
  27.4 10.5 %collective-permute-start.5 = (f32[4,16,128]{2,1,0:T(8,128)S(1)}, f32[4,16,128]{2,1,0:T(8,128)S(1)}, u32[]{:S(2)}, u32[]{:S(2)}) collective-permute-start(f32[4,16,128]{2,1,0:T(8,128)S(1)} %get-tuple-element.54), channel_id=1, source_target_pairs={{0,24},{8,0},{16,8},{24,16},{1,25},{9,1},{17,9},{25,17},{2,26},{10... | collective-permute-start | bytes 98312 | tf_op jit(solution)/shard_map/ppermute | solution.py:427
  30.8 7.2 %collective-permute-start.6 = (f32[4,16,128]{2,1,0:T(8,128)S(1)}, f32[4,16,128]{2,1,0:T(8,128)S(1)}, u32[]{:S(2)}, u32[]{:S(2)}) collective-permute-start(f32[4,16,128]{2,1,0:T(8,128)S(1)} %get-tuple-element.55), channel_id=1, source_target_pairs={{0,8},{8,16},{16,24},{24,0},{1,9},{9,17},{17,25},{25,1},{2,10},{10... | collective-permute-start | bytes 98312 | tf_op jit(solution)/shard_map/ppermute | solution.py:427
  34.5 8.5 %all-to-all-start.2 = ((f32[8,32,128]{2,1,0:T(8,128)}), f32[8,32,128]{2,1,0:T(8,128)S(1)}, u32[]{:S(2)}, u32[]{:S(2)}) async-start(f32[8,32,128]{2,1,0:T(8,128)} %rows.1), calls=%async_computation.2 | async-start | bytes 262144 | tf_op jit(solution)/shard_map/all_to_all | solution.py:899

commit v12 on v11

--- a/solution.py
+++ b/solution.py
@@ -442,7 +442,6 @@
         8,
         2.0,
         (from_hbm(magnetization), from_hbm(stiffness)),
-        in_hbm=(4,),
         refs=(0, 1),
         scratch=[
             pltpu.VMEM(magnetization.shape, f32),
@@ -516,9 +515,8 @@
     lags = np.arange(1, extent)
     window = 1.0 + 2.0 * np.cos(np.outer(m, lags) % size * (2.0 * math.pi / size)).sum(axis=1)
     i = np.arange(INNER)
-    place = np.arange(0, size, INNER)[:, None, None] + i[:, None] - ratio * i[None, :]
-    high, low = halves_of(window[place % size] / length)
-    tiles = np.stack([high, low], axis=1)
+    place = np.array([0, INNER])[:, None, None] + i[:, None] - ratio * np.arange(length)[None, :]
+    tiles = np.stack(halves_of(window[place % size] / length), axis=1)
     return tiles, transform_table(length)
 
 
@@ -549,9 +547,19 @@
 
 
 def narrow_kernel(top, side, tiles, top_out, side_out):
-    count = tiles.shape[0]
+    count = top.shape[3] // INNER
     parts = top_out.shape[3] // INNER
     step = count // parts
+    columns_of = tiles.shape[3] // LANES
+    ratio = top.shape[3] // top_out.shape[3]
+
+    def tile_of(place, k):
+        first = -(place // 2) * (2 * INNER // ratio // LANES)
+        columns = [(first + i) % columns_of * LANES for i in range(INNER // LANES)]
+        return jnp.concatenate(
+            [tiles[place % 2, k, :, column : column + LANES] for column in columns], axis=1
+        )
+
     top_rows, side_rows = top.shape[2], side.shape[2]
     totals = [None] * parts
     for k in range(count):
@@ -566,8 +574,8 @@
         high, low = split(lines)
         lines = jnp.concatenate([high, low, high], axis=1)
         for part in range(parts):
-            tile = tiles[(k - part * step) % count]
-            term = product(lines, jnp.concatenate([tile[0], tile[0], tile[1]], axis=0))
+            high, low = (tile_of((k - part * step) % count, i) for i in range(2))
+            term = product(lines, jnp.concatenate([high, high, low], axis=0))
             totals[part] = term if k == 0 else totals[part] + term
     for part in range(parts):
         columns = slice(part * INNER, (part + 1) * INNER)
@@ -583,8 +591,10 @@
 
 def dot3_with(values, table):
     high, low = split(values)
-    lines = jnp.concatenate([high, low, high], axis=1)
-    return product(lines, jnp.concatenate([table[0], table[0], table[1]], axis=0))
+    first = product(
+        jnp.concatenate([high, low], axis=1), jnp.concatenate([table[0], table[0]], axis=0)
+    )
+    return first + product(high, table[1])
 
 
 def there_and_back(real, imag, kernel, table):

time: 44.8 us -> 45 us (level)
  transfers between devices with their start and end apart: 10 -> 10, of which waited for: 3 -> 4; matrix products, arithmetic and copies ran while one was open for 0% -> 0% of each run, Pallas kernels for 26% -> 26%
where the time goes in v12:
time: 45 us; the launch traced here: 44.5 us
  starting transfers between devices  22.9 us (51%)
  Pallas kernels  16.5 us (37%)
  waiting for transfers between devices  4.37 us (10%)
  local copies, waits for them, and re-layouts  0.57 us (1%)
    pallas_call x8, Pallas kernels, call(): pl.pallas_call(body, out_shape=[pltpu.HBM(each, f32) if i in in_hbm else...  16.5 us
    all_to_all x1, starting transfers between devices, fast_on_device(): lax.all_to_all(sent, ALL, 0, 0, tiled=True, axis_index_groups=parities)  8.78 us
    ppermute x5, starting transfers between devices, ring(): lax.ppermute(block, axis, [(i, (i + distance) % count) for i in range(cou...  6.48 us
    all_to_all x1, starting transfers between devices, fast_on_device(): arrived = lax.all_to_all(lines, ALL, 0, 0, tiled=True)  3.99 us
    all_to_all x1, starting transfers between devices, fast_on_device(): arrived = lax.all_to_all(rows, ('gy', 'gz'), 0, 0, tiled=True)  3.37 us
    all_to_all x1, waiting for transfers between devices, fast_on_device(): arrived = lax.all_to_all(lines, ALL, 0, 0, tiled=True)  2.44 us
    ppermute x1, waiting for transfers between devices, fast_on_device(): swapped = lax.ppermute(gathered, 'gz', [(i, i ^ 1) for i in range(count_z)])  1.39 us
  transfers between devices with their start and end apart: 10, of which 4 were waited for; matrix products, arithmetic and copies ran while one was open for 0% of the time, Pallas kernels for 26%

profile of v12, /device:TPU:0, one launch (start us, length us, event | category | flops | bytes accessed | tf_op | source)
XLA Modules:
  0.0 44.5 jit_solution(5936241022342558893)
XLA Ops:
  0.0 1.5 %pack.1 = f32[16,5,4,128]{3,2,1,0:T(4,128)} custom-call(s32[1]{0:T(128)} %bitcast.1.at_x, f32[32,64]{1,0:T(8,128)} %bitcast.5, f32[16,128]{1,0:T(8,128)} %bitcast.6), custom_call_target="tpu_custom_call" | custom-call | flops 800000000 | bytes 180228 | tf_op jit(solution)/shard_map/pack/pallas_call | solution.py:63
  1.5 8.8 %all-to-all-start = ((f32[16,5,4,128]{3,2,1,0:T(4,128)}), f32[16,5,4,128]{3,2,1,0:T(4,128)S(1)}, u32[]{:S(2)}, u32[]{:S(2)}) async-start(f32[16,5,4,128]{3,2,1,0:T(4,128)} %pack.1), calls=%async_computation | async-start | bytes 327680 | tf_op jit(solution)/shard_map/all_to_all | solution.py:851
  10.3 0.0 copy-start.1
  10.3 0.0 copy-start.3
  10.3 2.1 %faces.1 = (f32[4,64,128]{2,1,0:T(8,128)S(1)}, f32[4,64,128]{2,1,0:T(8,128)S(1)}, f32[4,16,128]{2,1,0:T(8,128)S(1)}, f32[4,16,128]{2,1,0:T(8,128)S(1)}, f32[64,128]{1,0:T(8,128)S(1)}) custom-call(f32[3,16,64,128]{3,2,1,0:T(8,128)} %magnetization_from.1, f32[16,64,128]{2,1,0:T(8,128)} %stiffness_from.1), custom_call_target="tpu_custom_call" | custom-call | flops 2000000000 | bytes 2457600 | tf_op jit(solution)/shard_map/faces/pallas_call | solution.py:63
  12.3 0.1 copy-done
  12.5 0.1 copy-done.1
  12.6 0.3 copy-done.3
  12.9 2.2 %narrow.1 = (f32[2,2,64,512]{3,2,1,0:T(8,128)S(1)}, f32[2,2,16,512]{3,2,1,0:T(8,128)S(1)}) custom-call(f32[2,2,64,2048]{3,2,1,0:T(8,128)S(1)} %copy-done, f32[2,2,16,2048]{3,2,1,0:T(8,128)S(1)} %copy-done.1, bf16[2,2,256,512]{3,2,1,0:T(8,128)(2,1)S(1)} %copy-done.3), custom_call_target="tpu_custom_call" | custom-call | flops 2500000000 | bytes 4325376 | tf_op jit(solution)/shard_map/narrow/pallas_call | solution.py:63
  15.1 0.1 all-to-all-done.gathered
  15.2 0.0 collective-permute-start
  15.2 1.4 %collective-permute-done.swapped = f32[16,5,4,128]{3,2,1,0:T(4,128)S(1)} collective-permute-done((f32[16,5,4,128]{3,2,1,0:T(4,128)S(1)}, f32[16,5,4,128]{3,2,1,0:T(4,128)S(1)}, u32[]{:S(2)}, u32[]{:S(2)}) %collective-permute-start) | collective-permute-done | bytes 163872 | tf_op jit(solution)/shard_map/ppermute | solution.py:867
  16.6 2.3 %lines.1 = f32[32,16,128]{2,1,0:T(8,128)} custom-call(s32[1]{0:T(128)} %bitcast.here, f32[16,5,4,128]{3,2,1,0:T(4,128)S(1)} %all-to-all-done.gathered, f32[16,5,4,128]{3,2,1,0:T(4,128)S(1)} %collective-permute-done.swapped, bf16[2,512,256]{2,1,0:T(8,128)(2,1)S(1)} %copy-done.4, f32[2,2,64,512]{3,2,1,0:T(8,128)S(1)} %get-tuple-element.40.kernel), custom_call_target="tpu_custom_call" | custom-call | flops 2200000000 | bytes 1638404 | tf_op jit(solution)/shard_map/lines/pallas_call | solution.py:63
  18.9 4.0 %all-to-all-start.1 = ((f32[32,16,128]{2,1,0:T(8,128)}), f32[32,16,128]{2,1,0:T(8,128)S(1)}, u32[]{:S(2)}, u32[]{:S(2)}) async-start(f32[32,16,128]{2,1,0:T(8,128)} %lines.1), calls=%async_computation.1 | async-start | bytes 524288 | tf_op jit(solution)/shard_map/all_to_all | solution.py:879
  22.9 1.5 %side.3 = (f32[8,16,128]{2,1,0:T(8,128)S(1)}, f32[8,16,128]{2,1,0:T(8,128)S(1)}, bf16[2,512,256]{2,1,0:T(8,128)(2,1)S(1)}) custom-call(s32[1]{0:T(128)} %bitcast.4.here, f32[16,5,4,128]{3,2,1,0:T(4,128)S(1)} %all-to-all-done.gathered, f32[16,5,4,128]{3,2,1,0:T(4,128)S(1)} %collective-permute-done.swapped, bf16[2,512,256]{2,1,0:T(8,128)(2,1)S(1)} %copy-done.4, ...), custom_call_target="tpu_custom_call" | custom-call | flops 2000000000 | bytes 2686980 | tf_op jit(solution)/shard_map/side/pallas_call | solution.py:63
  24.4 0.3 collective-permute-start.1
  24.7 1.6 %collective-permute-start.2 = (f32[4,64,128]{2,1,0:T(8,128)S(1)}, f32[4,64,128]{2,1,0:T(8,128)S(1)}, u32[]{:S(2)}, u32[]{:S(2)}) collective-permute-start(f32[4,64,128]{2,1,0:T(8,128)S(1)} %get-tuple-element.49), channel_id=1, source_target_pairs={{0,3},{1,0},{2,1},{3,2},{4,7},{5,4},{6,5},{7,6},{8,11},{9,8},{10,9... | collective-permute-start | bytes 393224 | tf_op jit(solution)/shard_map/ppermute | solution.py:427
  26.4 0.0 collective-permute-start.3
  26.4 1.5 %collective-permute-start.4 = (f32[64,128]{1,0:T(8,128)S(1)}, f32[64,128]{1,0:T(8,128)S(1)}, u32[]{:S(2)}, u32[]{:S(2)}) collective-permute-start(f32[64,128]{1,0:T(8,128)S(1)} %get-tuple-element.56.y_faces_from), channel_id=1, source_target_pairs={{0,4},{4,0},{1,5},{5,1},{2,6},{6,2},{3,7},{7,3},{8,12},{12,8},{9,1... | collective-permute-start | bytes 98312 | tf_op jit(solution)/shard_map/ppermute | solution.py:427
  27.8 3.4 %collective-permute-start.5 = (f32[4,16,128]{2,1,0:T(8,128)S(1)}, f32[4,16,128]{2,1,0:T(8,128)S(1)}, u32[]{:S(2)}, u32[]{:S(2)}) collective-permute-start(f32[4,16,128]{2,1,0:T(8,128)S(1)} %get-tuple-element.54), channel_id=1, source_target_pairs={{0,24},{8,0},{16,8},{24,16},{1,25},{9,1},{17,9},{25,17},{2,26},{10... | collective-permute-start | bytes 98312 | tf_op jit(solution)/shard_map/ppermute | solution.py:427
  31.2 0.0 collective-permute-done.1.other
  31.2 0.0 collective-permute-start.6
  31.2 2.4 %all-to-all-done.1.arrived = f32[32,16,128]{2,1,0:T(8,128)S(1)} async-done(((f32[32,16,128]{2,1,0:T(8,128)}), f32[32,16,128]{2,1,0:T(8,128)S(1)}, u32[]{:S(2)}, u32[]{:S(2)}) %all-to-all-start.1) | async-done | bytes 262176 | tf_op jit(solution)/shard_map/all_to_all | solution.py:879
  33.7 1.1 %rows.1 = f32[8,32,128]{2,1,0:T(8,128)} custom-call(f32[32,16,128]{2,1,0:T(8,128)S(1)} %all-to-all-done.1.arrived, f32[8,16,128]{2,1,0:T(8,128)S(1)} %get-tuple-element.46.mine, f32[8,16,128]{2,1,0:T(8,128)S(1)} %collective-permute-done.1.other, bf16[2,512,256]{2,1,0:T(8,128)(2,1)S(1)} %get-tuple-element.48.table), custom_call_target="tpu_custom_call" | custom-call | flops 1100000000 | bytes 1048576 | tf_op jit(solution)/shard_map/rows/pallas_call | solution.py:63
  34.8 3.4 %all-to-all-start.2 = ((f32[8,32,128]{2,1,0:T(8,128)}), f32[8,32,128]{2,1,0:T(8,128)S(1)}, u32[]{:S(2)}, u32[]{:S(2)}) async-start(f32[8,32,128]{2,1,0:T(8,128)} %rows.1), calls=%async_computation.2 | async-start | bytes 262144 | tf_op jit(solution)/shard_map/all_to_all | solution.py:909
  38.2 0.0 collective-permute-done.2.z_next
  38.2 0.0 collective-permute-done.3.z_before
  38.2 0.0 collective-permute-done.5.x_next
  38.2 0.0 collective-permute-done.6.x_before
  38.2 4.6 %exchange.1.exchange_grad = f32[3,16,64,128]{3,2,1,0:T(8,128)S(1)} custom-call(s32[1]{0:T(128)} %bitcast.here, f32[3,16,64,128]{3,2,1,0:T(8,128)} %magnetization_from.1, f32[16,64,128]{2,1,0:T(8,128)} %stiffness_from.1, f32[64,128]{1,0:T(8,128)} %copy-done.2, f32[4,64,128]{2,1,0:T(8,128)S(1)} %collective-permute-done.2.z_next, ...), custom_call_target="tpu_custom_call" | custom-call | flops 5000000000 | bytes 4096004 | tf_op jit(solution)/shard_map/exchange/pallas_call | solution.py:63
  42.8 0.4 all-to-all-done.2.arrived
  43.3 1.2 %gradient.1 = f32[3,16,64,128]{3,2,1,0:T(8,128)} custom-call(f32[3,16,64,128]{3,2,1,0:T(8,128)S(1)} %exchange.1.exchange_grad, f32[8,32,128]{2,1,0:T(8,128)S(1)} %all-to-all-done.2.arrived), custom_call_target="tpu_custom_call" | custom-call | flops 1200000000 | bytes 3276800 | tf_op jit(solution)/shard_map/gradient/pallas_call | solution.py:63
  (6 shorter events, 0.0 us)
Async XLA Ops:
  1.5 13.7 %all-to-all-start = ((f32[16,5,4,128]{3,2,1,0:T(4,128)}), f32[16,5,4,128]{3,2,1,0:T(4,128)S(1)}, u32[]{:S(2)}, u32[]{:S(2)}) async-start(f32[16,5,4,128]{3,2,1,0:T(4,128)} %pack.1), calls=%async_computation | async-start | bytes 327680 | tf_op jit(solution)/shard_map/all_to_all | solution.py:851
  10.2 2.2 %copy-start = (f32[2,2,64,2048]{3,2,1,0:T(8,128)S(1)}, f32[2,2,64,2048]{3,2,1,0:T(8,128)}, u32[]{:S(2)}) copy-start(f32[2,2,64,2048]{3,2,1,0:T(8,128)} %top.1) | copy-start | bytes 6291460
  10.3 2.3 %copy-start.1 = (f32[2,2,16,2048]{3,2,1,0:T(8,128)S(1)}, f32[2,2,16,2048]{3,2,1,0:T(8,128)}, u32[]{:S(2)}) copy-start(f32[2,2,16,2048]{3,2,1,0:T(8,128)} %side.2) | copy-start | bytes 1572868
  10.3 2.6 %copy-start.3 = (bf16[2,2,256,512]{3,2,1,0:T(8,128)(2,1)S(1)}, bf16[2,2,256,512]{3,2,1,0:T(8,128)(2,1)}, u32[]{:S(2)}) copy-start(bf16[2,2,256,512]{3,2,1,0:T(8,128)(2,1)} %constant.22.clone.tiles) | copy-start | bytes 3145732
  12.9 13.5 %copy-start.2 = (f32[64,128]{1,0:T(8,128)}, f32[64,128]{1,0:T(8,128)S(1)}, u32[]{:S(2)}) copy-start(f32[64,128]{1,0:T(8,128)S(1)} %get-tuple-element.56.y_faces_from) | copy-start | bytes 98308
  12.9 3.7 %copy-start.4 = (bf16[2,512,256]{2,1,0:T(8,128)(2,1)S(1)}, bf16[2,512,256]{2,1,0:T(8,128)(2,1)}, u32[]{:S(2)}) copy-start(bf16[2,512,256]{2,1,0:T(8,128)(2,1)} %constant.23.clone.table.spectrum) | copy-start | bytes 1572868
  15.2 1.4 %collective-permute-start = (f32[16,5,4,128]{3,2,1,0:T(4,128)S(1)}, f32[16,5,4,128]{3,2,1,0:T(4,128)S(1)}, u32[]{:S(2)}, u32[]{:S(2)}) collective-permute-start(f32[16,5,4,128]{3,2,1,0:T(4,128)S(1)} %all-to-all-done.gathered), channel_id=1, source_target_pairs={{0,1},{1,0},{2,3},{3,2},{4,5},{5,4},{6,7},{7,6},{8,9},{9,8},{10,11... | collective-permute-start | bytes 491528 | tf_op jit(solution)/shard_map/ppermute | solution.py:867
  18.9 14.8 %all-to-all-start.1 = ((f32[32,16,128]{2,1,0:T(8,128)}), f32[32,16,128]{2,1,0:T(8,128)S(1)}, u32[]{:S(2)}, u32[]{:S(2)}) async-start(f32[32,16,128]{2,1,0:T(8,128)} %lines.1), calls=%async_computation.1 | async-start | bytes 524288 | tf_op jit(solution)/shard_map/all_to_all | solution.py:879
  24.4 6.8 %collective-permute-start.1 = (f32[8,16,128]{2,1,0:T(8,128)S(1)}, f32[8,16,128]{2,1,0:T(8,128)S(1)}, u32[]{:S(2)}, u32[]{:S(2)}) collective-permute-start(f32[8,16,128]{2,1,0:T(8,128)S(1)} %get-tuple-element.43), channel_id=1, source_target_pairs={{0,1},{1,0},{2,3},{3,2},{4,5},{5,4},{6,7},{7,6},{8,9},{9,8},{10,11... | collective-permute-start | bytes 196616 | tf_op jit(solution)/shard_map/ppermute | solution.py:896
  24.7 13.4 %collective-permute-start.2 = (f32[4,64,128]{2,1,0:T(8,128)S(1)}, f32[4,64,128]{2,1,0:T(8,128)S(1)}, u32[]{:S(2)}, u32[]{:S(2)}) collective-permute-start(f32[4,64,128]{2,1,0:T(8,128)S(1)} %get-tuple-element.49), channel_id=1, source_target_pairs={{0,3},{1,0},{2,1},{3,2},{4,7},{5,4},{6,5},{7,6},{8,11},{9,8},{10,9... | collective-permute-start | bytes 393224 | tf_op jit(solution)/shard_map/ppermute | solution.py:427
  26.4 11.8 %collective-permute-start.3 = (f32[4,64,128]{2,1,0:T(8,128)S(1)}, f32[4,64,128]{2,1,0:T(8,128)S(1)}, u32[]{:S(2)}, u32[]{:S(2)}) collective-permute-start(f32[4,64,128]{2,1,0:T(8,128)S(1)} %get-tuple-element.50), channel_id=1, source_target_pairs={{0,1},{1,2},{2,3},{3,0},{4,5},{5,6},{6,7},{7,4},{8,9},{9,10},{10,1... | collective-permute-start | bytes 393224 | tf_op jit(solution)/shard_map/ppermute | solution.py:427
  26.4 11.8 %collective-permute-start.4 = (f32[64,128]{1,0:T(8,128)S(1)}, f32[64,128]{1,0:T(8,128)S(1)}, u32[]{:S(2)}, u32[]{:S(2)}) collective-permute-start(f32[64,128]{1,0:T(8,128)S(1)} %get-tuple-element.56.y_faces_from), channel_id=1, source_target_pairs={{0,4},{4,0},{1,5},{5,1},{2,6},{6,2},{3,7},{7,3},{8,12},{12,8},{9,1... | collective-permute-start | bytes 98312 | tf_op jit(solution)/shard_map/ppermute | solution.py:427
  27.8 10.3 %collective-permute-start.5 = (f32[4,16,128]{2,1,0:T(8,128)S(1)}, f32[4,16,128]{2,1,0:T(8,128)S(1)}, u32[]{:S(2)}, u32[]{:S(2)}) collective-permute-start(f32[4,16,128]{2,1,0:T(8,128)S(1)} %get-tuple-element.54), channel_id=1, source_target_pairs={{0,24},{8,0},{16,8},{24,16},{1,25},{9,1},{17,9},{25,17},{2,26},{10... | collective-permute-start | bytes 98312 | tf_op jit(solution)/shard_map/ppermute | solution.py:427
  31.2 7.0 %collective-permute-start.6 = (f32[4,16,128]{2,1,0:T(8,128)S(1)}, f32[4,16,128]{2,1,0:T(8,128)S(1)}, u32[]{:S(2)}, u32[]{:S(2)}) collective-permute-start(f32[4,16,128]{2,1,0:T(8,128)S(1)} %get-tuple-element.55), channel_id=1, source_target_pairs={{0,8},{8,16},{16,24},{24,0},{1,9},{9,17},{17,25},{25,1},{2,10},{10... | collective-permute-start | bytes 98312 | tf_op jit(solution)/shard_map/ppermute | solution.py:427
  34.8 8.5 %all-to-all-start.2 = ((f32[8,32,128]{2,1,0:T(8,128)}), f32[8,32,128]{2,1,0:T(8,128)S(1)}, u32[]{:S(2)}, u32[]{:S(2)}) async-start(f32[8,32,128]{2,1,0:T(8,128)} %rows.1), calls=%async_computation.2 | async-start | bytes 262144 | tf_op jit(solution)/shard_map/all_to_all | solution.py:909

commit v13 on v11

--- a/solution.py
+++ b/solution.py
@@ -615,7 +615,9 @@
     return total[: 2 * rows], total[2 * rows :]
 
 
-def lines_kernel(counts, here, gathered, swapped, table, kernel, out, received):
+def lines_kernel(
+    counts, here, gathered, swapped, table, kernel, out, received, result, sending
+):
     count_x, count_y, count_z = counts
     group = count_y * count_z
     top_rows = LANES // group
@@ -646,8 +648,14 @@
             )
         )
     lines = jnp.concatenate(pieces, axis=1)
+    sends = []
     for k, part in enumerate(there_and_back(lines[:kys], lines[kys:], kernel, table)):
-        out[:, k * TILE : (k + 1) * TILE, :] = part.T.reshape(count_x * group, TILE, LANES)
+        rows = slice(k * TILE, (k + 1) * TILE)
+        result[:, rows, :] = part.T.reshape(count_x * group, TILE, LANES)
+        sends.append(pltpu.make_async_copy(result.at[:, rows], out.at[:, rows], sending.at[k]))
+        sends[-1].start()
+    for copy in sends:
+        copy.wait()
 
 
 def side_kernel_body(
@@ -864,7 +872,13 @@
         16,
         2.2,
         (index, gathered, swapped, table, top_spectra),
-        scratch=[pltpu.VMEM((count_x, LANES, LANES), f32)],
+        in_hbm=(0,),
+        out_refs=(0,),
+        scratch=[
+            pltpu.VMEM((count_x, LANES, LANES), f32),
+            pltpu.VMEM((devices, 2 * TILE, LANES), f32),
+            pltpu.SemaphoreType.DMA((2,)),
+        ],
     )
     arrived = lax.all_to_all(lines, ALL, 0, 0, tiled=True)
     lines, x_first, x_last = lax.optimization_barrier((lines, x_first, x_last))

time: 44.8 us -> 44.8 us (level)
  no operation moved by 1% of the time
where the time goes in v13:
time: 44.8 us; the launch traced here: 44.2 us
  starting transfers between devices  22.7 us (51%)
  Pallas kernels  16.6 us (37%)
  waiting for transfers between devices  4.45 us (10%)
    pallas_call x8, Pallas kernels, call(): pl.pallas_call(body, out_shape=[pltpu.HBM(each, f32) if i in in_hbm else...  16.6 us
    all_to_all x1, starting transfers between devices, fast_on_device(): lax.all_to_all(sent, ALL, 0, 0, tiled=True, axis_index_groups=parities)  8.78 us
    ppermute x5, starting transfers between devices, ring(): lax.ppermute(block, axis, [(i, (i + distance) % count) for i in range(cou...  6.48 us
    all_to_all x1, starting transfers between devices, fast_on_device(): arrived = lax.all_to_all(lines, ALL, 0, 0, tiled=True)  3.65 us
    all_to_all x1, starting transfers between devices, fast_on_device(): arrived = lax.all_to_all(rows, ('gy', 'gz'), 0, 0, tiled=True)  3.37 us
    all_to_all x1, waiting for transfers between devices, fast_on_device(): arrived = lax.all_to_all(lines, ALL, 0, 0, tiled=True)  2.64 us
    ppermute x1, waiting for transfers between devices, fast_on_device(): swapped = lax.ppermute(gathered, 'gz', [(i, i ^ 1) for i in range(count_z)])  1.37 us
  transfers between devices with their start and end apart: 10, of which 3 were waited for; matrix products, arithmetic and copies ran while one was open for 0% of the time, Pallas kernels for 26%

profile of v13, /device:TPU:0, one launch (start us, length us, event | category | flops | bytes accessed | tf_op | source)
XLA Modules:
  0.0 44.2 jit_solution(11951513986189655357)
XLA Ops:
  0.0 1.5 %pack.1 = f32[16,5,4,128]{3,2,1,0:T(4,128)} custom-call(s32[1]{0:T(128)} %bitcast.1.at_x, f32[32,64]{1,0:T(8,128)} %bitcast.5, f32[16,128]{1,0:T(8,128)} %bitcast.6), custom_call_target="tpu_custom_call" | custom-call | flops 800000000 | bytes 180228 | tf_op jit(solution)/shard_map/pack/pallas_call | solution.py:63
  1.5 8.8 %all-to-all-start = ((f32[16,5,4,128]{3,2,1,0:T(4,128)}), f32[16,5,4,128]{3,2,1,0:T(4,128)S(1)}, u32[]{:S(2)}, u32[]{:S(2)}) async-start(f32[16,5,4,128]{3,2,1,0:T(4,128)} %pack.1), calls=%async_computation | async-start | bytes 327680 | tf_op jit(solution)/shard_map/all_to_all | solution.py:849
  10.3 0.0 copy-start.1
  10.3 0.0 copy-start.2
  10.3 2.7 %faces.1 = (f32[4,64,128]{2,1,0:T(8,128)S(1)}, f32[4,64,128]{2,1,0:T(8,128)S(1)}, f32[4,16,128]{2,1,0:T(8,128)S(1)}, f32[4,16,128]{2,1,0:T(8,128)S(1)}, f32[64,128]{1,0:T(8,128)}) custom-call(f32[3,16,64,128]{3,2,1,0:T(8,128)} %magnetization_from.1, f32[16,64,128]{2,1,0:T(8,128)} %stiffness_from.1), custom_call_target="tpu_custom_call" | custom-call | flops 2000000000 | bytes 2457600 | tf_op jit(solution)/shard_map/faces/pallas_call | solution.py:63
  12.9 0.0 copy-done
  13.0 0.3 copy-done.2
  13.3 2.2 %narrow.1 = (f32[2,2,64,512]{3,2,1,0:T(8,128)S(1)}, f32[2,2,16,512]{3,2,1,0:T(8,128)S(1)}) custom-call(f32[2,2,64,2048]{3,2,1,0:T(8,128)S(1)} %copy-done, f32[2,2,16,2048]{3,2,1,0:T(8,128)S(1)} %copy-done.1, bf16[8,2,256,256]{3,2,1,0:T(8,128)(2,1)S(1)} %copy-done.2), custom_call_target="tpu_custom_call" | custom-call | flops 2500000000 | bytes 5373952 | tf_op jit(solution)/shard_map/narrow/pallas_call | solution.py:63
  15.5 0.0 all-to-all-done.gathered
  15.5 0.1 collective-permute-start
  15.6 1.4 %collective-permute-done.swapped = f32[16,5,4,128]{3,2,1,0:T(4,128)S(1)} collective-permute-done((f32[16,5,4,128]{3,2,1,0:T(4,128)S(1)}, f32[16,5,4,128]{3,2,1,0:T(4,128)S(1)}, u32[]{:S(2)}, u32[]{:S(2)}) %collective-permute-start) | collective-permute-done | bytes 163872 | tf_op jit(solution)/shard_map/ppermute | solution.py:865
  16.9 2.3 %lines.1 = f32[32,16,128]{2,1,0:T(8,128)} custom-call(s32[1]{0:T(128)} %bitcast.here, f32[16,5,4,128]{3,2,1,0:T(4,128)S(1)} %all-to-all-done.gathered, f32[16,5,4,128]{3,2,1,0:T(4,128)S(1)} %collective-permute-done.swapped, bf16[2,512,256]{2,1,0:T(8,128)(2,1)S(1)} %copy-done.3, f32[2,2,64,512]{3,2,1,0:T(8,128)S(1)} %get-tuple-element.40.kernel), custom_call_target="tpu_custom_call" | custom-call | flops 2200000000 | bytes 1638404 | tf_op jit(solution)/shard_map/lines/pallas_call | solution.py:63
  19.2 3.6 %all-to-all-start.1 = ((f32[32,16,128]{2,1,0:T(8,128)}), f32[32,16,128]{2,1,0:T(8,128)S(1)}, u32[]{:S(2)}, u32[]{:S(2)}) async-start(f32[32,16,128]{2,1,0:T(8,128)} %lines.1), calls=%async_computation.1 | async-start | bytes 524288 | tf_op jit(solution)/shard_map/all_to_all | solution.py:883
  22.9 1.1 %side.3 = (f32[8,16,128]{2,1,0:T(8,128)S(1)}, f32[8,16,128]{2,1,0:T(8,128)S(1)}, bf16[2,512,256]{2,1,0:T(8,128)(2,1)S(1)}) custom-call(s32[1]{0:T(128)} %bitcast.4.here, f32[16,5,4,128]{3,2,1,0:T(4,128)S(1)} %all-to-all-done.gathered, f32[16,5,4,128]{3,2,1,0:T(4,128)S(1)} %collective-permute-done.swapped, bf16[2,512,256]{2,1,0:T(8,128)(2,1)S(1)} %copy-done.3, ...), custom_call_target="tpu_custom_call" | custom-call | flops 2000000000 | bytes 2686980 | tf_op jit(solution)/shard_map/side/pallas_call | solution.py:63
  24.0 0.3 collective-permute-start.1
  24.3 1.6 %collective-permute-start.2 = (f32[4,64,128]{2,1,0:T(8,128)S(1)}, f32[4,64,128]{2,1,0:T(8,128)S(1)}, u32[]{:S(2)}, u32[]{:S(2)}) collective-permute-start(f32[4,64,128]{2,1,0:T(8,128)S(1)} %get-tuple-element.49), channel_id=1, source_target_pairs={{0,3},{1,0},{2,1},{3,2},{4,7},{5,4},{6,5},{7,6},{8,11},{9,8},{10,9... | collective-permute-start | bytes 393224 | tf_op jit(solution)/shard_map/ppermute | solution.py:427
  25.9 0.0 collective-permute-start.3
  26.0 1.5 %collective-permute-start.4 = (f32[64,128]{1,0:T(8,128)S(1)}, f32[64,128]{1,0:T(8,128)S(1)}, u32[]{:S(2)}, u32[]{:S(2)}) collective-permute-start(f32[64,128]{1,0:T(8,128)S(1)} %copy-done.4), channel_id=1, source_target_pairs={{0,4},{4,0},{1,5},{5,1},{2,6},{6,2},{3,7},{7,3},{8,12},{12,8},{9,1... | collective-permute-start | bytes 98312 | tf_op jit(solution)/shard_map/ppermute | solution.py:427
  27.4 3.4 %collective-permute-start.5 = (f32[4,16,128]{2,1,0:T(8,128)S(1)}, f32[4,16,128]{2,1,0:T(8,128)S(1)}, u32[]{:S(2)}, u32[]{:S(2)}) collective-permute-start(f32[4,16,128]{2,1,0:T(8,128)S(1)} %get-tuple-element.54), channel_id=1, source_target_pairs={{0,24},{8,0},{16,8},{24,16},{1,25},{9,1},{17,9},{25,17},{2,26},{10... | collective-permute-start | bytes 98312 | tf_op jit(solution)/shard_map/ppermute | solution.py:427
  30.8 0.0 collective-permute-done.1.other
  30.8 0.0 collective-permute-start.6
  30.8 2.6 %all-to-all-done.1.arrived = f32[32,16,128]{2,1,0:T(8,128)S(1)} async-done(((f32[32,16,128]{2,1,0:T(8,128)}), f32[32,16,128]{2,1,0:T(8,128)S(1)}, u32[]{:S(2)}, u32[]{:S(2)}) %all-to-all-start.1) | async-done | bytes 262176 | tf_op jit(solution)/shard_map/all_to_all | solution.py:883
  33.4 1.1 %rows.1 = f32[8,32,128]{2,1,0:T(8,128)} custom-call(f32[32,16,128]{2,1,0:T(8,128)S(1)} %all-to-all-done.1.arrived, f32[8,16,128]{2,1,0:T(8,128)S(1)} %get-tuple-element.46.mine, f32[8,16,128]{2,1,0:T(8,128)S(1)} %collective-permute-done.1.other, bf16[2,512,256]{2,1,0:T(8,128)(2,1)S(1)} %get-tuple-element.48.table), custom_call_target="tpu_custom_call" | custom-call | flops 1100000000 | bytes 1048576 | tf_op jit(solution)/shard_map/rows/pallas_call | solution.py:63
  34.5 3.4 %all-to-all-start.2 = ((f32[8,32,128]{2,1,0:T(8,128)}), f32[8,32,128]{2,1,0:T(8,128)S(1)}, u32[]{:S(2)}, u32[]{:S(2)}) async-start(f32[8,32,128]{2,1,0:T(8,128)} %rows.1), calls=%async_computation.2 | async-start | bytes 262144 | tf_op jit(solution)/shard_map/all_to_all | solution.py:913
  37.9 0.0 collective-permute-done.2.z_next
  37.9 0.0 collective-permute-done.3.z_before
  37.9 0.0 collective-permute-done.4.y_next.y_before
  37.9 0.0 collective-permute-done.5.x_next
  38.0 0.0 collective-permute-done.6.x_before
  38.0 4.6 %exchange.1.exchange_grad = f32[3,16,64,128]{3,2,1,0:T(8,128)S(1)} custom-call(s32[1]{0:T(128)} %bitcast.here, f32[3,16,64,128]{3,2,1,0:T(8,128)} %magnetization_from.1, f32[16,64,128]{2,1,0:T(8,128)} %stiffness_from.1, f32[64,128]{1,0:T(8,128)} %get-tuple-element.56.y_faces_from, f32[4,64,128]{2,1,0:T(8,128)S(1)} %collective-permute-done.2.z_next, ...), custom_call_target="tpu_custom_call" | custom-call | flops 5000000000 | bytes 4096004 | tf_op jit(solution)/shard_map/exchange/pallas_call | solution.py:63
  42.6 0.4 all-to-all-done.2.arrived
  43.0 1.2 %gradient.1 = f32[3,16,64,128]{3,2,1,0:T(8,128)} custom-call(f32[3,16,64,128]{3,2,1,0:T(8,128)S(1)} %exchange.1.exchange_grad, f32[8,32,128]{2,1,0:T(8,128)S(1)} %all-to-all-done.2.arrived), custom_call_target="tpu_custom_call" | custom-call | flops 1200000000 | bytes 3276800 | tf_op jit(solution)/shard_map/gradient/pallas_call | solution.py:63
  (6 shorter events, 0.0 us)
Async XLA Ops:
  1.5 14.0 %all-to-all-start = ((f32[16,5,4,128]{3,2,1,0:T(4,128)}), f32[16,5,4,128]{3,2,1,0:T(4,128)S(1)}, u32[]{:S(2)}, u32[]{:S(2)}) async-start(f32[16,5,4,128]{3,2,1,0:T(4,128)} %pack.1), calls=%async_computation | async-start | bytes 327680 | tf_op jit(solution)/shard_map/all_to_all | solution.py:849
  10.2 2.7 %copy-start = (f32[2,2,64,2048]{3,2,1,0:T(8,128)S(1)}, f32[2,2,64,2048]{3,2,1,0:T(8,128)}, u32[]{:S(2)}) copy-start(f32[2,2,64,2048]{3,2,1,0:T(8,128)} %top.1) | copy-start | bytes 6291460
  10.3 2.7 %copy-start.1 = (f32[2,2,16,2048]{3,2,1,0:T(8,128)S(1)}, f32[2,2,16,2048]{3,2,1,0:T(8,128)}, u32[]{:S(2)}) copy-start(f32[2,2,16,2048]{3,2,1,0:T(8,128)} %side.2) | copy-start | bytes 1572868
  10.3 3.0 %copy-start.2 = (bf16[8,2,256,256]{3,2,1,0:T(8,128)(2,1)S(1)}, bf16[8,2,256,256]{3,2,1,0:T(8,128)(2,1)}, u32[]{:S(2)}) copy-start(bf16[8,2,256,256]{3,2,1,0:T(8,128)(2,1)} %constant.22.clone.tiles) | copy-start | bytes 6291460
  13.3 3.7 %copy-start.3 = (bf16[2,512,256]{2,1,0:T(8,128)(2,1)S(1)}, bf16[2,512,256]{2,1,0:T(8,128)(2,1)}, u32[]{:S(2)}) copy-start(bf16[2,512,256]{2,1,0:T(8,128)(2,1)} %constant.23.clone.table.spectrum) | copy-start | bytes 1572868
  15.5 1.5 %collective-permute-start = (f32[16,5,4,128]{3,2,1,0:T(4,128)S(1)}, f32[16,5,4,128]{3,2,1,0:T(4,128)S(1)}, u32[]{:S(2)}, u32[]{:S(2)}) collective-permute-start(f32[16,5,4,128]{3,2,1,0:T(4,128)S(1)} %all-to-all-done.gathered), channel_id=1, source_target_pairs={{0,1},{1,0},{2,3},{3,2},{4,5},{5,4},{6,7},{7,6},{8,9},{9,8},{10,11... | collective-permute-start | bytes 491528 | tf_op jit(solution)/shard_map/ppermute | solution.py:865
  19.2 14.2 %all-to-all-start.1 = ((f32[32,16,128]{2,1,0:T(8,128)}), f32[32,16,128]{2,1,0:T(8,128)S(1)}, u32[]{:S(2)}, u32[]{:S(2)}) async-start(f32[32,16,128]{2,1,0:T(8,128)} %lines.1), calls=%async_computation.1 | async-start | bytes 524288 | tf_op jit(solution)/shard_map/all_to_all | solution.py:883
  22.9 3.0 %copy-start.4 = (f32[64,128]{1,0:T(8,128)S(1)}, f32[64,128]{1,0:T(8,128)}, u32[]{:S(2)}) copy-start(f32[64,128]{1,0:T(8,128)} %get-tuple-element.56.y_faces_from) | copy-start | bytes 98308
  24.0 6.8 %collective-permute-start.1 = (f32[8,16,128]{2,1,0:T(8,128)S(1)}, f32[8,16,128]{2,1,0:T(8,128)S(1)}, u32[]{:S(2)}, u32[]{:S(2)}) collective-permute-start(f32[8,16,128]{2,1,0:T(8,128)S(1)} %get-tuple-element.43), channel_id=1, source_target_pairs={{0,1},{1,0},{2,3},{3,2},{4,5},{5,4},{6,7},{7,6},{8,9},{9,8},{10,11... | collective-permute-start | bytes 196616 | tf_op jit(solution)/shard_map/ppermute | solution.py:900
  24.3 13.6 %collective-permute-start.2 = (f32[4,64,128]{2,1,0:T(8,128)S(1)}, f32[4,64,128]{2,1,0:T(8,128)S(1)}, u32[]{:S(2)}, u32[]{:S(2)}) collective-permute-start(f32[4,64,128]{2,1,0:T(8,128)S(1)} %get-tuple-element.49), channel_id=1, source_target_pairs={{0,3},{1,0},{2,1},{3,2},{4,7},{5,4},{6,5},{7,6},{8,11},{9,8},{10,9... | collective-permute-start | bytes 393224 | tf_op jit(solution)/shard_map/ppermute | solution.py:427
  25.9 12.0 %collective-permute-start.3 = (f32[4,64,128]{2,1,0:T(8,128)S(1)}, f32[4,64,128]{2,1,0:T(8,128)S(1)}, u32[]{:S(2)}, u32[]{:S(2)}) collective-permute-start(f32[4,64,128]{2,1,0:T(8,128)S(1)} %get-tuple-element.50), channel_id=1, source_target_pairs={{0,1},{1,2},{2,3},{3,0},{4,5},{5,6},{6,7},{7,4},{8,9},{9,10},{10,1... | collective-permute-start | bytes 393224 | tf_op jit(solution)/shard_map/ppermute | solution.py:427
  26.0 12.0 %collective-permute-start.4 = (f32[64,128]{1,0:T(8,128)S(1)}, f32[64,128]{1,0:T(8,128)S(1)}, u32[]{:S(2)}, u32[]{:S(2)}) collective-permute-start(f32[64,128]{1,0:T(8,128)S(1)} %copy-done.4), channel_id=1, source_target_pairs={{0,4},{4,0},{1,5},{5,1},{2,6},{6,2},{3,7},{7,3},{8,12},{12,8},{9,1... | collective-permute-start | bytes 98312 | tf_op jit(solution)/shard_map/ppermute | solution.py:427
  27.4 10.5 %collective-permute-start.5 = (f32[4,16,128]{2,1,0:T(8,128)S(1)}, f32[4,16,128]{2,1,0:T(8,128)S(1)}, u32[]{:S(2)}, u32[]{:S(2)}) collective-permute-start(f32[4,16,128]{2,1,0:T(8,128)S(1)} %get-tuple-element.54), channel_id=1, source_target_pairs={{0,24},{8,0},{16,8},{24,16},{1,25},{9,1},{17,9},{25,17},{2,26},{10... | collective-permute-start | bytes 98312 | tf_op jit(solution)/shard_map/ppermute | solution.py:427
  30.8 7.2 %collective-permute-start.6 = (f32[4,16,128]{2,1,0:T(8,128)S(1)}, f32[4,16,128]{2,1,0:T(8,128)S(1)}, u32[]{:S(2)}, u32[]{:S(2)}) collective-permute-start(f32[4,16,128]{2,1,0:T(8,128)S(1)} %get-tuple-element.55), channel_id=1, source_target_pairs={{0,8},{8,16},{16,24},{24,0},{1,9},{9,17},{17,25},{25,1},{2,10},{10... | collective-permute-start | bytes 98312 | tf_op jit(solution)/shard_map/ppermute | solution.py:427
  34.5 8.5 %all-to-all-start.2 = ((f32[8,32,128]{2,1,0:T(8,128)}), f32[8,32,128]{2,1,0:T(8,128)S(1)}, u32[]{:S(2)}, u32[]{:S(2)}) async-start(f32[8,32,128]{2,1,0:T(8,128)} %rows.1), calls=%async_computation.2 | async-start | bytes 262144 | tf_op jit(solution)/shard_map/all_to_all | solution.py:913
